TPU v7x, 512 devices: a whole 4x4x16 slice. The times are simulated.
512 devices in a mesh: dp: 32 (over z_lo, y), fsdp: 16 (over x, z_hi, core).
Axes of the slice: x: 4, y: 4, z: 16 (z_hi: 2, z_lo: 8; z = z_hi * 8 + z_lo), core: 2. Of those that a mesh axis runs over, the one named last changes fastest.
Arguments:
- image_feats: bfloat16 [9216, 1536], P('dp', 'fsdp'), may hold values from -6 to 6
- image_head: bfloat16 [1536, 1536], P('fsdp'), may hold values from -0.15625 to 0.15625
- text_embed: bfloat16 [9216, 1536], P('dp', 'fsdp'), may hold values from -6 to 6
- text_ids: int32 [9216], P('dp'), may hold values from 0 to 9215, each once
- logit_scale: float32 [], replicated, may hold values from 4 to 12
- logit_bias: float32 [], replicated, may hold values from -2 to 0
Outputs:
- feature_grad: bfloat16 [9216, 1536], P('dp', 'fsdp')
- head_grad: float32 [1536, 1536], P('fsdp')
- text_grad: bfloat16 [9216, 1536], P('dp', 'fsdp')
Inputs may be any that keep to these rules, and one draw needn't show every extreme that they name: `text_ids`: each of 0 to 9215 appears once.
All inputs are finite; a program needn't handle non-finite values.
Results may differ from a plain program's by a relative error of at most 0.029.
Values may be sent and summed in bfloat16 or wider, within the bound.
No kernel may reach another device: no remote copies, remote signals or barrier semaphores. Data moves between devices by JAX's collectives and lax.ppermute only.
A program may use at most 64 MiB of HBM per device.

v0:
```python
import jax
import jax.numpy as jnp
from jax import lax
from jax.sharding import PartitionSpec as P


def from_behind(value, axis, by):
    devices = lax.axis_size(axis)
    return lax.ppermute(value, axis, [(i, (i + by) % devices) for i in range(devices)])


def on_device(image_feats, image_head, text_embed, text_ids, logit_scale, logit_bias):
    rows = image_feats.shape[0]
    cycle = lax.axis_size("dp")
    group = lax.axis_size("fsdp")
    share = rows // group
    term = jnp.dot(image_feats, image_head, preferred_element_type=jnp.float32)
    embed = lax.psum_scatter(term, "fsdp", scatter_dimension=1, tiled=True)
    image_sq = lax.psum(jnp.sum(embed * embed, axis=1, keepdims=True), "fsdp")
    image_scale = lax.rsqrt(image_sq + 1e-06)
    image_unit = embed * image_scale
    image_low = lax.all_gather(image_unit.astype(jnp.bfloat16), "fsdp", axis=1, tiled=True)
    text_part = lax.all_to_all(text_embed, "fsdp", split_axis=0, concat_axis=1, tiled=True)
    text_vals = text_part.astype(jnp.float32)
    text_scale = lax.rsqrt(jnp.sum(text_vals * text_vals, axis=1, keepdims=True) + 1e-06)
    text_unit = text_vals * text_scale
    text_low = text_unit.astype(jnp.bfloat16)
    width = image_low.shape[1]
    my_ids = lax.dynamic_slice_in_dim(text_ids, lax.axis_index("fsdp") * share, share, 0)
    row_index = lax.axis_index("dp") * rows + lax.broadcasted_iota(jnp.int32, (rows, 1), 0)

    def coefs(block, ids):
        partial_value = jnp.einsum(
            "ie,je->ij", image_low, block, preferred_element_type=jnp.float32
        )
        logits = logit_scale * partial_value + logit_bias
        sign = jnp.where(row_index == ids[None, :], 1.0, -1.0).astype(jnp.float32)
        return (-sign * jax.nn.sigmoid(-sign * logits) * logit_scale).astype(jnp.bfloat16)

    def back(coef):
        return jnp.einsum("ij,ie->je", coef, image_low, preferred_element_type=jnp.float32)

    def turn(step, state):
        block, ids, acc, seen, coef_all = state
        coef = coefs(block, ids)
        acc = acc + back(coef)
        seen = lax.dynamic_update_index_in_dim(seen, block, step, 0)
        coef_all = lax.dynamic_update_index_in_dim(coef_all, coef, step, 0)
        block, ids = from_behind((block, ids), "dp", 1)
        acc = from_behind(acc, "dp", 1)
        return (block, ids, acc, seen, coef_all)

    start_state = (
        text_low,
        my_ids,
        jnp.zeros((share, width), jnp.float32),
        jnp.zeros((cycle, share, width), jnp.bfloat16),
        jnp.zeros((cycle, rows, share), jnp.bfloat16),
    )
    final = lax.fori_loop(0, cycle, turn, start_state)
    text_acc = final[2]
    unit_full = jnp.einsum("kis,kse->ie", final[4], final[3], preferred_element_type=jnp.float32)
    unit_grad = lax.psum_scatter(unit_full, "fsdp", scatter_dimension=1, tiled=True)
    image_dot = lax.psum(jnp.sum(image_unit * unit_grad, axis=1, keepdims=True), "fsdp")
    embed_grad = (image_scale * (unit_grad - image_unit * image_dot)).astype(jnp.bfloat16)
    text_dot = jnp.sum(text_unit * text_acc, axis=1, keepdims=True)
    text_rows_grad = (text_scale * (text_acc - text_unit * text_dot)).astype(jnp.bfloat16)
    text_grad = lax.all_to_all(text_rows_grad, "fsdp", split_axis=1, concat_axis=0, tiled=True)
    grads_all = lax.all_gather(embed_grad, "fsdp", axis=1, tiled=True)
    head_part = jnp.einsum("rw,re->we", image_feats, grads_all, preferred_element_type=jnp.float32)
    head_grad = lax.psum(head_part.astype(jnp.bfloat16), "dp").astype(jnp.float32)
    feature_grad = jnp.einsum(
        "re,we->rw", grads_all, image_head, preferred_element_type=jnp.float32
    ).astype(jnp.bfloat16)
    return (feature_grad, head_grad, text_grad)


def solution(mesh):
    placed = (P("dp", "fsdp"), P("fsdp", None), P("dp", "fsdp"), P("dp"), P(), P())
    return jax.shard_map(
        on_device,
        mesh=mesh,
        in_specs=placed,
        out_specs=(P("dp", "fsdp"), P("fsdp", None), P("dp", "fsdp")),
        check_vma=False,
    )
```

profile of v0, /device:TPU:1, one launch (start us, length us, event | category | flops | bytes accessed | tf_op | source)
XLA Modules:
  0.0 1662.8 jit_solution(16204829908092275635)
XLA Ops:
  11.6 19.1 %all-to-all-start = ((bf16[16,18,96]{2,1,0:T(8,128)(2,1)}), bf16[16,18,96]{2,1,0:T(8,128)(2,1)S(1)}, u32[]{:S(2)}, u32[]{:S(2)}) async-start(bf16[16,18,96]{2,1,0:T(8,128)(2,1)} %all_to_all.24), calls=%async_computation | async-start | bytes 196608 | tf_op jit(solution)/shard_map/all_to_all | solution.py:23
  31.6 13.8 all-to-all-done
  45.8 97.2 %reduce-scatter.7.cloned.1.call-done = f32[96,288]{1,0:T(8,128)} async-done(((f32[1536,288]{1,0:T(8,128)}), f32[96,288]{1,0:T(8,128)}) %reduce-scatter.7.cloned.1.call-update) | async-done | bytes 110608
  144.1 63.5 %psum.21 = f32[288,1]{0,1:T(1,128)S(1)} all-reduce(f32[288,1]{0,1:T(1,128)S(1)} %broadcast_in_dim.52), channel_id=1, replica_groups=mesh['dp'=32,'fsdp'=16] {'fsdp'}, use_global_device_ids=true, to_apply=%region_2.0 | all-reduce | flops 288 | bytes 2304 | tf_op jit(solution)/shard_map/psum | solution.py:19
  207.9 73.2 %all_gather.6 = bf16[288,1536]{0,1:T(8,128)(2,1)S(1)} all-gather(bf16[288,96]{0,1:T(8,128)(2,1)S(1)} %copy.19), channel_id=1, replica_groups=mesh['dp'=32,'fsdp'=16] {'fsdp'}, dimensions={1}, use_global_device_ids=true | all-gather | bytes 940032 | tf_op jit(solution)/shard_map/all_gather | solution.py:22
  281.6 667.7 %while.22 = (s32[]{:T(128)}, bf16[18,1536]{1,0:T(8,128)(2,1)S(1)}, s32[18]{0:T(128)S(1)}, f32[18,1536]{1,0:T(8,128)S(1)}, bf16[32,18,1536]{2,1,0:T(8,128)(2,1)},...) while((s32[]{:T(128)}, bf16[18,1536]{1,0:T(8,128)(2,1)S(1)}, ...), condition=%wide.region_5.6_spmd.clone, body=%wide.region_4.5_spmd.clone.sunk | while | flops 31940640 | bytes 3019685 | solution.py:60
  298.3 6.7 collective-permute-done.2
  320.8 4.7 collective-permute-done.2
  341.2 4.8 collective-permute-done.2
  361.7 5.5 collective-permute-done.2
  382.9 5.6 collective-permute-done.2
  404.3 5.7 collective-permute-done.2
  425.7 5.5 collective-permute-done.2
  446.9 5.1 collective-permute-done.2
  460.4 4.6 collective-permute-done.1
  467.8 4.7 collective-permute-done.2
  480.8 4.6 collective-permute-done.1
  488.2 4.8 collective-permute-done.2
  508.7 4.7 collective-permute-done.2
  529.1 4.7 collective-permute-done.2
  549.6 4.7 collective-permute-done.2
  570.0 4.7 collective-permute-done.2
  590.4 4.7 collective-permute-done.2
  603.4 4.8 collective-permute-done.1
  610.8 4.7 collective-permute-done.2
  623.9 4.9 collective-permute-done.1
  631.2 4.7 collective-permute-done.2
  644.3 4.6 collective-permute-done.1
  685.2 4.9 collective-permute-done.1
  692.5 4.7 collective-permute-done.2
  712.9 5.3 collective-permute-done.2
  734.9 5.5 collective-permute-done.2
  756.1 5.4 collective-permute-done.2
  769.9 4.6 collective-permute-done.1
  777.3 4.7 collective-permute-done.2
  797.7 4.7 collective-permute-done.2
  818.1 5.5 collective-permute-done.2
  839.3 5.6 collective-permute-done.2
  860.7 5.7 collective-permute-done.2
  882.1 5.5 collective-permute-done.2
  903.4 5.1 collective-permute-done.2
  924.2 4.7 collective-permute-done.2
  944.7 4.6 collective-permute-done.2
  955.0 38.4 %all-to-all-start.1 = ((bf16[18,16,96]{2,0,1:T(8,128)(2,1)}), bf16[18,16,96]{2,0,1:T(8,128)(2,1)S(1)}, u32[]{:S(2)}, u32[]{:S(2)}) async-start(bf16[18,16,96]{2,0,1:T(8,128)(2,1)} %copy.22), calls=%async_computation.1 | async-start | bytes 196608 | tf_op jit(solution)/shard_map/all_to_all | solution.py:68
  993.4 107.3 %reduce-scatter.9.cloned.1.call-done = f32[96,288]{1,0:T(8,128)} async-done(((f32[1536,288]{1,0:T(8,128)}), f32[96,288]{1,0:T(8,128)}) %reduce-scatter.9.cloned.1.call-update) | async-done | bytes 110608
  1102.0 63.5 %psum.22 = f32[288]{0:T(512)S(1)} all-reduce(f32[288]{0:T(512)S(1)} %multiply_reduce_fusion.1), channel_id=1, replica_groups=mesh['dp'=32,'fsdp'=16] {'fsdp'}, use_global_device_ids=true, to_apply=%region_8.9 | all-reduce | flops 288 | bytes 2304 | tf_op jit(solution)/shard_map/psum | solution.py:64
  1165.8 73.5 %all_gather.7 = bf16[288,1536]{0,1:T(8,128)(2,1)S(1)} all-gather(bf16[288,96]{0,1:T(8,128)(2,1)S(1)} %copy.21), channel_id=1, replica_groups=mesh['dp'=32,'fsdp'=16] {'fsdp'}, dimensions={1}, use_global_device_ids=true | all-gather | bytes 940032 | tf_op jit(solution)/shard_map/all_gather | solution.py:69
  1242.4 412.0 %all-reduce.2.cloned.1.call-done = bf16[96,1536]{1,0:T(8,128)(2,1)} async-done(((bf16[96,1536]{1,0:T(8,128)(2,1)}), bf16[96,1536]{1,0:T(8,128)(2,1)}) %all-reduce.2.cloned.1.call-update) | async-done | bytes 294928 | tf_op jit(solution)/shard_map/psum | solution.py:71
  (392 shorter events, 500.5 us)
Async XLA Ops:
  7.2 135.7 %reduce-scatter.7.cloned.1.call-start = ((), (), s32[]{:S(2)}) async-start(), calls=%async_computation.5 | async-start | bytes 2506752
  11.6 33.7 %all-to-all-start = ((bf16[16,18,96]{2,1,0:T(8,128)(2,1)}), bf16[16,18,96]{2,1,0:T(8,128)(2,1)S(1)}, u32[]{:S(2)}, u32[]{:S(2)}) async-start(bf16[16,18,96]{2,1,0:T(8,128)(2,1)} %all_to_all.24), calls=%async_computation | async-start | bytes 196608 | tf_op jit(solution)/shard_map/all_to_all | solution.py:23
  30.7 1070.1 %reduce-scatter.9.cloned.1.call-start = ((), (), s32[]{:S(2)}) async-start(), calls=%async_computation.6 | async-start | bytes 2506752
  284.5 13.8 collective-permute-start
  289.7 15.3 collective-permute-start.2
  306.9 13.8 collective-permute-start
  310.8 14.6 collective-permute-start.2
  327.4 13.8 collective-permute-start
  331.2 14.7 collective-permute-start.2
  347.9 13.8 collective-permute-start
  351.8 15.4 collective-permute-start.2
  369.1 13.8 collective-permute-start
  373.0 15.6 collective-permute-start.2
  390.5 13.8 collective-permute-start
  394.4 15.6 collective-permute-start.2
  415.8 15.4 collective-permute-start.2
  437.0 15.0 collective-permute-start.2
  457.8 14.6 collective-permute-start.2
  478.2 14.7 collective-permute-start.2
  498.8 14.6 collective-permute-start.2
  519.2 14.6 collective-permute-start.2
  539.6 14.6 collective-permute-start.2
  560.0 14.6 collective-permute-start.2
  580.5 14.6 collective-permute-start.2
  600.9 14.6 collective-permute-start.2
  621.3 14.6 collective-permute-start.2
  637.9 14.0 collective-permute-start
  641.7 14.6 collective-permute-start.2
  658.3 14.9 collective-permute-start
  662.2 14.6 collective-permute-start.2
  682.6 14.6 collective-permute-start.2
  703.0 15.3 collective-permute-start.2
  720.2 14.7 collective-permute-start
  724.1 16.3 collective-permute-start.2
  746.1 15.4 collective-permute-start.2
  763.5 13.8 collective-permute-start
  767.3 14.6 collective-permute-start.2
  787.8 14.6 collective-permute-start.2
  808.2 15.4 collective-permute-start.2
  829.4 15.6 collective-permute-start.2
  850.8 15.6 collective-permute-start.2
  872.2 15.4 collective-permute-start.2
  893.4 15.0 collective-permute-start.2
  914.3 14.6 collective-permute-start.2
  930.8 13.9 collective-permute-start
  934.7 14.7 collective-permute-start.2
  955.0 285.6 %all-to-all-start.1 = ((bf16[18,16,96]{2,0,1:T(8,128)(2,1)}), bf16[18,16,96]{2,0,1:T(8,128)(2,1)S(1)}, u32[]{:S(2)}, u32[]{:S(2)}) async-start(bf16[18,16,96]{2,0,1:T(8,128)(2,1)} %copy.22), calls=%async_computation.1 | async-start | bytes 196608 | tf_op jit(solution)/shard_map/all_to_all | solution.py:68
  993.4 661.1 %all-reduce.2.cloned.1.call-start = ((), (), s32[]{:S(2)}) async-start(), calls=%async_computation.4 | async-start | bytes 589824 | tf_op jit(solution)/shard_map/psum | solution.py:71
  (56 other events, 996.5 us)
Sparse Core Ops, SparseCore 0:
  12.9 129.9 reduce-scatter.6
  954.0 146.7 reduce-scatter.8
  1240.7 413.7 all-reduce.1
where the time goes:
time: 1680 us; the launch traced here: 1660 us
  waiting for transfers between devices  1030 us (61%)
  blocking collectives  274 us (16%)
  starting transfers between devices  245 us (15%)
  matrix products  71.1 us (4%)
  local copies, waits for them, and re-layouts  27.4 us (2%)
    psum x1, waiting for transfers between devices, on_device(): lax.psum(head_part.astype(jnp.bfloat16), 'dp').astype(jnp.float32)  412 us
    ppermute x96, waiting for transfers between devices, from_behind(): lax.ppermute(value, axis, [(i, (i + by) % devices) for i in range(devices)])  396 us
    unnamed x5, waiting for transfers between devices  205 us
    ppermute x96, starting transfers between devices, from_behind(): lax.ppermute(value, axis, [(i, (i + by) % devices) for i in range(devices)])  187 us
    all_gather x1, blocking collectives, on_device(): grads_all = lax.all_gather(embed_grad, 'fsdp', axis=1, tiled=True)  73.5 us
    all_gather x1, blocking collectives, on_device(): lax.all_gather(image_unit.astype(jnp.bfloat16), 'fsdp', axis=1, tiled=True)  73.2 us
    psum x1, blocking collectives, on_device(): lax.psum(jnp.sum(image_unit * unit_grad, axis=1, keepdims=True), 'fsdp')  63.5 us
    psum x1, blocking collectives, on_device(): image_sq = lax.psum(jnp.sum(embed * embed, axis=1, keepdims=True), 'fsdp')  63.5 us
  transfers between devices with their start and end apart: 101, of which 100 were waited for; matrix products, arithmetic and copies ran while one was open for 5% of the time, Pallas kernels for 0%

commit v1 on v0

v1 whole, which is shorter than its diff:
```python
import jax
import jax.numpy as jnp
from jax import lax
from jax.sharding import PartitionSpec as P

F32, BF16 = jnp.float32, jnp.bfloat16
X, ZH, CORE = 4, 2, 2
ZL, Y = 8, 4
PLANE = [[x * 4 + zh * 2 + c for x in range(X) for c in range(CORE)] for zh in range(ZH)]
LINE = [[z * Y + y for z in range(ZL)] for y in range(Y)]
RING = [[z * Y + y for y in range(Y)] for z in range(ZL)]
PAIR = [(i, i ^ 2) for i in range(16)]


def swap(value, axis, groups=None):
    return lax.all_to_all(value, axis, 0, 0, axis_index_groups=groups, tiled=True)


def spread(value, axis, groups, size):
    copies = jnp.broadcast_to(value[None], (size,) + value.shape)
    return swap(copies, axis, groups)


def on_device(image_feats, image_head, text_embed, text_ids, logit_scale, logit_bias):
    rows, width = image_feats.shape
    embed_width = image_head.shape[1]
    cycle = lax.axis_size("dp")
    group = lax.axis_size("fsdp")
    plane = X * CORE
    own = rows // plane
    held = -(-own // 8) * 8
    share = rows // group
    d = lax.axis_index("dp")
    f = lax.axis_index("fsdp")

    text_part = swap(text_embed.reshape(group, share, width), "fsdp")
    text_vals = text_part.transpose(1, 0, 2).reshape(share, embed_width).astype(F32)
    text_scale = lax.rsqrt(jnp.sum(text_vals * text_vals, axis=1, keepdims=True) + 1e-06)
    text_unit = text_vals * text_scale
    my_ids = lax.dynamic_slice_in_dim(text_ids, f * share, share, 0)
    marks = jnp.stack([my_ids // 128, my_ids % 128], axis=1).astype(BF16)
    marks = jnp.pad(marks, ((0, 0), (0, 126)))
    text_row = jnp.concatenate([text_unit.astype(BF16), marks], axis=1)
    line = spread(text_row, "dp", LINE, ZL).reshape(ZL * share, -1)
    texts = spread(line, "dp", RING, Y).reshape(cycle * share, -1)
    text_low = texts[:, :embed_width]
    ids = texts[:, embed_width].astype(jnp.int32) * 128 + texts[:, embed_width + 1].astype(jnp.int32)

    feats = jnp.pad(image_feats.reshape(plane, own, width), ((0, 0), (0, held - own), (0, 0)))
    feats = feats.reshape(plane * held, width)
    term = jnp.dot(feats, image_head, preferred_element_type=F32).astype(BF16)
    half = swap(term.reshape(plane, held, embed_width), "fsdp", PLANE)
    half = jnp.sum(half.astype(F32), axis=0).astype(BF16)
    embed = half.astype(F32) + lax.ppermute(half, "fsdp", PAIR).astype(F32)
    image_scale = lax.rsqrt(jnp.sum(embed * embed, axis=1, keepdims=True) + 1e-06)
    image_unit = embed * image_scale
    image_low = spread(image_unit.astype(BF16), "fsdp", PLANE, plane).reshape(plane * held, embed_width)

    partial_value = jnp.einsum("ie,je->ij", image_low, text_low, preferred_element_type=F32)
    logits = logit_scale * partial_value + logit_bias
    row = lax.broadcasted_iota(jnp.int32, (plane, held), 1)
    row_index = d * rows + lax.broadcasted_iota(jnp.int32, (plane, held), 0) * own + row
    row_index = jnp.where(row < own, row_index, -1).reshape(plane * held, 1)
    sign = jnp.where(row_index == ids[None, :], 1.0, -1.0).astype(F32)
    coef = (-sign * jax.nn.sigmoid(-sign * logits) * logit_scale).astype(BF16)
    unit_part = jnp.einsum("ij,je->ie", coef, text_low, preferred_element_type=F32).astype(BF16)
    text_acc = jnp.einsum("ij,ie->je", coef, image_low, preferred_element_type=F32).astype(BF16)

    back = swap(unit_part.reshape(plane, held, embed_width), "fsdp", PLANE)
    back = jnp.sum(back.astype(F32), axis=0).astype(BF16)
    unit_grad = back.astype(F32) + lax.ppermute(back, "fsdp", PAIR).astype(F32)
    image_dot = jnp.sum(image_unit * unit_grad, axis=1, keepdims=True)
    embed_grad = (image_scale * (unit_grad - image_unit * image_dot)).astype(BF16)
    grads = spread(embed_grad, "fsdp", PLANE, plane).reshape(plane * held, embed_width)
    lanes = embed_width // 128
    head_part = jnp.einsum("rw,re->we", feats, grads, preferred_element_type=F32).astype(BF16)
    head_part = head_part.reshape(width, lanes, 128).transpose(1, 0, 2).reshape(cycle, -1, 128)
    head_sum = jnp.sum(swap(head_part, "dp").astype(F32), axis=0).astype(BF16)
    head_all = spread(head_sum, "dp", None, cycle)
    head_grad = head_all.reshape(lanes, width, 128).transpose(1, 0, 2).reshape(width, embed_width).astype(F32)
    feature_grad = jnp.einsum("re,we->rw", grads, image_head, preferred_element_type=F32).astype(BF16)
    feature_grad = feature_grad.reshape(plane, held, width)[:, :own].reshape(rows, width)

    text_acc = swap(text_acc.reshape(Y, ZL * share, embed_width), "dp", RING)
    text_acc = jnp.sum(text_acc.astype(F32), axis=0).astype(BF16)
    text_acc = swap(text_acc.reshape(ZL, share, embed_width), "dp", LINE)
    text_acc = jnp.sum(text_acc.astype(F32), axis=0)
    text_dot = jnp.sum(text_unit * text_acc, axis=1, keepdims=True)
    text_rows = (text_scale * (text_acc - text_unit * text_dot)).astype(BF16)
    text_rows = text_rows.reshape(share, group, width).transpose(1, 0, 2)
    text_grad = swap(text_rows, "fsdp").reshape(rows, width)
    return (feature_grad, head_grad, text_grad)


def solution(mesh):
    placed = (P("dp", "fsdp"), P("fsdp", None), P("dp", "fsdp"), P("dp"), P(), P())
    return jax.shard_map(
        on_device,
        mesh=mesh,
        in_specs=placed,
        out_specs=(P("dp", "fsdp"), P("fsdp", None), P("dp", "fsdp")),
        check_vma=False,
    )
```

time: 1680 us -> 326 us (0.19)
  waiting for transfers between devices: 1030 us -> 195 us
  blocking collectives: 274 us -> 0 us
  starting transfers between devices: 245 us -> 97 us
  matrix products: 71.1 us -> 10.4 us
    psum x1 -> x0, waiting for transfers between devices: 412 us -> none  [on_device(): lax.psum(head_part.astype(jnp.bfloat16), 'dp').astype(jnp.float32)]
    ppermute x96 -> x2, waiting for transfers between devices: 396 us -> 24.4 us  [the longest x1 12.2 us: on_device(): embed = half.astype(F32) + lax.ppermute(half, 'fsdp', PAIR).astype(F32)]
    unnamed x5 -> x0, waiting for transfers between devices: 205 us -> none
    ppermute x96 -> x2, starting transfers between devices: 187 us -> 4.29 us  [the longest x1 2.15 us: on_device(): embed = half.astype(F32) + lax.ppermute(half, 'fsdp', PAIR).astype(F32)]
    all_to_all x2 -> x12, waiting for transfers between devices: 13.8 us -> 171 us  [swap(): lax.all_to_all(value, axis, 0, 0, axis_index_groups=groups, tiled=True)]
    all_gather x2 -> x0, blocking collectives: 147 us -> none  [the longest x1 73.5 us: on_device(): grads_all = lax.all_gather(embed_grad, 'fsdp', axis=1, tiled=True)]
    psum x2 -> x0, blocking collectives: 127 us -> none  [the longest x1 63.5 us: on_device(): lax.psum(jnp.sum(image_unit * unit_grad, axis=1, keepdims=True), 'fsdp')]
    dot_general x67 -> x6, matrix products: 68.3 us -> 10.4 us  [the longest x1 3.38 us: on_device(): jnp.einsum('ij,je->ie', coef, text_low, preferred_element_type=F32)]
  transfers between devices with their start and end apart: 101 -> 14, of which waited for: 100 -> 14; matrix products, arithmetic and copies ran while one was open for 5% -> 5% of each run, Pallas kernels for 0% -> 0%
where the time goes in v1:
time: 326 us; the launch traced here: 323 us
  waiting for transfers between devices  195 us (60%)
  starting transfers between devices  97 us (30%)
  local copies, waits for them, and re-layouts  12.8 us (4%)
  matrix products  10.4 us (3%)
  other arithmetic  5.5 us (2%)
    all_to_all x12, waiting for transfers between devices, swap(): lax.all_to_all(value, axis, 0, 0, axis_index_groups=groups, tiled=True)  171 us
    all_to_all x12, starting transfers between devices, swap(): lax.all_to_all(value, axis, 0, 0, axis_index_groups=groups, tiled=True)  92.7 us
    ppermute x1, waiting for transfers between devices, on_device(): embed = half.astype(F32) + lax.ppermute(half, 'fsdp', PAIR).astype(F32)  12.2 us
    ppermute x1, waiting for transfers between devices, on_device(): unit_grad = back.astype(F32) + lax.ppermute(back, 'fsdp', PAIR).astype(F32)  12.2 us
  transfers between devices with their start and end apart: 14, of which 14 were waited for; matrix products, arithmetic and copies ran while one was open for 5% of the time, Pallas kernels for 0%

profile of v1, /device:TPU:1, one launch (start us, length us, event | category | flops | bytes accessed | tf_op | source)
XLA Modules:
  0.0 322.9 jit_solution(3097880115818140108)
XLA Ops:
  0.7 1.6 reshape.149
  2.3 19.1 %all-to-all-start.1 = ((bf16[16,18,96]{2,1,0:T(8,128)(2,1)}), bf16[16,18,96]{2,1,0:T(8,128)(2,1)S(1)}, u32[]{:S(2)}, u32[]{:S(2)}) async-start(bf16[16,18,96]{2,1,0:T(8,128)(2,1)} %reshape.149), calls=%async_computation.1 | async-start | bytes 196608 | tf_op jit(solution)/shard_map/all_to_all | solution.py:16
  21.3 0.8 convert_bitcast_fusion.1
  22.2 13.7 %all-to-all-done.1 = bf16[16,18,96]{2,1,0:T(8,128)(2,1)S(1)} async-done(((bf16[16,18,96]{2,1,0:T(8,128)(2,1)}), bf16[16,18,96]{2,1,0:T(8,128)(2,1)S(1)}, u32[]{:S(2)}, u32[]{:S(2)}) %all-to-all-start.1) | async-done | bytes 55328 | tf_op jit(solution)/shard_map/all_to_all | solution.py:16
  36.4 0.9 broadcast_in_dim.25
  37.3 5.0 %all-to-all-start.2 = ((bf16[8,18,1664]{2,1,0:T(8,128)(2,1)}), bf16[8,18,1664]{2,1,0:T(8,128)(2,1)S(1)}, u32[]{:S(2)}, u32[]{:S(2)}) async-start(bf16[8,18,1664]{2,1,0:T(8,128)(2,1)} %broadcast_in_dim.25), calls=%async_computation.2 | async-start | bytes 1277952 | tf_op jit(solution)/shard_map/all_to_all | solution.py:16
  42.4 1.4 convolution_convert_fusion.2
  43.8 22.6 %all-to-all-done.2 = bf16[8,18,1664]{2,1,0:T(8,128)(2,1)S(1)} async-done(((bf16[8,18,1664]{2,1,0:T(8,128)(2,1)}), bf16[8,18,1664]{2,1,0:T(8,128)(2,1)S(1)}, u32[]{:S(2)}, u32[]{:S(2)}) %all-to-all-start.2) | async-done | bytes 479264 | tf_op jit(solution)/shard_map/all_to_all | solution.py:16
  66.3 14.0 %all-to-all-start = ((bf16[8,40,1536]{2,1,0:T(8,128)(2,1)}), bf16[8,40,1536]{2,1,0:T(8,128)(2,1)S(1)}, u32[]{:S(2)}, u32[]{:S(2)}) async-start(bf16[8,40,1536]{2,1,0:T(8,128)(2,1)} %bitcast.1), calls=%async_computation | async-start | bytes 1966080 | tf_op jit(solution)/shard_map/all_to_all | solution.py:16
  80.5 14.3 %all-to-all-done = bf16[8,40,1536]{2,1,0:T(8,128)(2,1)S(1)} async-done(((bf16[8,40,1536]{2,1,0:T(8,128)(2,1)}), bf16[8,40,1536]{2,1,0:T(8,128)(2,1)S(1)}, u32[]{:S(2)}, u32[]{:S(2)}) %all-to-all-start) | async-done | bytes 983072 | tf_op jit(solution)/shard_map/all_to_all | solution.py:16
  94.8 1.4 broadcast_in_dim.27
  96.2 4.4 %all-to-all-start.3 = ((bf16[4,144,1664]{2,1,0:T(8,128)(2,1)}), bf16[4,144,1664]{2,1,0:T(8,128)(2,1)}, u32[]{:S(2)}, u32[]{:S(2)}) async-start(bf16[4,144,1664]{2,1,0:T(8,128)(2,1)} %broadcast_in_dim.27), calls=%async_computation.3 | async-start | bytes 3833856 | tf_op jit(solution)/shard_map/all_to_all | solution.py:16
  100.8 2.1 collective-permute-start
  102.9 12.2 %collective-permute-done = bf16[40,1536]{1,0:T(8,128)(2,1)S(1)} collective-permute-done((bf16[40,1536]{1,0:T(8,128)(2,1)S(1)}, bf16[40,1536]{1,0:T(8,128)(2,1)S(1)}, u32[]{:S(2)}, u32[]{:S(2)}) %collective-permute-start) | collective-permute-done | bytes 122912 | tf_op jit(solution)/shard_map/ppermute | solution.py:54
  115.4 8.8 %all-to-all-done.3 = bf16[4,144,1664]{2,1,0:T(8,128)(2,1)} async-done(((bf16[4,144,1664]{2,1,0:T(8,128)(2,1)}), bf16[4,144,1664]{2,1,0:T(8,128)(2,1)}, u32[]{:S(2)}, u32[]{:S(2)}) %all-to-all-start.3) | async-done | bytes 1916960 | tf_op jit(solution)/shard_map/all_to_all | solution.py:16
  124.2 1.0 broadcast_in_dim.54
  125.2 5.3 %all-to-all-start.4 = ((bf16[8,40,1536]{2,1,0:T(8,128)(2,1)}), bf16[8,40,1536]{2,1,0:T(8,128)(2,1)S(1)}, u32[]{:S(2)}, u32[]{:S(2)}) async-start(bf16[8,40,1536]{2,1,0:T(8,128)(2,1)} %broadcast_in_dim.54), calls=%async_computation.4 | async-start | bytes 1966080 | tf_op jit(solution)/shard_map/all_to_all | solution.py:16
  132.0 1.2 add_reduce_fusion
  133.3 11.7 %all-to-all-done.4 = bf16[8,40,1536]{2,1,0:T(8,128)(2,1)S(1)} async-done(((bf16[8,40,1536]{2,1,0:T(8,128)(2,1)}), bf16[8,40,1536]{2,1,0:T(8,128)(2,1)S(1)}, u32[]{:S(2)}, u32[]{:S(2)}) %all-to-all-start.4) | async-done | bytes 983072 | tf_op jit(solution)/shard_map/all_to_all | solution.py:16
  144.9 2.6 fusion.31
  147.5 3.4 %convolution_convert_fusion.1 = bf16[320,1536]{1,0:T(8,128)(2,1)} fusion(bf16[320,576]{1,0:T(8,128)(2,1)S(1)} %fusion.31, bf16[576,1664]{1,0:T(8,128)(2,1)} %bitcast.5), kind=kOutput, calls=%fused_computation.1 | convolution fusion | flops 566722560 | bytes 3121152 | tf_op jit(solution)/shard_map/ij,je->ie/dot_general | solution.py:66
  150.9 4.3 %all-to-all-start.5 = ((bf16[8,40,1536]{2,1,0:T(8,128)(2,1)}), bf16[8,40,1536]{2,1,0:T(8,128)(2,1)S(1)}, u32[]{:S(2)}, u32[]{:S(2)}) async-start(bf16[8,40,1536]{2,1,0:T(8,128)(2,1)} %bitcast.52), calls=%async_computation.5 | async-start | bytes 1966080 | tf_op jit(solution)/shard_map/all_to_all | solution.py:16
  155.2 2.3 convolution_convert_fusion
  157.6 12.1 %all-to-all-done.5 = bf16[8,40,1536]{2,1,0:T(8,128)(2,1)S(1)} async-done(((bf16[8,40,1536]{2,1,0:T(8,128)(2,1)}), bf16[8,40,1536]{2,1,0:T(8,128)(2,1)S(1)}, u32[]{:S(2)}, u32[]{:S(2)}) %all-to-all-start.5) | async-done | bytes 983072 | tf_op jit(solution)/shard_map/all_to_all | solution.py:16
  169.7 3.6 %all-to-all-start.9 = ((bf16[4,144,1536]{2,1,0:T(8,128)(2,1)}), bf16[4,144,1536]{2,1,0:T(8,128)(2,1)S(1)}, u32[]{:S(2)}, u32[]{:S(2)}) async-start(bf16[4,144,1536]{2,1,0:T(8,128)(2,1)} %bitcast.48), calls=%async_computation.9 | async-start | bytes 3538944 | tf_op jit(solution)/shard_map/all_to_all | solution.py:16
  173.4 2.1 collective-permute-start.1
  175.5 12.2 %collective-permute-done.1 = bf16[40,1536]{1,0:T(8,128)(2,1)S(1)} collective-permute-done((bf16[40,1536]{1,0:T(8,128)(2,1)S(1)}, bf16[40,1536]{1,0:T(8,128)(2,1)S(1)}, u32[]{:S(2)}, u32[]{:S(2)}) %collective-permute-start.1) | collective-permute-done | bytes 122912 | tf_op jit(solution)/shard_map/ppermute | solution.py:71
  188.1 7.1 %all-to-all-done.9 = bf16[4,144,1536]{2,1,0:T(8,128)(2,1)S(1)} async-done(((bf16[4,144,1536]{2,1,0:T(8,128)(2,1)}), bf16[4,144,1536]{2,1,0:T(8,128)(2,1)S(1)}, u32[]{:S(2)}, u32[]{:S(2)}) %all-to-all-start.9) | async-done | bytes 1769504 | tf_op jit(solution)/shard_map/all_to_all | solution.py:16
  195.2 1.0 broadcast_in_dim.55
  196.2 5.2 %all-to-all-start.6 = ((bf16[8,40,1536]{2,1,0:T(8,128)(2,1)}), bf16[8,40,1536]{2,1,0:T(8,128)(2,1)S(1)}, u32[]{:S(2)}, u32[]{:S(2)}) async-start(bf16[8,40,1536]{2,1,0:T(8,128)(2,1)} %broadcast_in_dim.55), calls=%async_computation.6 | async-start | bytes 1966080 | tf_op jit(solution)/shard_map/all_to_all | solution.py:16
  201.5 1.2 reduce_sum.101
  202.6 2.0 reshape.159
  204.6 11.3 %all-to-all-done.6 = bf16[8,40,1536]{2,1,0:T(8,128)(2,1)S(1)} async-done(((bf16[8,40,1536]{2,1,0:T(8,128)(2,1)}), bf16[8,40,1536]{2,1,0:T(8,128)(2,1)S(1)}, u32[]{:S(2)}, u32[]{:S(2)}) %all-to-all-start.6) | async-done | bytes 983072 | tf_op jit(solution)/shard_map/all_to_all | solution.py:16
  215.9 4.0 %all-to-all-start.10 = ((bf16[8,18,1536]{2,1,0:T(8,128)(2,1)}), bf16[8,18,1536]{2,1,0:T(8,128)(2,1)S(1)}, u32[]{:S(2)}, u32[]{:S(2)}) async-start(bf16[8,18,1536]{2,1,0:T(8,128)(2,1)} %reshape.159), calls=%async_computation.10 | async-start | bytes 1179648 | tf_op jit(solution)/shard_map/all_to_all | solution.py:16
  220.6 0.8 reshape.157
  221.4 21.0 %all-to-all-done.10 = bf16[8,18,1536]{2,1,0:T(8,128)(2,1)S(1)} async-done(((bf16[8,18,1536]{2,1,0:T(8,128)(2,1)}), bf16[8,18,1536]{2,1,0:T(8,128)(2,1)S(1)}, u32[]{:S(2)}, u32[]{:S(2)}) %all-to-all-start.10) | async-done | bytes 442400 | tf_op jit(solution)/shard_map/all_to_all | solution.py:16
  242.3 14.1 %all-to-all-start.7 = ((bf16[32,36,128]{2,1,0:T(8,128)(2,1)}), bf16[32,36,128]{2,1,0:T(8,128)(2,1)S(1)}, u32[]{:S(2)}, u32[]{:S(2)}) async-start(bf16[32,36,128]{2,1,0:T(8,128)(2,1)} %reshape.157), calls=%async_computation.7 | async-start | bytes 655360 | tf_op jit(solution)/shard_map/all_to_all | solution.py:16
  256.9 0.8 fusion.43
  257.6 17.1 %all-to-all-done.7 = bf16[32,36,128]{2,1,0:T(8,128)(2,1)S(1)} async-done(((bf16[32,36,128]{2,1,0:T(8,128)(2,1)}), bf16[32,36,128]{2,1,0:T(8,128)(2,1)S(1)}, u32[]{:S(2)}, u32[]{:S(2)}) %all-to-all-start.7) | async-done | bytes 294944 | tf_op jit(solution)/shard_map/all_to_all | solution.py:16
  274.7 7.7 %all-to-all-start.11 = ((bf16[16,18,96]{2,1,0:T(8,128)(2,1)}), bf16[16,18,96]{2,1,0:T(8,128)(2,1)S(1)}, u32[]{:S(2)}, u32[]{:S(2)}) async-start(bf16[16,18,96]{2,1,0:T(8,128)(2,1)} %fusion.43), calls=%async_computation.11 | async-start | bytes 196608 | tf_op jit(solution)/shard_map/all_to_all | solution.py:16
  282.5 14.5 %all-to-all-done.11 = bf16[16,18,96]{2,1,0:T(8,128)(2,1)S(1)} async-done(((bf16[16,18,96]{2,1,0:T(8,128)(2,1)}), bf16[16,18,96]{2,1,0:T(8,128)(2,1)S(1)}, u32[]{:S(2)}, u32[]{:S(2)}) %all-to-all-start.11) | async-done | bytes 55328 | tf_op jit(solution)/shard_map/all_to_all | solution.py:16
  297.1 0.8 broadcast_in_dim.56
  297.8 5.9 %all-to-all-start.8 = ((bf16[32,36,128]{2,1,0:T(8,128)(2,1)}), bf16[32,36,128]{2,1,0:T(8,128)(2,1)S(1)}, u32[]{:S(2)}, u32[]{:S(2)}) async-start(bf16[32,36,128]{2,1,0:T(8,128)(2,1)} %broadcast_in_dim.56), calls=%async_computation.8 | async-start | bytes 655360 | tf_op jit(solution)/shard_map/all_to_all | solution.py:16
  303.7 0.4 convolution_convert_fusion.3
  304.3 0.7 reshape.155
  305.0 0.7 reshape.160
  305.6 16.4 %all-to-all-done.8 = bf16[32,36,128]{2,1,0:T(8,128)(2,1)S(1)} async-done(((bf16[32,36,128]{2,1,0:T(8,128)(2,1)}), bf16[32,36,128]{2,1,0:T(8,128)(2,1)S(1)}, u32[]{:S(2)}, u32[]{:S(2)}) %all-to-all-start.8) | async-done | bytes 294944 | tf_op jit(solution)/shard_map/all_to_all | solution.py:16
  322.1 0.9 copy_bitcast_fusion
  (41 shorter events, 3.1 us)
Async XLA Ops:
  0.6 41.8 %copy-start = (bf16[96,1536]{1,0:T(8,128)(2,1)S(1)}, bf16[96,1536]{1,0:T(8,128)(2,1)}, u32[]{:S(2)}) copy-start(bf16[96,1536]{1,0:T(8,128)(2,1)} %param.7) | copy-start | bytes 884740
  0.6 41.7 %copy-start.3 = (bf16[288,96]{1,0:T(8,128)(2,1)S(1)}, bf16[288,96]{1,0:T(8,128)(2,1)}, u32[]{:S(2)}) copy-start(bf16[288,96]{1,0:T(8,128)(2,1)} %param.6) | copy-start | bytes 165892
  2.3 33.7 %all-to-all-start.1 = ((bf16[16,18,96]{2,1,0:T(8,128)(2,1)}), bf16[16,18,96]{2,1,0:T(8,128)(2,1)S(1)}, u32[]{:S(2)}, u32[]{:S(2)}) async-start(bf16[16,18,96]{2,1,0:T(8,128)(2,1)} %reshape.149), calls=%async_computation.1 | async-start | bytes 196608 | tf_op jit(solution)/shard_map/all_to_all | solution.py:16
  37.3 29.1 %all-to-all-start.2 = ((bf16[8,18,1664]{2,1,0:T(8,128)(2,1)}), bf16[8,18,1664]{2,1,0:T(8,128)(2,1)S(1)}, u32[]{:S(2)}, u32[]{:S(2)}) async-start(bf16[8,18,1664]{2,1,0:T(8,128)(2,1)} %broadcast_in_dim.25), calls=%async_computation.2 | async-start | bytes 1277952 | tf_op jit(solution)/shard_map/all_to_all | solution.py:16
  42.4 24.0 %copy-start.1 = (bf16[8,36,96]{2,1,0:T(8,128)(2,1)}, bf16[8,36,96]{2,1,0:T(8,128)(2,1)S(1)}, u32[]{:S(2)}) copy-start(bf16[8,36,96]{2,1,0:T(8,128)(2,1)S(1)} %reshape.146) | copy-start | bytes 165892
  66.3 28.5 %all-to-all-start = ((bf16[8,40,1536]{2,1,0:T(8,128)(2,1)}), bf16[8,40,1536]{2,1,0:T(8,128)(2,1)S(1)}, u32[]{:S(2)}, u32[]{:S(2)}) async-start(bf16[8,40,1536]{2,1,0:T(8,128)(2,1)} %bitcast.1), calls=%async_computation | async-start | bytes 1966080 | tf_op jit(solution)/shard_map/all_to_all | solution.py:16
  96.2 28.0 %all-to-all-start.3 = ((bf16[4,144,1664]{2,1,0:T(8,128)(2,1)}), bf16[4,144,1664]{2,1,0:T(8,128)(2,1)}, u32[]{:S(2)}, u32[]{:S(2)}) async-start(bf16[4,144,1664]{2,1,0:T(8,128)(2,1)} %broadcast_in_dim.27), calls=%async_computation.3 | async-start | bytes 3833856 | tf_op jit(solution)/shard_map/all_to_all | solution.py:16
  100.8 14.4 %collective-permute-start = (bf16[40,1536]{1,0:T(8,128)(2,1)S(1)}, bf16[40,1536]{1,0:T(8,128)(2,1)S(1)}, u32[]{:S(2)}, u32[]{:S(2)}) collective-permute-start(bf16[40,1536]{1,0:T(8,128)(2,1)S(1)} %reduce_sum.95), channel_id=1, source_target_pairs={{0,2},{1,3},{2,0},{3,1},{4,6},{5,7},{6,4},{7,5},{8,10},{9,11},{10,... | collective-permute-start | bytes 368648 | tf_op jit(solution)/shard_map/ppermute | solution.py:54
  125.2 19.7 %all-to-all-start.4 = ((bf16[8,40,1536]{2,1,0:T(8,128)(2,1)}), bf16[8,40,1536]{2,1,0:T(8,128)(2,1)S(1)}, u32[]{:S(2)}, u32[]{:S(2)}) async-start(bf16[8,40,1536]{2,1,0:T(8,128)(2,1)} %broadcast_in_dim.54), calls=%async_computation.4 | async-start | bytes 1966080 | tf_op jit(solution)/shard_map/all_to_all | solution.py:16
  150.9 18.7 %all-to-all-start.5 = ((bf16[8,40,1536]{2,1,0:T(8,128)(2,1)}), bf16[8,40,1536]{2,1,0:T(8,128)(2,1)S(1)}, u32[]{:S(2)}, u32[]{:S(2)}) async-start(bf16[8,40,1536]{2,1,0:T(8,128)(2,1)} %bitcast.52), calls=%async_computation.5 | async-start | bytes 1966080 | tf_op jit(solution)/shard_map/all_to_all | solution.py:16
  169.7 25.6 %all-to-all-start.9 = ((bf16[4,144,1536]{2,1,0:T(8,128)(2,1)}), bf16[4,144,1536]{2,1,0:T(8,128)(2,1)S(1)}, u32[]{:S(2)}, u32[]{:S(2)}) async-start(bf16[4,144,1536]{2,1,0:T(8,128)(2,1)} %bitcast.48), calls=%async_computation.9 | async-start | bytes 3538944 | tf_op jit(solution)/shard_map/all_to_all | solution.py:16
  173.4 14.4 %collective-permute-start.1 = (bf16[40,1536]{1,0:T(8,128)(2,1)S(1)}, bf16[40,1536]{1,0:T(8,128)(2,1)S(1)}, u32[]{:S(2)}, u32[]{:S(2)}) collective-permute-start(bf16[40,1536]{1,0:T(8,128)(2,1)S(1)} %reduce_sum.98), channel_id=1, source_target_pairs={{0,2},{1,3},{2,0},{3,1},{4,6},{5,7},{6,4},{7,5},{8,10},{9,11},{10,... | collective-permute-start | bytes 368648 | tf_op jit(solution)/shard_map/ppermute | solution.py:71
  196.2 19.6 %all-to-all-start.6 = ((bf16[8,40,1536]{2,1,0:T(8,128)(2,1)}), bf16[8,40,1536]{2,1,0:T(8,128)(2,1)S(1)}, u32[]{:S(2)}, u32[]{:S(2)}) async-start(bf16[8,40,1536]{2,1,0:T(8,128)(2,1)} %broadcast_in_dim.55), calls=%async_computation.6 | async-start | bytes 1966080 | tf_op jit(solution)/shard_map/all_to_all | solution.py:16
  201.5 18.4 %copy-start.2 = (bf16[8,36,96]{2,1,0:T(8,128)(2,1)S(1)}, bf16[8,36,96]{2,1,0:T(8,128)(2,1)}, u32[]{:S(2)}) copy-start(bf16[8,36,96]{2,1,0:T(8,128)(2,1)} %copy-done.1) | copy-start | bytes 165892
  215.9 26.5 %all-to-all-start.10 = ((bf16[8,18,1536]{2,1,0:T(8,128)(2,1)}), bf16[8,18,1536]{2,1,0:T(8,128)(2,1)S(1)}, u32[]{:S(2)}, u32[]{:S(2)}) async-start(bf16[8,18,1536]{2,1,0:T(8,128)(2,1)} %reshape.159), calls=%async_computation.10 | async-start | bytes 1179648 | tf_op jit(solution)/shard_map/all_to_all | solution.py:16
  242.3 32.4 %all-to-all-start.7 = ((bf16[32,36,128]{2,1,0:T(8,128)(2,1)}), bf16[32,36,128]{2,1,0:T(8,128)(2,1)S(1)}, u32[]{:S(2)}, u32[]{:S(2)}) async-start(bf16[32,36,128]{2,1,0:T(8,128)(2,1)} %reshape.157), calls=%async_computation.7 | async-start | bytes 655360 | tf_op jit(solution)/shard_map/all_to_all | solution.py:16
  274.7 22.4 %all-to-all-start.11 = ((bf16[16,18,96]{2,1,0:T(8,128)(2,1)}), bf16[16,18,96]{2,1,0:T(8,128)(2,1)S(1)}, u32[]{:S(2)}, u32[]{:S(2)}) async-start(bf16[16,18,96]{2,1,0:T(8,128)(2,1)} %fusion.43), calls=%async_computation.11 | async-start | bytes 196608 | tf_op jit(solution)/shard_map/all_to_all | solution.py:16
  297.8 24.2 %all-to-all-start.8 = ((bf16[32,36,128]{2,1,0:T(8,128)(2,1)}), bf16[32,36,128]{2,1,0:T(8,128)(2,1)S(1)}, u32[]{:S(2)}, u32[]{:S(2)}) async-start(bf16[32,36,128]{2,1,0:T(8,128)(2,1)} %broadcast_in_dim.56), calls=%async_computation.8 | async-start | bytes 655360 | tf_op jit(solution)/shard_map/all_to_all | solution.py:16

commit v2 on v1

v2 whole, which is shorter than its diff:
```python
import jax
import jax.numpy as jnp
from jax import lax
from jax.sharding import PartitionSpec as P

F32, BF16 = jnp.float32, jnp.bfloat16
ZL, Y, X, ZH, CORE = 8, 4, 4, 2, 2
PLANE = [[x * 4 + zh * 2 + c for x in range(X) for c in range(CORE)] for zh in range(ZH)]
PAIR = [(i, i ^ 2) for i in range(16)]


def moves(target):
    pairs = []
    for zl in range(ZL):
        for y in range(Y):
            for x in range(X):
                for zh in range(ZH):
                    for c in range(CORE):
                        a, b, e, g, h = target(zl, y, x, zh, c)
                        there = ((a * Y + b) * X + e) * 4 + g * 2 + h
                        pairs.append((((zl * Y + y) * X + x) * 4 + zh * 2 + c, there))
    return pairs


def along_z(by):
    def target(zl, y, x, zh, c):
        step = by if abs(by) < 4 or c == 0 else -by
        z = (zh * ZL + zl + step) % 16
        return z % ZL, y, x, z // ZL, c

    return moves(target)


def along_line(by):
    return moves(lambda zl, y, x, zh, c: ((zl + by) % ZL, y, x, zh, c))


def along_y(by):
    return moves(lambda zl, y, x, zh, c: (zl, (y + by) % Y, x, zh, c))


def along_plane(by):
    def target(zl, y, x, zh, c):
        k = (x * CORE + c + by) % (X * CORE)
        return zl, y, k // CORE, zh, k % CORE

    return moves(target)


def send(value, pairs):
    return lax.ppermute(value, ("dp", "fsdp"), pairs)


def swap(value, axis, groups=None):
    return lax.all_to_all(value, axis, 0, 0, axis_index_groups=groups, tiled=True)


def spread(value, axis, groups, size):
    copies = jnp.broadcast_to(value[None], (size,) + value.shape)
    return swap(copies, axis, groups)


Z_STEPS = (1, -1, 2, -2, 3, -3, 4)
Y_STEPS = (1, -1, 2)


def on_device(image_feats, image_head, text_embed, text_ids, logit_scale, logit_bias):
    rows, width = image_feats.shape
    embed_width = image_head.shape[1]
    cycle = lax.axis_size("dp")
    plane = X * CORE
    own = rows // plane
    held = -(-own // 8) * 8
    share = own // ZH
    piece = -(-share // 8) * 8
    d = lax.axis_index("dp")
    f = lax.axis_index("fsdp")
    zl, zh = d // Y, (f // CORE) % ZH
    k = (f // 4) * CORE + f % CORE

    parts = text_embed.reshape(X, 1, CORE, own, width)
    parts = jnp.broadcast_to(parts, (X, ZH, CORE, own, width)).reshape(X * ZH * CORE, own, width)
    text_part = swap(parts, "fsdp")
    text_vals = text_part.transpose(1, 0, 2).reshape(own, embed_width).astype(F32)
    text_scale = lax.rsqrt(jnp.sum(text_vals * text_vals, axis=1, keepdims=True) + 1e-06)
    text_unit = text_vals * text_scale
    my_ids = lax.dynamic_slice_in_dim(text_ids, k * own, own, 0).reshape(ZH, share)
    marks = jnp.concatenate([my_ids // 128, my_ids % 128], axis=1).astype(BF16)
    marks = jnp.pad(marks[:, None], ((0, 0), (0, piece - share - 1), (0, embed_width - 2 * share)))
    halves = jnp.concatenate([text_unit.astype(BF16).reshape(ZH, share, embed_width), marks], axis=1)
    first = zh == 0
    mine = jnp.where(first, halves[0], halves[1])
    other = jnp.where(first, halves[1], halves[0])
    unit_mine = jnp.where(first, text_unit[:share], text_unit[share:])
    scale_mine = jnp.where(first, text_scale[:share], text_scale[share:])

    blocks = [mine]
    core = f % CORE
    for by in Z_STEPS:
        step = jnp.where(core == 0, by, -by) if by == 4 else by
        there = (zh * ZL + zl + step + 16) % 16 // ZL
        blocks.append(send(jnp.where(there == zh, mine, other), along_z(by)))
    blocks = jnp.stack(blocks)
    line = blocks[:, :share].reshape(ZL * share, embed_width)
    line = jnp.concatenate([line, blocks[:, share]], axis=0)
    lines = [line] + [send(line, along_y(by)) for by in Y_STEPS]
    count = ZL * share
    texts = jnp.concatenate([part[:count] for part in lines], axis=0)
    notes = jnp.stack([part[count:, : 2 * share] for part in lines]).astype(jnp.int32)
    ids = (notes[:, :, :share] * 128 + notes[:, :, share:]).reshape(cycle * share)

    feats = jnp.pad(image_feats.reshape(plane, own, width), ((0, 0), (0, held - own), (0, 0)))
    feats = feats.reshape(plane * held, width)
    term = jnp.dot(feats, image_head, preferred_element_type=F32).astype(BF16)
    half = swap(term.reshape(plane, held, embed_width), "fsdp", PLANE)
    half = jnp.sum(half.astype(F32), axis=0).astype(BF16)
    embed = half.astype(F32) + lax.ppermute(half, "fsdp", PAIR).astype(F32)
    image_scale = lax.rsqrt(jnp.sum(embed * embed, axis=1, keepdims=True) + 1e-06)
    image_unit = embed * image_scale
    image_low = spread(image_unit.astype(BF16), "fsdp", PLANE, plane).reshape(plane * held, embed_width)

    partial_value = jnp.einsum("ie,je->ij", image_low, texts, preferred_element_type=F32)
    logits = logit_scale * partial_value + logit_bias
    row = lax.broadcasted_iota(jnp.int32, (plane, held), 1)
    row_index = d * rows + lax.broadcasted_iota(jnp.int32, (plane, held), 0) * own + row
    row_index = jnp.where(row < own, row_index, -1).reshape(plane * held, 1)
    sign = jnp.where(row_index == ids[None, :], 1.0, -1.0).astype(F32)
    coef = (-sign * jax.nn.sigmoid(-sign * logits) * logit_scale).astype(BF16)
    unit_part = jnp.einsum("ij,je->ie", coef, texts, preferred_element_type=F32).astype(BF16)
    text_acc = jnp.einsum("ij,ie->je", coef, image_low, preferred_element_type=F32).astype(BF16)

    back = swap(unit_part.reshape(plane, held, embed_width), "fsdp", PLANE)
    back = jnp.sum(back.astype(F32), axis=0).astype(BF16)
    unit_grad = back.astype(F32) + lax.ppermute(back, "fsdp", PAIR).astype(F32)
    image_dot = jnp.sum(image_unit * unit_grad, axis=1, keepdims=True)
    embed_grad = (image_scale * (unit_grad - image_unit * image_dot)).astype(BF16)
    grads = spread(embed_grad, "fsdp", PLANE, plane).reshape(plane * held, embed_width)
    lanes = embed_width // 128
    head_part = jnp.einsum("rw,re->we", feats, grads, preferred_element_type=F32).astype(BF16)
    head_part = head_part.reshape(width, lanes, 128).transpose(1, 0, 2).reshape(cycle, -1, 128)
    head_sum = jnp.sum(swap(head_part, "dp").astype(F32), axis=0).astype(BF16)
    head_all = spread(head_sum, "dp", None, cycle)
    head_grad = head_all.reshape(lanes, width, 128).transpose(1, 0, 2).reshape(width, embed_width).astype(F32)
    feature_grad = jnp.einsum("re,we->rw", grads, image_head, preferred_element_type=F32).astype(BF16)
    feature_grad = feature_grad.reshape(plane, held, width)[:, :own].reshape(rows, width)

    text_acc = text_acc.reshape(Y, count, embed_width)
    total = text_acc[0].astype(F32)
    for slot, by in enumerate(Y_STEPS):
        total = total + send(text_acc[slot + 1], along_y(-by)).astype(F32)
    total = total.astype(BF16).reshape(ZL, share, embed_width)
    text_grads = total[0].astype(F32)
    for slot, by in enumerate(Z_STEPS):
        text_grads = text_grads + send(total[slot + 1], along_line(-by)).astype(F32)
    text_dot = jnp.sum(unit_mine * text_grads, axis=1, keepdims=True)
    text_rows = (scale_mine * (text_grads - unit_mine * text_dot)).astype(BF16)
    text_rows = text_rows.reshape(share, X, ZH, CORE, width).transpose(2, 1, 3, 0, 4)
    near = jnp.where(first, text_rows[0], text_rows[1])
    far = jnp.where(first, text_rows[1], text_rows[0])
    came = lax.ppermute(far, "fsdp", PAIR)
    both = jnp.where(first, jnp.stack([near, came], axis=2), jnp.stack([came, near], axis=2))
    both = both.reshape(plane, own, width)
    turned = lax.dynamic_slice_in_dim(jnp.concatenate([both, both], axis=0), k, plane, 0)
    got = [turned[0]] + [send(turned[by], along_plane(by)) for by in range(1, plane)]
    got = jnp.stack(got[::-1] * 2)
    text_grad = lax.dynamic_slice_in_dim(got, plane - 1 - k, plane, 0).reshape(rows, width)
    return (feature_grad, head_grad, text_grad)


def solution(mesh):
    placed = (P("dp", "fsdp"), P("fsdp", None), P("dp", "fsdp"), P("dp"), P(), P())
    return jax.shard_map(
        on_device,
        mesh=mesh,
        in_specs=placed,
        out_specs=(P("dp", "fsdp"), P("fsdp", None), P("dp", "fsdp")),
        check_vma=False,
    )
```

time: 326 us -> 312 us (0.957)
  waiting for transfers between devices: 195 us -> 72.7 us
  starting transfers between devices: 97 us -> 198 us
  local copies, waits for them, and re-layouts: 12.8 us -> 20.6 us
    all_to_all x12 -> x7, waiting for transfers between devices: 171 us -> 30.1 us  [swap(): lax.all_to_all(value, axis, 0, 0, axis_index_groups=groups, tiled=True)]
    ppermute x0 -> x28, starting transfers between devices: none -> 112 us  [the longest x27 107 us: send(): return lax.ppermute(value, ('dp', 'fsdp'), pairs)]
    ppermute x0 -> x28, waiting for transfers between devices: none -> 38.6 us  [the longest x27 29.7 us: send(): return lax.ppermute(value, ('dp', 'fsdp'), pairs)]
    all_to_all x12 -> x7, starting transfers between devices: 92.7 us -> 65 us  [swap(): lax.all_to_all(value, axis, 0, 0, axis_index_groups=groups, tiled=True)]
    ppermute x1, waiting for transfers between devices: 12.2 us -> 0.01 us  [on_device(): unit_grad = back.astype(F32) + lax.ppermute(back, 'fsdp', PAIR).astype(F32)]
    ppermute x1, starting transfers between devices: 2.15 us -> 10.6 us  [on_device(): embed = half.astype(F32) + lax.ppermute(half, 'fsdp', PAIR).astype(F32)]
    ppermute x1, waiting for transfers between devices: 12.2 us -> 3.93 us  [on_device(): embed = half.astype(F32) + lax.ppermute(half, 'fsdp', PAIR).astype(F32)]
    ppermute x1, starting transfers between devices: 2.14 us -> 10 us  [on_device(): unit_grad = back.astype(F32) + lax.ppermute(back, 'fsdp', PAIR).astype(F32)]
  transfers between devices with their start and end apart: 14 -> 37, of which waited for: 14 -> 13; matrix products, arithmetic and copies ran while one was open for 5% -> 8% of each run, Pallas kernels for 0% -> 0%
where the time goes in v2:
time: 312 us; the launch traced here: 310 us
  starting transfers between devices  198 us (63%)
  waiting for transfers between devices  72.7 us (23%)
  local copies, waits for them, and re-layouts  20.6 us (7%)
  matrix products  11.2 us (4%)
  other arithmetic  4.62 us (1%)
    ppermute x27, starting transfers between devices, send(): return lax.ppermute(value, ('dp', 'fsdp'), pairs)  107 us
    all_to_all x7, starting transfers between devices, swap(): lax.all_to_all(value, axis, 0, 0, axis_index_groups=groups, tiled=True)  65 us
    all_to_all x7, waiting for transfers between devices, swap(): lax.all_to_all(value, axis, 0, 0, axis_index_groups=groups, tiled=True)  30.1 us
    ppermute x27, waiting for transfers between devices, send(): return lax.ppermute(value, ('dp', 'fsdp'), pairs)  29.7 us
    ppermute x1, starting transfers between devices, on_device(): embed = half.astype(F32) + lax.ppermute(half, 'fsdp', PAIR).astype(F32)  10.6 us
    ppermute x1, starting transfers between devices, on_device(): unit_grad = back.astype(F32) + lax.ppermute(back, 'fsdp', PAIR).astype(F32)  10 us
    ppermute x1, waiting for transfers between devices, on_device(): came = lax.ppermute(far, 'fsdp', PAIR)  8.96 us
  transfers between devices with their start and end apart: 37, of which 13 were waited for; matrix products, arithmetic and copies ran while one was open for 8% of the time, Pallas kernels for 0%

profile of v2, /device:TPU:1, one launch (start us, length us, event | category | flops | bytes accessed | tf_op | source)
XLA Modules:
  0.0 309.8 jit_solution(14439996839073528305)
XLA Ops:
  2.3 19.1 %all-to-all-start.1 = ((bf16[16,36,96]{2,1,0:T(8,128)(2,1)}), bf16[16,36,96]{2,1,0:T(8,128)(2,1)S(1)}, u32[]{:S(2)}, u32[]{:S(2)}) async-start(bf16[16,36,96]{2,1,0:T(8,128)(2,1)} %bitcast.2), calls=%async_computation.1 | async-start | bytes 327680 | tf_op jit(solution)/shard_map/all_to_all | solution.py:55
  24.9 11.7 %all-to-all-done.1 = bf16[16,36,96]{2,1,0:T(8,128)(2,1)S(1)} async-done(((bf16[16,36,96]{2,1,0:T(8,128)(2,1)}), bf16[16,36,96]{2,1,0:T(8,128)(2,1)S(1)}, u32[]{:S(2)}, u32[]{:S(2)}) %all-to-all-start.1) | async-done | bytes 110624 | tf_op jit(solution)/shard_map/all_to_all | solution.py:55
  36.6 4.2 %all-to-all-start = ((bf16[8,40,1536]{2,1,0:T(8,128)(2,1)}), bf16[8,40,1536]{2,1,0:T(8,128)(2,1)S(1)}, u32[]{:S(2)}, u32[]{:S(2)}) async-start(bf16[8,40,1536]{2,1,0:T(8,128)(2,1)} %bitcast.1), calls=%async_computation | async-start | bytes 1966080 | tf_op jit(solution)/shard_map/all_to_all | solution.py:55
  41.5 7.8 %collective-permute-start.1 = (bf16[24,1536]{1,0:T(8,128)(2,1)S(1)}, bf16[24,1536]{1,0:T(8,128)(2,1)S(1)}, u32[]{:S(2)}, u32[]{:S(2)}) collective-permute-start(bf16[24,1536]{1,0:T(8,128)(2,1)S(1)} %get-tuple-element.23), channel_id=1, source_target_pairs={{0,64},{1,65},{2,66},{3,67},{4,68},{5,69},{6,70},{7,71},{8,72},{9,... | collective-permute-start | bytes 221192 | tf_op jit(solution)/shard_map/ppermute | solution.py:51
  52.8 1.9 collective-permute-start.6
  54.7 5.2 %collective-permute-start.5 = (bf16[24,1536]{1,0:T(8,128)(2,1)S(1)}, bf16[24,1536]{1,0:T(8,128)(2,1)S(1)}, u32[]{:S(2)}, u32[]{:S(2)}) collective-permute-start(bf16[24,1536]{1,0:T(8,128)(2,1)S(1)} %get-tuple-element.19), channel_id=1, source_target_pairs={{0,192},{1,193},{2,194},{3,195},{4,196},{5,197},{6,198},{7,199},{8... | collective-permute-start | bytes 221192 | tf_op jit(solution)/shard_map/ppermute | solution.py:51
  59.9 1.9 collective-permute-start.4
  61.8 4.7 %collective-permute-start.2 = (bf16[24,1536]{1,0:T(8,128)(2,1)S(1)}, bf16[24,1536]{1,0:T(8,128)(2,1)S(1)}, u32[]{:S(2)}, u32[]{:S(2)}) collective-permute-start(bf16[24,1536]{1,0:T(8,128)(2,1)S(1)} %get-tuple-element.22), channel_id=1, source_target_pairs={{0,450},{1,451},{2,448},{3,449},{4,454},{5,455},{6,452},{7,453},{8... | collective-permute-start | bytes 221192 | tf_op jit(solution)/shard_map/ppermute | solution.py:51
  68.2 4.1 %collective-permute-start.3 = (bf16[24,1536]{1,0:T(8,128)(2,1)S(1)}, bf16[24,1536]{1,0:T(8,128)(2,1)S(1)}, u32[]{:S(2)}, u32[]{:S(2)}) collective-permute-start(bf16[24,1536]{1,0:T(8,128)(2,1)S(1)} %get-tuple-element.21), channel_id=1, source_target_pairs={{0,128},{1,129},{2,130},{3,131},{4,132},{5,133},{6,134},{7,135},{8... | collective-permute-start | bytes 221192 | tf_op jit(solution)/shard_map/ppermute | solution.py:51
  72.3 3.1 collective-permute-done.3
  76.5 4.8 %collective-permute-start.10 = (bf16[152,1536]{1,0:T(8,128)(2,1)}, bf16[152,1536]{1,0:T(8,128)(2,1)}, u32[]{:S(2)}, u32[]{:S(2)}) collective-permute-start(bf16[152,1536]{1,0:T(8,128)(2,1)} %pad_maximum_fusion.1), channel_id=1, source_target_pairs={{0,32},{1,33},{2,34},{3,35},{4,36},{5,37},{6,38},{7,39},{8,40},{9,... | collective-permute-start | bytes 1400840 | tf_op jit(solution)/shard_map/ppermute | solution.py:51
  81.3 2.7 collective-permute-start.9
  84.0 2.6 collective-permute-start.8
  86.8 10.6 %collective-permute-start = (bf16[40,1536]{1,0:T(8,128)(2,1)S(1)}, bf16[40,1536]{1,0:T(8,128)(2,1)S(1)}, u32[]{:S(2)}, u32[]{:S(2)}) collective-permute-start(bf16[40,1536]{1,0:T(8,128)(2,1)S(1)} %reduce_sum.72), channel_id=1, source_target_pairs={{0,2},{1,3},{2,0},{3,1},{4,6},{5,7},{6,4},{7,5},{8,10},{9,11},{10,... | collective-permute-start | bytes 368648 | tf_op jit(solution)/shard_map/ppermute | solution.py:117
  97.4 3.9 %collective-permute-done = bf16[40,1536]{1,0:T(8,128)(2,1)S(1)} collective-permute-done((bf16[40,1536]{1,0:T(8,128)(2,1)S(1)}, bf16[40,1536]{1,0:T(8,128)(2,1)S(1)}, u32[]{:S(2)}, u32[]{:S(2)}) %collective-permute-start) | collective-permute-done | bytes 122912 | tf_op jit(solution)/shard_map/ppermute | solution.py:117
  102.6 14.6 %all-to-all-start.2 = ((bf16[8,40,1536]{2,1,0:T(8,128)(2,1)}), bf16[8,40,1536]{2,1,0:T(8,128)(2,1)S(1)}, u32[]{:S(2)}, u32[]{:S(2)}) async-start(bf16[8,40,1536]{2,1,0:T(8,128)(2,1)} %broadcast_in_dim.47), calls=%async_computation.2 | async-start | bytes 1966080 | tf_op jit(solution)/shard_map/all_to_all | solution.py:55
  124.1 7.6 %all-to-all-done.2 = bf16[8,40,1536]{2,1,0:T(8,128)(2,1)S(1)} async-done(((bf16[8,40,1536]{2,1,0:T(8,128)(2,1)}), bf16[8,40,1536]{2,1,0:T(8,128)(2,1)S(1)}, u32[]{:S(2)}, u32[]{:S(2)}) %all-to-all-start.2) | async-done | bytes 983072 | tf_op jit(solution)/shard_map/all_to_all | solution.py:55
  131.6 2.6 fusion.9
  134.3 2.9 convolution_convert_fusion.1
  137.2 4.3 %all-to-all-start.3 = ((bf16[8,40,1536]{2,1,0:T(8,128)(2,1)}), bf16[8,40,1536]{2,1,0:T(8,128)(2,1)S(1)}, u32[]{:S(2)}, u32[]{:S(2)}) async-start(bf16[8,40,1536]{2,1,0:T(8,128)(2,1)} %bitcast.115), calls=%async_computation.3 | async-start | bytes 1966080 | tf_op jit(solution)/shard_map/all_to_all | solution.py:55
  141.5 3.5 %convolution_convert_fusion = bf16[576,1536]{1,0:T(8,128)(2,1)} fusion(bf16[320,576]{1,0:T(8,128)(2,1)S(1)} %fusion.9, bf16[320,1536]{1,0:T(8,128)(2,1)} %bitcast.114), kind=kOutput, calls=%fused_computation | convolution fusion | flops 567115776 | bytes 3121152 | tf_op jit(solution)/shard_map/ij,ie->je/dot_general | solution.py:130
  145.1 10.9 %all-to-all-done.3 = bf16[8,40,1536]{2,1,0:T(8,128)(2,1)S(1)} async-done(((bf16[8,40,1536]{2,1,0:T(8,128)(2,1)}), bf16[8,40,1536]{2,1,0:T(8,128)(2,1)S(1)}, u32[]{:S(2)}, u32[]{:S(2)}) %all-to-all-start.3) | async-done | bytes 983072 | tf_op jit(solution)/shard_map/all_to_all | solution.py:55
  156.1 10.0 %collective-permute-start.11 = (bf16[40,1536]{1,0:T(8,128)(2,1)S(1)}, bf16[40,1536]{1,0:T(8,128)(2,1)S(1)}, u32[]{:S(2)}, u32[]{:S(2)}) collective-permute-start(bf16[40,1536]{1,0:T(8,128)(2,1)S(1)} %reduce_sum.75), channel_id=1, source_target_pairs={{0,2},{1,3},{2,0},{3,1},{4,6},{5,7},{6,4},{7,5},{8,10},{9,11},{10,... | collective-permute-start | bytes 368648 | tf_op jit(solution)/shard_map/ppermute | solution.py:134
  166.1 2.3 fusion.30
  168.4 3.9 %collective-permute-start.12 = (bf16[144,1536]{1,0:T(8,128)(2,1)}, bf16[144,1536]{1,0:T(8,128)(2,1)S(1)}, u32[]{:S(2)}, u32[]{:S(2)}) collective-permute-start(bf16[144,1536]{1,0:T(8,128)(2,1)} %get-tuple-element.8), channel_id=1, source_target_pairs={{0,48},{1,49},{2,50},{3,51},{4,52},{5,53},{6,54},{7,55},{8,56},{9,... | collective-permute-start | bytes 1327112 | tf_op jit(solution)/shard_map/ppermute | solution.py:51
  172.3 2.1 collective-permute-start.14
  174.4 2.3 collective-permute-start.13
  178.1 6.4 %all-to-all-start.4 = ((bf16[8,40,1536]{2,1,0:T(8,128)(2,1)}), bf16[8,40,1536]{2,1,0:T(8,128)(2,1)S(1)}, u32[]{:S(2)}, u32[]{:S(2)}) async-start(bf16[8,40,1536]{2,1,0:T(8,128)(2,1)} %broadcast_in_dim.48), calls=%async_computation.4 | async-start | bytes 1966080 | tf_op jit(solution)/shard_map/all_to_all | solution.py:55
  186.3 11.3 %collective-permute-done.13 = bf16[144,1536]{1,0:T(8,128)(2,1)} collective-permute-done((bf16[144,1536]{1,0:T(8,128)(2,1)S(1)}, bf16[144,1536]{1,0:T(8,128)(2,1)}, u32[]{:S(2)}, u32[]{:S(2)}) %collective-permute-start.13) | collective-permute-done | bytes 442400 | tf_op jit(solution)/shard_map/ppermute | solution.py:51
  200.6 10.5 %all-to-all-start.5 = ((bf16[32,36,128]{2,1,0:T(8,128)(2,1)}), bf16[32,36,128]{2,1,0:T(8,128)(2,1)S(1)}, u32[]{:S(2)}, u32[]{:S(2)}) async-start(bf16[32,36,128]{2,1,0:T(8,128)(2,1)} %reshape.247), calls=%async_computation.5 | async-start | bytes 655360 | tf_op jit(solution)/shard_map/all_to_all | solution.py:55
  211.2 9.8 %collective-permute-start.15 = (bf16[18,1536]{1,0:T(8,128)(2,1)S(1)}, bf16[18,1536]{1,0:T(8,128)(2,1)S(1)}, u32[]{:S(2)}, u32[]{:S(2)}) collective-permute-start(bf16[18,1536]{1,0:T(8,128)(2,1)S(1)} %get-tuple-element.11), channel_id=1, source_target_pairs={{0,448},{1,449},{2,450},{3,451},{4,452},{5,453},{6,454},{7,455},{8... | collective-permute-start | bytes 165896 | tf_op jit(solution)/shard_map/ppermute | solution.py:51
  221.0 1.9 collective-permute-start.21
  223.0 2.4 collective-permute-start.20
  225.5 7.7 %collective-permute-start.19 = (bf16[18,1536]{1,0:T(8,128)(2,1)S(1)}, bf16[18,1536]{1,0:T(8,128)(2,1)S(1)}, u32[]{:S(2)}, u32[]{:S(2)}) collective-permute-start(bf16[18,1536]{1,0:T(8,128)(2,1)S(1)} %get-tuple-element.14), channel_id=1, source_target_pairs={{0,320},{1,321},{2,322},{3,323},{4,324},{5,325},{6,326},{7,327},{8... | collective-permute-start | bytes 165896 | tf_op jit(solution)/shard_map/ppermute | solution.py:51
  233.1 1.9 collective-permute-start.18
  235.1 9.1 %collective-permute-start.17 = (bf16[18,1536]{1,0:T(8,128)(2,1)S(1)}, bf16[18,1536]{1,0:T(8,128)(2,1)S(1)}, u32[]{:S(2)}, u32[]{:S(2)}) collective-permute-start(bf16[18,1536]{1,0:T(8,128)(2,1)S(1)} %get-tuple-element.16), channel_id=1, source_target_pairs={{0,384},{1,385},{2,386},{3,387},{4,388},{5,389},{6,390},{7,391},{8... | collective-permute-start | bytes 165896 | tf_op jit(solution)/shard_map/ppermute | solution.py:51
  244.2 2.4 collective-permute-start.16
  248.4 3.0 collective-permute-done.17
  251.4 4.5 %collective-permute-done.16 = bf16[18,1536]{1,0:T(8,128)(2,1)S(1)} collective-permute-done((bf16[18,1536]{1,0:T(8,128)(2,1)S(1)}, bf16[18,1536]{1,0:T(8,128)(2,1)S(1)}, u32[]{:S(2)}, u32[]{:S(2)}) %collective-permute-start.16) | collective-permute-done | bytes 55328 | tf_op jit(solution)/shard_map/ppermute | solution.py:51
  256.9 5.9 %all-to-all-start.6 = ((bf16[32,36,128]{2,1,0:T(8,128)(2,1)}), bf16[32,36,128]{2,1,0:T(8,128)(2,1)S(1)}, u32[]{:S(2)}, u32[]{:S(2)}) async-start(bf16[32,36,128]{2,1,0:T(8,128)(2,1)} %broadcast_in_dim.49), calls=%async_computation.6 | async-start | bytes 655360 | tf_op jit(solution)/shard_map/all_to_all | solution.py:55
  263.2 4.9 %collective-permute-start.22 = (bf16[4,2,18,96]{3,1,0,2:T(2,128)(2,1)S(1)}, bf16[4,2,18,96]{3,1,0,2:T(2,128)(2,1)S(1)}, u32[]{:S(2)}, u32[]{:S(2)}) collective-permute-start(bf16[4,2,18,96]{3,1,0,2:T(2,128)(2,1)S(1)} %get-tuple-element.33), channel_id=1, source_target_pairs={{0,2},{1,3},{2,0},{3,1},{4,6},{5,7},{6,4},{7,5},{8,10},{9,11},{10,... | collective-permute-start | bytes 82952 | tf_op jit(solution)/shard_map/ppermute | solution.py:160
  268.1 9.0 %collective-permute-done.22 = bf16[4,2,18,96]{3,1,0,2:T(2,128)(2,1)S(1)} collective-permute-done((bf16[4,2,18,96]{3,1,0,2:T(2,128)(2,1)S(1)}, bf16[4,2,18,96]{3,1,0,2:T(2,128)(2,1)S(1)}, u32[]{:S(2)}, u32[]{:S(2)}) %collective-permute-start.22) | collective-permute-done | bytes 27680 | tf_op jit(solution)/shard_map/ppermute | solution.py:160
  277.5 10.0 %collective-permute-start.23 = (bf16[36,96]{1,0:T(8,128)(2,1)S(1)}, bf16[36,96]{1,0:T(8,128)(2,1)S(1)}, u32[]{:S(2)}, u32[]{:S(2)}) collective-permute-start(bf16[36,96]{1,0:T(8,128)(2,1)S(1)} %bitcast.137), channel_id=1, source_target_pairs={{0,13},{1,0},{2,15},{3,2},{4,1},{5,4},{6,3},{7,6},{8,5},{9,8},{10,... | collective-permute-start | bytes 20744 | tf_op jit(solution)/shard_map/ppermute | solution.py:51
  287.4 2.8 collective-permute-start.24
  292.2 4.5 %collective-permute-start.26 = (bf16[36,96]{1,0:T(8,128)(2,1)S(1)}, bf16[36,96]{1,0:T(8,128)(2,1)S(1)}, u32[]{:S(2)}, u32[]{:S(2)}) collective-permute-start(bf16[36,96]{1,0:T(8,128)(2,1)S(1)} %bitcast.127), channel_id=1, source_target_pairs={{0,8},{1,9},{2,10},{3,11},{4,12},{5,13},{6,14},{7,15},{8,0},{9,1},... | collective-permute-start | bytes 20744 | tf_op jit(solution)/shard_map/ppermute | solution.py:51
  296.7 4.1 %collective-permute-start.27 = (bf16[36,96]{1,0:T(8,128)(2,1)S(1)}, bf16[36,96]{1,0:T(8,128)(2,1)S(1)}, u32[]{:S(2)}, u32[]{:S(2)}) collective-permute-start(bf16[36,96]{1,0:T(8,128)(2,1)S(1)} %bitcast.130), channel_id=1, source_target_pairs={{0,5},{1,8},{2,7},{3,10},{4,9},{5,12},{6,11},{7,14},{8,13},{9,0},{... | collective-permute-start | bytes 20744 | tf_op jit(solution)/shard_map/ppermute | solution.py:51
  300.8 1.9 collective-permute-start.28
  303.6 2.8 collective-permute-done.28
  (132 shorter events, 34.6 us)
Async XLA Ops:
  0.6 22.9 %copy-start = (bf16[96,1536]{1,0:T(8,128)(2,1)S(1)}, bf16[96,1536]{1,0:T(8,128)(2,1)}, u32[]{:S(2)}) copy-start(bf16[96,1536]{1,0:T(8,128)(2,1)} %param.7) | copy-start | bytes 884740
  2.3 34.3 %all-to-all-start.1 = ((bf16[16,36,96]{2,1,0:T(8,128)(2,1)}), bf16[16,36,96]{2,1,0:T(8,128)(2,1)S(1)}, u32[]{:S(2)}, u32[]{:S(2)}) async-start(bf16[16,36,96]{2,1,0:T(8,128)(2,1)} %bitcast.2), calls=%async_computation.1 | async-start | bytes 327680 | tf_op jit(solution)/shard_map/all_to_all | solution.py:55
  36.6 50.0 %all-to-all-start = ((bf16[8,40,1536]{2,1,0:T(8,128)(2,1)}), bf16[8,40,1536]{2,1,0:T(8,128)(2,1)S(1)}, u32[]{:S(2)}, u32[]{:S(2)}) async-start(bf16[8,40,1536]{2,1,0:T(8,128)(2,1)} %bitcast.1), calls=%async_computation | async-start | bytes 1966080 | tf_op jit(solution)/shard_map/all_to_all | solution.py:55
  41.5 20.3 %collective-permute-start.1 = (bf16[24,1536]{1,0:T(8,128)(2,1)S(1)}, bf16[24,1536]{1,0:T(8,128)(2,1)S(1)}, u32[]{:S(2)}, u32[]{:S(2)}) collective-permute-start(bf16[24,1536]{1,0:T(8,128)(2,1)S(1)} %get-tuple-element.23), channel_id=1, source_target_pairs={{0,64},{1,65},{2,66},{3,67},{4,68},{5,69},{6,70},{7,71},{8,72},{9,... | collective-permute-start | bytes 221192 | tf_op jit(solution)/shard_map/ppermute | solution.py:51
  50.8 24.6 %collective-permute-start.7 = (bf16[24,1536]{1,0:T(8,128)(2,1)S(1)}, bf16[24,1536]{1,0:T(8,128)(2,1)S(1)}, u32[]{:S(2)}, u32[]{:S(2)}) collective-permute-start(bf16[24,1536]{1,0:T(8,128)(2,1)S(1)} %get-tuple-element.5), channel_id=1, source_target_pairs={{0,256},{1,259},{2,258},{3,257},{4,260},{5,263},{6,262},{7,261},{8... | collective-permute-start | bytes 221192 | tf_op jit(solution)/shard_map/ppermute | solution.py:51
  52.8 22.7 %collective-permute-start.6 = (bf16[24,1536]{1,0:T(8,128)(2,1)S(1)}, bf16[24,1536]{1,0:T(8,128)(2,1)S(1)}, u32[]{:S(2)}, u32[]{:S(2)}) collective-permute-start(bf16[24,1536]{1,0:T(8,128)(2,1)S(1)} %get-tuple-element.18), channel_id=1, source_target_pairs={{0,322},{1,323},{2,320},{3,321},{4,326},{5,327},{6,324},{7,325},{8... | collective-permute-start | bytes 221192 | tf_op jit(solution)/shard_map/ppermute | solution.py:51
  54.7 20.7 %collective-permute-start.5 = (bf16[24,1536]{1,0:T(8,128)(2,1)S(1)}, bf16[24,1536]{1,0:T(8,128)(2,1)S(1)}, u32[]{:S(2)}, u32[]{:S(2)}) collective-permute-start(bf16[24,1536]{1,0:T(8,128)(2,1)S(1)} %get-tuple-element.19), channel_id=1, source_target_pairs={{0,192},{1,193},{2,194},{3,195},{4,196},{5,197},{6,198},{7,199},{8... | collective-permute-start | bytes 221192 | tf_op jit(solution)/shard_map/ppermute | solution.py:51
  59.9 15.5 %collective-permute-start.4 = (bf16[24,1536]{1,0:T(8,128)(2,1)S(1)}, bf16[24,1536]{1,0:T(8,128)(2,1)S(1)}, u32[]{:S(2)}, u32[]{:S(2)}) collective-permute-start(bf16[24,1536]{1,0:T(8,128)(2,1)S(1)} %get-tuple-element.20), channel_id=1, source_target_pairs={{0,386},{1,387},{2,384},{3,385},{4,390},{5,391},{6,388},{7,389},{8... | collective-permute-start | bytes 221192 | tf_op jit(solution)/shard_map/ppermute | solution.py:51
  61.8 6.3 %collective-permute-start.2 = (bf16[24,1536]{1,0:T(8,128)(2,1)S(1)}, bf16[24,1536]{1,0:T(8,128)(2,1)S(1)}, u32[]{:S(2)}, u32[]{:S(2)}) collective-permute-start(bf16[24,1536]{1,0:T(8,128)(2,1)S(1)} %get-tuple-element.22), channel_id=1, source_target_pairs={{0,450},{1,451},{2,448},{3,449},{4,454},{5,455},{6,452},{7,453},{8... | collective-permute-start | bytes 221192 | tf_op jit(solution)/shard_map/ppermute | solution.py:51
  68.2 7.2 %collective-permute-start.3 = (bf16[24,1536]{1,0:T(8,128)(2,1)S(1)}, bf16[24,1536]{1,0:T(8,128)(2,1)S(1)}, u32[]{:S(2)}, u32[]{:S(2)}) collective-permute-start(bf16[24,1536]{1,0:T(8,128)(2,1)S(1)} %get-tuple-element.21), channel_id=1, source_target_pairs={{0,128},{1,129},{2,130},{3,131},{4,132},{5,133},{6,134},{7,135},{8... | collective-permute-start | bytes 221192 | tf_op jit(solution)/shard_map/ppermute | solution.py:51
  76.5 40.7 %collective-permute-start.10 = (bf16[152,1536]{1,0:T(8,128)(2,1)}, bf16[152,1536]{1,0:T(8,128)(2,1)}, u32[]{:S(2)}, u32[]{:S(2)}) collective-permute-start(bf16[152,1536]{1,0:T(8,128)(2,1)} %pad_maximum_fusion.1), channel_id=1, source_target_pairs={{0,32},{1,33},{2,34},{3,35},{4,36},{5,37},{6,38},{7,39},{8,40},{9,... | collective-permute-start | bytes 1400840 | tf_op jit(solution)/shard_map/ppermute | solution.py:51
  81.3 36.6 %collective-permute-start.9 = (bf16[152,1536]{1,0:T(8,128)(2,1)}, bf16[152,1536]{1,0:T(8,128)(2,1)}, u32[]{:S(2)}, u32[]{:S(2)}) collective-permute-start(bf16[152,1536]{1,0:T(8,128)(2,1)} %pad_maximum_fusion.1), channel_id=1, source_target_pairs={{0,48},{1,49},{2,50},{3,51},{4,52},{5,53},{6,54},{7,55},{8,56},{9,... | collective-permute-start | bytes 1400840 | tf_op jit(solution)/shard_map/ppermute | solution.py:51
  84.0 34.5 %collective-permute-start.8 = (bf16[152,1536]{1,0:T(8,128)(2,1)}, bf16[152,1536]{1,0:T(8,128)(2,1)}, u32[]{:S(2)}, u32[]{:S(2)}) collective-permute-start(bf16[152,1536]{1,0:T(8,128)(2,1)} %pad_maximum_fusion.1), channel_id=1, source_target_pairs={{0,16},{1,17},{2,18},{3,19},{4,20},{5,21},{6,22},{7,23},{8,24},{9,... | collective-permute-start | bytes 1400840 | tf_op jit(solution)/shard_map/ppermute | solution.py:51
  86.8 14.6 %collective-permute-start = (bf16[40,1536]{1,0:T(8,128)(2,1)S(1)}, bf16[40,1536]{1,0:T(8,128)(2,1)S(1)}, u32[]{:S(2)}, u32[]{:S(2)}) collective-permute-start(bf16[40,1536]{1,0:T(8,128)(2,1)S(1)} %reduce_sum.72), channel_id=1, source_target_pairs={{0,2},{1,3},{2,0},{3,1},{4,6},{5,7},{6,4},{7,5},{8,10},{9,11},{10,... | collective-permute-start | bytes 368648 | tf_op jit(solution)/shard_map/ppermute | solution.py:117
  102.6 29.0 %all-to-all-start.2 = ((bf16[8,40,1536]{2,1,0:T(8,128)(2,1)}), bf16[8,40,1536]{2,1,0:T(8,128)(2,1)S(1)}, u32[]{:S(2)}, u32[]{:S(2)}) async-start(bf16[8,40,1536]{2,1,0:T(8,128)(2,1)} %broadcast_in_dim.47), calls=%async_computation.2 | async-start | bytes 1966080 | tf_op jit(solution)/shard_map/all_to_all | solution.py:55
  131.6 2.6 copy-start.1
  131.6 2.6 copy-start.2
  137.2 18.7 %all-to-all-start.3 = ((bf16[8,40,1536]{2,1,0:T(8,128)(2,1)}), bf16[8,40,1536]{2,1,0:T(8,128)(2,1)S(1)}, u32[]{:S(2)}, u32[]{:S(2)}) async-start(bf16[8,40,1536]{2,1,0:T(8,128)(2,1)} %bitcast.115), calls=%async_computation.3 | async-start | bytes 1966080 | tf_op jit(solution)/shard_map/all_to_all | solution.py:55
  156.1 20.6 %collective-permute-start.11 = (bf16[40,1536]{1,0:T(8,128)(2,1)S(1)}, bf16[40,1536]{1,0:T(8,128)(2,1)S(1)}, u32[]{:S(2)}, u32[]{:S(2)}) collective-permute-start(bf16[40,1536]{1,0:T(8,128)(2,1)S(1)} %reduce_sum.75), channel_id=1, source_target_pairs={{0,2},{1,3},{2,0},{3,1},{4,6},{5,7},{6,4},{7,5},{8,10},{9,11},{10,... | collective-permute-start | bytes 368648 | tf_op jit(solution)/shard_map/ppermute | solution.py:134
  168.4 16.3 %collective-permute-start.12 = (bf16[144,1536]{1,0:T(8,128)(2,1)}, bf16[144,1536]{1,0:T(8,128)(2,1)S(1)}, u32[]{:S(2)}, u32[]{:S(2)}) collective-permute-start(bf16[144,1536]{1,0:T(8,128)(2,1)} %get-tuple-element.8), channel_id=1, source_target_pairs={{0,48},{1,49},{2,50},{3,51},{4,52},{5,53},{6,54},{7,55},{8,56},{9,... | collective-permute-start | bytes 1327112 | tf_op jit(solution)/shard_map/ppermute | solution.py:51
  172.3 14.0 %collective-permute-start.14 = (bf16[144,1536]{1,0:T(8,128)(2,1)}, bf16[144,1536]{1,0:T(8,128)(2,1)}, u32[]{:S(2)}, u32[]{:S(2)}) collective-permute-start(bf16[144,1536]{1,0:T(8,128)(2,1)} %get-tuple-element.9), channel_id=1, source_target_pairs={{0,32},{1,33},{2,34},{3,35},{4,36},{5,37},{6,38},{7,39},{8,40},{9,... | collective-permute-start | bytes 1327112 | tf_op jit(solution)/shard_map/ppermute | solution.py:51
  174.4 23.2 %collective-permute-start.13 = (bf16[144,1536]{1,0:T(8,128)(2,1)S(1)}, bf16[144,1536]{1,0:T(8,128)(2,1)}, u32[]{:S(2)}, u32[]{:S(2)}) collective-permute-start(bf16[144,1536]{1,0:T(8,128)(2,1)S(1)} %get-tuple-element.10), channel_id=1, source_target_pairs={{0,16},{1,17},{2,18},{3,19},{4,20},{5,21},{6,22},{7,23},{8,24},{9,... | collective-permute-start | bytes 1327112 | tf_op jit(solution)/shard_map/ppermute | solution.py:51
  178.1 21.0 %all-to-all-start.4 = ((bf16[8,40,1536]{2,1,0:T(8,128)(2,1)}), bf16[8,40,1536]{2,1,0:T(8,128)(2,1)S(1)}, u32[]{:S(2)}, u32[]{:S(2)}) async-start(bf16[8,40,1536]{2,1,0:T(8,128)(2,1)} %broadcast_in_dim.48), calls=%async_computation.4 | async-start | bytes 1966080 | tf_op jit(solution)/shard_map/all_to_all | solution.py:55
  200.6 55.5 %all-to-all-start.5 = ((bf16[32,36,128]{2,1,0:T(8,128)(2,1)}), bf16[32,36,128]{2,1,0:T(8,128)(2,1)S(1)}, u32[]{:S(2)}, u32[]{:S(2)}) async-start(bf16[32,36,128]{2,1,0:T(8,128)(2,1)} %reshape.247), calls=%async_computation.5 | async-start | bytes 655360 | tf_op jit(solution)/shard_map/all_to_all | solution.py:55
  211.2 23.9 %collective-permute-start.15 = (bf16[18,1536]{1,0:T(8,128)(2,1)S(1)}, bf16[18,1536]{1,0:T(8,128)(2,1)S(1)}, u32[]{:S(2)}, u32[]{:S(2)}) collective-permute-start(bf16[18,1536]{1,0:T(8,128)(2,1)S(1)} %get-tuple-element.11), channel_id=1, source_target_pairs={{0,448},{1,449},{2,450},{3,451},{4,452},{5,453},{6,454},{7,455},{8... | collective-permute-start | bytes 165896 | tf_op jit(solution)/shard_map/ppermute | solution.py:51
  221.0 23.1 %collective-permute-start.21 = (bf16[18,1536]{1,0:T(8,128)(2,1)S(1)}, bf16[18,1536]{1,0:T(8,128)(2,1)S(1)}, u32[]{:S(2)}, u32[]{:S(2)}) collective-permute-start(bf16[18,1536]{1,0:T(8,128)(2,1)S(1)} %get-tuple-element.12), channel_id=1, source_target_pairs={{0,256},{1,257},{2,258},{3,259},{4,260},{5,261},{6,262},{7,263},{8... | collective-permute-start | bytes 165896 | tf_op jit(solution)/shard_map/ppermute | solution.py:51
  223.0 25.4 %collective-permute-start.20 = (bf16[18,1536]{1,0:T(8,128)(2,1)S(1)}, bf16[18,1536]{1,0:T(8,128)(2,1)S(1)}, u32[]{:S(2)}, u32[]{:S(2)}) collective-permute-start(bf16[18,1536]{1,0:T(8,128)(2,1)S(1)} %get-tuple-element.13), channel_id=1, source_target_pairs={{0,192},{1,193},{2,194},{3,195},{4,196},{5,197},{6,198},{7,199},{8... | collective-permute-start | bytes 165896 | tf_op jit(solution)/shard_map/ppermute | solution.py:51
  225.5 22.9 %collective-permute-start.19 = (bf16[18,1536]{1,0:T(8,128)(2,1)S(1)}, bf16[18,1536]{1,0:T(8,128)(2,1)S(1)}, u32[]{:S(2)}, u32[]{:S(2)}) collective-permute-start(bf16[18,1536]{1,0:T(8,128)(2,1)S(1)} %get-tuple-element.14), channel_id=1, source_target_pairs={{0,320},{1,321},{2,322},{3,323},{4,324},{5,325},{6,326},{7,327},{8... | collective-permute-start | bytes 165896 | tf_op jit(solution)/shard_map/ppermute | solution.py:51
  233.1 15.3 %collective-permute-start.18 = (bf16[18,1536]{1,0:T(8,128)(2,1)S(1)}, bf16[18,1536]{1,0:T(8,128)(2,1)S(1)}, u32[]{:S(2)}, u32[]{:S(2)}) collective-permute-start(bf16[18,1536]{1,0:T(8,128)(2,1)S(1)} %get-tuple-element.15), channel_id=1, source_target_pairs={{0,128},{1,129},{2,130},{3,131},{4,132},{5,133},{6,134},{7,135},{8... | collective-permute-start | bytes 165896 | tf_op jit(solution)/shard_map/ppermute | solution.py:51
  235.1 16.3 %collective-permute-start.17 = (bf16[18,1536]{1,0:T(8,128)(2,1)S(1)}, bf16[18,1536]{1,0:T(8,128)(2,1)S(1)}, u32[]{:S(2)}, u32[]{:S(2)}) collective-permute-start(bf16[18,1536]{1,0:T(8,128)(2,1)S(1)} %get-tuple-element.16), channel_id=1, source_target_pairs={{0,384},{1,385},{2,386},{3,387},{4,388},{5,389},{6,390},{7,391},{8... | collective-permute-start | bytes 165896 | tf_op jit(solution)/shard_map/ppermute | solution.py:51
  244.2 11.7 %collective-permute-start.16 = (bf16[18,1536]{1,0:T(8,128)(2,1)S(1)}, bf16[18,1536]{1,0:T(8,128)(2,1)S(1)}, u32[]{:S(2)}, u32[]{:S(2)}) collective-permute-start(bf16[18,1536]{1,0:T(8,128)(2,1)S(1)} %get-tuple-element.17), channel_id=1, source_target_pairs={{0,64},{1,65},{2,66},{3,67},{4,68},{5,69},{6,70},{7,71},{8,72},{9,... | collective-permute-start | bytes 165896 | tf_op jit(solution)/shard_map/ppermute | solution.py:51
  256.9 51.9 %all-to-all-start.6 = ((bf16[32,36,128]{2,1,0:T(8,128)(2,1)}), bf16[32,36,128]{2,1,0:T(8,128)(2,1)S(1)}, u32[]{:S(2)}, u32[]{:S(2)}) async-start(bf16[32,36,128]{2,1,0:T(8,128)(2,1)} %broadcast_in_dim.49), calls=%async_computation.6 | async-start | bytes 655360 | tf_op jit(solution)/shard_map/all_to_all | solution.py:55
  263.2 13.9 %collective-permute-start.22 = (bf16[4,2,18,96]{3,1,0,2:T(2,128)(2,1)S(1)}, bf16[4,2,18,96]{3,1,0,2:T(2,128)(2,1)S(1)}, u32[]{:S(2)}, u32[]{:S(2)}) collective-permute-start(bf16[4,2,18,96]{3,1,0,2:T(2,128)(2,1)S(1)} %get-tuple-element.33), channel_id=1, source_target_pairs={{0,2},{1,3},{2,0},{3,1},{4,6},{5,7},{6,4},{7,5},{8,10},{9,11},{10,... | collective-permute-start | bytes 82952 | tf_op jit(solution)/shard_map/ppermute | solution.py:160
  277.5 23.3 %collective-permute-start.23 = (bf16[36,96]{1,0:T(8,128)(2,1)S(1)}, bf16[36,96]{1,0:T(8,128)(2,1)S(1)}, u32[]{:S(2)}, u32[]{:S(2)}) collective-permute-start(bf16[36,96]{1,0:T(8,128)(2,1)S(1)} %bitcast.137), channel_id=1, source_target_pairs={{0,13},{1,0},{2,15},{3,2},{4,1},{5,4},{6,3},{7,6},{8,5},{9,8},{10,... | collective-permute-start | bytes 20744 | tf_op jit(solution)/shard_map/ppermute | solution.py:51
  287.4 15.3 %collective-permute-start.24 = (bf16[36,96]{1,0:T(8,128)(2,1)S(1)}, bf16[36,96]{1,0:T(8,128)(2,1)S(1)}, u32[]{:S(2)}, u32[]{:S(2)}) collective-permute-start(bf16[36,96]{1,0:T(8,128)(2,1)S(1)} %bitcast.136), channel_id=1, source_target_pairs={{0,12},{1,13},{2,14},{3,15},{4,0},{5,1},{6,2},{7,3},{8,4},{9,5},{1... | collective-permute-start | bytes 20744 | tf_op jit(solution)/shard_map/ppermute | solution.py:51
  290.2 13.2 %collective-permute-start.25 = (bf16[36,96]{1,0:T(8,128)(2,1)S(1)}, bf16[36,96]{1,0:T(8,128)(2,1)S(1)}, u32[]{:S(2)}, u32[]{:S(2)}) collective-permute-start(bf16[36,96]{1,0:T(8,128)(2,1)S(1)} %bitcast.132), channel_id=1, source_target_pairs={{0,9},{1,12},{2,11},{3,14},{4,13},{5,0},{6,15},{7,2},{8,1},{9,4},{... | collective-permute-start | bytes 20744 | tf_op jit(solution)/shard_map/ppermute | solution.py:51
  292.2 11.3 %collective-permute-start.26 = (bf16[36,96]{1,0:T(8,128)(2,1)S(1)}, bf16[36,96]{1,0:T(8,128)(2,1)S(1)}, u32[]{:S(2)}, u32[]{:S(2)}) collective-permute-start(bf16[36,96]{1,0:T(8,128)(2,1)S(1)} %bitcast.127), channel_id=1, source_target_pairs={{0,8},{1,9},{2,10},{3,11},{4,12},{5,13},{6,14},{7,15},{8,0},{9,1},... | collective-permute-start | bytes 20744 | tf_op jit(solution)/shard_map/ppermute | solution.py:51
  296.7 6.9 %collective-permute-start.27 = (bf16[36,96]{1,0:T(8,128)(2,1)S(1)}, bf16[36,96]{1,0:T(8,128)(2,1)S(1)}, u32[]{:S(2)}, u32[]{:S(2)}) collective-permute-start(bf16[36,96]{1,0:T(8,128)(2,1)S(1)} %bitcast.130), channel_id=1, source_target_pairs={{0,5},{1,8},{2,7},{3,10},{4,9},{5,12},{6,11},{7,14},{8,13},{9,0},{... | collective-permute-start | bytes 20744 | tf_op jit(solution)/shard_map/ppermute | solution.py:51
  300.8 5.6 %collective-permute-start.28 = (bf16[36,96]{1,0:T(8,128)(2,1)S(1)}, bf16[36,96]{1,0:T(8,128)(2,1)S(1)}, u32[]{:S(2)}, u32[]{:S(2)}) collective-permute-start(bf16[36,96]{1,0:T(8,128)(2,1)S(1)} %bitcast.125), channel_id=1, source_target_pairs={{0,4},{1,5},{2,6},{3,7},{4,8},{5,9},{6,10},{7,11},{8,12},{9,13},{1... | collective-permute-start | bytes 20744 | tf_op jit(solution)/shard_map/ppermute | solution.py:51
  302.7 3.7 %collective-permute-start.29 = (bf16[36,96]{1,0:T(8,128)(2,1)S(1)}, bf16[36,96]{1,0:T(8,128)(2,1)S(1)}, u32[]{:S(2)}, u32[]{:S(2)}) collective-permute-start(bf16[36,96]{1,0:T(8,128)(2,1)S(1)} %bitcast.124), channel_id=1, source_target_pairs={{0,1},{1,4},{2,3},{3,6},{4,5},{5,8},{6,7},{7,10},{8,9},{9,12},{10,... | collective-permute-start | bytes 20744 | tf_op jit(solution)/shard_map/ppermute | solution.py:51

commit v3 on v1

--- a/solution.py
+++ b/solution.py
@@ -38,13 +38,17 @@
     text_scale = lax.rsqrt(jnp.sum(text_vals * text_vals, axis=1, keepdims=True) + 1e-06)
     text_unit = text_vals * text_scale
     my_ids = lax.dynamic_slice_in_dim(text_ids, f * share, share, 0)
-    marks = jnp.stack([my_ids // 128, my_ids % 128], axis=1).astype(BF16)
-    marks = jnp.pad(marks, ((0, 0), (0, 126)))
-    text_row = jnp.concatenate([text_unit.astype(BF16), marks], axis=1)
-    line = spread(text_row, "dp", LINE, ZL).reshape(ZL * share, -1)
-    texts = spread(line, "dp", RING, Y).reshape(cycle * share, -1)
-    text_low = texts[:, :embed_width]
-    ids = texts[:, embed_width].astype(jnp.int32) * 128 + texts[:, embed_width + 1].astype(jnp.int32)
+    marks = jnp.concatenate([my_ids // 128, my_ids % 128]).astype(BF16)
+    piece = -(-share // 8) * 8
+    marks = jnp.pad(marks[None], ((0, piece - share - 1), (0, embed_width - 2 * share)))
+    block = jnp.concatenate([text_unit.astype(BF16), marks], axis=0)
+    blocks = lax.all_gather(block, "dp", axis_index_groups=LINE)
+    count = ZL * share
+    line = jnp.concatenate([blocks[:, :share].reshape(count, embed_width), blocks[:, share]], axis=0)
+    lines = lax.all_gather(line, "dp", axis_index_groups=RING)
+    text_low = lines[:, :count].reshape(cycle * share, embed_width)
+    notes = lines[:, count:, : 2 * share].astype(jnp.int32)
+    ids = (notes[:, :, :share] * 128 + notes[:, :, share:]).reshape(cycle * share)
 
     feats = jnp.pad(image_feats.reshape(plane, own, width), ((0, 0), (0, held - own), (0, 0)))
     feats = feats.reshape(plane * held, width)
@@ -81,10 +85,9 @@
     feature_grad = jnp.einsum("re,we->rw", grads, image_head, preferred_element_type=F32).astype(BF16)
     feature_grad = feature_grad.reshape(plane, held, width)[:, :own].reshape(rows, width)
 
-    text_acc = swap(text_acc.reshape(Y, ZL * share, embed_width), "dp", RING)
-    text_acc = jnp.sum(text_acc.astype(F32), axis=0).astype(BF16)
-    text_acc = swap(text_acc.reshape(ZL, share, embed_width), "dp", LINE)
-    text_acc = jnp.sum(text_acc.astype(F32), axis=0)
+    text_acc = lax.psum_scatter(text_acc.reshape(Y, count, embed_width), "dp", axis_index_groups=RING)
+    text_acc = lax.psum_scatter(text_acc.reshape(ZL, share, embed_width), "dp", axis_index_groups=LINE)
+    text_acc = text_acc.astype(F32)
     text_dot = jnp.sum(text_unit * text_acc, axis=1, keepdims=True)
     text_rows = (text_scale * (text_acc - text_unit * text_dot)).astype(BF16)
     text_rows = text_rows.reshape(share, group, width).transpose(1, 0, 2)

time: 326 us -> 340 us (1.043)
  blocking collectives: 0 us -> 111 us
  waiting for transfers between devices: 195 us -> 129 us
  starting transfers between devices: 97 us -> 60.6 us
  between operations: 2.18 us -> 15.3 us
  matrix products: 10.4 us -> 6.53 us
    all_to_all x12 -> x5, waiting for transfers between devices: 171 us -> 66.2 us  [swap(): lax.all_to_all(value, axis, 0, 0, axis_index_groups=groups, tiled=True)]
    all_to_all x0 -> x3, blocking collectives: none -> 69.1 us  [swap(): lax.all_to_all(value, axis, 0, 0, axis_index_groups=groups, tiled=True)]
    reduce_scatter x0 -> x2, waiting for transfers between devices: none -> 45.3 us  [the longest x1 45.3 us: on_device(): lax.psum_scatter(text_acc.reshape(ZL, share, embed_width), 'dp', axis_ind...]
    all_gather x0 -> x1, blocking collectives: none -> 42.4 us  [on_device(): blocks = lax.all_gather(block, 'dp', axis_index_groups=LINE)]
    all_to_all x12 -> x5, starting transfers between devices: 92.7 us -> 50.9 us  [swap(): lax.all_to_all(value, axis, 0, 0, axis_index_groups=groups, tiled=True)]
    ppermute x1, waiting for transfers between devices: 12.2 us -> 6.85 us  [on_device(): unit_grad = back.astype(F32) + lax.ppermute(back, 'fsdp', PAIR).astype(F32)]
    ppermute x1, starting transfers between devices: 2.14 us -> 7.48 us  [on_device(): unit_grad = back.astype(F32) + lax.ppermute(back, 'fsdp', PAIR).astype(F32)]
  transfers between devices with their start and end apart: 14 -> 10, of which waited for: 14 -> 8; matrix products, arithmetic and copies ran while one was open for 5% -> 4% of each run, Pallas kernels for 0% -> 0%
where the time goes in v3:
time: 340 us; the launch traced here: 339 us
  waiting for transfers between devices  129 us (38%)
  blocking collectives  111 us (33%)
  starting transfers between devices  60.6 us (18%)
  between operations  15.3 us (4%)
  local copies, waits for them, and re-layouts  11.4 us (3%)
  matrix products  6.53 us (2%)
  other arithmetic  4.64 us (1%)
    all_to_all x3, blocking collectives, swap(): lax.all_to_all(value, axis, 0, 0, axis_index_groups=groups, tiled=True)  69.1 us
    all_to_all x5, waiting for transfers between devices, swap(): lax.all_to_all(value, axis, 0, 0, axis_index_groups=groups, tiled=True)  66.2 us
    all_to_all x5, starting transfers between devices, swap(): lax.all_to_all(value, axis, 0, 0, axis_index_groups=groups, tiled=True)  50.9 us
    reduce_scatter x1, waiting for transfers between devices, on_device(): lax.psum_scatter(text_acc.reshape(ZL, share, embed_width), 'dp', axis_ind...  45.3 us
    all_gather x1, blocking collectives, on_device(): blocks = lax.all_gather(block, 'dp', axis_index_groups=LINE)  42.4 us
    ppermute x1, waiting for transfers between devices, on_device(): embed = half.astype(F32) + lax.ppermute(half, 'fsdp', PAIR).astype(F32)  10.9 us
    ppermute x1, starting transfers between devices, on_device(): unit_grad = back.astype(F32) + lax.ppermute(back, 'fsdp', PAIR).astype(F32)  7.48 us
    ppermute x1, waiting for transfers between devices, on_device(): unit_grad = back.astype(F32) + lax.ppermute(back, 'fsdp', PAIR).astype(F32)  6.85 us
  transfers between devices with their start and end apart: 10, of which 8 were waited for; matrix products, arithmetic and copies ran while one was open for 4% of the time, Pallas kernels for 0%

profile of v3, /device:TPU:1, one launch (start us, length us, event | category | flops | bytes accessed | tf_op | source)
XLA Modules:
  0.0 339.2 jit_solution(12824421435902156762)
XLA Ops:
  7.2 1.6 reshape.164
  8.8 19.1 %all-to-all-start.1 = ((bf16[16,18,96]{2,1,0:T(8,128)(2,1)}), bf16[16,18,96]{2,1,0:T(8,128)(2,1)S(1)}, u32[]{:S(2)}, u32[]{:S(2)}) async-start(bf16[16,18,96]{2,1,0:T(8,128)(2,1)} %reshape.164), calls=%async_computation.1 | async-start | bytes 196608 | tf_op jit(solution)/shard_map/all_to_all | solution.py:16
  27.9 0.8 convert_bitcast_fusion.1
  28.7 13.7 %all-to-all-done.1 = bf16[16,18,96]{2,1,0:T(8,128)(2,1)S(1)} async-done(((bf16[16,18,96]{2,1,0:T(8,128)(2,1)}), bf16[16,18,96]{2,1,0:T(8,128)(2,1)S(1)}, u32[]{:S(2)}, u32[]{:S(2)}) %all-to-all-start.1) | async-done | bytes 55328 | tf_op jit(solution)/shard_map/all_to_all | solution.py:16
  42.5 0.1 fusion.14
  42.7 0.1 reshape.176
  42.9 42.4 %all-gather = bf16[192,1536]{1,0:T(8,128)(2,1)S(1)} all-gather(bf16[24,1536]{1,0:T(8,128)(2,1)S(1)} %pad_maximum_fusion.1), channel_id=2, replica_groups={{0,64,128,192,256,320,384,448},{16,80,144,208,272,336,400,464},{32,96,1..., dimensions={0}, use_global_device_ids=true | all-gather | bytes 663552 | tf_op jit(solution)/shard_map/all_gather | solution.py:45
  85.4 0.1 reshape.165
  85.6 0.8 pad_maximum_fusion
  86.5 0.4 convolution_convert_fusion.2
  86.9 23.5 %all_to_all.40 = bf16[8,40,1536]{2,1,0:T(8,128)(2,1)S(1)} all-to-all(bf16[8,40,1536]{2,1,0:T(8,128)(2,1)S(1)} %bitcast.56), channel_id=1, replica_groups={{0,1,4,5,8,9,12,13},{2,3,6,7,10,11,14,15},{16,17,20,21,24,25,28,29},{18..., dimensions={0} | all-to-all | bytes 1966080 | tf_op jit(solution)/shard_map/all_to_all | solution.py:16
  110.4 0.1 reduce_sum.72
  110.5 2.2 collective-permute-start
  114.0 10.9 %collective-permute-done = bf16[40,1536]{1,0:T(8,128)(2,1)S(1)} collective-permute-done((bf16[40,1536]{1,0:T(8,128)(2,1)S(1)}, bf16[40,1536]{1,0:T(8,128)(2,1)S(1)}, u32[]{:S(2)}, u32[]{:S(2)}) %collective-permute-start) | collective-permute-done | bytes 122912 | tf_op jit(solution)/shard_map/ppermute | solution.py:58
  124.9 0.1 multiply_reduce_fusion.1
  125.1 1.0 broadcast_in_dim.21
  126.2 5.5 %all-to-all-start.2 = ((bf16[8,40,1536]{2,1,0:T(8,128)(2,1)}), bf16[8,40,1536]{2,1,0:T(8,128)(2,1)S(1)}, u32[]{:S(2)}, u32[]{:S(2)}) async-start(bf16[8,40,1536]{2,1,0:T(8,128)(2,1)} %broadcast_in_dim.21), calls=%async_computation.2 | async-start | bytes 1966080 | tf_op jit(solution)/shard_map/all_to_all | solution.py:16
  131.8 1.6 slice.33
  133.4 0.7 slice_convert_fusion
  134.3 11.8 %all-to-all-done.2 = bf16[8,40,1536]{2,1,0:T(8,128)(2,1)S(1)} async-done(((bf16[8,40,1536]{2,1,0:T(8,128)(2,1)}), bf16[8,40,1536]{2,1,0:T(8,128)(2,1)S(1)}, u32[]{:S(2)}, u32[]{:S(2)}) %all-to-all-start.2) | async-done | bytes 983072 | tf_op jit(solution)/shard_map/all_to_all | solution.py:16
  146.1 1.1 fusion.9
  147.2 1.9 convolution_convert_fusion.1
  149.1 4.5 %all-to-all-start.3 = ((bf16[8,40,1536]{2,1,0:T(8,128)(2,1)}), bf16[8,40,1536]{2,1,0:T(8,128)(2,1)S(1)}, u32[]{:S(2)}, u32[]{:S(2)}) async-start(bf16[8,40,1536]{2,1,0:T(8,128)(2,1)} %bitcast.67), calls=%async_computation.3 | async-start | bytes 1966080 | tf_op jit(solution)/shard_map/all_to_all | solution.py:16
  153.6 2.3 convolution_convert_fusion
  155.9 12.1 %all-to-all-done.3 = bf16[8,40,1536]{2,1,0:T(8,128)(2,1)S(1)} async-done(((bf16[8,40,1536]{2,1,0:T(8,128)(2,1)}), bf16[8,40,1536]{2,1,0:T(8,128)(2,1)S(1)}, u32[]{:S(2)}, u32[]{:S(2)}) %all-to-all-start.3) | async-done | bytes 983072 | tf_op jit(solution)/shard_map/all_to_all | solution.py:16
  168.0 0.1 reduce_sum.75
  168.1 7.5 %collective-permute-start.1 = (bf16[40,1536]{1,0:T(8,128)(2,1)S(1)}, bf16[40,1536]{1,0:T(8,128)(2,1)S(1)}, u32[]{:S(2)}, u32[]{:S(2)}) collective-permute-start(bf16[40,1536]{1,0:T(8,128)(2,1)S(1)} %reduce_sum.75), channel_id=1, source_target_pairs={{0,2},{1,3},{2,0},{3,1},{4,6},{5,7},{6,4},{7,5},{8,10},{9,11},{10,... | collective-permute-start | bytes 368648 | tf_op jit(solution)/shard_map/ppermute | solution.py:75
  175.6 6.9 %collective-permute-done.1 = bf16[40,1536]{1,0:T(8,128)(2,1)S(1)} collective-permute-done((bf16[40,1536]{1,0:T(8,128)(2,1)S(1)}, bf16[40,1536]{1,0:T(8,128)(2,1)S(1)}, u32[]{:S(2)}, u32[]{:S(2)}) %collective-permute-start.1) | collective-permute-done | bytes 122912 | tf_op jit(solution)/shard_map/ppermute | solution.py:75
  182.5 0.2 multiply_reduce_fusion
  182.9 18.9 %all_to_all.41 = bf16[8,40,1536]{2,1,0:T(8,128)(2,1)S(1)} all-to-all(bf16[8,40,1536]{2,1,0:T(8,128)(2,1)S(1)} %broadcast_in_dim.22), channel_id=1, replica_groups={{0,1,4,5,8,9,12,13},{2,3,6,7,10,11,14,15},{16,17,20,21,24,25,28,29},{18..., dimensions={0} | all-to-all | bytes 1966080 | tf_op jit(solution)/shard_map/all_to_all | solution.py:16
  201.7 0.4 fusion
  202.1 0.2 reshape.172
  202.5 26.7 %all_to_all.42 = bf16[32,36,128]{2,1,0:T(8,128)(2,1)S(1)} all-to-all(bf16[32,36,128]{2,1,0:T(8,128)(2,1)S(1)} %reshape.173), channel_id=1, replica_groups=mesh['dp'=32,'fsdp'=16] {'dp'}, dimensions={0} | all-to-all | bytes 589824 | tf_op jit(solution)/shard_map/all_to_all | solution.py:16
  229.2 0.8 broadcast_in_dim.40
  230.0 8.9 %all-to-all-start.6 = ((bf16[32,36,128]{2,1,0:T(8,128)(2,1)}), bf16[32,36,128]{2,1,0:T(8,128)(2,1)S(1)}, u32[]{:S(2)}, u32[]{:S(2)}) async-start(bf16[32,36,128]{2,1,0:T(8,128)(2,1)} %broadcast_in_dim.40), calls=%async_computation.6 | async-start | bytes 655360 | tf_op jit(solution)/shard_map/all_to_all | solution.py:16
  239.0 2.0 reshape_reduce_scatter.3
  241.0 0.4 convolution_convert_fusion.3
  241.4 0.1 copy.12
  241.5 0.7 reshape.171
  242.2 15.0 %all-to-all-done.6 = bf16[32,36,128]{2,1,0:T(8,128)(2,1)S(1)} async-done(((bf16[32,36,128]{2,1,0:T(8,128)(2,1)}), bf16[32,36,128]{2,1,0:T(8,128)(2,1)S(1)}, u32[]{:S(2)}, u32[]{:S(2)}) %all-to-all-start.6) | async-done | bytes 294944 | tf_op jit(solution)/shard_map/all_to_all | solution.py:16
  257.3 45.3 %reduce-scatter.5.cloned.1.call-done = bf16[1,18,1536]{2,1,0:T(8,128)(2,1)} async-done(((bf16[8,18,1536]{2,1,0:T(8,128)(2,1)}), bf16[1,18,1536]{2,1,0:T(8,128)(2,1)}) %reduce-scatter.5.cloned.1.call-update) | async-done | bytes 55312 | tf_op jit(solution)/shard_map/reduce_scatter | solution.py:89
  302.5 1.0 reshape.178
  303.5 0.2 fusion.13
  303.7 0.7 fusion.18
  304.5 12.9 %all-to-all-start.7 = ((bf16[16,18,96]{2,1,0:T(8,128)(2,1)}), bf16[16,18,96]{2,1,0:T(8,128)(2,1)S(1)}, u32[]{:S(2)}, u32[]{:S(2)}) async-start(bf16[16,18,96]{2,1,0:T(8,128)(2,1)} %fusion.18), calls=%async_computation.9 | async-start | bytes 196608 | tf_op jit(solution)/shard_map/all_to_all | solution.py:16
  317.4 0.9 copy_bitcast_fusion
  318.3 13.7 %all-to-all-done.7 = bf16[16,18,96]{2,1,0:T(8,128)(2,1)S(1)} async-done(((bf16[16,18,96]{2,1,0:T(8,128)(2,1)}), bf16[16,18,96]{2,1,0:T(8,128)(2,1)S(1)}, u32[]{:S(2)}, u32[]{:S(2)}) %all-to-all-start.7) | async-done | bytes 55328 | tf_op jit(solution)/shard_map/all_to_all | solution.py:16
  332.0 0.7 reshape.175
  (41 shorter events, 1.4 us)
Async XLA Ops:
  7.2 79.3 %copy-start = (bf16[96,1536]{1,0:T(8,128)(2,1)S(1)}, bf16[96,1536]{1,0:T(8,128)(2,1)}, u32[]{:S(2)}) copy-start(bf16[96,1536]{1,0:T(8,128)(2,1)} %param.7) | copy-start | bytes 884740
  8.8 33.7 %all-to-all-start.1 = ((bf16[16,18,96]{2,1,0:T(8,128)(2,1)}), bf16[16,18,96]{2,1,0:T(8,128)(2,1)S(1)}, u32[]{:S(2)}, u32[]{:S(2)}) async-start(bf16[16,18,96]{2,1,0:T(8,128)(2,1)} %reshape.164), calls=%async_computation.1 | async-start | bytes 196608 | tf_op jit(solution)/shard_map/all_to_all | solution.py:16
  27.8 104.0 %all-gather.4.cloned.1.call-start = ((), (), s32[]{:S(2)}) async-start(), calls=%async_computation.12 | async-start | bytes 2334720 | tf_op jit(solution)/shard_map/all_gather | solution.py:48
  42.9 43.5 %copy-start.1 = (bf16[288,96]{1,0:T(8,128)(2,1)S(1)}, bf16[288,96]{1,0:T(8,128)(2,1)}, u32[]{:S(2)}) copy-start(bf16[288,96]{1,0:T(8,128)(2,1)} %param.6) | copy-start | bytes 165892
  110.5 14.3 %collective-permute-start = (bf16[40,1536]{1,0:T(8,128)(2,1)S(1)}, bf16[40,1536]{1,0:T(8,128)(2,1)S(1)}, u32[]{:S(2)}, u32[]{:S(2)}) collective-permute-start(bf16[40,1536]{1,0:T(8,128)(2,1)S(1)} %reduce_sum.72), channel_id=1, source_target_pairs={{0,2},{1,3},{2,0},{3,1},{4,6},{5,7},{6,4},{7,5},{8,10},{9,11},{10,... | collective-permute-start | bytes 368648 | tf_op jit(solution)/shard_map/ppermute | solution.py:58
  126.2 19.9 %all-to-all-start.2 = ((bf16[8,40,1536]{2,1,0:T(8,128)(2,1)}), bf16[8,40,1536]{2,1,0:T(8,128)(2,1)S(1)}, u32[]{:S(2)}, u32[]{:S(2)}) async-start(bf16[8,40,1536]{2,1,0:T(8,128)(2,1)} %broadcast_in_dim.21), calls=%async_computation.2 | async-start | bytes 1966080 | tf_op jit(solution)/shard_map/all_to_all | solution.py:16
  147.2 1.9 copy-start.2
  149.1 4.5 %copy-start.3 = (bf16[320,576]{1,0:T(8,128)(2,1)S(1)}, bf16[320,576]{1,0:T(8,128)(2,1)}, u32[]{:S(2)}) copy-start(bf16[320,576]{1,0:T(8,128)(2,1)} %copy-done.2) | copy-start | bytes 1105924
  149.1 18.9 %all-to-all-start.3 = ((bf16[8,40,1536]{2,1,0:T(8,128)(2,1)}), bf16[8,40,1536]{2,1,0:T(8,128)(2,1)S(1)}, u32[]{:S(2)}, u32[]{:S(2)}) async-start(bf16[8,40,1536]{2,1,0:T(8,128)(2,1)} %bitcast.67), calls=%async_computation.3 | async-start | bytes 1966080 | tf_op jit(solution)/shard_map/all_to_all | solution.py:16
  153.6 85.4 %reduce-scatter.3.cloned.1.call-start = ((), (), s32[]{:S(2)}) async-start(), calls=%async_computation.10 | async-start | bytes 2211840 | tf_op jit(solution)/shard_map/reduce_scatter | solution.py:88
  168.1 14.3 %collective-permute-start.1 = (bf16[40,1536]{1,0:T(8,128)(2,1)S(1)}, bf16[40,1536]{1,0:T(8,128)(2,1)S(1)}, u32[]{:S(2)}, u32[]{:S(2)}) collective-permute-start(bf16[40,1536]{1,0:T(8,128)(2,1)S(1)} %reduce_sum.75), channel_id=1, source_target_pairs={{0,2},{1,3},{2,0},{3,1},{4,6},{5,7},{6,4},{7,5},{8,10},{9,11},{10,... | collective-permute-start | bytes 368648 | tf_op jit(solution)/shard_map/ppermute | solution.py:75
  230.0 27.2 %all-to-all-start.6 = ((bf16[32,36,128]{2,1,0:T(8,128)(2,1)}), bf16[32,36,128]{2,1,0:T(8,128)(2,1)S(1)}, u32[]{:S(2)}, u32[]{:S(2)}) async-start(bf16[32,36,128]{2,1,0:T(8,128)(2,1)} %broadcast_in_dim.40), calls=%async_computation.6 | async-start | bytes 655360 | tf_op jit(solution)/shard_map/all_to_all | solution.py:16
  238.9 63.6 %reduce-scatter.5.cloned.1.call-start = ((), (), s32[]{:S(2)}) async-start(), calls=%async_computation.11 | async-start | bytes 663552 | tf_op jit(solution)/shard_map/reduce_scatter | solution.py:89
  304.5 27.5 %all-to-all-start.7 = ((bf16[16,18,96]{2,1,0:T(8,128)(2,1)}), bf16[16,18,96]{2,1,0:T(8,128)(2,1)S(1)}, u32[]{:S(2)}, u32[]{:S(2)}) async-start(bf16[16,18,96]{2,1,0:T(8,128)(2,1)} %fusion.18), calls=%async_computation.9 | async-start | bytes 196608 | tf_op jit(solution)/shard_map/all_to_all | solution.py:16
Sparse Core Ops, SparseCore 0:
  86.5 35.2 all-gather.3
  157.3 31.1 reduce-scatter.2
  243.4 59.0 reduce-scatter.4

commit v4 on v3

--- a/solution.py
+++ b/solution.py
@@ -10,6 +10,8 @@
 LINE = [[z * Y + y for z in range(ZL)] for y in range(Y)]
 RING = [[z * Y + y for y in range(Y)] for z in range(ZL)]
 PAIR = [(i, i ^ 2) for i in range(16)]
+QUAD = [[(q * 4 + i) * Y + y for i in range(4)] for q in range(ZL // 4) for y in range(Y)]
+ACROSS = [(i, i ^ (4 * Y)) for i in range(ZL * Y)]
 
 
 def swap(value, axis, groups=None):
@@ -42,23 +44,29 @@
     piece = -(-share // 8) * 8
     marks = jnp.pad(marks[None], ((0, piece - share - 1), (0, embed_width - 2 * share)))
     block = jnp.concatenate([text_unit.astype(BF16), marks], axis=0)
-    blocks = lax.all_gather(block, "dp", axis_index_groups=LINE)
-    count = ZL * share
-    line = jnp.concatenate([blocks[:, :share].reshape(count, embed_width), blocks[:, share]], axis=0)
-    lines = lax.all_gather(line, "dp", axis_index_groups=RING)
-    text_low = lines[:, :count].reshape(cycle * share, embed_width)
-    notes = lines[:, count:, : 2 * share].astype(jnp.int32)
-    ids = (notes[:, :, :share] * 128 + notes[:, :, share:]).reshape(cycle * share)
+    blocks = spread(block, "dp", QUAD, 4).reshape(4, piece, embed_width)
+    count = 4 * share
+    quad = jnp.concatenate([blocks[:, :share].reshape(count, embed_width), blocks[:, share]], axis=0)
+    quad = jnp.pad(quad, ((0, 4), (0, 0)))
 
     feats = jnp.pad(image_feats.reshape(plane, own, width), ((0, 0), (0, held - own), (0, 0)))
     feats = feats.reshape(plane * held, width)
     term = jnp.dot(feats, image_head, preferred_element_type=F32).astype(BF16)
+    term, quad = lax.optimization_barrier((term, quad))
+    crossed = lax.ppermute(quad, "dp", ACROSS)
     half = swap(term.reshape(plane, held, embed_width), "fsdp", PLANE)
     half = jnp.sum(half.astype(F32), axis=0).astype(BF16)
+    line = jnp.stack([quad, crossed])
+    half, line = lax.optimization_barrier((half, line))
+
+    lines = lax.all_gather(line, "dp", axis_index_groups=RING)
     embed = half.astype(F32) + lax.ppermute(half, "fsdp", PAIR).astype(F32)
     image_scale = lax.rsqrt(jnp.sum(embed * embed, axis=1, keepdims=True) + 1e-06)
     image_unit = embed * image_scale
     image_low = spread(image_unit.astype(BF16), "fsdp", PLANE, plane).reshape(plane * held, embed_width)
+    text_low = lines[:, :, :count].reshape(cycle * share, embed_width)
+    notes = lines[:, :, count : count + 4, : 2 * share].astype(jnp.int32)
+    ids = (notes[..., :share] * 128 + notes[..., share:]).reshape(cycle * share)
 
     partial_value = jnp.einsum("ie,je->ij", image_low, text_low, preferred_element_type=F32)
     logits = logit_scale * partial_value + logit_bias
@@ -70,23 +78,30 @@
     unit_part = jnp.einsum("ij,je->ie", coef, text_low, preferred_element_type=F32).astype(BF16)
     text_acc = jnp.einsum("ij,ie->je", coef, image_low, preferred_element_type=F32).astype(BF16)
 
+    unit_part, text_acc = lax.optimization_barrier((unit_part, text_acc))
+
+    text_acc = lax.psum_scatter(text_acc.reshape(Y, ZL * share, embed_width), "dp", axis_index_groups=RING)
     back = swap(unit_part.reshape(plane, held, embed_width), "fsdp", PLANE)
     back = jnp.sum(back.astype(F32), axis=0).astype(BF16)
     unit_grad = back.astype(F32) + lax.ppermute(back, "fsdp", PAIR).astype(F32)
     image_dot = jnp.sum(image_unit * unit_grad, axis=1, keepdims=True)
     embed_grad = (image_scale * (unit_grad - image_unit * image_dot)).astype(BF16)
+    text_acc = text_acc.reshape(2, 4, share, embed_width)
+    text_acc = jnp.where(d // Y < 4, text_acc, text_acc[::-1]).reshape(ZL, share, embed_width)
+    embed_grad, text_acc = lax.optimization_barrier((embed_grad, text_acc))
+    text_acc = lax.psum_scatter(text_acc, "dp", axis_index_groups=LINE)
     grads = spread(embed_grad, "fsdp", PLANE, plane).reshape(plane * held, embed_width)
-    lanes = embed_width // 128
     head_part = jnp.einsum("rw,re->we", feats, grads, preferred_element_type=F32).astype(BF16)
-    head_part = head_part.reshape(width, lanes, 128).transpose(1, 0, 2).reshape(cycle, -1, 128)
-    head_sum = jnp.sum(swap(head_part, "dp").astype(F32), axis=0).astype(BF16)
-    head_all = spread(head_sum, "dp", None, cycle)
-    head_grad = head_all.reshape(lanes, width, 128).transpose(1, 0, 2).reshape(width, embed_width).astype(F32)
+    head_sum = jnp.sum(swap(head_part.reshape(Y, width // Y, embed_width), "dp", RING).astype(F32), axis=0)
+    head_sum = head_sum.astype(BF16).reshape(width // Y, ZL, embed_width // ZL).transpose(1, 0, 2)
+    head_sum = jnp.sum(swap(head_sum, "dp", LINE).astype(F32), axis=0).astype(BF16)
+    head_all = spread(head_sum, "dp", LINE, ZL).transpose(1, 0, 2).reshape(width // Y, embed_width)
+    head_all = spread(head_all, "dp", RING, Y).reshape(width, embed_width)
+    head_all, text_acc = lax.optimization_barrier((head_all, text_acc))
+    head_grad = head_all.astype(F32)
     feature_grad = jnp.einsum("re,we->rw", grads, image_head, preferred_element_type=F32).astype(BF16)
     feature_grad = feature_grad.reshape(plane, held, width)[:, :own].reshape(rows, width)
 
-    text_acc = lax.psum_scatter(text_acc.reshape(Y, count, embed_width), "dp", axis_index_groups=RING)
-    text_acc = lax.psum_scatter(text_acc.reshape(ZL, share, embed_width), "dp", axis_index_groups=LINE)
     text_acc = text_acc.astype(F32)
     text_dot = jnp.sum(text_unit * text_acc, axis=1, keepdims=True)
     text_rows = (text_scale * (text_acc - text_unit * text_dot)).astype(BF16)

time: 340 us -> 304 us (0.89)
  blocking collectives: 111 us -> 66.8 us
  starting transfers between devices: 60.6 us -> 82.2 us
  waiting for transfers between devices: 129 us -> 112 us
    all_gather x1 -> x0, blocking collectives: 42.4 us -> none  [on_device(): blocks = lax.all_gather(block, 'dp', axis_index_groups=LINE)]
    all_to_all x5 -> x7, waiting for transfers between devices: 66.2 us -> 38 us  [swap(): lax.all_to_all(value, axis, 0, 0, axis_index_groups=groups, tiled=True)]
    ppermute x0 -> x1, waiting for transfers between devices: none -> 27.3 us  [on_device(): crossed = lax.ppermute(quad, 'dp', ACROSS)]
    reduce_scatter x2, waiting for transfers between devices: 45.3 us -> 21.5 us  [the longest x1 21.4 us: on_device(): text_acc = lax.psum_scatter(text_acc, 'dp', axis_index_groups=LINE)]
    all_to_all x5 -> x7, starting transfers between devices: 50.9 us -> 64.7 us  [swap(): lax.all_to_all(value, axis, 0, 0, axis_index_groups=groups, tiled=True)]
    all_gather x1, waiting for transfers between devices: 0.01 us -> 9.35 us  [on_device(): lines = lax.all_gather(line, 'dp', axis_index_groups=RING)]
    ppermute x1, starting transfers between devices: 7.48 us -> 11.6 us  [on_device(): unit_grad = back.astype(F32) + lax.ppermute(back, 'fsdp', PAIR).astype(F32)]
    ppermute x0 -> x1, starting transfers between devices: none -> 3.93 us  [on_device(): crossed = lax.ppermute(quad, 'dp', ACROSS)]
  transfers between devices with their start and end apart: 10 -> 13, of which waited for: 8 -> 10; matrix products, arithmetic and copies ran while one was open for 4% -> 4% of each run, Pallas kernels for 0% -> 0%
where the time goes in v4:
time: 304 us; the launch traced here: 303 us
  waiting for transfers between devices  112 us (37%)
  starting transfers between devices  82.2 us (27%)
  blocking collectives  66.8 us (22%)
  between operations  15.3 us (5%)
  local copies, waits for them, and re-layouts  11.1 us (4%)
  matrix products  8.21 us (3%)
  other arithmetic  7.59 us (2%)
    all_to_all x4, blocking collectives, swap(): lax.all_to_all(value, axis, 0, 0, axis_index_groups=groups, tiled=True)  66.8 us
    all_to_all x7, starting transfers between devices, swap(): lax.all_to_all(value, axis, 0, 0, axis_index_groups=groups, tiled=True)  64.7 us
    all_to_all x7, waiting for transfers between devices, swap(): lax.all_to_all(value, axis, 0, 0, axis_index_groups=groups, tiled=True)  38 us
    ppermute x1, waiting for transfers between devices, on_device(): crossed = lax.ppermute(quad, 'dp', ACROSS)  27.3 us
    reduce_scatter x1, waiting for transfers between devices, on_device(): text_acc = lax.psum_scatter(text_acc, 'dp', axis_index_groups=LINE)  21.4 us
    ppermute x1, waiting for transfers between devices, on_device(): embed = half.astype(F32) + lax.ppermute(half, 'fsdp', PAIR).astype(F32)  11.7 us
    ppermute x1, starting transfers between devices, on_device(): unit_grad = back.astype(F32) + lax.ppermute(back, 'fsdp', PAIR).astype(F32)  11.6 us
    all_gather x1, waiting for transfers between devices, on_device(): lines = lax.all_gather(line, 'dp', axis_index_groups=RING)  9.35 us
  transfers between devices with their start and end apart: 13, of which 10 were waited for; matrix products, arithmetic and copies ran while one was open for 4% of the time, Pallas kernels for 0%

profile of v4, /device:TPU:1, one launch (start us, length us, event | category | flops | bytes accessed | tf_op | source)
XLA Modules:
  0.0 302.7 jit_solution(13185691282830098633)
XLA Ops:
  7.2 1.6 reshape.143
  8.8 19.1 %all-to-all-start = ((bf16[16,18,96]{2,1,0:T(8,128)(2,1)}), bf16[16,18,96]{2,1,0:T(8,128)(2,1)S(1)}, u32[]{:S(2)}, u32[]{:S(2)}) async-start(bf16[16,18,96]{2,1,0:T(8,128)(2,1)} %reshape.143), calls=%async_computation | async-start | bytes 196608 | tf_op jit(solution)/shard_map/all_to_all | solution.py:18
  27.9 0.8 convert_bitcast_fusion.1
  28.7 13.8 %all-to-all-done = bf16[16,18,96]{2,1,0:T(8,128)(2,1)S(1)} async-done(((bf16[16,18,96]{2,1,0:T(8,128)(2,1)}), bf16[16,18,96]{2,1,0:T(8,128)(2,1)S(1)}, u32[]{:S(2)}, u32[]{:S(2)}) %all-to-all-start) | async-done | bytes 55328 | tf_op jit(solution)/shard_map/all_to_all | solution.py:18
  42.9 0.7 broadcast_in_dim.24
  43.7 3.5 %all-to-all-start.1 = ((bf16[4,24,1536]{2,1,0:T(8,128)(2,1)}), bf16[4,24,1536]{2,1,0:T(8,128)(2,1)S(1)}, u32[]{:S(2)}, u32[]{:S(2)}) async-start(bf16[4,24,1536]{2,1,0:T(8,128)(2,1)} %broadcast_in_dim.24), calls=%async_computation.1 | async-start | bytes 589824 | tf_op jit(solution)/shard_map/all_to_all | solution.py:18
  47.2 1.3 convolution_convert_fusion.2
  48.6 4.4 %all-to-all-done.1 = bf16[4,24,1536]{2,1,0:T(8,128)(2,1)S(1)} async-done(((bf16[4,24,1536]{2,1,0:T(8,128)(2,1)}), bf16[4,24,1536]{2,1,0:T(8,128)(2,1)S(1)}, u32[]{:S(2)}, u32[]{:S(2)}) %all-to-all-start.1) | async-done | bytes 294944 | tf_op jit(solution)/shard_map/all_to_all | solution.py:18
  53.2 8.2 %all-to-all-start.2 = ((bf16[8,40,1536]{2,1,0:T(8,128)(2,1)}), bf16[8,40,1536]{2,1,0:T(8,128)(2,1)S(1)}, u32[]{:S(2)}, u32[]{:S(2)}) async-start(bf16[8,40,1536]{2,1,0:T(8,128)(2,1)} %bitcast.4), calls=%async_computation.2 | async-start | bytes 1966080 | tf_op jit(solution)/shard_map/all_to_all | solution.py:18
  61.4 3.9 %collective-permute-start = (bf16[80,1536]{1,0:T(8,128)(2,1)S(1)}, bf16[80,1536]{1,0:T(8,128)(2,1)S(1)}, u32[]{:S(2)}, u32[]{:S(2)}) collective-permute-start(bf16[80,1536]{1,0:T(8,128)(2,1)S(1)} %fusion.12), channel_id=1, source_target_pairs={{0,256},{16,272},{32,288},{48,304},{64,320},{80,336},{96,352},{112... | collective-permute-start | bytes 737288 | tf_op jit(solution)/shard_map/ppermute | solution.py:56
  65.3 27.3 %collective-permute-done = bf16[80,1536]{1,0:T(8,128)(2,1)S(1)} collective-permute-done((bf16[80,1536]{1,0:T(8,128)(2,1)S(1)}, bf16[80,1536]{1,0:T(8,128)(2,1)S(1)}, u32[]{:S(2)}, u32[]{:S(2)}) %collective-permute-start) | collective-permute-done | bytes 245792 | tf_op jit(solution)/shard_map/ppermute | solution.py:56
  92.6 0.8 pad_maximum_fusion
  93.6 1.9 collective-permute-start.1
  96.8 11.7 %collective-permute-done.1 = bf16[40,1536]{1,0:T(8,128)(2,1)S(1)} collective-permute-done((bf16[40,1536]{1,0:T(8,128)(2,1)S(1)}, bf16[40,1536]{1,0:T(8,128)(2,1)S(1)}, u32[]{:S(2)}, u32[]{:S(2)}) %collective-permute-start.1) | collective-permute-done | bytes 122912 | tf_op jit(solution)/shard_map/ppermute | solution.py:63
  108.8 1.0 broadcast_in_dim.28
  109.8 5.9 %all-to-all-start.3 = ((bf16[8,40,1536]{2,1,0:T(8,128)(2,1)}), bf16[8,40,1536]{2,1,0:T(8,128)(2,1)S(1)}, u32[]{:S(2)}, u32[]{:S(2)}) async-start(bf16[8,40,1536]{2,1,0:T(8,128)(2,1)} %broadcast_in_dim.28), calls=%async_computation.3 | async-start | bytes 1966080 | tf_op jit(solution)/shard_map/all_to_all | solution.py:18
  115.8 9.3 %all-gather.3.cloned.1.call-done = bf16[8,80,1536]{2,1,0:T(8,128)(2,1)} async-done(((bf16[2,80,1536]{2,1,0:T(8,128)(2,1)}), bf16[8,80,1536]{2,1,0:T(8,128)(2,1)}) %all-gather.3.cloned.1.call-update) | async-done | bytes 1966096 | tf_op jit(solution)/shard_map/all_gather | solution.py:62
  125.2 1.6 slice.33
  126.8 0.7 slice_convert_fusion
  127.7 2.4 all-to-all-done.3
  130.1 1.1 fusion.9
  131.2 1.9 convolution_convert_fusion.1
  133.1 2.3 convolution_convert_fusion
  135.4 1.2 copy-done.1
  136.6 17.7 %all_to_all.55 = bf16[8,40,1536]{2,1,0:T(8,128)(2,1)S(1)} all-to-all(bf16[8,40,1536]{2,1,0:T(8,128)(2,1)S(1)} %bitcast.55), channel_id=1, replica_groups={{0,1,4,5,8,9,12,13},{2,3,6,7,10,11,14,15},{16,17,20,21,24,25,28,29},{18..., dimensions={0} | all-to-all | bytes 1966080 | tf_op jit(solution)/shard_map/all_to_all | solution.py:18
  154.5 11.6 %collective-permute-start.2 = (bf16[40,1536]{1,0:T(8,128)(2,1)S(1)}, bf16[40,1536]{1,0:T(8,128)(2,1)S(1)}, u32[]{:S(2)}, u32[]{:S(2)}) collective-permute-start(bf16[40,1536]{1,0:T(8,128)(2,1)S(1)} %reduce_sum.87), channel_id=1, source_target_pairs={{0,2},{1,3},{2,0},{3,1},{4,6},{5,7},{6,4},{7,5},{8,10},{9,11},{10,... | collective-permute-start | bytes 368648 | tf_op jit(solution)/shard_map/ppermute | solution.py:86
  166.1 3.0 collective-permute-done.2
  169.4 1.1 reshape_reduce_scatter.3
  170.6 0.9 reverse_select_fusion
  171.6 18.9 %all_to_all.56 = bf16[8,40,1536]{2,1,0:T(8,128)(2,1)S(1)} all-to-all(bf16[8,40,1536]{2,1,0:T(8,128)(2,1)S(1)} %broadcast_in_dim.29), channel_id=1, replica_groups={{0,1,4,5,8,9,12,13},{2,3,6,7,10,11,14,15},{16,17,20,21,24,25,28,29},{18..., dimensions={0} | all-to-all | bytes 1966080 | tf_op jit(solution)/shard_map/all_to_all | solution.py:18
  190.4 1.1 fusion
  191.5 11.9 %all-to-all-start.6 = ((bf16[4,24,1536]{2,1,0:T(8,128)(2,1)}), bf16[4,24,1536]{2,1,0:T(8,128)(2,1)S(1)}, u32[]{:S(2)}, u32[]{:S(2)}) async-start(bf16[4,24,1536]{2,1,0:T(8,128)(2,1)} %bitcast.16), calls=%async_computation.7 | async-start | bytes 589824 | tf_op jit(solution)/shard_map/all_to_all | solution.py:18
  203.4 0.7 reduce-scatter.5.cloned.1.call-update
  204.1 5.0 %all-to-all-done.6 = bf16[4,24,1536]{2,1,0:T(8,128)(2,1)S(1)} async-done(((bf16[4,24,1536]{2,1,0:T(8,128)(2,1)}), bf16[4,24,1536]{2,1,0:T(8,128)(2,1)S(1)}, u32[]{:S(2)}, u32[]{:S(2)}) %all-to-all-start.6) | async-done | bytes 294944 | tf_op jit(solution)/shard_map/all_to_all | solution.py:18
  209.3 17.4 %all_to_all.57 = bf16[8,24,192]{2,1,0:T(8,128)(2,1)S(1)} all-to-all(bf16[8,24,192]{2,1,0:T(8,128)(2,1)S(1)} %copy.19), channel_id=1, replica_groups={{0,64,128,192,256,320,384,448},{16,80,144,208,272,336,400,464},{32,96,1..., dimensions={0} | all-to-all | bytes 147456 | tf_op jit(solution)/shard_map/all_to_all | solution.py:18
  226.8 12.8 %all_to_all.58 = bf16[8,24,192]{2,1,0:T(8,128)(2,1)S(1)} all-to-all(bf16[8,24,192]{2,1,0:T(8,128)(2,1)S(1)} %broadcast_in_dim.54), channel_id=1, replica_groups={{0,64,128,192,256,320,384,448},{16,80,144,208,272,336,400,464},{32,96,1..., dimensions={0} | all-to-all | bytes 147456 | tf_op jit(solution)/shard_map/all_to_all | solution.py:18
  239.7 0.7 broadcast_in_dim.56
  240.5 3.5 %all-to-all-start.9 = ((bf16[4,24,1536]{2,1,0:T(8,128)(2,1)}), bf16[4,24,1536]{2,1,0:T(8,128)(2,1)S(1)}, u32[]{:S(2)}, u32[]{:S(2)}) async-start(bf16[4,24,1536]{2,1,0:T(8,128)(2,1)} %broadcast_in_dim.56), calls=%async_computation.10 | async-start | bytes 589824 | tf_op jit(solution)/shard_map/all_to_all | solution.py:18
  243.9 21.4 %reduce-scatter.5.cloned.1.call-done = bf16[1,18,1536]{2,1,0:T(8,128)(2,1)} async-done(((bf16[8,18,1536]{2,1,0:T(8,128)(2,1)}), bf16[1,18,1536]{2,1,0:T(8,128)(2,1)}) %reduce-scatter.5.cloned.1.call-update) | async-done | bytes 55312 | tf_op jit(solution)/shard_map/reduce_scatter | solution.py:92
  265.3 1.1 fusion.16
  266.4 1.0 fusion.18
  267.5 0.7 copy.21
  268.2 12.8 %all-to-all-start.10 = ((bf16[16,18,96]{2,1,0:T(8,128)(2,1)}), bf16[16,18,96]{2,1,0:T(8,128)(2,1)S(1)}, u32[]{:S(2)}, u32[]{:S(2)}) async-start(bf16[16,18,96]{2,1,0:T(8,128)(2,1)} %copy.21), calls=%async_computation.12 | async-start | bytes 196608 | tf_op jit(solution)/shard_map/all_to_all | solution.py:18
  281.0 0.4 convolution_convert_fusion.3
  281.5 0.7 reshape.153
  282.2 0.9 convert_element_type.104
  283.1 12.5 %all-to-all-done.10 = bf16[16,18,96]{2,1,0:T(8,128)(2,1)S(1)} async-done(((bf16[16,18,96]{2,1,0:T(8,128)(2,1)}), bf16[16,18,96]{2,1,0:T(8,128)(2,1)S(1)}, u32[]{:S(2)}, u32[]{:S(2)}) %all-to-all-start.10) | async-done | bytes 55328 | tf_op jit(solution)/shard_map/all_to_all | solution.py:18
  295.5 0.7 reshape.158
  (51 shorter events, 2.6 us)
Async XLA Ops:
  7.2 40.0 %copy-start = (bf16[96,1536]{1,0:T(8,128)(2,1)S(1)}, bf16[96,1536]{1,0:T(8,128)(2,1)}, u32[]{:S(2)}) copy-start(bf16[96,1536]{1,0:T(8,128)(2,1)} %param.7) | copy-start | bytes 884740
  7.2 39.9 %copy-start.2 = (bf16[288,96]{1,0:T(8,128)(2,1)S(1)}, bf16[288,96]{1,0:T(8,128)(2,1)}, u32[]{:S(2)}) copy-start(bf16[288,96]{1,0:T(8,128)(2,1)} %param.6) | copy-start | bytes 165892
  8.8 33.7 %all-to-all-start = ((bf16[16,18,96]{2,1,0:T(8,128)(2,1)}), bf16[16,18,96]{2,1,0:T(8,128)(2,1)S(1)}, u32[]{:S(2)}, u32[]{:S(2)}) async-start(bf16[16,18,96]{2,1,0:T(8,128)(2,1)} %reshape.143), calls=%async_computation | async-start | bytes 196608 | tf_op jit(solution)/shard_map/all_to_all | solution.py:18
  43.7 9.3 %all-to-all-start.1 = ((bf16[4,24,1536]{2,1,0:T(8,128)(2,1)}), bf16[4,24,1536]{2,1,0:T(8,128)(2,1)S(1)}, u32[]{:S(2)}, u32[]{:S(2)}) async-start(bf16[4,24,1536]{2,1,0:T(8,128)(2,1)} %broadcast_in_dim.24), calls=%async_computation.1 | async-start | bytes 589824 | tf_op jit(solution)/shard_map/all_to_all | solution.py:18
  53.2 40.3 %all-to-all-start.2 = ((bf16[8,40,1536]{2,1,0:T(8,128)(2,1)}), bf16[8,40,1536]{2,1,0:T(8,128)(2,1)S(1)}, u32[]{:S(2)}, u32[]{:S(2)}) async-start(bf16[8,40,1536]{2,1,0:T(8,128)(2,1)} %bitcast.4), calls=%async_computation.2 | async-start | bytes 1966080 | tf_op jit(solution)/shard_map/all_to_all | solution.py:18
  61.4 63.8 %all-gather.3.cloned.1.call-start = ((), (), s32[]{:S(2)}) async-start(), calls=%async_computation.15 | async-start | bytes 2457600 | tf_op jit(solution)/shard_map/all_gather | solution.py:62
  61.4 31.2 %collective-permute-start = (bf16[80,1536]{1,0:T(8,128)(2,1)S(1)}, bf16[80,1536]{1,0:T(8,128)(2,1)S(1)}, u32[]{:S(2)}, u32[]{:S(2)}) collective-permute-start(bf16[80,1536]{1,0:T(8,128)(2,1)S(1)} %fusion.12), channel_id=1, source_target_pairs={{0,256},{16,272},{32,288},{48,304},{64,320},{80,336},{96,352},{112... | collective-permute-start | bytes 737288 | tf_op jit(solution)/shard_map/ppermute | solution.py:56
  93.6 14.9 %collective-permute-start.1 = (bf16[40,1536]{1,0:T(8,128)(2,1)S(1)}, bf16[40,1536]{1,0:T(8,128)(2,1)S(1)}, u32[]{:S(2)}, u32[]{:S(2)}) collective-permute-start(bf16[40,1536]{1,0:T(8,128)(2,1)S(1)} %reduce_sum.85), channel_id=1, source_target_pairs={{0,2},{1,3},{2,0},{3,1},{4,6},{5,7},{6,4},{7,5},{8,10},{9,11},{10,... | collective-permute-start | bytes 368648 | tf_op jit(solution)/shard_map/ppermute | solution.py:63
  109.8 20.3 %all-to-all-start.3 = ((bf16[8,40,1536]{2,1,0:T(8,128)(2,1)}), bf16[8,40,1536]{2,1,0:T(8,128)(2,1)S(1)}, u32[]{:S(2)}, u32[]{:S(2)}) async-start(bf16[8,40,1536]{2,1,0:T(8,128)(2,1)} %broadcast_in_dim.28), calls=%async_computation.3 | async-start | bytes 1966080 | tf_op jit(solution)/shard_map/all_to_all | solution.py:18
  115.7 53.8 %reduce-scatter.3.cloned.1.call-start = ((), (), s32[]{:S(2)}) async-start(), calls=%async_computation.13 | async-start | bytes 2211840 | tf_op jit(solution)/shard_map/reduce_scatter | solution.py:83
  135.4 1.2 copy-start.1
  154.5 14.6 %collective-permute-start.2 = (bf16[40,1536]{1,0:T(8,128)(2,1)S(1)}, bf16[40,1536]{1,0:T(8,128)(2,1)S(1)}, u32[]{:S(2)}, u32[]{:S(2)}) collective-permute-start(bf16[40,1536]{1,0:T(8,128)(2,1)S(1)} %reduce_sum.87), channel_id=1, source_target_pairs={{0,2},{1,3},{2,0},{3,1},{4,6},{5,7},{6,4},{7,5},{8,10},{9,11},{10,... | collective-permute-start | bytes 368648 | tf_op jit(solution)/shard_map/ppermute | solution.py:86
  191.5 17.6 %all-to-all-start.6 = ((bf16[4,24,1536]{2,1,0:T(8,128)(2,1)}), bf16[4,24,1536]{2,1,0:T(8,128)(2,1)S(1)}, u32[]{:S(2)}, u32[]{:S(2)}) async-start(bf16[4,24,1536]{2,1,0:T(8,128)(2,1)} %bitcast.16), calls=%async_computation.7 | async-start | bytes 589824 | tf_op jit(solution)/shard_map/all_to_all | solution.py:18
  203.4 62.0 %reduce-scatter.5.cloned.1.call-start = ((), (), s32[]{:S(2)}) async-start(), calls=%async_computation.14 | async-start | bytes 663552 | tf_op jit(solution)/shard_map/reduce_scatter | solution.py:92
  240.5 24.9 %all-to-all-start.9 = ((bf16[4,24,1536]{2,1,0:T(8,128)(2,1)}), bf16[4,24,1536]{2,1,0:T(8,128)(2,1)S(1)}, u32[]{:S(2)}, u32[]{:S(2)}) async-start(bf16[4,24,1536]{2,1,0:T(8,128)(2,1)} %broadcast_in_dim.56), calls=%async_computation.10 | async-start | bytes 589824 | tf_op jit(solution)/shard_map/all_to_all | solution.py:18
  268.2 27.3 %all-to-all-start.10 = ((bf16[16,18,96]{2,1,0:T(8,128)(2,1)}), bf16[16,18,96]{2,1,0:T(8,128)(2,1)S(1)}, u32[]{:S(2)}, u32[]{:S(2)}) async-start(bf16[16,18,96]{2,1,0:T(8,128)(2,1)} %copy.21), calls=%async_computation.12 | async-start | bytes 196608 | tf_op jit(solution)/shard_map/all_to_all | solution.py:18
Sparse Core Ops, SparseCore 0:
  93.7 31.4 all-gather.2
  135.6 32.4 reduce-scatter.2
  207.8 57.4 reduce-scatter.4

commit v5 on v4

--- a/solution.py
+++ b/solution.py
@@ -7,10 +7,12 @@
 X, ZH, CORE = 4, 2, 2
 ZL, Y = 8, 4
 PLANE = [[x * 4 + zh * 2 + c for x in range(X) for c in range(CORE)] for zh in range(ZH)]
-LINE = [[z * Y + y for z in range(ZL)] for y in range(Y)]
+FOLD = (0, 2, 4, 6, 7, 5, 3, 1)
+LINE = [[z * Y + y for z in FOLD] for y in range(Y)]
 RING = [[z * Y + y for y in range(Y)] for z in range(ZL)]
 PAIR = [(i, i ^ 2) for i in range(16)]
 QUAD = [[(q * 4 + i) * Y + y for i in range(4)] for q in range(ZL // 4) for y in range(Y)]
+SLAB = [[(q * 4 + i) * Y + y for y in range(Y) for i in range(4)] for q in range(ZL // 4)]
 ACROSS = [(i, i ^ (4 * Y)) for i in range(ZL * Y)]
 
 
@@ -47,25 +49,26 @@
     blocks = spread(block, "dp", QUAD, 4).reshape(4, piece, embed_width)
     count = 4 * share
     quad = jnp.concatenate([blocks[:, :share].reshape(count, embed_width), blocks[:, share]], axis=0)
-    quad = jnp.pad(quad, ((0, 4), (0, 0)))
+    quad = jnp.pad(quad, ((0, 12), (0, 0)))
 
     feats = jnp.pad(image_feats.reshape(plane, own, width), ((0, 0), (0, held - own), (0, 0)))
     feats = feats.reshape(plane * held, width)
     term = jnp.dot(feats, image_head, preferred_element_type=F32).astype(BF16)
     term, quad = lax.optimization_barrier((term, quad))
+    near = lax.all_gather(quad, "dp", axis_index_groups=RING)
     crossed = lax.ppermute(quad, "dp", ACROSS)
     half = swap(term.reshape(plane, held, embed_width), "fsdp", PLANE)
     half = jnp.sum(half.astype(F32), axis=0).astype(BF16)
-    line = jnp.stack([quad, crossed])
-    half, line = lax.optimization_barrier((half, line))
+    half, crossed = lax.optimization_barrier((half, crossed))
 
-    lines = lax.all_gather(line, "dp", axis_index_groups=RING)
+    far = lax.all_gather(crossed, "dp", axis_index_groups=RING)
     embed = half.astype(F32) + lax.ppermute(half, "fsdp", PAIR).astype(F32)
     image_scale = lax.rsqrt(jnp.sum(embed * embed, axis=1, keepdims=True) + 1e-06)
     image_unit = embed * image_scale
     image_low = spread(image_unit.astype(BF16), "fsdp", PLANE, plane).reshape(plane * held, embed_width)
-    text_low = lines[:, :, :count].reshape(cycle * share, embed_width)
-    notes = lines[:, :, count : count + 4, : 2 * share].astype(jnp.int32)
+    lines = (near, far)
+    text_low = jnp.concatenate([part[:, :count] for part in lines]).reshape(cycle * share, embed_width)
+    notes = jnp.concatenate([part[:, count : count + 4, : 2 * share] for part in lines]).astype(jnp.int32)
     ids = (notes[..., :share] * 128 + notes[..., share:]).reshape(cycle * share)
 
     partial_value = jnp.einsum("ie,je->ij", image_low, text_low, preferred_element_type=F32)
@@ -80,6 +83,7 @@
 
     unit_part, text_acc = lax.optimization_barrier((unit_part, text_acc))
 
+    text_acc = text_acc.reshape(2, Y, 4 * share, embed_width).transpose(1, 0, 2, 3)
     text_acc = lax.psum_scatter(text_acc.reshape(Y, ZL * share, embed_width), "dp", axis_index_groups=RING)
     back = swap(unit_part.reshape(plane, held, embed_width), "fsdp", PLANE)
     back = jnp.sum(back.astype(F32), axis=0).astype(BF16)
@@ -88,16 +92,19 @@
     embed_grad = (image_scale * (unit_grad - image_unit * image_dot)).astype(BF16)
     text_acc = text_acc.reshape(2, 4, share, embed_width)
     text_acc = jnp.where(d // Y < 4, text_acc, text_acc[::-1]).reshape(ZL, share, embed_width)
+    text_acc = jnp.stack([text_acc[z] for z in FOLD])
     embed_grad, text_acc = lax.optimization_barrier((embed_grad, text_acc))
     text_acc = lax.psum_scatter(text_acc, "dp", axis_index_groups=LINE)
     grads = spread(embed_grad, "fsdp", PLANE, plane).reshape(plane * held, embed_width)
     head_part = jnp.einsum("rw,re->we", feats, grads, preferred_element_type=F32).astype(BF16)
-    head_sum = jnp.sum(swap(head_part.reshape(Y, width // Y, embed_width), "dp", RING).astype(F32), axis=0)
-    head_sum = head_sum.astype(BF16).reshape(width // Y, ZL, embed_width // ZL).transpose(1, 0, 2)
-    head_sum = jnp.sum(swap(head_sum, "dp", LINE).astype(F32), axis=0).astype(BF16)
-    head_all = spread(head_sum, "dp", LINE, ZL).transpose(1, 0, 2).reshape(width // Y, embed_width)
-    head_all = spread(head_all, "dp", RING, Y).reshape(width, embed_width)
-    head_all, text_acc = lax.optimization_barrier((head_all, text_acc))
+    head_part = head_part.reshape(Y, width // Y, 4, embed_width // 4).transpose(0, 2, 1, 3)
+    head_part = head_part.reshape(4 * Y, width // Y, embed_width // 4)
+    head_sum = jnp.sum(swap(head_part, "dp", SLAB).astype(F32), axis=0)
+    head_sum = lax.reduce_precision(head_sum, 8, 7)
+    head_sum = head_sum + lax.ppermute(head_sum.astype(BF16), "dp", ACROSS).astype(F32)
+    head_sum, text_acc = lax.optimization_barrier((head_sum.astype(BF16), text_acc))
+    head_all = spread(head_sum, "dp", SLAB, 4 * Y).reshape(Y, 4, width // Y, embed_width // 4)
+    head_all = head_all.transpose(0, 2, 1, 3).reshape(width, embed_width)
     head_grad = head_all.astype(F32)
     feature_grad = jnp.einsum("re,we->rw", grads, image_head, preferred_element_type=F32).astype(BF16)
     feature_grad = feature_grad.reshape(plane, held, width)[:, :own].reshape(rows, width)

time: 304 us -> 309 us (1.016)
  waiting for transfers between devices: 112 us -> 130 us
  starting transfers between devices: 82.2 us -> 67 us
  local copies, waits for them, and re-layouts: 11.1 us -> 16.5 us
    all_to_all x7 -> x6, starting transfers between devices: 64.7 us -> 46.9 us  [swap(): lax.all_to_all(value, axis, 0, 0, axis_index_groups=groups, tiled=True)]
    all_to_all x7 -> x6, waiting for transfers between devices: 38 us -> 54.5 us  [swap(): lax.all_to_all(value, axis, 0, 0, axis_index_groups=groups, tiled=True)]
    ppermute x1, waiting for transfers between devices: 2.97 us -> 15.5 us  [on_device(): unit_grad = back.astype(F32) + lax.ppermute(back, 'fsdp', PAIR).astype(F32)]
    all_gather x1 -> x2, waiting for transfers between devices: 9.35 us -> 0.02 us  [the longest x1 0.02 us: on_device(): far = lax.all_gather(crossed, 'dp', axis_index_groups=RING)]
    ppermute x1, waiting for transfers between devices: 27.3 us -> 18.8 us  [on_device(): crossed = lax.ppermute(quad, 'dp', ACROSS)]
    ppermute x0 -> x1, starting transfers between devices: none -> 7.11 us  [on_device(): lax.ppermute(head_sum.astype(BF16), 'dp', ACROSS).astype(F32)]
    reduce_scatter x1, waiting for transfers between devices: 21.4 us -> 26.2 us  [on_device(): text_acc = lax.psum_scatter(text_acc, 'dp', axis_index_groups=LINE)]
    ppermute x1, starting transfers between devices: 11.6 us -> 6.97 us  [on_device(): unit_grad = back.astype(F32) + lax.ppermute(back, 'fsdp', PAIR).astype(F32)]
  transfers between devices with their start and end apart: 13 -> 14, of which waited for: 10 -> 11; matrix products, arithmetic and copies ran while one was open for 4% -> 4% of each run, Pallas kernels for 0% -> 0%
where the time goes in v5:
time: 309 us; the launch traced here: 308 us
  waiting for transfers between devices  130 us (42%)
  starting transfers between devices  67 us (22%)
  blocking collectives  64.7 us (21%)
  local copies, waits for them, and re-layouts  16.5 us (5%)
  between operations  15.5 us (5%)
  matrix products  7.94 us (3%)
  other arithmetic  6.49 us (2%)
    all_to_all x3, blocking collectives, swap(): lax.all_to_all(value, axis, 0, 0, axis_index_groups=groups, tiled=True)  64.7 us
    all_to_all x6, waiting for transfers between devices, swap(): lax.all_to_all(value, axis, 0, 0, axis_index_groups=groups, tiled=True)  54.5 us
    all_to_all x6, starting transfers between devices, swap(): lax.all_to_all(value, axis, 0, 0, axis_index_groups=groups, tiled=True)  46.9 us
    reduce_scatter x1, waiting for transfers between devices, on_device(): text_acc = lax.psum_scatter(text_acc, 'dp', axis_index_groups=LINE)  26.2 us
    ppermute x1, waiting for transfers between devices, on_device(): crossed = lax.ppermute(quad, 'dp', ACROSS)  18.8 us
    ppermute x1, waiting for transfers between devices, on_device(): unit_grad = back.astype(F32) + lax.ppermute(back, 'fsdp', PAIR).astype(F32)  15.5 us
    ppermute x1, waiting for transfers between devices, on_device(): embed = half.astype(F32) + lax.ppermute(half, 'fsdp', PAIR).astype(F32)  13 us
    ppermute x1, starting transfers between devices, on_device(): lax.ppermute(head_sum.astype(BF16), 'dp', ACROSS).astype(F32)  7.11 us
  transfers between devices with their start and end apart: 14, of which 11 were waited for; matrix products, arithmetic and copies ran while one was open for 4% of the time, Pallas kernels for 0%

profile of v5, /device:TPU:1, one launch (start us, length us, event | category | flops | bytes accessed | tf_op | source)
XLA Modules:
  0.0 308.0 jit_solution(15087522088493805541)
XLA Ops:
  7.2 1.6 reshape.148
  8.8 19.1 %all-to-all-start = ((bf16[16,18,96]{2,1,0:T(8,128)(2,1)}), bf16[16,18,96]{2,1,0:T(8,128)(2,1)S(1)}, u32[]{:S(2)}, u32[]{:S(2)}) async-start(bf16[16,18,96]{2,1,0:T(8,128)(2,1)} %reshape.148), calls=%async_computation | async-start | bytes 196608 | tf_op jit(solution)/shard_map/all_to_all | solution.py:20
  27.9 0.8 convert_bitcast_fusion.2
  28.7 13.8 %all-to-all-done = bf16[16,18,96]{2,1,0:T(8,128)(2,1)S(1)} async-done(((bf16[16,18,96]{2,1,0:T(8,128)(2,1)}), bf16[16,18,96]{2,1,0:T(8,128)(2,1)S(1)}, u32[]{:S(2)}, u32[]{:S(2)}) %all-to-all-start) | async-done | bytes 55328 | tf_op jit(solution)/shard_map/all_to_all | solution.py:20
  42.9 0.7 broadcast_in_dim.20
  43.7 3.5 %all-to-all-start.1 = ((bf16[4,24,1536]{2,1,0:T(8,128)(2,1)}), bf16[4,24,1536]{2,1,0:T(8,128)(2,1)S(1)}, u32[]{:S(2)}, u32[]{:S(2)}) async-start(bf16[4,24,1536]{2,1,0:T(8,128)(2,1)} %broadcast_in_dim.20), calls=%async_computation.1 | async-start | bytes 589824 | tf_op jit(solution)/shard_map/all_to_all | solution.py:20
  47.3 1.4 convolution_convert_fusion.2
  48.7 4.3 %all-to-all-done.1 = bf16[4,24,1536]{2,1,0:T(8,128)(2,1)S(1)} async-done(((bf16[4,24,1536]{2,1,0:T(8,128)(2,1)}), bf16[4,24,1536]{2,1,0:T(8,128)(2,1)S(1)}, u32[]{:S(2)}, u32[]{:S(2)}) %all-to-all-start.1) | async-done | bytes 294944 | tf_op jit(solution)/shard_map/all_to_all | solution.py:20
  53.1 0.7 fusion.12
  53.9 8.3 %all-to-all-start.2 = ((bf16[8,40,1536]{2,1,0:T(8,128)(2,1)}), bf16[8,40,1536]{2,1,0:T(8,128)(2,1)S(1)}, u32[]{:S(2)}, u32[]{:S(2)}) async-start(bf16[8,40,1536]{2,1,0:T(8,128)(2,1)} %bitcast.4), calls=%async_computation.2 | async-start | bytes 1966080 | tf_op jit(solution)/shard_map/all_to_all | solution.py:20
  62.2 3.9 %collective-permute-start = (bf16[88,1536]{1,0:T(8,128)(2,1)S(1)}, bf16[88,1536]{1,0:T(8,128)(2,1)S(1)}, u32[]{:S(2)}, u32[]{:S(2)}) collective-permute-start(bf16[88,1536]{1,0:T(8,128)(2,1)S(1)} %copy-done.2), channel_id=1, source_target_pairs={{0,256},{16,272},{32,288},{48,304},{64,320},{80,336},{96,352},{112... | collective-permute-start | bytes 811016 | tf_op jit(solution)/shard_map/ppermute | solution.py:59
  66.2 10.5 %all-to-all-done.2 = bf16[8,40,1536]{2,1,0:T(8,128)(2,1)S(1)} async-done(((bf16[8,40,1536]{2,1,0:T(8,128)(2,1)}), bf16[8,40,1536]{2,1,0:T(8,128)(2,1)S(1)}, u32[]{:S(2)}, u32[]{:S(2)}) %all-to-all-start.2) | async-done | bytes 983072 | tf_op jit(solution)/shard_map/all_to_all | solution.py:20
  76.8 18.8 %collective-permute-done = bf16[88,1536]{1,0:T(8,128)(2,1)S(1)} collective-permute-done((bf16[88,1536]{1,0:T(8,128)(2,1)S(1)}, bf16[88,1536]{1,0:T(8,128)(2,1)S(1)}, u32[]{:S(2)}, u32[]{:S(2)}) %collective-permute-start) | collective-permute-done | bytes 270368 | tf_op jit(solution)/shard_map/ppermute | solution.py:59
  95.6 0.7 copy-done.5
  96.3 1.9 collective-permute-start.1
  98.2 13.0 %collective-permute-done.1 = bf16[40,1536]{1,0:T(8,128)(2,1)S(1)} collective-permute-done((bf16[40,1536]{1,0:T(8,128)(2,1)S(1)}, bf16[40,1536]{1,0:T(8,128)(2,1)S(1)}, u32[]{:S(2)}, u32[]{:S(2)}) %collective-permute-start.1) | collective-permute-done | bytes 122912 | tf_op jit(solution)/shard_map/ppermute | solution.py:65
  111.5 1.0 broadcast_in_dim.24
  112.5 5.9 %all-to-all-start.3 = ((bf16[8,40,1536]{2,1,0:T(8,128)(2,1)}), bf16[8,40,1536]{2,1,0:T(8,128)(2,1)S(1)}, u32[]{:S(2)}, u32[]{:S(2)}) async-start(bf16[8,40,1536]{2,1,0:T(8,128)(2,1)} %broadcast_in_dim.24), calls=%async_computation.3 | async-start | bytes 1966080 | tf_op jit(solution)/shard_map/all_to_all | solution.py:20
  119.8 0.7 slice.68
  120.5 1.2 slice.72
  121.8 0.7 slice.69
  122.5 1.2 slice.73
  123.9 1.4 pad_maximum_fusion
  125.3 7.4 %all-to-all-done.3 = bf16[8,40,1536]{2,1,0:T(8,128)(2,1)S(1)} async-done(((bf16[8,40,1536]{2,1,0:T(8,128)(2,1)}), bf16[8,40,1536]{2,1,0:T(8,128)(2,1)S(1)}, u32[]{:S(2)}, u32[]{:S(2)}) %all-to-all-start.3) | async-done | bytes 983072 | tf_op jit(solution)/shard_map/all_to_all | solution.py:20
  132.8 2.7 fusion.9
  135.5 1.9 convolution_convert_fusion.1
  137.4 1.1 convolution_convert_fusion
  138.5 1.4 copy.24
  139.9 1.2 copy-done.3
  141.1 17.7 %all_to_all.45 = bf16[8,40,1536]{2,1,0:T(8,128)(2,1)S(1)} all-to-all(bf16[8,40,1536]{2,1,0:T(8,128)(2,1)S(1)} %bitcast.69), channel_id=1, replica_groups={{0,1,4,5,8,9,12,13},{2,3,6,7,10,11,14,15},{16,17,20,21,24,25,28,29},{18..., dimensions={0} | all-to-all | bytes 1966080 | tf_op jit(solution)/shard_map/all_to_all | solution.py:20
  159.0 7.0 %collective-permute-start.2 = (bf16[40,1536]{1,0:T(8,128)(2,1)S(1)}, bf16[40,1536]{1,0:T(8,128)(2,1)S(1)}, u32[]{:S(2)}, u32[]{:S(2)}) collective-permute-start(bf16[40,1536]{1,0:T(8,128)(2,1)S(1)} %reduce_sum.72), channel_id=1, source_target_pairs={{0,2},{1,3},{2,0},{3,1},{4,6},{5,7},{6,4},{7,5},{8,10},{9,11},{10,... | collective-permute-start | bytes 368648 | tf_op jit(solution)/shard_map/ppermute | solution.py:90
  166.0 15.5 %collective-permute-done.2 = bf16[40,1536]{1,0:T(8,128)(2,1)S(1)} collective-permute-done((bf16[40,1536]{1,0:T(8,128)(2,1)S(1)}, bf16[40,1536]{1,0:T(8,128)(2,1)S(1)}, u32[]{:S(2)}, u32[]{:S(2)}) %collective-permute-start.2) | collective-permute-done | bytes 122912 | tf_op jit(solution)/shard_map/ppermute | solution.py:90
  181.8 1.1 reshape_reduce_scatter.3
  183.2 17.3 %all_to_all.46 = bf16[8,40,1536]{2,1,0:T(8,128)(2,1)S(1)} all-to-all(bf16[8,40,1536]{2,1,0:T(8,128)(2,1)S(1)} %broadcast_in_dim.25), channel_id=1, replica_groups={{0,1,4,5,8,9,12,13},{2,3,6,7,10,11,14,15},{16,17,20,21,24,25,28,29},{18..., dimensions={0} | all-to-all | bytes 1966080 | tf_op jit(solution)/shard_map/all_to_all | solution.py:20
  201.0 0.8 copy.26
  201.8 3.5 %all-to-all-start.6 = ((bf16[16,24,384]{2,1,0:T(8,128)(2,1)}), bf16[16,24,384]{2,1,0:T(8,128)(2,1)S(1)}, u32[]{:S(2)}, u32[]{:S(2)}) async-start(bf16[16,24,384]{2,1,0:T(8,128)(2,1)} %bitcast.18), calls=%async_computation.7 | async-start | bytes 589824 | tf_op jit(solution)/shard_map/all_to_all | solution.py:20
  205.9 9.9 %all-to-all-done.6 = bf16[16,24,384]{2,1,0:T(8,128)(2,1)S(1)} async-done(((bf16[16,24,384]{2,1,0:T(8,128)(2,1)}), bf16[16,24,384]{2,1,0:T(8,128)(2,1)S(1)}, u32[]{:S(2)}, u32[]{:S(2)}) %all-to-all-start.6) | async-done | bytes 294944 | tf_op jit(solution)/shard_map/all_to_all | solution.py:20
  215.8 7.1 %collective-permute-start.3 = (bf16[24,384]{1,0:T(8,128)(2,1)S(1)}, bf16[24,384]{1,0:T(8,128)(2,1)S(1)}, u32[]{:S(2)}, u32[]{:S(2)}) collective-permute-start(bf16[24,384]{1,0:T(8,128)(2,1)S(1)} %reduce-precision_convert_fusion), channel_id=1, source_target_pairs={{0,256},{16,272},{32,288},{48,304},{64,320},{80,336},{96,352},{112... | collective-permute-start | bytes 55304 | tf_op jit(solution)/shard_map/ppermute | solution.py:104
  223.0 1.3 collective-permute-done.3
  224.3 26.2 %reduce-scatter.5.cloned.1.call-done = bf16[1,18,1536]{2,1,0:T(8,128)(2,1)} async-done(((bf16[8,18,1536]{2,1,0:T(8,128)(2,1)}), bf16[1,18,1536]{2,1,0:T(8,128)(2,1)}) %reduce-scatter.5.cloned.1.call-update) | async-done | bytes 55312 | tf_op jit(solution)/shard_map/reduce_scatter | solution.py:97
  250.5 1.1 fusion.16
  251.6 1.0 fusion.18
  252.7 29.6 %all_to_all.47 = bf16[16,18,96]{2,1,0:T(8,128)(2,1)S(1)} all-to-all(bf16[16,18,96]{2,1,0:T(8,128)(2,1)S(1)} %copy.28), channel_id=1, replica_groups=mesh['dp'=32,'fsdp'=16] {'fsdp'}, dimensions={0} | all-to-all | bytes 110592 | tf_op jit(solution)/shard_map/all_to_all | solution.py:20
  282.4 0.7 broadcast_in_dim.26
  283.1 6.7 %all-to-all-start.7 = ((bf16[16,24,384]{2,1,0:T(8,128)(2,1)}), bf16[16,24,384]{2,1,0:T(8,128)(2,1)S(1)}, u32[]{:S(2)}, u32[]{:S(2)}) async-start(bf16[16,24,384]{2,1,0:T(8,128)(2,1)} %broadcast_in_dim.26), calls=%async_computation.9 | async-start | bytes 589824 | tf_op jit(solution)/shard_map/all_to_all | solution.py:20
  290.4 0.7 reshape.159
  291.7 8.7 %all-to-all-done.7 = bf16[16,24,384]{2,1,0:T(8,128)(2,1)S(1)} async-done(((bf16[16,24,384]{2,1,0:T(8,128)(2,1)}), bf16[16,24,384]{2,1,0:T(8,128)(2,1)S(1)}, u32[]{:S(2)}, u32[]{:S(2)}) %all-to-all-start.7) | async-done | bytes 294944 | tf_op jit(solution)/shard_map/all_to_all | solution.py:20
  300.6 0.9 copy.30
  (72 shorter events, 4.9 us)
Async XLA Ops:
  7.2 40.1 %copy-start = (bf16[96,1536]{1,0:T(8,128)(2,1)S(1)}, bf16[96,1536]{1,0:T(8,128)(2,1)}, u32[]{:S(2)}) copy-start(bf16[96,1536]{1,0:T(8,128)(2,1)} %param.7) | copy-start | bytes 884740
  7.2 40.0 %copy-start.6 = (bf16[288,96]{1,0:T(8,128)(2,1)S(1)}, bf16[288,96]{1,0:T(8,128)(2,1)}, u32[]{:S(2)}) copy-start(bf16[288,96]{1,0:T(8,128)(2,1)} %param.6) | copy-start | bytes 165892
  8.8 33.7 %all-to-all-start = ((bf16[16,18,96]{2,1,0:T(8,128)(2,1)}), bf16[16,18,96]{2,1,0:T(8,128)(2,1)S(1)}, u32[]{:S(2)}, u32[]{:S(2)}) async-start(bf16[16,18,96]{2,1,0:T(8,128)(2,1)} %reshape.148), calls=%async_computation | async-start | bytes 196608 | tf_op jit(solution)/shard_map/all_to_all | solution.py:20
  43.7 9.3 %all-to-all-start.1 = ((bf16[4,24,1536]{2,1,0:T(8,128)(2,1)}), bf16[4,24,1536]{2,1,0:T(8,128)(2,1)S(1)}, u32[]{:S(2)}, u32[]{:S(2)}) async-start(bf16[4,24,1536]{2,1,0:T(8,128)(2,1)} %broadcast_in_dim.20), calls=%async_computation.1 | async-start | bytes 589824 | tf_op jit(solution)/shard_map/all_to_all | solution.py:20
  47.1 72.7 %all-gather.5.cloned.1.call-start = ((), (), s32[]{:S(2)}) async-start(), calls=%async_computation.13 | async-start | bytes 1351680 | tf_op jit(solution)/shard_map/all_gather | solution.py:58
  53.8 8.4 %copy-start.2 = (bf16[88,1536]{1,0:T(8,128)(2,1)S(1)}, bf16[88,1536]{1,0:T(8,128)(2,1)}, u32[]{:S(2)}) copy-start(bf16[88,1536]{1,0:T(8,128)(2,1)} %fusion.12) | copy-start | bytes 811012
  53.9 22.8 %all-to-all-start.2 = ((bf16[8,40,1536]{2,1,0:T(8,128)(2,1)}), bf16[8,40,1536]{2,1,0:T(8,128)(2,1)S(1)}, u32[]{:S(2)}, u32[]{:S(2)}) async-start(bf16[8,40,1536]{2,1,0:T(8,128)(2,1)} %bitcast.4), calls=%async_computation.2 | async-start | bytes 1966080 | tf_op jit(solution)/shard_map/all_to_all | solution.py:20
  62.2 59.6 %all-gather.7.cloned.1.call-start = ((), (), s32[]{:S(2)}) async-start(), calls=%async_computation.14 | async-start | bytes 1351680 | tf_op jit(solution)/shard_map/all_gather | solution.py:64
  62.2 33.4 %collective-permute-start = (bf16[88,1536]{1,0:T(8,128)(2,1)S(1)}, bf16[88,1536]{1,0:T(8,128)(2,1)S(1)}, u32[]{:S(2)}, u32[]{:S(2)}) collective-permute-start(bf16[88,1536]{1,0:T(8,128)(2,1)S(1)} %copy-done.2), channel_id=1, source_target_pairs={{0,256},{16,272},{32,288},{48,304},{64,320},{80,336},{96,352},{112... | collective-permute-start | bytes 811016 | tf_op jit(solution)/shard_map/ppermute | solution.py:59
  95.6 0.7 copy-start.5
  96.3 14.9 %collective-permute-start.1 = (bf16[40,1536]{1,0:T(8,128)(2,1)S(1)}, bf16[40,1536]{1,0:T(8,128)(2,1)S(1)}, u32[]{:S(2)}, u32[]{:S(2)}) collective-permute-start(bf16[40,1536]{1,0:T(8,128)(2,1)S(1)} %reduce_sum.70), channel_id=1, source_target_pairs={{0,2},{1,3},{2,0},{3,1},{4,6},{5,7},{6,4},{7,5},{8,10},{9,11},{10,... | collective-permute-start | bytes 368648 | tf_op jit(solution)/shard_map/ppermute | solution.py:65
  112.5 20.3 %all-to-all-start.3 = ((bf16[8,40,1536]{2,1,0:T(8,128)(2,1)}), bf16[8,40,1536]{2,1,0:T(8,128)(2,1)S(1)}, u32[]{:S(2)}, u32[]{:S(2)}) async-start(bf16[8,40,1536]{2,1,0:T(8,128)(2,1)} %broadcast_in_dim.24), calls=%async_computation.3 | async-start | bytes 1966080 | tf_op jit(solution)/shard_map/all_to_all | solution.py:20
  118.4 63.4 %reduce-scatter.3.cloned.1.call-start = ((), (), s32[]{:S(2)}) async-start(), calls=%async_computation.11 | async-start | bytes 2211840 | tf_op jit(solution)/shard_map/reduce_scatter | solution.py:87
  132.8 2.7 copy-start.1
  139.9 1.2 copy-start.3
  159.0 22.5 %collective-permute-start.2 = (bf16[40,1536]{1,0:T(8,128)(2,1)S(1)}, bf16[40,1536]{1,0:T(8,128)(2,1)S(1)}, u32[]{:S(2)}, u32[]{:S(2)}) collective-permute-start(bf16[40,1536]{1,0:T(8,128)(2,1)S(1)} %reduce_sum.72), channel_id=1, source_target_pairs={{0,2},{1,3},{2,0},{3,1},{4,6},{5,7},{6,4},{7,5},{8,10},{9,11},{10,... | collective-permute-start | bytes 368648 | tf_op jit(solution)/shard_map/ppermute | solution.py:90
  183.1 17.8 %copy-start.4 = (bf16[8,18,1536]{2,1,0:T(8,128)(2,1)}, bf16[8,18,1536]{2,1,0:T(8,128)(2,1)S(1)}, u32[]{:S(2)}) copy-start(bf16[8,18,1536]{2,1,0:T(8,128)(2,1)S(1)} %slice_dynamic-update-slice_fusion.1) | copy-start | bytes 1327108
  201.8 14.0 %all-to-all-start.6 = ((bf16[16,24,384]{2,1,0:T(8,128)(2,1)}), bf16[16,24,384]{2,1,0:T(8,128)(2,1)S(1)}, u32[]{:S(2)}, u32[]{:S(2)}) async-start(bf16[16,24,384]{2,1,0:T(8,128)(2,1)} %bitcast.18), calls=%async_computation.7 | async-start | bytes 589824 | tf_op jit(solution)/shard_map/all_to_all | solution.py:20
  205.3 45.2 %reduce-scatter.5.cloned.1.call-start = ((), (), s32[]{:S(2)}) async-start(), calls=%async_computation.12 | async-start | bytes 663552 | tf_op jit(solution)/shard_map/reduce_scatter | solution.py:97
  215.8 8.4 %collective-permute-start.3 = (bf16[24,384]{1,0:T(8,128)(2,1)S(1)}, bf16[24,384]{1,0:T(8,128)(2,1)S(1)}, u32[]{:S(2)}, u32[]{:S(2)}) collective-permute-start(bf16[24,384]{1,0:T(8,128)(2,1)S(1)} %reduce-precision_convert_fusion), channel_id=1, source_target_pairs={{0,256},{16,272},{32,288},{48,304},{64,320},{80,336},{96,352},{112... | collective-permute-start | bytes 55304 | tf_op jit(solution)/shard_map/ppermute | solution.py:104
  283.1 17.3 %all-to-all-start.7 = ((bf16[16,24,384]{2,1,0:T(8,128)(2,1)}), bf16[16,24,384]{2,1,0:T(8,128)(2,1)S(1)}, u32[]{:S(2)}, u32[]{:S(2)}) async-start(bf16[16,24,384]{2,1,0:T(8,128)(2,1)} %broadcast_in_dim.26), calls=%async_computation.9 | async-start | bytes 589824 | tf_op jit(solution)/shard_map/all_to_all | solution.py:20
Sparse Core Ops, SparseCore 0:
  54.0 26.9 all-gather.4
  96.4 24.8 all-gather.6
  140.1 28.3 reduce-scatter.2
  209.5 40.9 reduce-scatter.4

commit v6 on v5

--- a/solution.py
+++ b/solution.py
@@ -7,13 +7,27 @@
 X, ZH, CORE = 4, 2, 2
 ZL, Y = 8, 4
 PLANE = [[x * 4 + zh * 2 + c for x in range(X) for c in range(CORE)] for zh in range(ZH)]
-FOLD = (0, 2, 4, 6, 7, 5, 3, 1)
-LINE = [[z * Y + y for z in FOLD] for y in range(Y)]
 RING = [[z * Y + y for y in range(Y)] for z in range(ZL)]
 PAIR = [(i, i ^ 2) for i in range(16)]
 QUAD = [[(q * 4 + i) * Y + y for i in range(4)] for q in range(ZL // 4) for y in range(Y)]
 SLAB = [[(q * 4 + i) * Y + y for y in range(Y) for i in range(4)] for q in range(ZL // 4)]
 ACROSS = [(i, i ^ (4 * Y)) for i in range(ZL * Y)]
+
+
+def place(z, y, x, c):
+    return ((z % ZL * Y + y) * X + x) * 4 + z % 16 // ZL * 2 + c
+
+
+def mirror(z):
+    edge = z // 4 * 4 if z % 4 < 2 else z // 4 * 4 + 4
+    return (2 * edge - 1 - z) % 16
+
+
+COLUMNS = [(y, x, c) for y in range(Y) for x in range(X) for c in range(CORE)]
+MIRROR = [(place(z, *at), place(mirror(z), *at)) for z in range(16) for at in COLUMNS]
+FOLD = (0, 2, 4, 6, 7, 5, 3, 1)
+LINE = [[place(z0 + p, *at) for p in FOLD] for z0 in (14, 6) for at in COLUMNS]
+LINE_ZL = [(6 + p) % ZL for p in FOLD]
 
 
 def swap(value, axis, groups=None):
@@ -33,20 +47,29 @@
     plane = X * CORE
     own = rows // plane
     held = -(-own // 8) * 8
-    share = rows // group
+    share = own // ZH
     d = lax.axis_index("dp")
     f = lax.axis_index("fsdp")
 
-    text_part = swap(text_embed.reshape(group, share, width), "fsdp")
-    text_vals = text_part.transpose(1, 0, 2).reshape(share, embed_width).astype(F32)
+    zl, zh = d // Y, f // CORE % ZH
+    k = f // 4 * CORE + f % CORE
+    z = zh * ZL + zl
+    second = (z >= 6) & (z < 14)
+    parts = jnp.broadcast_to(text_embed.reshape(X, 1, CORE, own, width), (X, ZH, CORE, own, width))
+    text_part = swap(parts.reshape(group, own, width), "fsdp")
+    text_vals = text_part.transpose(1, 0, 2).reshape(own, embed_width).astype(F32)
     text_scale = lax.rsqrt(jnp.sum(text_vals * text_vals, axis=1, keepdims=True) + 1e-06)
     text_unit = text_vals * text_scale
-    my_ids = lax.dynamic_slice_in_dim(text_ids, f * share, share, 0)
-    marks = jnp.concatenate([my_ids // 128, my_ids % 128]).astype(BF16)
+    my_ids = lax.dynamic_slice_in_dim(text_ids, k * own, own, 0).reshape(ZH, share)
+    marks = jnp.concatenate([my_ids // 128, my_ids % 128], axis=1).astype(BF16)
     piece = -(-share // 8) * 8
-    marks = jnp.pad(marks[None], ((0, piece - share - 1), (0, embed_width - 2 * share)))
-    block = jnp.concatenate([text_unit.astype(BF16), marks], axis=0)
-    blocks = spread(block, "dp", QUAD, 4).reshape(4, piece, embed_width)
+    marks = jnp.pad(marks[:, None], ((0, 0), (0, piece - share - 1), (0, embed_width - 2 * share)))
+    halves = jnp.concatenate([text_unit.astype(BF16).reshape(ZH, share, embed_width), marks], axis=1)
+    text_unit = jnp.where(second, text_unit[share:], text_unit[:share])
+    text_scale = jnp.where(second, text_scale[share:], text_scale[:share])
+    there = z // 4 * 4 + jnp.arange(4)
+    there = ((there >= 6) & (there < 14))[:, None, None]
+    blocks = swap(jnp.where(there, halves[1], halves[0]), "dp", QUAD)
     count = 4 * share
     quad = jnp.concatenate([blocks[:, :share].reshape(count, embed_width), blocks[:, share]], axis=0)
     quad = jnp.pad(quad, ((0, 12), (0, 0)))
@@ -56,10 +79,9 @@
     term = jnp.dot(feats, image_head, preferred_element_type=F32).astype(BF16)
     term, quad = lax.optimization_barrier((term, quad))
     near = lax.all_gather(quad, "dp", axis_index_groups=RING)
-    crossed = lax.ppermute(quad, "dp", ACROSS)
+    crossed = lax.ppermute(quad, ("dp", "fsdp"), MIRROR)
     half = swap(term.reshape(plane, held, embed_width), "fsdp", PLANE)
     half = jnp.sum(half.astype(F32), axis=0).astype(BF16)
-    half, crossed = lax.optimization_barrier((half, crossed))
 
     far = lax.all_gather(crossed, "dp", axis_index_groups=RING)
     embed = half.astype(F32) + lax.ppermute(half, "fsdp", PAIR).astype(F32)
@@ -81,7 +103,6 @@
     unit_part = jnp.einsum("ij,je->ie", coef, text_low, preferred_element_type=F32).astype(BF16)
     text_acc = jnp.einsum("ij,ie->je", coef, image_low, preferred_element_type=F32).astype(BF16)
 
-    unit_part, text_acc = lax.optimization_barrier((unit_part, text_acc))
 
     text_acc = text_acc.reshape(2, Y, 4 * share, embed_width).transpose(1, 0, 2, 3)
     text_acc = lax.psum_scatter(text_acc.reshape(Y, ZL * share, embed_width), "dp", axis_index_groups=RING)
@@ -91,19 +112,19 @@
     image_dot = jnp.sum(image_unit * unit_grad, axis=1, keepdims=True)
     embed_grad = (image_scale * (unit_grad - image_unit * image_dot)).astype(BF16)
     text_acc = text_acc.reshape(2, 4, share, embed_width)
-    text_acc = jnp.where(d // Y < 4, text_acc, text_acc[::-1]).reshape(ZL, share, embed_width)
-    text_acc = jnp.stack([text_acc[z] for z in FOLD])
+    text_acc = jnp.where(zl < 4, text_acc, text_acc[::-1]).reshape(ZL, share, embed_width)
+    text_acc = jnp.stack([text_acc[at] for at in LINE_ZL])
     embed_grad, text_acc = lax.optimization_barrier((embed_grad, text_acc))
-    text_acc = lax.psum_scatter(text_acc, "dp", axis_index_groups=LINE)
+    text_acc = lax.psum_scatter(text_acc, ("dp", "fsdp"), axis_index_groups=LINE)
     grads = spread(embed_grad, "fsdp", PLANE, plane).reshape(plane * held, embed_width)
     head_part = jnp.einsum("rw,re->we", feats, grads, preferred_element_type=F32).astype(BF16)
     head_part = head_part.reshape(Y, width // Y, 4, embed_width // 4).transpose(0, 2, 1, 3)
     head_part = head_part.reshape(4 * Y, width // Y, embed_width // 4)
     head_sum = jnp.sum(swap(head_part, "dp", SLAB).astype(F32), axis=0)
+    head_sum, text_acc = lax.optimization_barrier((head_sum, text_acc))
     head_sum = lax.reduce_precision(head_sum, 8, 7)
     head_sum = head_sum + lax.ppermute(head_sum.astype(BF16), "dp", ACROSS).astype(F32)
-    head_sum, text_acc = lax.optimization_barrier((head_sum.astype(BF16), text_acc))
-    head_all = spread(head_sum, "dp", SLAB, 4 * Y).reshape(Y, 4, width // Y, embed_width // 4)
+    head_all = spread(head_sum.astype(BF16), "dp", SLAB, 4 * Y).reshape(Y, 4, width // Y, embed_width // 4)
     head_all = head_all.transpose(0, 2, 1, 3).reshape(width, embed_width)
     head_grad = head_all.astype(F32)
     feature_grad = jnp.einsum("re,we->rw", grads, image_head, preferred_element_type=F32).astype(BF16)
@@ -113,7 +134,9 @@
     text_dot = jnp.sum(text_unit * text_acc, axis=1, keepdims=True)
     text_rows = (text_scale * (text_acc - text_unit * text_dot)).astype(BF16)
     text_rows = text_rows.reshape(share, group, width).transpose(1, 0, 2)
-    text_grad = swap(text_rows, "fsdp").reshape(rows, width)
+    text_grad = swap(text_rows, "fsdp").reshape(X, ZH, CORE, share, width)
+    text_grad = jnp.where(zl < 6, text_grad, text_grad[:, ::-1])
+    text_grad = text_grad.transpose(0, 2, 1, 3, 4).reshape(rows, width)
     return (feature_grad, head_grad, text_grad)
 
 

time: 309 us -> 312 us (level)
  starting transfers between devices: 67 us -> 94.2 us
  blocking collectives: 64.7 us -> 38.8 us
    all_to_all x3 -> x2, blocking collectives: 64.7 us -> 38.8 us  [swap(): lax.all_to_all(value, axis, 0, 0, axis_index_groups=groups, tiled=True)]
    all_to_all x6 -> x7, starting transfers between devices: 46.9 us -> 70.6 us  [swap(): lax.all_to_all(value, axis, 0, 0, axis_index_groups=groups, tiled=True)]
    ppermute x1, waiting for transfers between devices: 15.5 us -> 2.72 us  [on_device(): unit_grad = back.astype(F32) + lax.ppermute(back, 'fsdp', PAIR).astype(F32)]
    reduce_scatter x1, waiting for transfers between devices: 26.2 us -> 35.3 us  [on_device(): lax.psum_scatter(text_acc, ('dp', 'fsdp'), axis_index_groups=LINE)]
    all_gather x1, waiting for transfers between devices: 0.02 us -> 8.88 us  [on_device(): far = lax.all_gather(crossed, 'dp', axis_index_groups=RING)]
    ppermute x1, starting transfers between devices: 6.97 us -> 12.5 us  [on_device(): unit_grad = back.astype(F32) + lax.ppermute(back, 'fsdp', PAIR).astype(F32)]
    ppermute x1, waiting for transfers between devices: 18.8 us -> 15.1 us  [on_device(): crossed = lax.ppermute(quad, ('dp', 'fsdp'), MIRROR)]
    all_to_all x6 -> x7, waiting for transfers between devices: 54.5 us -> 53.5 us  [swap(): lax.all_to_all(value, axis, 0, 0, axis_index_groups=groups, tiled=True)]
  transfers between devices with their start and end apart: 14 -> 15, of which waited for: 11 -> 10; matrix products, arithmetic and copies ran while one was open for 4% -> 5% of each run, Pallas kernels for 0% -> 0%
where the time goes in v6:
time: 312 us; the launch traced here: 311 us
  waiting for transfers between devices  129 us (41%)
  starting transfers between devices  94.2 us (30%)
  blocking collectives  38.8 us (12%)
  local copies, waits for them, and re-layouts  17.8 us (6%)
  between operations  15.6 us (5%)
  matrix products  8.29 us (3%)
  other arithmetic  6.77 us (2%)
    all_to_all x7, starting transfers between devices, swap(): lax.all_to_all(value, axis, 0, 0, axis_index_groups=groups, tiled=True)  70.6 us
    all_to_all x7, waiting for transfers between devices, swap(): lax.all_to_all(value, axis, 0, 0, axis_index_groups=groups, tiled=True)  53.5 us
    all_to_all x2, blocking collectives, swap(): lax.all_to_all(value, axis, 0, 0, axis_index_groups=groups, tiled=True)  38.8 us
    reduce_scatter x1, waiting for transfers between devices, on_device(): lax.psum_scatter(text_acc, ('dp', 'fsdp'), axis_index_groups=LINE)  35.3 us
    ppermute x1, waiting for transfers between devices, on_device(): crossed = lax.ppermute(quad, ('dp', 'fsdp'), MIRROR)  15.1 us
    ppermute x1, waiting for transfers between devices, on_device(): embed = half.astype(F32) + lax.ppermute(half, 'fsdp', PAIR).astype(F32)  12.9 us
    ppermute x1, starting transfers between devices, on_device(): unit_grad = back.astype(F32) + lax.ppermute(back, 'fsdp', PAIR).astype(F32)  12.5 us
    all_gather x1, waiting for transfers between devices, on_device(): far = lax.all_gather(crossed, 'dp', axis_index_groups=RING)  8.88 us
  transfers between devices with their start and end apart: 15, of which 10 were waited for; matrix products, arithmetic and copies ran while one was open for 5% of the time, Pallas kernels for 0%

profile of v6, /device:TPU:1, one launch (start us, length us, event | category | flops | bytes accessed | tf_op | source)
XLA Modules:
  0.0 310.6 jit_solution(16518230329169115875)
XLA Ops:
  7.2 1.0 broadcast_in_dim.60
  8.1 0.7 broadcast_in_dim.61
  8.8 19.1 %all-to-all-start = ((bf16[16,36,96]{2,1,0:T(8,128)(2,1)}), bf16[16,36,96]{2,1,0:T(8,128)(2,1)S(1)}, u32[]{:S(2)}, u32[]{:S(2)}) async-start(bf16[16,36,96]{2,1,0:T(8,128)(2,1)} %bitcast.1), calls=%async_computation | async-start | bytes 327680 | tf_op jit(solution)/shard_map/all_to_all | solution.py:34
  27.9 0.8 dynamic_slice.3
  28.9 14.2 %all-to-all-done = bf16[16,36,96]{2,1,0:T(8,128)(2,1)S(1)} async-done(((bf16[16,36,96]{2,1,0:T(8,128)(2,1)}), bf16[16,36,96]{2,1,0:T(8,128)(2,1)S(1)}, u32[]{:S(2)}, u32[]{:S(2)}) %all-to-all-start) | async-done | bytes 110624 | tf_op jit(solution)/shard_map/all_to_all | solution.py:34
  43.8 0.8 broadcast_select_fusion
  44.6 7.2 %all-to-all-start.1 = ((bf16[4,24,1536]{2,1,0:T(8,128)(2,1)}), bf16[4,24,1536]{2,1,0:T(8,128)(2,1)S(1)}, u32[]{:S(2)}, u32[]{:S(2)}) async-start(bf16[4,24,1536]{2,1,0:T(8,128)(2,1)} %broadcast_select_fusion), calls=%async_computation.1 | async-start | bytes 589824 | tf_op jit(solution)/shard_map/all_to_all | solution.py:34
  51.8 1.3 convolution_convert_fusion.2
  53.2 6.6 %all-to-all-done.1 = bf16[4,24,1536]{2,1,0:T(8,128)(2,1)S(1)} async-done(((bf16[4,24,1536]{2,1,0:T(8,128)(2,1)}), bf16[4,24,1536]{2,1,0:T(8,128)(2,1)S(1)}, u32[]{:S(2)}, u32[]{:S(2)}) %all-to-all-start.1) | async-done | bytes 294944 | tf_op jit(solution)/shard_map/all_to_all | solution.py:34
  59.9 0.7 fusion.13
  60.7 6.1 %all-to-all-start.2 = ((bf16[8,40,1536]{2,1,0:T(8,128)(2,1)}), bf16[8,40,1536]{2,1,0:T(8,128)(2,1)S(1)}, u32[]{:S(2)}, u32[]{:S(2)}) async-start(bf16[8,40,1536]{2,1,0:T(8,128)(2,1)} %bitcast.7), calls=%async_computation.2 | async-start | bytes 1966080 | tf_op jit(solution)/shard_map/all_to_all | solution.py:34
  66.8 1.9 collective-permute-start.1
  68.8 15.1 %collective-permute-done.1 = bf16[88,1536]{1,0:T(8,128)(2,1)S(1)} collective-permute-done((bf16[88,1536]{1,0:T(8,128)(2,1)S(1)}, bf16[88,1536]{1,0:T(8,128)(2,1)S(1)}, u32[]{:S(2)}, u32[]{:S(2)}) %collective-permute-start.1) | collective-permute-done | bytes 270368 | tf_op jit(solution)/shard_map/ppermute | solution.py:82
  83.9 0.7 copy-done.4
  84.8 4.6 %collective-permute-start = (bf16[40,1536]{1,0:T(8,128)(2,1)S(1)}, bf16[40,1536]{1,0:T(8,128)(2,1)S(1)}, u32[]{:S(2)}, u32[]{:S(2)}) collective-permute-start(bf16[40,1536]{1,0:T(8,128)(2,1)S(1)} %reduce_sum.70), channel_id=1, source_target_pairs={{0,2},{1,3},{2,0},{3,1},{4,6},{5,7},{6,4},{7,5},{8,10},{9,11},{10,... | collective-permute-start | bytes 368648 | tf_op jit(solution)/shard_map/ppermute | solution.py:87
  89.4 12.9 %collective-permute-done = bf16[40,1536]{1,0:T(8,128)(2,1)S(1)} collective-permute-done((bf16[40,1536]{1,0:T(8,128)(2,1)S(1)}, bf16[40,1536]{1,0:T(8,128)(2,1)S(1)}, u32[]{:S(2)}, u32[]{:S(2)}) %collective-permute-start) | collective-permute-done | bytes 122912 | tf_op jit(solution)/shard_map/ppermute | solution.py:87
  102.5 1.0 broadcast_in_dim.67
  103.6 4.8 %all-to-all-start.3 = ((bf16[8,40,1536]{2,1,0:T(8,128)(2,1)}), bf16[8,40,1536]{2,1,0:T(8,128)(2,1)}, u32[]{:S(2)}, u32[]{:S(2)}) async-start(bf16[8,40,1536]{2,1,0:T(8,128)(2,1)} %broadcast_in_dim.67), calls=%async_computation.3 | async-start | bytes 1966080 | tf_op jit(solution)/shard_map/all_to_all | solution.py:34
  109.8 0.7 slice.96
  110.5 1.2 slice.100
  111.7 8.9 %all-gather.7.cloned.1.call-done = bf16[352,1536]{1,0:T(8,128)(2,1)} async-done(((bf16[88,1536]{1,0:T(8,128)(2,1)}), bf16[352,1536]{1,0:T(8,128)(2,1)}) %all-gather.7.cloned.1.call-update) | async-done | bytes 1081360 | tf_op jit(solution)/shard_map/all_gather | solution.py:86
  120.6 0.7 slice.97
  121.3 1.2 slice.101
  122.8 1.4 pad_maximum_fusion
  124.1 2.9 fusion.9
  127.0 2.3 convolution_convert_fusion
  129.3 1.4 copy.41
  130.7 1.4 copy-done.1
  132.2 0.9 convolution_convert_fusion.1
  133.1 20.1 %all_to_all.45 = bf16[8,40,1536]{2,1,0:T(8,128)(2,1)S(1)} all-to-all(bf16[8,40,1536]{2,1,0:T(8,128)(2,1)S(1)} %bitcast.75), channel_id=1, replica_groups={{0,1,4,5,8,9,12,13},{2,3,6,7,10,11,14,15},{16,17,20,21,24,25,28,29},{18..., dimensions={0} | all-to-all | bytes 1966080 | tf_op jit(solution)/shard_map/all_to_all | solution.py:34
  153.4 12.5 %collective-permute-start.2 = (bf16[40,1536]{1,0:T(8,128)(2,1)S(1)}, bf16[40,1536]{1,0:T(8,128)(2,1)S(1)}, u32[]{:S(2)}, u32[]{:S(2)}) collective-permute-start(bf16[40,1536]{1,0:T(8,128)(2,1)S(1)} %reduce_sum.72), channel_id=1, source_target_pairs={{0,2},{1,3},{2,0},{3,1},{4,6},{5,7},{6,4},{7,5},{8,10},{9,11},{10,... | collective-permute-start | bytes 368648 | tf_op jit(solution)/shard_map/ppermute | solution.py:111
  165.9 2.7 collective-permute-done.2
  169.0 1.1 reshape_reduce_scatter.3
  170.4 18.7 %all_to_all.46 = bf16[8,40,1536]{2,1,0:T(8,128)(2,1)S(1)} all-to-all(bf16[8,40,1536]{2,1,0:T(8,128)(2,1)S(1)} %broadcast_in_dim.68), channel_id=1, replica_groups={{0,1,4,5,8,9,12,13},{2,3,6,7,10,11,14,15},{16,17,20,21,24,25,28,29},{18..., dimensions={0} | all-to-all | bytes 1966080 | tf_op jit(solution)/shard_map/all_to_all | solution.py:34
  189.6 0.7 copy.43
  190.3 11.8 %all-to-all-start.6 = ((bf16[16,24,384]{2,1,0:T(8,128)(2,1)}), bf16[16,24,384]{2,1,0:T(8,128)(2,1)S(1)}, u32[]{:S(2)}, u32[]{:S(2)}) async-start(bf16[16,24,384]{2,1,0:T(8,128)(2,1)} %bitcast.21), calls=%async_computation.7 | async-start | bytes 589824 | tf_op jit(solution)/shard_map/all_to_all | solution.py:34
  203.0 9.7 %all-to-all-done.6 = bf16[16,24,384]{2,1,0:T(8,128)(2,1)S(1)} async-done(((bf16[16,24,384]{2,1,0:T(8,128)(2,1)}), bf16[16,24,384]{2,1,0:T(8,128)(2,1)S(1)}, u32[]{:S(2)}, u32[]{:S(2)}) %all-to-all-start.6) | async-done | bytes 294944 | tf_op jit(solution)/shard_map/all_to_all | solution.py:34
  212.7 35.3 %reduce-scatter.5.cloned.1.call-done = bf16[1,18,1536]{2,1,0:T(8,128)(2,1)} async-done(((bf16[8,18,1536]{2,1,0:T(8,128)(2,1)}), bf16[1,18,1536]{2,1,0:T(8,128)(2,1)}) %reduce-scatter.5.cloned.1.call-update) | async-done | bytes 55312 | tf_op jit(solution)/shard_map/reduce_scatter | solution.py:118
  248.1 4.5 %collective-permute-start.3 = (bf16[24,384]{1,0:T(8,128)(2,1)S(1)}, bf16[24,384]{1,0:T(8,128)(2,1)S(1)}, u32[]{:S(2)}, u32[]{:S(2)}) collective-permute-start(bf16[24,384]{1,0:T(8,128)(2,1)S(1)} %reduce-precision_convert_fusion), channel_id=1, source_target_pairs={{0,256},{16,272},{32,288},{48,304},{64,320},{80,336},{96,352},{112... | collective-permute-start | bytes 55304 | tf_op jit(solution)/shard_map/ppermute | solution.py:126
  252.6 1.0 fusion.16
  253.6 1.0 fusion.18
  255.4 17.1 %all-to-all-start.8 = ((bf16[16,18,96]{2,1,0:T(8,128)(2,1)}), bf16[16,18,96]{2,1,0:T(8,128)(2,1)S(1)}, u32[]{:S(2)}, u32[]{:S(2)}) async-start(bf16[16,18,96]{2,1,0:T(8,128)(2,1)} %copy.46), calls=%async_computation.10 | async-start | bytes 196608 | tf_op jit(solution)/shard_map/all_to_all | solution.py:34
  272.5 14.5 %all-to-all-done.8 = bf16[16,18,96]{2,1,0:T(8,128)(2,1)S(1)} async-done(((bf16[16,18,96]{2,1,0:T(8,128)(2,1)}), bf16[16,18,96]{2,1,0:T(8,128)(2,1)S(1)}, u32[]{:S(2)}, u32[]{:S(2)}) %all-to-all-start.8) | async-done | bytes 55328 | tf_op jit(solution)/shard_map/all_to_all | solution.py:34
  287.1 0.7 broadcast_in_dim.69
  287.8 4.6 %all-to-all-start.7 = ((bf16[16,24,384]{2,1,0:T(8,128)(2,1)}), bf16[16,24,384]{2,1,0:T(8,128)(2,1)S(1)}, u32[]{:S(2)}, u32[]{:S(2)}) async-start(bf16[16,24,384]{2,1,0:T(8,128)(2,1)} %broadcast_in_dim.69), calls=%async_computation.9 | async-start | bytes 589824 | tf_op jit(solution)/shard_map/all_to_all | solution.py:34
  293.0 0.7 reshape.201
  294.5 8.5 %all-to-all-done.7 = bf16[16,24,384]{2,1,0:T(8,128)(2,1)S(1)} async-done(((bf16[16,24,384]{2,1,0:T(8,128)(2,1)}), bf16[16,24,384]{2,1,0:T(8,128)(2,1)S(1)}, u32[]{:S(2)}, u32[]{:S(2)}) %all-to-all-start.7) | async-done | bytes 294944 | tf_op jit(solution)/shard_map/all_to_all | solution.py:34
  303.2 0.9 copy.50
  (83 shorter events, 6.2 us)
Async XLA Ops:
  7.2 44.7 %copy-start = (bf16[96,1536]{1,0:T(8,128)(2,1)S(1)}, bf16[96,1536]{1,0:T(8,128)(2,1)}, u32[]{:S(2)}) copy-start(bf16[96,1536]{1,0:T(8,128)(2,1)} %param.7) | copy-start | bytes 884740
  8.8 34.3 %all-to-all-start = ((bf16[16,36,96]{2,1,0:T(8,128)(2,1)}), bf16[16,36,96]{2,1,0:T(8,128)(2,1)S(1)}, u32[]{:S(2)}, u32[]{:S(2)}) async-start(bf16[16,36,96]{2,1,0:T(8,128)(2,1)} %bitcast.1), calls=%async_computation | async-start | bytes 327680 | tf_op jit(solution)/shard_map/all_to_all | solution.py:34
  43.3 8.5 %copy-start.5 = (bf16[288,96]{1,0:T(8,128)(2,1)S(1)}, bf16[288,96]{1,0:T(8,128)(2,1)}, u32[]{:S(2)}) copy-start(bf16[288,96]{1,0:T(8,128)(2,1)} %param.6) | copy-start | bytes 165892
  44.6 15.2 %all-to-all-start.1 = ((bf16[4,24,1536]{2,1,0:T(8,128)(2,1)}), bf16[4,24,1536]{2,1,0:T(8,128)(2,1)S(1)}, u32[]{:S(2)}, u32[]{:S(2)}) async-start(bf16[4,24,1536]{2,1,0:T(8,128)(2,1)} %broadcast_select_fusion), calls=%async_computation.1 | async-start | bytes 589824 | tf_op jit(solution)/shard_map/all_to_all | solution.py:34
  51.8 58.0 %all-gather.5.cloned.1.call-start = ((), (), s32[]{:S(2)}) async-start(), calls=%async_computation.13 | async-start | bytes 1351680 | tf_op jit(solution)/shard_map/all_gather | solution.py:81
  60.7 6.2 %copy-start.2 = (bf16[88,1536]{1,0:T(8,128)(2,1)S(1)}, bf16[88,1536]{1,0:T(8,128)(2,1)}, u32[]{:S(2)}) copy-start(bf16[88,1536]{1,0:T(8,128)(2,1)} %fusion.13) | copy-start | bytes 811012
  60.7 23.9 %all-to-all-start.2 = ((bf16[8,40,1536]{2,1,0:T(8,128)(2,1)}), bf16[8,40,1536]{2,1,0:T(8,128)(2,1)S(1)}, u32[]{:S(2)}, u32[]{:S(2)}) async-start(bf16[8,40,1536]{2,1,0:T(8,128)(2,1)} %bitcast.7), calls=%async_computation.2 | async-start | bytes 1966080 | tf_op jit(solution)/shard_map/all_to_all | solution.py:34
  66.8 53.8 %all-gather.7.cloned.1.call-start = ((), (), s32[]{:S(2)}) async-start(), calls=%async_computation.14 | async-start | bytes 1351680 | tf_op jit(solution)/shard_map/all_gather | solution.py:86
  66.8 17.1 %collective-permute-start.1 = (bf16[88,1536]{1,0:T(8,128)(2,1)S(1)}, bf16[88,1536]{1,0:T(8,128)(2,1)S(1)}, u32[]{:S(2)}, u32[]{:S(2)}) collective-permute-start(bf16[88,1536]{1,0:T(8,128)(2,1)S(1)} %copy-done.2), channel_id=1, source_target_pairs={{0,450},{1,451},{4,454},{5,455},{8,458},{9,459},{12,462},{13,463},... | collective-permute-start | bytes 811016 | tf_op jit(solution)/shard_map/ppermute | solution.py:82
  83.9 0.7 copy-start.4
  84.8 17.5 %collective-permute-start = (bf16[40,1536]{1,0:T(8,128)(2,1)S(1)}, bf16[40,1536]{1,0:T(8,128)(2,1)S(1)}, u32[]{:S(2)}, u32[]{:S(2)}) collective-permute-start(bf16[40,1536]{1,0:T(8,128)(2,1)S(1)} %reduce_sum.70), channel_id=1, source_target_pairs={{0,2},{1,3},{2,0},{3,1},{4,6},{5,7},{6,4},{7,5},{8,10},{9,11},{10,... | collective-permute-start | bytes 368648 | tf_op jit(solution)/shard_map/ppermute | solution.py:87
  103.6 20.6 %all-to-all-start.3 = ((bf16[8,40,1536]{2,1,0:T(8,128)(2,1)}), bf16[8,40,1536]{2,1,0:T(8,128)(2,1)}, u32[]{:S(2)}, u32[]{:S(2)}) async-start(bf16[8,40,1536]{2,1,0:T(8,128)(2,1)} %broadcast_in_dim.67), calls=%async_computation.3 | async-start | bytes 1966080 | tf_op jit(solution)/shard_map/all_to_all | solution.py:34
  108.3 60.6 %reduce-scatter.3.cloned.1.call-start = ((), (), s32[]{:S(2)}) async-start(), calls=%async_computation.11 | async-start | bytes 2211840 | tf_op jit(solution)/shard_map/reduce_scatter | solution.py:108
  130.7 1.5 copy-start.1
  153.4 15.3 %collective-permute-start.2 = (bf16[40,1536]{1,0:T(8,128)(2,1)S(1)}, bf16[40,1536]{1,0:T(8,128)(2,1)S(1)}, u32[]{:S(2)}, u32[]{:S(2)}) collective-permute-start(bf16[40,1536]{1,0:T(8,128)(2,1)S(1)} %reduce_sum.72), channel_id=1, source_target_pairs={{0,2},{1,3},{2,0},{3,1},{4,6},{5,7},{6,4},{7,5},{8,10},{9,11},{10,... | collective-permute-start | bytes 368648 | tf_op jit(solution)/shard_map/ppermute | solution.py:111
  170.3 19.2 %copy-start.3 = (bf16[8,18,1536]{2,1,0:T(8,128)(2,1)}, bf16[8,18,1536]{2,1,0:T(8,128)(2,1)S(1)}, u32[]{:S(2)}) copy-start(bf16[8,18,1536]{2,1,0:T(8,128)(2,1)S(1)} %slice_dynamic-update-slice_fusion.1) | copy-start | bytes 1327108
  190.3 22.4 %all-to-all-start.6 = ((bf16[16,24,384]{2,1,0:T(8,128)(2,1)}), bf16[16,24,384]{2,1,0:T(8,128)(2,1)S(1)}, u32[]{:S(2)}, u32[]{:S(2)}) async-start(bf16[16,24,384]{2,1,0:T(8,128)(2,1)} %bitcast.21), calls=%async_computation.7 | async-start | bytes 589824 | tf_op jit(solution)/shard_map/all_to_all | solution.py:34
  202.1 46.0 %reduce-scatter.5.cloned.1.call-start = ((), (), s32[]{:S(2)}) async-start(), calls=%async_computation.12 | async-start | bytes 663552 | tf_op jit(solution)/shard_map/reduce_scatter | solution.py:118
  248.1 24.4 %collective-permute-start.3 = (bf16[24,384]{1,0:T(8,128)(2,1)S(1)}, bf16[24,384]{1,0:T(8,128)(2,1)S(1)}, u32[]{:S(2)}, u32[]{:S(2)}) collective-permute-start(bf16[24,384]{1,0:T(8,128)(2,1)S(1)} %reduce-precision_convert_fusion), channel_id=1, source_target_pairs={{0,256},{16,272},{32,288},{48,304},{64,320},{80,336},{96,352},{112... | collective-permute-start | bytes 55304 | tf_op jit(solution)/shard_map/ppermute | solution.py:126
  255.4 31.7 %all-to-all-start.8 = ((bf16[16,18,96]{2,1,0:T(8,128)(2,1)}), bf16[16,18,96]{2,1,0:T(8,128)(2,1)S(1)}, u32[]{:S(2)}, u32[]{:S(2)}) async-start(bf16[16,18,96]{2,1,0:T(8,128)(2,1)} %copy.46), calls=%async_computation.10 | async-start | bytes 196608 | tf_op jit(solution)/shard_map/all_to_all | solution.py:34
  287.8 15.2 %all-to-all-start.7 = ((bf16[16,24,384]{2,1,0:T(8,128)(2,1)}), bf16[16,24,384]{2,1,0:T(8,128)(2,1)S(1)}, u32[]{:S(2)}, u32[]{:S(2)}) async-start(bf16[16,24,384]{2,1,0:T(8,128)(2,1)} %broadcast_in_dim.69), calls=%async_computation.9 | async-start | bytes 589824 | tf_op jit(solution)/shard_map/all_to_all | solution.py:34
Sparse Core Ops, SparseCore 0:
  60.8 25.2 all-gather.4
  88.2 32.3 all-gather.6
  130.9 36.2 reduce-scatter.2
  206.3 41.7 reduce-scatter.4

commit v7 on v6

--- a/solution.py
+++ b/solution.py
@@ -89,8 +89,8 @@
     image_unit = embed * image_scale
     image_low = spread(image_unit.astype(BF16), "fsdp", PLANE, plane).reshape(plane * held, embed_width)
     lines = (near, far)
-    text_low = jnp.concatenate([part[:, :count] for part in lines]).reshape(cycle * share, embed_width)
-    notes = jnp.concatenate([part[:, count : count + 4, : 2 * share] for part in lines]).astype(jnp.int32)
+    text_low = jnp.stack([part[:, :count] for part in lines], axis=1).reshape(cycle * share, embed_width)
+    notes = jnp.stack([part[:, count : count + 4, : 2 * share] for part in lines], axis=1).astype(jnp.int32)
     ids = (notes[..., :share] * 128 + notes[..., share:]).reshape(cycle * share)
 
     partial_value = jnp.einsum("ie,je->ij", image_low, text_low, preferred_element_type=F32)
@@ -101,10 +101,9 @@
     sign = jnp.where(row_index == ids[None, :], 1.0, -1.0).astype(F32)
     coef = (-sign * jax.nn.sigmoid(-sign * logits) * logit_scale).astype(BF16)
     unit_part = jnp.einsum("ij,je->ie", coef, text_low, preferred_element_type=F32).astype(BF16)
+    unit_part, coef = lax.optimization_barrier((unit_part, coef))
     text_acc = jnp.einsum("ij,ie->je", coef, image_low, preferred_element_type=F32).astype(BF16)
 
-
-    text_acc = text_acc.reshape(2, Y, 4 * share, embed_width).transpose(1, 0, 2, 3)
     text_acc = lax.psum_scatter(text_acc.reshape(Y, ZL * share, embed_width), "dp", axis_index_groups=RING)
     back = swap(unit_part.reshape(plane, held, embed_width), "fsdp", PLANE)
     back = jnp.sum(back.astype(F32), axis=0).astype(BF16)
@@ -112,7 +111,7 @@
     image_dot = jnp.sum(image_unit * unit_grad, axis=1, keepdims=True)
     embed_grad = (image_scale * (unit_grad - image_unit * image_dot)).astype(BF16)
     text_acc = text_acc.reshape(2, 4, share, embed_width)
-    text_acc = jnp.where(zl < 4, text_acc, text_acc[::-1]).reshape(ZL, share, embed_width)
+    text_acc = jnp.where(zl < 4, text_acc, text_acc[::-1]).reshape(ZL, share, embed_width).astype(F32)
     text_acc = jnp.stack([text_acc[at] for at in LINE_ZL])
     embed_grad, text_acc = lax.optimization_barrier((embed_grad, text_acc))
     text_acc = lax.psum_scatter(text_acc, ("dp", "fsdp"), axis_index_groups=LINE)
@@ -121,16 +120,15 @@
     head_part = head_part.reshape(Y, width // Y, 4, embed_width // 4).transpose(0, 2, 1, 3)
     head_part = head_part.reshape(4 * Y, width // Y, embed_width // 4)
     head_sum = jnp.sum(swap(head_part, "dp", SLAB).astype(F32), axis=0)
-    head_sum, text_acc = lax.optimization_barrier((head_sum, text_acc))
     head_sum = lax.reduce_precision(head_sum, 8, 7)
     head_sum = head_sum + lax.ppermute(head_sum.astype(BF16), "dp", ACROSS).astype(F32)
-    head_all = spread(head_sum.astype(BF16), "dp", SLAB, 4 * Y).reshape(Y, 4, width // Y, embed_width // 4)
+    head_sum, text_acc = lax.optimization_barrier((head_sum.astype(BF16), text_acc))
+    head_all = spread(head_sum, "dp", SLAB, 4 * Y).reshape(Y, 4, width // Y, embed_width // 4)
     head_all = head_all.transpose(0, 2, 1, 3).reshape(width, embed_width)
     head_grad = head_all.astype(F32)
     feature_grad = jnp.einsum("re,we->rw", grads, image_head, preferred_element_type=F32).astype(BF16)
     feature_grad = feature_grad.reshape(plane, held, width)[:, :own].reshape(rows, width)
 
-    text_acc = text_acc.astype(F32)
     text_dot = jnp.sum(text_unit * text_acc, axis=1, keepdims=True)
     text_rows = (text_scale * (text_acc - text_unit * text_dot)).astype(BF16)
     text_rows = text_rows.reshape(share, group, width).transpose(1, 0, 2)

time: 312 us -> 312 us (level)
  blocking collectives: 38.8 us -> 70.2 us
  waiting for transfers between devices: 129 us -> 109 us
  starting transfers between devices: 94.2 us -> 84.1 us
    all_to_all x2 -> x3, blocking collectives: 38.8 us -> 70.2 us  [swap(): lax.all_to_all(value, axis, 0, 0, axis_index_groups=groups, tiled=True)]
    all_to_all x7 -> x6, waiting for transfers between devices: 53.5 us -> 39.1 us  [swap(): lax.all_to_all(value, axis, 0, 0, axis_index_groups=groups, tiled=True)]
    all_to_all x7 -> x6, starting transfers between devices: 70.6 us -> 56.5 us  [swap(): lax.all_to_all(value, axis, 0, 0, axis_index_groups=groups, tiled=True)]
    reduce_scatter x1, waiting for transfers between devices: 35.3 us -> 28.9 us  [on_device(): lax.psum_scatter(text_acc, ('dp', 'fsdp'), axis_index_groups=LINE)]
    ppermute x1, starting transfers between devices: 4.53 us -> 8.55 us  [on_device(): lax.ppermute(head_sum.astype(BF16), 'dp', ACROSS).astype(F32)]
    another operation x0 -> x4, local copies, waits for them, and re-layouts: none -> 3.86 us  [the longest x2 2.45 us: on_device(): jnp.stack([part[:, :count] for part in lines], axis=1)]
    slice x4 -> x0, local copies, waits for them, and re-layouts: 3.85 us -> none  [the longest x2 2.45 us: on_device(): part[:, :count]]
  transfers between devices with their start and end apart: 15 -> 14, of which waited for: 10 -> 10; matrix products, arithmetic and copies ran while one was open for 5% -> 4% of each run, Pallas kernels for 0% -> 0%
where the time goes in v7:
time: 312 us; the launch traced here: 311 us
  waiting for transfers between devices  109 us (35%)
  starting transfers between devices  84.1 us (27%)
  blocking collectives  70.2 us (22%)
  local copies, waits for them, and re-layouts  15.6 us (5%)
  between operations  15.6 us (5%)
  matrix products  9.88 us (3%)
  other arithmetic  5.78 us (2%)
    all_to_all x3, blocking collectives, swap(): lax.all_to_all(value, axis, 0, 0, axis_index_groups=groups, tiled=True)  70.2 us
    all_to_all x6, starting transfers between devices, swap(): lax.all_to_all(value, axis, 0, 0, axis_index_groups=groups, tiled=True)  56.5 us
    all_to_all x6, waiting for transfers between devices, swap(): lax.all_to_all(value, axis, 0, 0, axis_index_groups=groups, tiled=True)  39.1 us
    reduce_scatter x1, waiting for transfers between devices, on_device(): lax.psum_scatter(text_acc, ('dp', 'fsdp'), axis_index_groups=LINE)  28.9 us
    ppermute x1, waiting for transfers between devices, on_device(): crossed = lax.ppermute(quad, ('dp', 'fsdp'), MIRROR)  15.1 us
    ppermute x1, starting transfers between devices, on_device(): unit_grad = back.astype(F32) + lax.ppermute(back, 'fsdp', PAIR).astype(F32)  12.5 us
    ppermute x1, waiting for transfers between devices, on_device(): embed = half.astype(F32) + lax.ppermute(half, 'fsdp', PAIR).astype(F32)  11.5 us
    all_gather x1, waiting for transfers between devices, on_device(): far = lax.all_gather(crossed, 'dp', axis_index_groups=RING)  10.3 us
  transfers between devices with their start and end apart: 14, of which 10 were waited for; matrix products, arithmetic and copies ran while one was open for 4% of the time, Pallas kernels for 0%

profile of v7, /device:TPU:1, one launch (start us, length us, event | category | flops | bytes accessed | tf_op | source)
XLA Modules:
  0.0 310.5 jit_solution(358719464674073222)
XLA Ops:
  7.2 1.0 broadcast_in_dim.60
  8.1 0.7 broadcast_in_dim.61
  8.8 19.1 %all-to-all-start = ((bf16[16,36,96]{2,1,0:T(8,128)(2,1)}), bf16[16,36,96]{2,1,0:T(8,128)(2,1)S(1)}, u32[]{:S(2)}, u32[]{:S(2)}) async-start(bf16[16,36,96]{2,1,0:T(8,128)(2,1)} %bitcast.1), calls=%async_computation | async-start | bytes 327680 | tf_op jit(solution)/shard_map/all_to_all | solution.py:34
  27.9 0.8 dynamic_slice.3
  28.9 14.2 %all-to-all-done = bf16[16,36,96]{2,1,0:T(8,128)(2,1)S(1)} async-done(((bf16[16,36,96]{2,1,0:T(8,128)(2,1)}), bf16[16,36,96]{2,1,0:T(8,128)(2,1)S(1)}, u32[]{:S(2)}, u32[]{:S(2)}) %all-to-all-start) | async-done | bytes 110624 | tf_op jit(solution)/shard_map/all_to_all | solution.py:34
  43.8 0.8 broadcast_select_fusion
  44.6 7.2 %all-to-all-start.1 = ((bf16[4,24,1536]{2,1,0:T(8,128)(2,1)}), bf16[4,24,1536]{2,1,0:T(8,128)(2,1)S(1)}, u32[]{:S(2)}, u32[]{:S(2)}) async-start(bf16[4,24,1536]{2,1,0:T(8,128)(2,1)} %broadcast_select_fusion), calls=%async_computation.1 | async-start | bytes 589824 | tf_op jit(solution)/shard_map/all_to_all | solution.py:34
  51.9 1.3 convolution_convert_fusion.2
  53.2 6.6 %all-to-all-done.1 = bf16[4,24,1536]{2,1,0:T(8,128)(2,1)S(1)} async-done(((bf16[4,24,1536]{2,1,0:T(8,128)(2,1)}), bf16[4,24,1536]{2,1,0:T(8,128)(2,1)S(1)}, u32[]{:S(2)}, u32[]{:S(2)}) %all-to-all-start.1) | async-done | bytes 294944 | tf_op jit(solution)/shard_map/all_to_all | solution.py:34
  60.0 0.7 fusion.13
  60.7 6.1 %all-to-all-start.2 = ((bf16[8,40,1536]{2,1,0:T(8,128)(2,1)}), bf16[8,40,1536]{2,1,0:T(8,128)(2,1)S(1)}, u32[]{:S(2)}, u32[]{:S(2)}) async-start(bf16[8,40,1536]{2,1,0:T(8,128)(2,1)} %bitcast.7), calls=%async_computation.2 | async-start | bytes 1966080 | tf_op jit(solution)/shard_map/all_to_all | solution.py:34
  66.9 1.9 collective-permute-start.1
  68.8 15.1 %collective-permute-done.1 = bf16[88,1536]{1,0:T(8,128)(2,1)S(1)} collective-permute-done((bf16[88,1536]{1,0:T(8,128)(2,1)S(1)}, bf16[88,1536]{1,0:T(8,128)(2,1)S(1)}, u32[]{:S(2)}, u32[]{:S(2)}) %collective-permute-start.1) | collective-permute-done | bytes 270368 | tf_op jit(solution)/shard_map/ppermute | solution.py:82
  83.9 0.7 copy-done.6
  84.8 4.6 %collective-permute-start = (bf16[40,1536]{1,0:T(8,128)(2,1)S(1)}, bf16[40,1536]{1,0:T(8,128)(2,1)S(1)}, u32[]{:S(2)}, u32[]{:S(2)}) collective-permute-start(bf16[40,1536]{1,0:T(8,128)(2,1)S(1)} %reduce_sum.70), channel_id=1, source_target_pairs={{0,2},{1,3},{2,0},{3,1},{4,6},{5,7},{6,4},{7,5},{8,10},{9,11},{10,... | collective-permute-start | bytes 368648 | tf_op jit(solution)/shard_map/ppermute | solution.py:87
  90.8 11.5 %collective-permute-done = bf16[40,1536]{1,0:T(8,128)(2,1)S(1)} collective-permute-done((bf16[40,1536]{1,0:T(8,128)(2,1)S(1)}, bf16[40,1536]{1,0:T(8,128)(2,1)S(1)}, u32[]{:S(2)}, u32[]{:S(2)}) %collective-permute-start) | collective-permute-done | bytes 122912 | tf_op jit(solution)/shard_map/ppermute | solution.py:87
  102.6 1.0 broadcast_in_dim.67
  103.6 4.8 %all-to-all-start.3 = ((bf16[8,40,1536]{2,1,0:T(8,128)(2,1)}), bf16[8,40,1536]{2,1,0:T(8,128)(2,1)}, u32[]{:S(2)}, u32[]{:S(2)}) async-start(bf16[8,40,1536]{2,1,0:T(8,128)(2,1)} %broadcast_in_dim.67), calls=%async_computation.3 | async-start | bytes 1966080 | tf_op jit(solution)/shard_map/all_to_all | solution.py:34
  108.4 0.7 slice_bitcast_fusion.3
  109.1 1.2 slice_bitcast_fusion.1
  110.3 10.3 %all-gather.7.cloned.1.call-done = bf16[352,1536]{1,0:T(8,128)(2,1)} async-done(((bf16[88,1536]{1,0:T(8,128)(2,1)}), bf16[352,1536]{1,0:T(8,128)(2,1)}) %all-gather.7.cloned.1.call-update) | async-done | bytes 1081360 | tf_op jit(solution)/shard_map/all_gather | solution.py:86
  120.6 0.7 slice_bitcast_fusion.2
  121.6 1.2 slice_bitcast_fusion
  123.0 2.3 fusion.9
  125.3 1.9 convolution_convert_fusion.1
  127.2 3.5 %convolution_convert_fusion = bf16[576,1536]{1,0:T(8,128)(2,1)} fusion(bf16[320,576]{1,0:T(8,128)(2,1)S(1)} %fusion.9, bf16[320,1536]{1,0:T(8,128)(2,1)} %bitcast.12), kind=kOutput, calls=%fused_computation | convolution fusion | flops 567115776 | bytes 3121152 | tf_op jit(solution)/shard_map/ij,ie->je/dot_general | solution.py:105
  130.7 1.2 copy-done.3
  131.9 20.1 %all_to_all.45 = bf16[8,40,1536]{2,1,0:T(8,128)(2,1)S(1)} all-to-all(bf16[8,40,1536]{2,1,0:T(8,128)(2,1)S(1)} %bitcast.76), channel_id=1, replica_groups={{0,1,4,5,8,9,12,13},{2,3,6,7,10,11,14,15},{16,17,20,21,24,25,28,29},{18..., dimensions={0} | all-to-all | bytes 1966080 | tf_op jit(solution)/shard_map/all_to_all | solution.py:34
  152.1 12.5 %collective-permute-start.2 = (bf16[40,1536]{1,0:T(8,128)(2,1)S(1)}, bf16[40,1536]{1,0:T(8,128)(2,1)S(1)}, u32[]{:S(2)}, u32[]{:S(2)}) collective-permute-start(bf16[40,1536]{1,0:T(8,128)(2,1)S(1)} %reduce_sum.72), channel_id=1, source_target_pairs={{0,2},{1,3},{2,0},{3,1},{4,6},{5,7},{6,4},{7,5},{8,10},{9,11},{10,... | collective-permute-start | bytes 368648 | tf_op jit(solution)/shard_map/ppermute | solution.py:110
  164.7 2.7 collective-permute-done.2
  167.7 1.1 reshape_reduce_scatter.3
  169.4 18.8 %all_to_all.46 = bf16[8,40,1536]{2,1,0:T(8,128)(2,1)S(1)} all-to-all(bf16[8,40,1536]{2,1,0:T(8,128)(2,1)S(1)} %broadcast_in_dim.68), channel_id=1, replica_groups={{0,1,4,5,8,9,12,13},{2,3,6,7,10,11,14,15},{16,17,20,21,24,25,28,29},{18..., dimensions={0} | all-to-all | bytes 1966080 | tf_op jit(solution)/shard_map/all_to_all | solution.py:34
  188.7 0.7 copy.47
  189.4 11.8 %all-to-all-start.6 = ((bf16[16,24,384]{2,1,0:T(8,128)(2,1)}), bf16[16,24,384]{2,1,0:T(8,128)(2,1)S(1)}, u32[]{:S(2)}, u32[]{:S(2)}) async-start(bf16[16,24,384]{2,1,0:T(8,128)(2,1)} %bitcast.25), calls=%async_computation.7 | async-start | bytes 589824 | tf_op jit(solution)/shard_map/all_to_all | solution.py:34
  201.3 0.5 reduce-scatter.5.cloned.1.call-update
  202.1 9.7 %all-to-all-done.6 = bf16[16,24,384]{2,1,0:T(8,128)(2,1)S(1)} async-done(((bf16[16,24,384]{2,1,0:T(8,128)(2,1)}), bf16[16,24,384]{2,1,0:T(8,128)(2,1)S(1)}, u32[]{:S(2)}, u32[]{:S(2)}) %all-to-all-start.6) | async-done | bytes 294944 | tf_op jit(solution)/shard_map/all_to_all | solution.py:34
  211.9 8.5 %collective-permute-start.3 = (bf16[24,384]{1,0:T(8,128)(2,1)S(1)}, bf16[24,384]{1,0:T(8,128)(2,1)S(1)}, u32[]{:S(2)}, u32[]{:S(2)}) collective-permute-start(bf16[24,384]{1,0:T(8,128)(2,1)S(1)} %reduce-precision_convert_fusion), channel_id=1, source_target_pairs={{0,256},{16,272},{32,288},{48,304},{64,320},{80,336},{96,352},{112... | collective-permute-start | bytes 55304 | tf_op jit(solution)/shard_map/ppermute | solution.py:124
  220.5 1.1 collective-permute-done.3
  221.6 28.9 %reduce-scatter.5.cloned.1.call-done = f32[1,18,1536]{2,1,0:T(8,128)} async-done(((f32[8,18,1536]{2,1,0:T(8,128)}), f32[1,18,1536]{2,1,0:T(8,128)}) %reduce-scatter.5.cloned.1.call-update) | async-done | bytes 110608 | tf_op jit(solution)/shard_map/reduce_scatter | solution.py:117
  250.5 1.0 multiply_reduce_fusion.2
  251.6 1.0 multiply_convert_fusion.2
  252.8 31.3 %all_to_all.47 = bf16[16,18,96]{2,1,0:T(8,128)(2,1)S(1)} all-to-all(bf16[16,18,96]{2,1,0:T(8,128)(2,1)S(1)} %copy.50), channel_id=1, replica_groups=mesh['dp'=32,'fsdp'=16] {'fsdp'}, dimensions={0} | all-to-all | bytes 110592 | tf_op jit(solution)/shard_map/all_to_all | solution.py:34
  284.1 0.7 broadcast_in_dim.69
  284.8 7.6 %all-to-all-start.7 = ((bf16[16,24,384]{2,1,0:T(8,128)(2,1)}), bf16[16,24,384]{2,1,0:T(8,128)(2,1)S(1)}, u32[]{:S(2)}, u32[]{:S(2)}) async-start(bf16[16,24,384]{2,1,0:T(8,128)(2,1)} %broadcast_in_dim.69), calls=%async_computation.9 | async-start | bytes 589824 | tf_op jit(solution)/shard_map/all_to_all | solution.py:34
  292.9 0.7 reshape.196
  293.8 0.7 reshape.201
  294.4 8.5 %all-to-all-done.7 = bf16[16,24,384]{2,1,0:T(8,128)(2,1)S(1)} async-done(((bf16[16,24,384]{2,1,0:T(8,128)(2,1)}), bf16[16,24,384]{2,1,0:T(8,128)(2,1)S(1)}, u32[]{:S(2)}, u32[]{:S(2)}) %all-to-all-start.7) | async-done | bytes 294944 | tf_op jit(solution)/shard_map/all_to_all | solution.py:34
  303.1 0.9 copy.54
  (87 shorter events, 4.8 us)
Async XLA Ops:
  7.2 44.7 %copy-start = (bf16[96,1536]{1,0:T(8,128)(2,1)S(1)}, bf16[96,1536]{1,0:T(8,128)(2,1)}, u32[]{:S(2)}) copy-start(bf16[96,1536]{1,0:T(8,128)(2,1)} %param.7) | copy-start | bytes 884740
  8.8 34.3 %all-to-all-start = ((bf16[16,36,96]{2,1,0:T(8,128)(2,1)}), bf16[16,36,96]{2,1,0:T(8,128)(2,1)S(1)}, u32[]{:S(2)}, u32[]{:S(2)}) async-start(bf16[16,36,96]{2,1,0:T(8,128)(2,1)} %bitcast.1), calls=%async_computation | async-start | bytes 327680 | tf_op jit(solution)/shard_map/all_to_all | solution.py:34
  43.5 8.3 %copy-start.7 = (bf16[288,96]{1,0:T(8,128)(2,1)S(1)}, bf16[288,96]{1,0:T(8,128)(2,1)}, u32[]{:S(2)}) copy-start(bf16[288,96]{1,0:T(8,128)(2,1)} %param.6) | copy-start | bytes 165892
  44.6 15.2 %all-to-all-start.1 = ((bf16[4,24,1536]{2,1,0:T(8,128)(2,1)}), bf16[4,24,1536]{2,1,0:T(8,128)(2,1)S(1)}, u32[]{:S(2)}, u32[]{:S(2)}) async-start(bf16[4,24,1536]{2,1,0:T(8,128)(2,1)} %broadcast_select_fusion), calls=%async_computation.1 | async-start | bytes 589824 | tf_op jit(solution)/shard_map/all_to_all | solution.py:34
  51.8 56.6 %all-gather.5.cloned.1.call-start = ((), (), s32[]{:S(2)}) async-start(), calls=%async_computation.13 | async-start | bytes 1351680 | tf_op jit(solution)/shard_map/all_gather | solution.py:81
  51.8 8.1 %copy-start.4 = (bf16[8,36,96]{2,1,0:T(8,128)(2,1)}, bf16[8,36,96]{2,1,0:T(8,128)(2,1)S(1)}, u32[]{:S(2)}) copy-start(bf16[8,36,96]{2,1,0:T(8,128)(2,1)S(1)} %reshape.184) | copy-start | bytes 165892
  60.7 6.2 %copy-start.2 = (bf16[88,1536]{1,0:T(8,128)(2,1)S(1)}, bf16[88,1536]{1,0:T(8,128)(2,1)}, u32[]{:S(2)}) copy-start(bf16[88,1536]{1,0:T(8,128)(2,1)} %fusion.13) | copy-start | bytes 811012
  60.7 23.9 %all-to-all-start.2 = ((bf16[8,40,1536]{2,1,0:T(8,128)(2,1)}), bf16[8,40,1536]{2,1,0:T(8,128)(2,1)S(1)}, u32[]{:S(2)}, u32[]{:S(2)}) async-start(bf16[8,40,1536]{2,1,0:T(8,128)(2,1)} %bitcast.7), calls=%async_computation.2 | async-start | bytes 1966080 | tf_op jit(solution)/shard_map/all_to_all | solution.py:34
  66.9 53.8 %all-gather.7.cloned.1.call-start = ((), (), s32[]{:S(2)}) async-start(), calls=%async_computation.14 | async-start | bytes 1351680 | tf_op jit(solution)/shard_map/all_gather | solution.py:86
  66.9 17.1 %collective-permute-start.1 = (bf16[88,1536]{1,0:T(8,128)(2,1)S(1)}, bf16[88,1536]{1,0:T(8,128)(2,1)S(1)}, u32[]{:S(2)}, u32[]{:S(2)}) collective-permute-start(bf16[88,1536]{1,0:T(8,128)(2,1)S(1)} %copy-done.2), channel_id=1, source_target_pairs={{0,450},{1,451},{4,454},{5,455},{8,458},{9,459},{12,462},{13,463},... | collective-permute-start | bytes 811016 | tf_op jit(solution)/shard_map/ppermute | solution.py:82
  83.9 0.7 copy-start.6
  84.8 17.5 %collective-permute-start = (bf16[40,1536]{1,0:T(8,128)(2,1)S(1)}, bf16[40,1536]{1,0:T(8,128)(2,1)S(1)}, u32[]{:S(2)}, u32[]{:S(2)}) collective-permute-start(bf16[40,1536]{1,0:T(8,128)(2,1)S(1)} %reduce_sum.70), channel_id=1, source_target_pairs={{0,2},{1,3},{2,0},{3,1},{4,6},{5,7},{6,4},{7,5},{8,10},{9,11},{10,... | collective-permute-start | bytes 368648 | tf_op jit(solution)/shard_map/ppermute | solution.py:87
  103.6 19.4 %all-to-all-start.3 = ((bf16[8,40,1536]{2,1,0:T(8,128)(2,1)}), bf16[8,40,1536]{2,1,0:T(8,128)(2,1)}, u32[]{:S(2)}, u32[]{:S(2)}) async-start(bf16[8,40,1536]{2,1,0:T(8,128)(2,1)} %broadcast_in_dim.67), calls=%async_computation.3 | async-start | bytes 1966080 | tf_op jit(solution)/shard_map/all_to_all | solution.py:34
  108.4 59.4 %reduce-scatter.3.cloned.1.call-start = ((), (), s32[]{:S(2)}) async-start(), calls=%async_computation.11 | async-start | bytes 2211840 | tf_op jit(solution)/shard_map/reduce_scatter | solution.py:107
  130.7 1.2 copy-start.3
  152.1 15.3 %collective-permute-start.2 = (bf16[40,1536]{1,0:T(8,128)(2,1)S(1)}, bf16[40,1536]{1,0:T(8,128)(2,1)S(1)}, u32[]{:S(2)}, u32[]{:S(2)}) collective-permute-start(bf16[40,1536]{1,0:T(8,128)(2,1)S(1)} %reduce_sum.72), channel_id=1, source_target_pairs={{0,2},{1,3},{2,0},{3,1},{4,6},{5,7},{6,4},{7,5},{8,10},{9,11},{10,... | collective-permute-start | bytes 368648 | tf_op jit(solution)/shard_map/ppermute | solution.py:110
  169.3 18.9 %copy-start.1 = (f32[8,18,1536]{2,1,0:T(8,128)}, f32[8,18,1536]{2,1,0:T(8,128)S(1)}, u32[]{:S(2)}) copy-start(f32[8,18,1536]{2,1,0:T(8,128)S(1)} %slice_dynamic-update-slice_fusion.1) | copy-start | bytes 2654212
  169.4 18.8 %copy-start.5 = (bf16[8,36,96]{2,1,0:T(8,128)(2,1)S(1)}, bf16[8,36,96]{2,1,0:T(8,128)(2,1)}, u32[]{:S(2)}) copy-start(bf16[8,36,96]{2,1,0:T(8,128)(2,1)} %copy-done.4) | copy-start | bytes 165892
  189.4 22.4 %all-to-all-start.6 = ((bf16[16,24,384]{2,1,0:T(8,128)(2,1)}), bf16[16,24,384]{2,1,0:T(8,128)(2,1)S(1)}, u32[]{:S(2)}, u32[]{:S(2)}) async-start(bf16[16,24,384]{2,1,0:T(8,128)(2,1)} %bitcast.25), calls=%async_computation.7 | async-start | bytes 589824 | tf_op jit(solution)/shard_map/all_to_all | solution.py:34
  201.3 49.3 %reduce-scatter.5.cloned.1.call-start = ((), (), s32[]{:S(2)}) async-start(), calls=%async_computation.12 | async-start | bytes 1327104 | tf_op jit(solution)/shard_map/reduce_scatter | solution.py:117
  211.9 9.7 %collective-permute-start.3 = (bf16[24,384]{1,0:T(8,128)(2,1)S(1)}, bf16[24,384]{1,0:T(8,128)(2,1)S(1)}, u32[]{:S(2)}, u32[]{:S(2)}) collective-permute-start(bf16[24,384]{1,0:T(8,128)(2,1)S(1)} %reduce-precision_convert_fusion), channel_id=1, source_target_pairs={{0,256},{16,272},{32,288},{48,304},{64,320},{80,336},{96,352},{112... | collective-permute-start | bytes 55304 | tf_op jit(solution)/shard_map/ppermute | solution.py:124
  284.8 18.1 %all-to-all-start.7 = ((bf16[16,24,384]{2,1,0:T(8,128)(2,1)}), bf16[16,24,384]{2,1,0:T(8,128)(2,1)S(1)}, u32[]{:S(2)}, u32[]{:S(2)}) async-start(bf16[16,24,384]{2,1,0:T(8,128)(2,1)} %broadcast_in_dim.69), calls=%async_computation.9 | async-start | bytes 589824 | tf_op jit(solution)/shard_map/all_to_all | solution.py:34
Sparse Core Ops, SparseCore 0:
  60.8 25.2 all-gather.4
  88.2 32.3 all-gather.6
  130.8 36.2 reduce-scatter.2
  204.9 45.6 reduce-scatter.4

commit v8 on v7

--- a/solution.py
+++ b/solution.py
@@ -25,9 +25,10 @@
 
 COLUMNS = [(y, x, c) for y in range(Y) for x in range(X) for c in range(CORE)]
 MIRROR = [(place(z, *at), place(mirror(z), *at)) for z in range(16) for at in COLUMNS]
-FOLD = (0, 2, 4, 6, 7, 5, 3, 1)
-LINE = [[place(z0 + p, *at) for p in FOLD] for z0 in (14, 6) for at in COLUMNS]
-LINE_ZL = [(6 + p) % ZL for p in FOLD]
+ORDER = (2, 3, 1, 0)
+FOUR = [
+    [place(z0 + (q * 4 + i - 6) % ZL, *at) for i in ORDER] for z0 in (14, 6) for q in range(2) for at in COLUMNS
+]
 
 
 def swap(value, axis, groups=None):
@@ -83,6 +84,7 @@
     half = swap(term.reshape(plane, held, embed_width), "fsdp", PLANE)
     half = jnp.sum(half.astype(F32), axis=0).astype(BF16)
 
+    _, crossed = lax.optimization_barrier((half, crossed))
     far = lax.all_gather(crossed, "dp", axis_index_groups=RING)
     embed = half.astype(F32) + lax.ppermute(half, "fsdp", PAIR).astype(F32)
     image_scale = lax.rsqrt(jnp.sum(embed * embed, axis=1, keepdims=True) + 1e-06)
@@ -110,12 +112,13 @@
     unit_grad = back.astype(F32) + lax.ppermute(back, "fsdp", PAIR).astype(F32)
     image_dot = jnp.sum(image_unit * unit_grad, axis=1, keepdims=True)
     embed_grad = (image_scale * (unit_grad - image_unit * image_dot)).astype(BF16)
-    text_acc = text_acc.reshape(2, 4, share, embed_width)
-    text_acc = jnp.where(zl < 4, text_acc, text_acc[::-1]).reshape(ZL, share, embed_width).astype(F32)
-    text_acc = jnp.stack([text_acc[at] for at in LINE_ZL])
+    text_acc = text_acc.reshape(2, count, embed_width)
     embed_grad, text_acc = lax.optimization_barrier((embed_grad, text_acc))
-    text_acc = lax.psum_scatter(text_acc, ("dp", "fsdp"), axis_index_groups=LINE)
+    crossed = lax.ppermute(text_acc[1], ("dp", "fsdp"), MIRROR)
     grads = spread(embed_grad, "fsdp", PLANE, plane).reshape(plane * held, embed_width)
+    text_acc = (text_acc[0].astype(F32) + crossed.astype(F32)).astype(BF16).reshape(4, share, embed_width)
+    text_acc = jnp.stack([text_acc[i] for i in ORDER])
+    text_acc = lax.psum_scatter(text_acc, ("dp", "fsdp"), axis_index_groups=FOUR)
     head_part = jnp.einsum("rw,re->we", feats, grads, preferred_element_type=F32).astype(BF16)
     head_part = head_part.reshape(Y, width // Y, 4, embed_width // 4).transpose(0, 2, 1, 3)
     head_part = head_part.reshape(4 * Y, width // Y, embed_width // 4)
@@ -129,6 +132,7 @@
     feature_grad = jnp.einsum("re,we->rw", grads, image_head, preferred_element_type=F32).astype(BF16)
     feature_grad = feature_grad.reshape(plane, held, width)[:, :own].reshape(rows, width)
 
+    text_acc = text_acc.astype(F32)
     text_dot = jnp.sum(text_unit * text_acc, axis=1, keepdims=True)
     text_rows = (text_scale * (text_acc - text_unit * text_dot)).astype(BF16)
     text_rows = text_rows.reshape(share, group, width).transpose(1, 0, 2)

time: 312 us -> 293 us (0.939)
  blocking collectives: 70.2 us -> 50.9 us
  waiting for transfers between devices: 109 us -> 93.4 us
  starting transfers between devices: 84.1 us -> 98.6 us
    all_to_all x3 -> x2, blocking collectives: 70.2 us -> 50.9 us  [swap(): lax.all_to_all(value, axis, 0, 0, axis_index_groups=groups, tiled=True)]
    reduce_scatter x1, waiting for transfers between devices: 28.9 us -> 10.3 us  [on_device(): lax.psum_scatter(text_acc, ('dp', 'fsdp'), axis_index_groups=FOUR)]
    all_to_all x6 -> x7, waiting for transfers between devices: 39.1 us -> 53.8 us  [swap(): lax.all_to_all(value, axis, 0, 0, axis_index_groups=groups, tiled=True)]
    ppermute x1, waiting for transfers between devices: 15.1 us -> 0.59 us  [on_device(): crossed = lax.ppermute(quad, ('dp', 'fsdp'), MIRROR)]
    ppermute x0 -> x1, starting transfers between devices: none -> 11.9 us  [on_device(): crossed = lax.ppermute(text_acc[1], ('dp', 'fsdp'), MIRROR)]
    all_to_all x6 -> x7, starting transfers between devices: 56.5 us -> 61.7 us  [swap(): lax.all_to_all(value, axis, 0, 0, axis_index_groups=groups, tiled=True)]
    all_gather x1, waiting for transfers between devices: 10.3 us -> 15.2 us  [on_device(): far = lax.all_gather(crossed, 'dp', axis_index_groups=RING)]
  transfers between devices with their start and end apart: 14 -> 16, of which waited for: 10 -> 12; matrix products, arithmetic and copies ran while one was open for 4% -> 5% of each run, Pallas kernels for 0% -> 0%
where the time goes in v8:
time: 293 us; the launch traced here: 290 us
  starting transfers between devices  98.6 us (34%)
  waiting for transfers between devices  93.4 us (32%)
  blocking collectives  50.9 us (17%)
  local copies, waits for them, and re-layouts  15.5 us (5%)
  between operations  15.5 us (5%)
  matrix products  9.91 us (3%)
  other arithmetic  6.27 us (2%)
    all_to_all x7, starting transfers between devices, swap(): lax.all_to_all(value, axis, 0, 0, axis_index_groups=groups, tiled=True)  61.7 us
    all_to_all x7, waiting for transfers between devices, swap(): lax.all_to_all(value, axis, 0, 0, axis_index_groups=groups, tiled=True)  53.8 us
    all_to_all x2, blocking collectives, swap(): lax.all_to_all(value, axis, 0, 0, axis_index_groups=groups, tiled=True)  50.9 us
    all_gather x1, waiting for transfers between devices, on_device(): far = lax.all_gather(crossed, 'dp', axis_index_groups=RING)  15.2 us
    ppermute x1, starting transfers between devices, on_device(): unit_grad = back.astype(F32) + lax.ppermute(back, 'fsdp', PAIR).astype(F32)  12.5 us
    ppermute x1, starting transfers between devices, on_device(): crossed = lax.ppermute(text_acc[1], ('dp', 'fsdp'), MIRROR)  11.9 us
    reduce_scatter x1, waiting for transfers between devices, on_device(): lax.psum_scatter(text_acc, ('dp', 'fsdp'), axis_index_groups=FOUR)  10.3 us
    ppermute x1, waiting for transfers between devices, on_device(): embed = half.astype(F32) + lax.ppermute(half, 'fsdp', PAIR).astype(F32)  9.83 us
  transfers between devices with their start and end apart: 16, of which 12 were waited for; matrix products, arithmetic and copies ran while one was open for 5% of the time, Pallas kernels for 0%

profile of v8, /device:TPU:1, one launch (start us, length us, event | category | flops | bytes accessed | tf_op | source)
XLA Modules:
  0.0 290.2 jit_solution(14542463456998772230)
XLA Ops:
  7.2 1.0 broadcast_in_dim.60
  8.1 0.7 broadcast_in_dim.61
  8.8 19.1 %all-to-all-start = ((bf16[16,36,96]{2,1,0:T(8,128)(2,1)}), bf16[16,36,96]{2,1,0:T(8,128)(2,1)S(1)}, u32[]{:S(2)}, u32[]{:S(2)}) async-start(bf16[16,36,96]{2,1,0:T(8,128)(2,1)} %bitcast.1), calls=%async_computation | async-start | bytes 327680 | tf_op jit(solution)/shard_map/all_to_all | solution.py:35
  27.9 0.8 dynamic_slice.3
  28.9 14.2 %all-to-all-done = bf16[16,36,96]{2,1,0:T(8,128)(2,1)S(1)} async-done(((bf16[16,36,96]{2,1,0:T(8,128)(2,1)}), bf16[16,36,96]{2,1,0:T(8,128)(2,1)S(1)}, u32[]{:S(2)}, u32[]{:S(2)}) %all-to-all-start) | async-done | bytes 110624 | tf_op jit(solution)/shard_map/all_to_all | solution.py:35
  43.8 0.8 broadcast_select_fusion
  44.6 7.2 %all-to-all-start.1 = ((bf16[4,24,1536]{2,1,0:T(8,128)(2,1)}), bf16[4,24,1536]{2,1,0:T(8,128)(2,1)S(1)}, u32[]{:S(2)}, u32[]{:S(2)}) async-start(bf16[4,24,1536]{2,1,0:T(8,128)(2,1)} %broadcast_select_fusion), calls=%async_computation.1 | async-start | bytes 589824 | tf_op jit(solution)/shard_map/all_to_all | solution.py:35
  51.9 1.4 convolution_convert_fusion.2
  53.2 6.6 %all-to-all-done.1 = bf16[4,24,1536]{2,1,0:T(8,128)(2,1)S(1)} async-done(((bf16[4,24,1536]{2,1,0:T(8,128)(2,1)}), bf16[4,24,1536]{2,1,0:T(8,128)(2,1)S(1)}, u32[]{:S(2)}, u32[]{:S(2)}) %all-to-all-start.1) | async-done | bytes 294944 | tf_op jit(solution)/shard_map/all_to_all | solution.py:35
  59.9 0.7 fusion.14
  60.7 6.1 %all-to-all-start.2 = ((bf16[8,40,1536]{2,1,0:T(8,128)(2,1)}), bf16[8,40,1536]{2,1,0:T(8,128)(2,1)S(1)}, u32[]{:S(2)}, u32[]{:S(2)}) async-start(bf16[8,40,1536]{2,1,0:T(8,128)(2,1)} %bitcast.7), calls=%async_computation.2 | async-start | bytes 1966080 | tf_op jit(solution)/shard_map/all_to_all | solution.py:35
  66.9 1.9 collective-permute-start.1
  68.8 12.5 %all-to-all-done.2 = bf16[8,40,1536]{2,1,0:T(8,128)(2,1)S(1)} async-done(((bf16[8,40,1536]{2,1,0:T(8,128)(2,1)}), bf16[8,40,1536]{2,1,0:T(8,128)(2,1)S(1)}, u32[]{:S(2)}, u32[]{:S(2)}) %all-to-all-start.2) | async-done | bytes 983072 | tf_op jit(solution)/shard_map/all_to_all | solution.py:35
  81.4 1.9 collective-permute-start
  83.9 0.7 copy-done.6
  86.1 9.8 %collective-permute-done = bf16[40,1536]{1,0:T(8,128)(2,1)S(1)} collective-permute-done((bf16[40,1536]{1,0:T(8,128)(2,1)S(1)}, bf16[40,1536]{1,0:T(8,128)(2,1)S(1)}, u32[]{:S(2)}, u32[]{:S(2)}) %collective-permute-start) | collective-permute-done | bytes 122912 | tf_op jit(solution)/shard_map/ppermute | solution.py:89
  96.2 1.1 broadcast_in_dim.67
  97.2 6.2 %all-to-all-start.3 = ((bf16[8,40,1536]{2,1,0:T(8,128)(2,1)}), bf16[8,40,1536]{2,1,0:T(8,128)(2,1)}, u32[]{:S(2)}, u32[]{:S(2)}) async-start(bf16[8,40,1536]{2,1,0:T(8,128)(2,1)} %broadcast_in_dim.67), calls=%async_computation.3 | async-start | bytes 1966080 | tf_op jit(solution)/shard_map/all_to_all | solution.py:35
  103.4 0.7 slice_bitcast_fusion.8
  104.2 1.2 slice_bitcast_fusion.1
  105.4 15.2 %all-gather.7.cloned.1.call-done = bf16[352,1536]{1,0:T(8,128)(2,1)} async-done(((bf16[88,1536]{1,0:T(8,128)(2,1)}), bf16[352,1536]{1,0:T(8,128)(2,1)}) %all-gather.7.cloned.1.call-update) | async-done | bytes 1081360 | tf_op jit(solution)/shard_map/all_gather | solution.py:88
  120.6 0.7 slice_bitcast_fusion.7
  121.5 1.2 slice_bitcast_fusion
  123.0 2.3 fusion.9
  125.3 1.9 convolution_convert_fusion.1
  127.2 3.5 %convolution_convert_fusion = bf16[576,1536]{1,0:T(8,128)(2,1)} fusion(bf16[320,576]{1,0:T(8,128)(2,1)S(1)} %fusion.9, bf16[320,1536]{1,0:T(8,128)(2,1)} %bitcast.12), kind=kOutput, calls=%fused_computation | convolution fusion | flops 567115776 | bytes 3121152 | tf_op jit(solution)/shard_map/ij,ie->je/dot_general | solution.py:107
  130.7 1.2 copy-done.2
  131.9 20.1 %all_to_all.45 = bf16[8,40,1536]{2,1,0:T(8,128)(2,1)S(1)} all-to-all(bf16[8,40,1536]{2,1,0:T(8,128)(2,1)S(1)} %bitcast.87), channel_id=1, replica_groups={{0,1,4,5,8,9,12,13},{2,3,6,7,10,11,14,15},{16,17,20,21,24,25,28,29},{18..., dimensions={0} | all-to-all | bytes 1966080 | tf_op jit(solution)/shard_map/all_to_all | solution.py:35
  152.1 12.5 %collective-permute-start.2 = (bf16[40,1536]{1,0:T(8,128)(2,1)S(1)}, bf16[40,1536]{1,0:T(8,128)(2,1)S(1)}, u32[]{:S(2)}, u32[]{:S(2)}) collective-permute-start(bf16[40,1536]{1,0:T(8,128)(2,1)S(1)} %reduce_sum.72), channel_id=1, source_target_pairs={{0,2},{1,3},{2,0},{3,1},{4,6},{5,7},{6,4},{7,5},{8,10},{9,11},{10,... | collective-permute-start | bytes 368648 | tf_op jit(solution)/shard_map/ppermute | solution.py:112
  164.8 2.6 collective-permute-done.2
  167.8 1.0 broadcast_in_dim.68
  168.8 5.3 %all-to-all-start.5 = ((bf16[8,40,1536]{2,1,0:T(8,128)(2,1)}), bf16[8,40,1536]{2,1,0:T(8,128)(2,1)S(1)}, u32[]{:S(2)}, u32[]{:S(2)}) async-start(bf16[8,40,1536]{2,1,0:T(8,128)(2,1)} %broadcast_in_dim.68), calls=%async_computation.6 | async-start | bytes 1966080 | tf_op jit(solution)/shard_map/all_to_all | solution.py:35
  174.2 11.9 %collective-permute-start.4 = (bf16[72,1536]{1,0:T(8,128)(2,1)S(1)}, bf16[72,1536]{1,0:T(8,128)(2,1)S(1)}, u32[]{:S(2)}, u32[]{:S(2)}) collective-permute-start(bf16[72,1536]{1,0:T(8,128)(2,1)S(1)} %slice_bitcast_fusion.2), channel_id=1, source_target_pairs={{0,450},{1,451},{4,454},{5,455},{8,458},{9,459},{12,462},{13,463},... | collective-permute-start | bytes 663560 | tf_op jit(solution)/shard_map/ppermute | solution.py:117
  186.1 2.4 all-to-all-done.5
  189.0 0.7 copy.47
  189.7 11.8 %all-to-all-start.6 = ((bf16[16,24,384]{2,1,0:T(8,128)(2,1)}), bf16[16,24,384]{2,1,0:T(8,128)(2,1)S(1)}, u32[]{:S(2)}, u32[]{:S(2)}) async-start(bf16[16,24,384]{2,1,0:T(8,128)(2,1)} %bitcast.24), calls=%async_computation.7 | async-start | bytes 589824 | tf_op jit(solution)/shard_map/all_to_all | solution.py:35
  201.7 0.7 pad_maximum_fusion.1
  202.5 9.6 %all-to-all-done.6 = bf16[16,24,384]{2,1,0:T(8,128)(2,1)S(1)} async-done(((bf16[16,24,384]{2,1,0:T(8,128)(2,1)}), bf16[16,24,384]{2,1,0:T(8,128)(2,1)S(1)}, u32[]{:S(2)}, u32[]{:S(2)}) %all-to-all-start.6) | async-done | bytes 294944 | tf_op jit(solution)/shard_map/all_to_all | solution.py:35
  212.1 8.6 %collective-permute-start.3 = (bf16[24,384]{1,0:T(8,128)(2,1)S(1)}, bf16[24,384]{1,0:T(8,128)(2,1)S(1)}, u32[]{:S(2)}, u32[]{:S(2)}) collective-permute-start(bf16[24,384]{1,0:T(8,128)(2,1)S(1)} %reduce-precision_convert_fusion), channel_id=1, source_target_pairs={{0,256},{16,272},{32,288},{48,304},{64,320},{80,336},{96,352},{112... | collective-permute-start | bytes 55304 | tf_op jit(solution)/shard_map/ppermute | solution.py:127
  220.8 1.1 collective-permute-done.3
  221.8 10.3 %reduce-scatter.5.cloned.1.call-done = bf16[1,18,1536]{2,1,0:T(8,128)(2,1)} async-done(((bf16[4,18,1536]{2,1,0:T(8,128)(2,1)}), bf16[1,18,1536]{2,1,0:T(8,128)(2,1)}) %reduce-scatter.5.cloned.1.call-update) | async-done | bytes 55312 | tf_op jit(solution)/shard_map/reduce_scatter | solution.py:121
  232.1 1.0 fusion.17
  233.2 1.0 fusion.19
  234.3 30.9 %all_to_all.46 = bf16[16,18,96]{2,1,0:T(8,128)(2,1)S(1)} all-to-all(bf16[16,18,96]{2,1,0:T(8,128)(2,1)S(1)} %copy.50), channel_id=1, replica_groups=mesh['dp'=32,'fsdp'=16] {'fsdp'}, dimensions={0} | all-to-all | bytes 110592 | tf_op jit(solution)/shard_map/all_to_all | solution.py:35
  265.2 0.7 broadcast_in_dim.69
  265.9 6.1 %all-to-all-start.7 = ((bf16[16,24,384]{2,1,0:T(8,128)(2,1)}), bf16[16,24,384]{2,1,0:T(8,128)(2,1)S(1)}, u32[]{:S(2)}, u32[]{:S(2)}) async-start(bf16[16,24,384]{2,1,0:T(8,128)(2,1)} %broadcast_in_dim.69), calls=%async_computation.9 | async-start | bytes 589824 | tf_op jit(solution)/shard_map/all_to_all | solution.py:35
  274.0 8.5 %all-to-all-done.7 = bf16[16,24,384]{2,1,0:T(8,128)(2,1)S(1)} async-done(((bf16[16,24,384]{2,1,0:T(8,128)(2,1)}), bf16[16,24,384]{2,1,0:T(8,128)(2,1)S(1)}, u32[]{:S(2)}, u32[]{:S(2)}) %all-to-all-start.7) | async-done | bytes 294944 | tf_op jit(solution)/shard_map/all_to_all | solution.py:35
  282.8 0.9 copy.54
  (84 shorter events, 6.4 us)
Async XLA Ops:
  7.2 44.7 %copy-start = (bf16[96,1536]{1,0:T(8,128)(2,1)S(1)}, bf16[96,1536]{1,0:T(8,128)(2,1)}, u32[]{:S(2)}) copy-start(bf16[96,1536]{1,0:T(8,128)(2,1)} %param.7) | copy-start | bytes 884740
  8.8 34.3 %all-to-all-start = ((bf16[16,36,96]{2,1,0:T(8,128)(2,1)}), bf16[16,36,96]{2,1,0:T(8,128)(2,1)S(1)}, u32[]{:S(2)}, u32[]{:S(2)}) async-start(bf16[16,36,96]{2,1,0:T(8,128)(2,1)} %bitcast.1), calls=%async_computation | async-start | bytes 327680 | tf_op jit(solution)/shard_map/all_to_all | solution.py:35
  43.3 8.5 %copy-start.7 = (bf16[288,96]{1,0:T(8,128)(2,1)S(1)}, bf16[288,96]{1,0:T(8,128)(2,1)}, u32[]{:S(2)}) copy-start(bf16[288,96]{1,0:T(8,128)(2,1)} %param.6) | copy-start | bytes 165892
  44.6 15.2 %all-to-all-start.1 = ((bf16[4,24,1536]{2,1,0:T(8,128)(2,1)}), bf16[4,24,1536]{2,1,0:T(8,128)(2,1)S(1)}, u32[]{:S(2)}, u32[]{:S(2)}) async-start(bf16[4,24,1536]{2,1,0:T(8,128)(2,1)} %broadcast_select_fusion), calls=%async_computation.1 | async-start | bytes 589824 | tf_op jit(solution)/shard_map/all_to_all | solution.py:35
  51.8 51.7 %all-gather.5.cloned.1.call-start = ((), (), s32[]{:S(2)}) async-start(), calls=%async_computation.13 | async-start | bytes 1351680 | tf_op jit(solution)/shard_map/all_gather | solution.py:82
  51.8 8.1 %copy-start.3 = (bf16[8,36,96]{2,1,0:T(8,128)(2,1)}, bf16[8,36,96]{2,1,0:T(8,128)(2,1)S(1)}, u32[]{:S(2)}) copy-start(bf16[8,36,96]{2,1,0:T(8,128)(2,1)S(1)} %reshape.188) | copy-start | bytes 165892
  60.7 6.2 %copy-start.1 = (bf16[88,1536]{1,0:T(8,128)(2,1)S(1)}, bf16[88,1536]{1,0:T(8,128)(2,1)}, u32[]{:S(2)}) copy-start(bf16[88,1536]{1,0:T(8,128)(2,1)} %fusion.14) | copy-start | bytes 811012
  60.7 20.6 %all-to-all-start.2 = ((bf16[8,40,1536]{2,1,0:T(8,128)(2,1)}), bf16[8,40,1536]{2,1,0:T(8,128)(2,1)S(1)}, u32[]{:S(2)}, u32[]{:S(2)}) async-start(bf16[8,40,1536]{2,1,0:T(8,128)(2,1)} %bitcast.7), calls=%async_computation.2 | async-start | bytes 1966080 | tf_op jit(solution)/shard_map/all_to_all | solution.py:35
  66.8 53.8 %all-gather.7.cloned.1.call-start = ((), (), s32[]{:S(2)}) async-start(), calls=%async_computation.14 | async-start | bytes 1351680 | tf_op jit(solution)/shard_map/all_gather | solution.py:88
  66.9 17.1 %collective-permute-start.1 = (bf16[88,1536]{1,0:T(8,128)(2,1)S(1)}, bf16[88,1536]{1,0:T(8,128)(2,1)S(1)}, u32[]{:S(2)}, u32[]{:S(2)}) collective-permute-start(bf16[88,1536]{1,0:T(8,128)(2,1)S(1)} %copy-done.1), channel_id=1, source_target_pairs={{0,450},{1,451},{4,454},{5,455},{8,458},{9,459},{12,462},{13,463},... | collective-permute-start | bytes 811016 | tf_op jit(solution)/shard_map/ppermute | solution.py:83
  81.4 14.5 %collective-permute-start = (bf16[40,1536]{1,0:T(8,128)(2,1)S(1)}, bf16[40,1536]{1,0:T(8,128)(2,1)S(1)}, u32[]{:S(2)}, u32[]{:S(2)}) collective-permute-start(bf16[40,1536]{1,0:T(8,128)(2,1)S(1)} %reduce_sum.70), channel_id=1, source_target_pairs={{0,2},{1,3},{2,0},{3,1},{4,6},{5,7},{6,4},{7,5},{8,10},{9,11},{10,... | collective-permute-start | bytes 368648 | tf_op jit(solution)/shard_map/ppermute | solution.py:89
  83.9 0.7 copy-start.6
  97.2 25.7 %all-to-all-start.3 = ((bf16[8,40,1536]{2,1,0:T(8,128)(2,1)}), bf16[8,40,1536]{2,1,0:T(8,128)(2,1)}, u32[]{:S(2)}, u32[]{:S(2)}) async-start(bf16[8,40,1536]{2,1,0:T(8,128)(2,1)} %broadcast_in_dim.67), calls=%async_computation.3 | async-start | bytes 1966080 | tf_op jit(solution)/shard_map/all_to_all | solution.py:35
  103.4 64.3 %reduce-scatter.3.cloned.1.call-start = ((), (), s32[]{:S(2)}) async-start(), calls=%async_computation.11 | async-start | bytes 2211840 | tf_op jit(solution)/shard_map/reduce_scatter | solution.py:109
  130.7 1.2 copy-start.2
  152.1 15.3 %collective-permute-start.2 = (bf16[40,1536]{1,0:T(8,128)(2,1)S(1)}, bf16[40,1536]{1,0:T(8,128)(2,1)S(1)}, u32[]{:S(2)}, u32[]{:S(2)}) collective-permute-start(bf16[40,1536]{1,0:T(8,128)(2,1)S(1)} %reduce_sum.72), channel_id=1, source_target_pairs={{0,2},{1,3},{2,0},{3,1},{4,6},{5,7},{6,4},{7,5},{8,10},{9,11},{10,... | collective-permute-start | bytes 368648 | tf_op jit(solution)/shard_map/ppermute | solution.py:112
  167.7 6.4 %copy-start.5 = (bf16[1,144,1536]{2,1,0:T(8,128)(2,1)S(1)}, bf16[1,144,1536]{2,1,0:T(8,128)(2,1)}, u32[]{:S(2)}) copy-start(bf16[1,144,1536]{2,1,0:T(8,128)(2,1)} %reduce-scatter.3.cloned.1.call-done) | copy-start | bytes 1327108
  167.7 20.8 %copy-start.4 = (bf16[8,36,96]{2,1,0:T(8,128)(2,1)S(1)}, bf16[8,36,96]{2,1,0:T(8,128)(2,1)}, u32[]{:S(2)}) copy-start(bf16[8,36,96]{2,1,0:T(8,128)(2,1)} %copy-done.3) | copy-start | bytes 165892
  168.8 19.7 %all-to-all-start.5 = ((bf16[8,40,1536]{2,1,0:T(8,128)(2,1)}), bf16[8,40,1536]{2,1,0:T(8,128)(2,1)S(1)}, u32[]{:S(2)}, u32[]{:S(2)}) async-start(bf16[8,40,1536]{2,1,0:T(8,128)(2,1)} %broadcast_in_dim.68), calls=%async_computation.6 | async-start | bytes 1966080 | tf_op jit(solution)/shard_map/all_to_all | solution.py:35
  174.2 27.3 %collective-permute-start.4 = (bf16[72,1536]{1,0:T(8,128)(2,1)S(1)}, bf16[72,1536]{1,0:T(8,128)(2,1)S(1)}, u32[]{:S(2)}, u32[]{:S(2)}) collective-permute-start(bf16[72,1536]{1,0:T(8,128)(2,1)S(1)} %slice_bitcast_fusion.2), channel_id=1, source_target_pairs={{0,450},{1,451},{4,454},{5,455},{8,458},{9,459},{12,462},{13,463},... | collective-permute-start | bytes 663560 | tf_op jit(solution)/shard_map/ppermute | solution.py:117
  189.7 22.4 %all-to-all-start.6 = ((bf16[16,24,384]{2,1,0:T(8,128)(2,1)}), bf16[16,24,384]{2,1,0:T(8,128)(2,1)S(1)}, u32[]{:S(2)}, u32[]{:S(2)}) async-start(bf16[16,24,384]{2,1,0:T(8,128)(2,1)} %bitcast.24), calls=%async_computation.7 | async-start | bytes 589824 | tf_op jit(solution)/shard_map/all_to_all | solution.py:35
  201.5 30.6 %reduce-scatter.5.cloned.1.call-start = ((), (), s32[]{:S(2)}) async-start(), calls=%async_computation.12 | async-start | bytes 368640 | tf_op jit(solution)/shard_map/reduce_scatter | solution.py:121
  212.1 9.7 %collective-permute-start.3 = (bf16[24,384]{1,0:T(8,128)(2,1)S(1)}, bf16[24,384]{1,0:T(8,128)(2,1)S(1)}, u32[]{:S(2)}, u32[]{:S(2)}) collective-permute-start(bf16[24,384]{1,0:T(8,128)(2,1)S(1)} %reduce-precision_convert_fusion), channel_id=1, source_target_pairs={{0,256},{16,272},{32,288},{48,304},{64,320},{80,336},{96,352},{112... | collective-permute-start | bytes 55304 | tf_op jit(solution)/shard_map/ppermute | solution.py:127
  265.9 16.7 %all-to-all-start.7 = ((bf16[16,24,384]{2,1,0:T(8,128)(2,1)}), bf16[16,24,384]{2,1,0:T(8,128)(2,1)S(1)}, u32[]{:S(2)}, u32[]{:S(2)}) async-start(bf16[16,24,384]{2,1,0:T(8,128)(2,1)} %broadcast_in_dim.69), calls=%async_computation.9 | async-start | bytes 589824 | tf_op jit(solution)/shard_map/all_to_all | solution.py:35
Sparse Core Ops, SparseCore 0:
  60.8 25.2 all-gather.4
  88.2 32.3 all-gather.6
  130.9 36.2 reduce-scatter.2
  205.1 27.0 reduce-scatter.4

commit v9 on v7

v9 whole, which is shorter than its diff:
```python
import jax
import jax.numpy as jnp
from jax import lax
from jax.sharding import PartitionSpec as P

F32, BF16 = jnp.float32, jnp.bfloat16
X, ZH, CORE = 4, 2, 2
ZL, Y = 8, 4
PLANE = [[x * 4 + zh * 2 + c for x in range(X) for c in range(CORE)] for zh in range(ZH)]
RING = [[z * Y + y for y in range(Y)] for z in range(ZL)]
SLAB = [[(q * 4 + i) * Y + y for y in range(Y) for i in range(4)] for q in range(ZL // 4)]
ACROSS = [(i, i ^ (4 * Y)) for i in range(ZL * Y)]


def place(z, y, x, c):
    return ((z % ZL * Y + y) * X + x) * 4 + z % 16 // ZL * 2 + c


def mirror(z):
    edge = z // 4 * 4 if z % 4 < 2 else z // 4 * 4 + 4
    return (2 * edge - 1 - z) % 16


COLUMNS = [(y, x, c) for y in range(Y) for x in range(X) for c in range(CORE)]
MIRROR = [(place(z, *at), place(mirror(z), *at)) for z in range(16) for at in COLUMNS]
UP = [(place(z, *at), place(z + 4, *at)) for z in range(16) for at in COLUMNS]
DOWN = [(place(z, *at), place(z - 4, *at)) for z in range(16) for at in COLUMNS]


def across(by):
    def there(z):
        z0 = 6 if 6 <= z < 14 else 14
        return z0 + (z % ZL ^ by) - 6 if (z % ZL ^ by) >= 6 else z0 + (z % ZL ^ by) + 2

    return [(place(z, *at), place(there(z), *at)) for z in range(16) for at in COLUMNS]


def send(value, pairs):
    return lax.ppermute(value, ("dp", "fsdp"), pairs)


def pick(at, parts):
    return jnp.where(at < 2, jnp.where(at == 0, parts[0], parts[1]), jnp.where(at == 2, parts[2], parts[3]))


def swap(value, axis, groups=None):
    return lax.all_to_all(value, axis, 0, 0, axis_index_groups=groups, tiled=True)


def spread(value, axis, groups, size):
    copies = jnp.broadcast_to(value[None], (size,) + value.shape)
    return swap(copies, axis, groups)


def on_device(image_feats, image_head, text_embed, text_ids, logit_scale, logit_bias):
    rows, width = image_feats.shape
    embed_width = image_head.shape[1]
    cycle = lax.axis_size("dp")
    group = lax.axis_size("fsdp")
    plane = X * CORE
    own = rows // plane
    held = -(-own // 8) * 8
    share = own // ZH
    d = lax.axis_index("dp")
    f = lax.axis_index("fsdp")

    zl, zh = d // Y, f // CORE % ZH
    k = f // 4 * CORE + f % CORE
    z = zh * ZL + zl
    second = (z >= 6) & (z < 14)
    parts = jnp.broadcast_to(text_embed.reshape(X, 1, CORE, own, width), (X, ZH, CORE, own, width))
    text_part = swap(parts.reshape(group, own, width), "fsdp")
    text_vals = text_part.transpose(1, 0, 2).reshape(own, embed_width).astype(F32)
    text_scale = lax.rsqrt(jnp.sum(text_vals * text_vals, axis=1, keepdims=True) + 1e-06)
    text_unit = text_vals * text_scale
    my_ids = lax.dynamic_slice_in_dim(text_ids, k * own, own, 0).reshape(ZH, share)
    marks = jnp.concatenate([my_ids // 128, my_ids % 128], axis=1).astype(BF16)
    piece = -(-share // 8) * 8
    marks = jnp.pad(marks[:, None], ((0, 0), (0, piece - share - 1), (0, embed_width - 2 * share)))
    halves = jnp.concatenate([text_unit.astype(BF16).reshape(ZH, share, embed_width), marks], axis=1)
    text_unit = jnp.where(second, text_unit[share:], text_unit[:share])
    text_scale = jnp.where(second, text_scale[share:], text_scale[:share])

    feats = jnp.pad(image_feats.reshape(plane, own, width), ((0, 0), (0, held - own), (0, 0)))
    feats = feats.reshape(plane * held, width)
    term = jnp.dot(feats, image_head, preferred_element_type=F32).astype(BF16)
    term, halves = lax.optimization_barrier((term, halves))

    parts = [jnp.where(second, halves[1], halves[0])]
    for by in (1, 2, 3):
        there = z ^ by
        part = jnp.where((there >= 6) & (there < 14), halves[1], halves[0])
        parts.append(lax.ppermute(part, "dp", [(i, i ^ (by * Y)) for i in range(cycle)]))
    half = swap(term.reshape(plane, held, embed_width), "fsdp", PLANE)
    half = jnp.sum(half.astype(F32), axis=0).astype(BF16)
    half, *parts = lax.optimization_barrier((half, *parts))
    blocks = jnp.stack([pick(z % 4 ^ i, parts) for i in range(4)])
    count = 4 * share
    quad = jnp.concatenate([blocks[:, :share].reshape(count, embed_width), blocks[:, share]], axis=0)
    quad = jnp.pad(quad, ((0, 12), (0, 0)))

    near = lax.all_gather(quad, "dp", axis_index_groups=RING)
    embed = send(half, UP).astype(F32) + send(half, DOWN).astype(F32)
    crossed = send(quad[: count + 8], MIRROR)
    embed, crossed = lax.optimization_barrier((embed, crossed))

    image_scale = lax.rsqrt(jnp.sum(embed * embed, axis=1, keepdims=True) + 1e-06)
    image_unit = embed * image_scale
    image_low = spread(image_unit.astype(BF16), "fsdp", PLANE, plane).reshape(plane * held, embed_width)
    y = d % Y
    far = [crossed] + [lax.ppermute(crossed, "dp", [(i, i ^ by) for i in range(cycle)]) for by in (1, 2, 3)]
    far = jnp.stack([pick(y ^ i, far) for i in range(Y)])
    lines = (near, far)
    text_low = jnp.stack([part[:, :count] for part in lines], axis=1).reshape(cycle * share, embed_width)
    notes = jnp.stack([part[:, count : count + 4, : 2 * share] for part in lines], axis=1).astype(jnp.int32)
    ids = (notes[..., :share] * 128 + notes[..., share:]).reshape(cycle * share)

    partial_value = jnp.einsum("ie,je->ij", image_low, text_low, preferred_element_type=F32)
    logits = logit_scale * partial_value + logit_bias
    row = lax.broadcasted_iota(jnp.int32, (plane, held), 1)
    row_index = (d ^ (4 * Y)) * rows + lax.broadcasted_iota(jnp.int32, (plane, held), 0) * own + row
    row_index = jnp.where(row < own, row_index, -1).reshape(plane * held, 1)
    sign = jnp.where(row_index == ids[None, :], 1.0, -1.0).astype(F32)
    coef = (-sign * jax.nn.sigmoid(-sign * logits) * logit_scale).astype(BF16)
    unit_part = jnp.einsum("ij,je->ie", coef, text_low, preferred_element_type=F32).astype(BF16)
    unit_part, coef = lax.optimization_barrier((unit_part, coef))
    text_acc = jnp.einsum("ij,ie->je", coef, image_low, preferred_element_type=F32).astype(BF16)

    text_acc = lax.psum_scatter(text_acc.reshape(Y, ZL * share, embed_width), "dp", axis_index_groups=RING)
    back = swap(unit_part.reshape(plane, held, embed_width), "fsdp", PLANE)
    unit_grad = jnp.sum(back.astype(F32), axis=0)
    image_dot = jnp.sum(image_unit * unit_grad, axis=1, keepdims=True)
    embed_grad = (image_scale * (unit_grad - image_unit * image_dot)).astype(BF16)
    embed_grad = (send(embed_grad, UP).astype(F32) + send(embed_grad, DOWN).astype(F32)).astype(BF16)
    text_acc = text_acc.reshape(2, count, embed_width)
    embed_grad, text_acc = lax.optimization_barrier((embed_grad, text_acc))
    crossed = send(text_acc[1], MIRROR)
    grads = spread(embed_grad, "fsdp", PLANE, plane).reshape(plane * held, embed_width)
    grads, crossed = lax.optimization_barrier((grads, crossed))
    text_acc = (text_acc[0].astype(F32) + crossed.astype(F32)).reshape(4, share, embed_width)
    i = z % 4
    parts = [send(pick(i ^ by, text_acc).astype(BF16), across(by)) for by in (1, 2, 3)]
    head_part = jnp.einsum("rw,re->we", feats, grads, preferred_element_type=F32).astype(BF16)
    head_part = head_part.reshape(Y, width // Y, 4, embed_width // 4).transpose(0, 2, 1, 3)
    head_part = head_part.reshape(4 * Y, width // Y, embed_width // 4)
    head_sum = jnp.sum(swap(head_part, "dp", SLAB).astype(F32), axis=0)
    head_sum, *parts = lax.optimization_barrier((head_sum, *parts))
    head_sum = lax.reduce_precision(head_sum, 8, 7)
    head_sum = head_sum + lax.ppermute(head_sum.astype(BF16), "dp", ACROSS).astype(F32)
    text_acc = pick(i, text_acc)
    for part in parts:
        text_acc = text_acc + part.astype(F32)
    text_dot = jnp.sum(text_unit * text_acc, axis=1, keepdims=True)
    text_rows = (text_scale * (text_acc - text_unit * text_dot)).astype(BF16)
    text_rows = text_rows.reshape(share, group, width).transpose(1, 0, 2)
    text_grad = swap(text_rows, "fsdp")
    text_grad, head_sum = lax.optimization_barrier((text_grad, head_sum))
    text_grad = text_grad.reshape(X, ZH, CORE, share, width)
    text_grad = jnp.where(zl < 6, text_grad, text_grad[:, ::-1])
    text_grad = text_grad.transpose(0, 2, 1, 3, 4).reshape(rows, width)

    head_all = spread(head_sum.astype(BF16), "dp", SLAB, 4 * Y).reshape(Y, 4, width // Y, embed_width // 4)
    head_all = head_all.transpose(0, 2, 1, 3).reshape(width, embed_width)
    head_grad = head_all.astype(F32)
    feature_grad = jnp.einsum("re,we->rw", grads, image_head, preferred_element_type=F32).astype(BF16)
    feature_grad = feature_grad.reshape(plane, held, width)[:, :own].reshape(rows, width)
    return (feature_grad, head_grad, text_grad)


def solution(mesh):
    placed = (P("dp", "fsdp"), P("fsdp", None), P("dp", "fsdp"), P("dp"), P(), P())
    return jax.shard_map(
        on_device,
        mesh=mesh,
        in_specs=placed,
        out_specs=(P("dp", "fsdp"), P("fsdp", None), P("dp", "fsdp")),
        check_vma=False,
    )
```

time: 312 us -> 279 us (0.89)
  blocking collectives: 70.2 us -> 17.8 us
  starting transfers between devices: 84.1 us -> 116 us
  waiting for transfers between devices: 109 us -> 98.3 us
    all_to_all x3 -> x1, blocking collectives: 70.2 us -> 17.8 us  [swap(): lax.all_to_all(value, axis, 0, 0, axis_index_groups=groups, tiled=True)]
    ppermute x3 -> x15, starting transfers between devices: 19 us -> 53.9 us  [the longest x9 32.1 us: send(): return lax.ppermute(value, ('dp', 'fsdp'), pairs)]
    reduce_scatter x1 -> x0, waiting for transfers between devices: 28.9 us -> none  [on_device(): lax.psum_scatter(text_acc, ('dp', 'fsdp'), axis_index_groups=LINE)]
    ppermute x3 -> x15, waiting for transfers between devices: 29.3 us -> 46.8 us  [the longest x9 44.1 us: send(): return lax.ppermute(value, ('dp', 'fsdp'), pairs)]
    all_to_all x6 -> x7, waiting for transfers between devices: 39.1 us -> 51.4 us  [swap(): lax.all_to_all(value, axis, 0, 0, axis_index_groups=groups, tiled=True)]
    all_gather x1 -> x0, waiting for transfers between devices: 10.3 us -> none  [on_device(): far = lax.all_gather(crossed, 'dp', axis_index_groups=RING)]
    ppermute x1, starting transfers between devices: 8.55 us -> 4.01 us  [on_device(): lax.ppermute(head_sum.astype(BF16), 'dp', ACROSS).astype(F32)]
    all_to_all x6 -> x7, starting transfers between devices: 56.5 us -> 58 us  [swap(): lax.all_to_all(value, axis, 0, 0, axis_index_groups=groups, tiled=True)]
  transfers between devices with their start and end apart: 14 -> 25, of which waited for: 10 -> 15; matrix products, arithmetic and copies ran while one was open for 4% -> 5% of each run, Pallas kernels for 0% -> 0%
where the time goes in v9:
time: 279 us; the launch traced here: 277 us
  starting transfers between devices  116 us (42%)
  waiting for transfers between devices  98.3 us (35%)
  blocking collectives  17.8 us (6%)
  between operations  15.9 us (6%)
  local copies, waits for them, and re-layouts  15.8 us (6%)
  matrix products  9.87 us (4%)
  other arithmetic  3.48 us (1%)
    all_to_all x7, starting transfers between devices, swap(): lax.all_to_all(value, axis, 0, 0, axis_index_groups=groups, tiled=True)  58 us
    all_to_all x7, waiting for transfers between devices, swap(): lax.all_to_all(value, axis, 0, 0, axis_index_groups=groups, tiled=True)  51.4 us
    ppermute x9, waiting for transfers between devices, send(): return lax.ppermute(value, ('dp', 'fsdp'), pairs)  44.1 us
    ppermute x9, starting transfers between devices, send(): return lax.ppermute(value, ('dp', 'fsdp'), pairs)  32.1 us
    all_to_all x1, blocking collectives, swap(): lax.all_to_all(value, axis, 0, 0, axis_index_groups=groups, tiled=True)  17.8 us
    ppermute x3, starting transfers between devices, on_device(): lax.ppermute(part, 'dp', [(i, i ^ by * Y) for i in range(cycle)])  12.8 us
    ppermute x3, starting transfers between devices, on_device(): lax.ppermute(crossed, 'dp', [(i, i ^ by) for i in range(cycle)])  8.97 us
  transfers between devices with their start and end apart: 25, of which 15 were waited for; matrix products, arithmetic and copies ran while one was open for 5% of the time, Pallas kernels for 0%

profile of v9, /device:TPU:1, one launch (start us, length us, event | category | flops | bytes accessed | tf_op | source)
XLA Modules:
  0.0 277.1 jit_solution(15916132919601265609)
XLA Ops:
  7.2 1.0 broadcast_in_dim.22
  8.8 19.1 %all-to-all-start = ((bf16[16,36,96]{2,1,0:T(8,128)(2,1)}), bf16[16,36,96]{2,1,0:T(8,128)(2,1)S(1)}, u32[]{:S(2)}, u32[]{:S(2)}) async-start(bf16[16,36,96]{2,1,0:T(8,128)(2,1)} %bitcast.1), calls=%async_computation | async-start | bytes 327680 | tf_op jit(solution)/shard_map/all_to_all | solution.py:47
  30.4 1.4 convolution_convert_fusion.2
  31.7 11.4 %all-to-all-done = bf16[16,36,96]{2,1,0:T(8,128)(2,1)S(1)} async-done(((bf16[16,36,96]{2,1,0:T(8,128)(2,1)}), bf16[16,36,96]{2,1,0:T(8,128)(2,1)S(1)}, u32[]{:S(2)}, u32[]{:S(2)}) %all-to-all-start) | async-done | bytes 110624 | tf_op jit(solution)/shard_map/all_to_all | solution.py:47
  43.8 4.2 %all-to-all-start.1 = ((bf16[8,40,1536]{2,1,0:T(8,128)(2,1)}), bf16[8,40,1536]{2,1,0:T(8,128)(2,1)S(1)}, u32[]{:S(2)}, u32[]{:S(2)}) async-start(bf16[8,40,1536]{2,1,0:T(8,128)(2,1)} %bitcast.5), calls=%async_computation.1 | async-start | bytes 1966080 | tf_op jit(solution)/shard_map/all_to_all | solution.py:47
  48.0 7.1 %collective-permute-start.2 = (bf16[24,1536]{1,0:T(8,128)(2,1)S(1)}, bf16[24,1536]{1,0:T(8,128)(2,1)S(1)}, u32[]{:S(2)}, u32[]{:S(2)}) collective-permute-start(bf16[24,1536]{1,0:T(8,128)(2,1)S(1)} %get-tuple-element.57), channel_id=1, source_target_pairs={{0,192},{16,208},{32,224},{48,240},{64,128},{80,144},{96,160},{112... | collective-permute-start | bytes 221192 | tf_op jit(solution)/shard_map/ppermute | solution.py:93
  55.1 3.8 %collective-permute-start.1 = (bf16[24,1536]{1,0:T(8,128)(2,1)S(1)}, bf16[24,1536]{1,0:T(8,128)(2,1)S(1)}, u32[]{:S(2)}, u32[]{:S(2)}) collective-permute-start(bf16[24,1536]{1,0:T(8,128)(2,1)S(1)} %get-tuple-element.58), channel_id=1, source_target_pairs={{0,128},{16,144},{32,160},{48,176},{64,192},{80,208},{96,224},{112... | collective-permute-start | bytes 221192 | tf_op jit(solution)/shard_map/ppermute | solution.py:93
  59.0 1.9 collective-permute-start
  63.2 1.1 collective-permute-done
  64.4 1.9 collective-permute-start.4
  66.3 7.3 %collective-permute-start.3 = (bf16[40,1536]{1,0:T(8,128)(2,1)S(1)}, bf16[40,1536]{1,0:T(8,128)(2,1)S(1)}, u32[]{:S(2)}, u32[]{:S(2)}) collective-permute-start(bf16[40,1536]{1,0:T(8,128)(2,1)S(1)} %reduce_sum.67), channel_id=1, source_target_pairs={{0,256},{1,257},{4,260},{5,261},{8,264},{9,265},{12,268},{13,269},... | collective-permute-start | bytes 368648 | tf_op jit(solution)/shard_map/ppermute | solution.py:39
  74.5 1.0 slice.113
  75.4 2.4 collective-permute-start.5
  77.9 16.4 %collective-permute-done.5 = bf16[80,1536]{1,0:T(8,128)(2,1)S(1)} collective-permute-done((bf16[80,1536]{1,0:T(8,128)(2,1)S(1)}, bf16[80,1536]{1,0:T(8,128)(2,1)S(1)}, u32[]{:S(2)}, u32[]{:S(2)}) %collective-permute-start.5) | collective-permute-done | bytes 245792 | tf_op jit(solution)/shard_map/ppermute | solution.py:39
  94.3 4.5 %collective-permute-start.8 = (bf16[80,1536]{1,0:T(8,128)(2,1)S(1)}, bf16[80,1536]{1,0:T(8,128)(2,1)S(1)}, u32[]{:S(2)}, u32[]{:S(2)}) collective-permute-start(bf16[80,1536]{1,0:T(8,128)(2,1)S(1)} %collective-permute-done.5), channel_id=1, source_target_pairs={{0,48},{16,32},{32,16},{48,0},{64,112},{80,96},{96,80},{112,64},{1... | collective-permute-start | bytes 737288 | tf_op jit(solution)/shard_map/ppermute | solution.py:111
  98.8 2.3 collective-permute-start.7
  101.1 2.2 collective-permute-start.6
  103.5 1.0 broadcast_in_dim.47
  104.5 6.1 %all-to-all-start.2 = ((bf16[8,40,1536]{2,1,0:T(8,128)(2,1)}), bf16[8,40,1536]{2,1,0:T(8,128)(2,1)}, u32[]{:S(2)}, u32[]{:S(2)}) async-start(bf16[8,40,1536]{2,1,0:T(8,128)(2,1)} %broadcast_in_dim.47), calls=%async_computation.2 | async-start | bytes 1966080 | tf_op jit(solution)/shard_map/all_to_all | solution.py:47
  110.6 0.9 collective-permute-done.8
  111.8 1.2 slice_bitcast_fusion
  114.3 10.9 %all-to-all-done.2 = bf16[8,40,1536]{2,1,0:T(8,128)(2,1)} async-done(((bf16[8,40,1536]{2,1,0:T(8,128)(2,1)}), bf16[8,40,1536]{2,1,0:T(8,128)(2,1)}, u32[]{:S(2)}, u32[]{:S(2)}) %all-to-all-start.2) | async-done | bytes 983072 | tf_op jit(solution)/shard_map/all_to_all | solution.py:47
  125.2 2.3 fusion.8
  127.5 1.9 convolution_convert_fusion.1
  129.3 3.5 %convolution_convert_fusion = bf16[576,1536]{1,0:T(8,128)(2,1)} fusion(bf16[320,576]{1,0:T(8,128)(2,1)S(1)} %fusion.8, bf16[320,1536]{1,0:T(8,128)(2,1)} %bitcast.21), kind=kOutput, calls=%fused_computation | convolution fusion | flops 567115776 | bytes 3121152 | tf_op jit(solution)/shard_map/ij,ie->je/dot_general | solution.py:127
  132.9 1.2 copy-done.1
  134.1 17.8 %all_to_all.40 = bf16[8,40,1536]{2,1,0:T(8,128)(2,1)S(1)} all-to-all(bf16[8,40,1536]{2,1,0:T(8,128)(2,1)S(1)} %bitcast.93), channel_id=1, replica_groups={{0,1,4,5,8,9,12,13},{2,3,6,7,10,11,14,15},{16,17,20,21,24,25,28,29},{18..., dimensions={0} | all-to-all | bytes 1966080 | tf_op jit(solution)/shard_map/all_to_all | solution.py:47
  152.3 3.6 %collective-permute-start.10 = (bf16[40,1536]{1,0:T(8,128)(2,1)S(1)}, bf16[40,1536]{1,0:T(8,128)(2,1)S(1)}, u32[]{:S(2)}, u32[]{:S(2)}) collective-permute-start(bf16[40,1536]{1,0:T(8,128)(2,1)S(1)} %multiply_convert_fusion.1), channel_id=1, source_target_pairs={{0,258},{1,259},{4,262},{5,263},{8,266},{9,267},{12,270},{13,271},... | collective-permute-start | bytes 368648 | tf_op jit(solution)/shard_map/ppermute | solution.py:39
  155.9 5.8 %collective-permute-start.9 = (bf16[40,1536]{1,0:T(8,128)(2,1)S(1)}, bf16[40,1536]{1,0:T(8,128)(2,1)S(1)}, u32[]{:S(2)}, u32[]{:S(2)}) collective-permute-start(bf16[40,1536]{1,0:T(8,128)(2,1)S(1)} %multiply_convert_fusion.1), channel_id=1, source_target_pairs={{0,256},{1,257},{4,260},{5,261},{8,264},{9,265},{12,268},{13,269},... | collective-permute-start | bytes 368648 | tf_op jit(solution)/shard_map/ppermute | solution.py:39
  161.9 2.8 %collective-permute-done.10 = bf16[40,1536]{1,0:T(8,128)(2,1)S(1)} collective-permute-done((bf16[40,1536]{1,0:T(8,128)(2,1)S(1)}, bf16[40,1536]{1,0:T(8,128)(2,1)S(1)}, u32[]{:S(2)}, u32[]{:S(2)}) %collective-permute-start.10) | collective-permute-done | bytes 122912 | tf_op jit(solution)/shard_map/ppermute | solution.py:39
  164.8 7.1 %collective-permute-done.9 = bf16[40,1536]{1,0:T(8,128)(2,1)S(1)} collective-permute-done((bf16[40,1536]{1,0:T(8,128)(2,1)S(1)}, bf16[40,1536]{1,0:T(8,128)(2,1)S(1)}, u32[]{:S(2)}, u32[]{:S(2)}) %collective-permute-start.9) | collective-permute-done | bytes 122912 | tf_op jit(solution)/shard_map/ppermute | solution.py:39
  172.0 1.0 broadcast_in_dim.48
  173.0 4.3 %all-to-all-start.4 = ((bf16[8,40,1536]{2,1,0:T(8,128)(2,1)}), bf16[8,40,1536]{2,1,0:T(8,128)(2,1)S(1)}, u32[]{:S(2)}, u32[]{:S(2)}) async-start(bf16[8,40,1536]{2,1,0:T(8,128)(2,1)} %broadcast_in_dim.48), calls=%async_computation.5 | async-start | bytes 1966080 | tf_op jit(solution)/shard_map/all_to_all | solution.py:47
  177.4 1.9 collective-permute-start.11
  179.4 8.1 %collective-permute-done.11 = bf16[72,1536]{1,0:T(8,128)(2,1)S(1)} collective-permute-done((bf16[72,1536]{1,0:T(8,128)(2,1)S(1)}, bf16[72,1536]{1,0:T(8,128)(2,1)S(1)}, u32[]{:S(2)}, u32[]{:S(2)}) %collective-permute-start.11) | collective-permute-done | bytes 221216 | tf_op jit(solution)/shard_map/ppermute | solution.py:39
  187.5 4.2 %all-to-all-done.4 = bf16[8,40,1536]{2,1,0:T(8,128)(2,1)S(1)} async-done(((bf16[8,40,1536]{2,1,0:T(8,128)(2,1)}), bf16[8,40,1536]{2,1,0:T(8,128)(2,1)S(1)}, u32[]{:S(2)}, u32[]{:S(2)}) %all-to-all-start.4) | async-done | bytes 983072 | tf_op jit(solution)/shard_map/all_to_all | solution.py:47
  192.9 4.3 %all-to-all-start.5 = ((bf16[16,24,384]{2,1,0:T(8,128)(2,1)}), bf16[16,24,384]{2,1,0:T(8,128)(2,1)S(1)}, u32[]{:S(2)}, u32[]{:S(2)}) async-start(bf16[16,24,384]{2,1,0:T(8,128)(2,1)} %bitcast.33), calls=%async_computation.6 | async-start | bytes 589824 | tf_op jit(solution)/shard_map/all_to_all | solution.py:47
  197.3 4.2 %collective-permute-start.13 = (bf16[18,1536]{1,0:T(8,128)(2,1)S(1)}, bf16[18,1536]{1,0:T(8,128)(2,1)S(1)}, u32[]{:S(2)}, u32[]{:S(2)}) collective-permute-start(bf16[18,1536]{1,0:T(8,128)(2,1)S(1)} %select_convert_fusion.1), channel_id=1, source_target_pairs={{0,128},{1,129},{4,132},{5,133},{8,136},{9,137},{12,140},{13,141},... | collective-permute-start | bytes 165896 | tf_op jit(solution)/shard_map/ppermute | solution.py:39
  201.6 3.1 %collective-permute-start.14 = (bf16[18,1536]{1,0:T(8,128)(2,1)S(1)}, bf16[18,1536]{1,0:T(8,128)(2,1)S(1)}, u32[]{:S(2)}, u32[]{:S(2)}) collective-permute-start(bf16[18,1536]{1,0:T(8,128)(2,1)S(1)} %get-tuple-element.51), channel_id=1, source_target_pairs={{0,192},{1,193},{4,196},{5,197},{8,200},{9,201},{12,204},{13,205},... | collective-permute-start | bytes 165896 | tf_op jit(solution)/shard_map/ppermute | solution.py:39
  204.7 1.9 collective-permute-start.12
  206.6 1.8 all-to-all-done.5
  208.5 1.4 collective-permute-done.13
  209.9 8.3 %collective-permute-done.12 = bf16[18,1536]{1,0:T(8,128)(2,1)S(1)} collective-permute-done((bf16[18,1536]{1,0:T(8,128)(2,1)S(1)}, bf16[18,1536]{1,0:T(8,128)(2,1)S(1)}, u32[]{:S(2)}, u32[]{:S(2)}) %collective-permute-start.12) | collective-permute-done | bytes 55328 | tf_op jit(solution)/shard_map/ppermute | solution.py:39
  218.1 4.0 %collective-permute-start.15 = (bf16[24,384]{1,0:T(8,128)(2,1)S(1)}, bf16[24,384]{1,0:T(8,128)(2,1)S(1)}, u32[]{:S(2)}, u32[]{:S(2)}) collective-permute-start(bf16[24,384]{1,0:T(8,128)(2,1)S(1)} %reduce-precision_convert_fusion), channel_id=1, source_target_pairs={{0,256},{16,272},{32,288},{48,304},{64,320},{80,336},{96,352},{112... | collective-permute-start | bytes 55304 | tf_op jit(solution)/shard_map/ppermute | solution.py:149
  223.3 11.2 %all-to-all-start.6 = ((bf16[16,18,96]{2,1,0:T(8,128)(2,1)}), bf16[16,18,96]{2,1,0:T(8,128)(2,1)S(1)}, u32[]{:S(2)}, u32[]{:S(2)}) async-start(bf16[16,18,96]{2,1,0:T(8,128)(2,1)} %copy.59), calls=%async_computation.7 | async-start | bytes 196608 | tf_op jit(solution)/shard_map/all_to_all | solution.py:47
  234.5 14.6 %all-to-all-done.6 = bf16[16,18,96]{2,1,0:T(8,128)(2,1)S(1)} async-done(((bf16[16,18,96]{2,1,0:T(8,128)(2,1)}), bf16[16,18,96]{2,1,0:T(8,128)(2,1)S(1)}, u32[]{:S(2)}, u32[]{:S(2)}) %all-to-all-start.6) | async-done | bytes 55328 | tf_op jit(solution)/shard_map/all_to_all | solution.py:47
  249.8 8.9 %all-to-all-start.7 = ((bf16[16,24,384]{2,1,0:T(8,128)(2,1)}), bf16[16,24,384]{2,1,0:T(8,128)(2,1)S(1)}, u32[]{:S(2)}, u32[]{:S(2)}) async-start(bf16[16,24,384]{2,1,0:T(8,128)(2,1)} %broadcast_in_dim.49), calls=%async_computation.8 | async-start | bytes 589824 | tf_op jit(solution)/shard_map/all_to_all | solution.py:47
  260.7 8.5 %all-to-all-done.7 = bf16[16,24,384]{2,1,0:T(8,128)(2,1)S(1)} async-done(((bf16[16,24,384]{2,1,0:T(8,128)(2,1)}), bf16[16,24,384]{2,1,0:T(8,128)(2,1)S(1)}, u32[]{:S(2)}, u32[]{:S(2)}) %all-to-all-start.7) | async-done | bytes 294944 | tf_op jit(solution)/shard_map/all_to_all | solution.py:47
  (99 shorter events, 14.5 us)
Async XLA Ops:
  7.2 23.2 %copy-start = (bf16[96,1536]{1,0:T(8,128)(2,1)S(1)}, bf16[96,1536]{1,0:T(8,128)(2,1)}, u32[]{:S(2)}) copy-start(bf16[96,1536]{1,0:T(8,128)(2,1)} %param.7) | copy-start | bytes 884740
  8.8 34.3 %all-to-all-start = ((bf16[16,36,96]{2,1,0:T(8,128)(2,1)}), bf16[16,36,96]{2,1,0:T(8,128)(2,1)S(1)}, u32[]{:S(2)}, u32[]{:S(2)}) async-start(bf16[16,36,96]{2,1,0:T(8,128)(2,1)} %bitcast.1), calls=%async_computation | async-start | bytes 327680 | tf_op jit(solution)/shard_map/all_to_all | solution.py:47
  29.7 0.6 copy-start.2
  43.8 18.6 %all-to-all-start.1 = ((bf16[8,40,1536]{2,1,0:T(8,128)(2,1)}), bf16[8,40,1536]{2,1,0:T(8,128)(2,1)S(1)}, u32[]{:S(2)}, u32[]{:S(2)}) async-start(bf16[8,40,1536]{2,1,0:T(8,128)(2,1)} %bitcast.5), calls=%async_computation.1 | async-start | bytes 1966080 | tf_op jit(solution)/shard_map/all_to_all | solution.py:47
  48.0 63.8 %all-gather.3.cloned.1.call-start = ((), (), s32[]{:S(2)}) async-start(), calls=%async_computation.10 | async-start | bytes 1351680 | tf_op jit(solution)/shard_map/all_gather | solution.py:102
  48.0 14.5 %collective-permute-start.2 = (bf16[24,1536]{1,0:T(8,128)(2,1)S(1)}, bf16[24,1536]{1,0:T(8,128)(2,1)S(1)}, u32[]{:S(2)}, u32[]{:S(2)}) collective-permute-start(bf16[24,1536]{1,0:T(8,128)(2,1)S(1)} %get-tuple-element.57), channel_id=1, source_target_pairs={{0,192},{16,208},{32,224},{48,240},{64,128},{80,144},{96,160},{112... | collective-permute-start | bytes 221192 | tf_op jit(solution)/shard_map/ppermute | solution.py:93
  55.1 8.1 %collective-permute-start.1 = (bf16[24,1536]{1,0:T(8,128)(2,1)S(1)}, bf16[24,1536]{1,0:T(8,128)(2,1)S(1)}, u32[]{:S(2)}, u32[]{:S(2)}) collective-permute-start(bf16[24,1536]{1,0:T(8,128)(2,1)S(1)} %get-tuple-element.58), channel_id=1, source_target_pairs={{0,128},{16,144},{32,160},{48,176},{64,192},{80,208},{96,224},{112... | collective-permute-start | bytes 221192 | tf_op jit(solution)/shard_map/ppermute | solution.py:93
  59.0 5.3 %collective-permute-start = (bf16[24,1536]{1,0:T(8,128)(2,1)S(1)}, bf16[24,1536]{1,0:T(8,128)(2,1)S(1)}, u32[]{:S(2)}, u32[]{:S(2)}) collective-permute-start(bf16[24,1536]{1,0:T(8,128)(2,1)S(1)} %get-tuple-element.60), channel_id=1, source_target_pairs={{0,64},{16,80},{32,96},{48,112},{64,0},{80,16},{96,32},{112,48},{1... | collective-permute-start | bytes 221192 | tf_op jit(solution)/shard_map/ppermute | solution.py:93
  64.4 13.4 %collective-permute-start.4 = (bf16[40,1536]{1,0:T(8,128)(2,1)S(1)}, bf16[40,1536]{1,0:T(8,128)(2,1)S(1)}, u32[]{:S(2)}, u32[]{:S(2)}) collective-permute-start(bf16[40,1536]{1,0:T(8,128)(2,1)S(1)} %reduce_sum.67), channel_id=1, source_target_pairs={{0,258},{1,259},{4,262},{5,263},{8,266},{9,267},{12,270},{13,271},... | collective-permute-start | bytes 368648 | tf_op jit(solution)/shard_map/ppermute | solution.py:39
  66.3 11.5 %collective-permute-start.3 = (bf16[40,1536]{1,0:T(8,128)(2,1)S(1)}, bf16[40,1536]{1,0:T(8,128)(2,1)S(1)}, u32[]{:S(2)}, u32[]{:S(2)}) collective-permute-start(bf16[40,1536]{1,0:T(8,128)(2,1)S(1)} %reduce_sum.67), channel_id=1, source_target_pairs={{0,256},{1,257},{4,260},{5,261},{8,264},{9,265},{12,268},{13,269},... | collective-permute-start | bytes 368648 | tf_op jit(solution)/shard_map/ppermute | solution.py:39
  75.4 18.9 %collective-permute-start.5 = (bf16[80,1536]{1,0:T(8,128)(2,1)S(1)}, bf16[80,1536]{1,0:T(8,128)(2,1)S(1)}, u32[]{:S(2)}, u32[]{:S(2)}) collective-permute-start(bf16[80,1536]{1,0:T(8,128)(2,1)S(1)} %slice.113), channel_id=1, source_target_pairs={{0,450},{1,451},{4,454},{5,455},{8,458},{9,459},{12,462},{13,463},... | collective-permute-start | bytes 737288 | tf_op jit(solution)/shard_map/ppermute | solution.py:39
  94.3 17.3 %collective-permute-start.8 = (bf16[80,1536]{1,0:T(8,128)(2,1)S(1)}, bf16[80,1536]{1,0:T(8,128)(2,1)S(1)}, u32[]{:S(2)}, u32[]{:S(2)}) collective-permute-start(bf16[80,1536]{1,0:T(8,128)(2,1)S(1)} %collective-permute-done.5), channel_id=1, source_target_pairs={{0,48},{16,32},{32,16},{48,0},{64,112},{80,96},{96,80},{112,64},{1... | collective-permute-start | bytes 737288 | tf_op jit(solution)/shard_map/ppermute | solution.py:111
  98.8 12.7 %collective-permute-start.7 = (bf16[80,1536]{1,0:T(8,128)(2,1)S(1)}, bf16[80,1536]{1,0:T(8,128)(2,1)S(1)}, u32[]{:S(2)}, u32[]{:S(2)}) collective-permute-start(bf16[80,1536]{1,0:T(8,128)(2,1)S(1)} %collective-permute-done.5), channel_id=1, source_target_pairs={{0,32},{16,48},{32,0},{48,16},{64,96},{80,112},{96,64},{112,80},{1... | collective-permute-start | bytes 737288 | tf_op jit(solution)/shard_map/ppermute | solution.py:111
  101.1 10.5 %collective-permute-start.6 = (bf16[80,1536]{1,0:T(8,128)(2,1)S(1)}, bf16[80,1536]{1,0:T(8,128)(2,1)S(1)}, u32[]{:S(2)}, u32[]{:S(2)}) collective-permute-start(bf16[80,1536]{1,0:T(8,128)(2,1)S(1)} %collective-permute-done.5), channel_id=1, source_target_pairs={{0,16},{16,0},{32,48},{48,32},{64,80},{80,64},{96,112},{112,96},{1... | collective-permute-start | bytes 737288 | tf_op jit(solution)/shard_map/ppermute | solution.py:111
  104.5 20.6 %all-to-all-start.2 = ((bf16[8,40,1536]{2,1,0:T(8,128)(2,1)}), bf16[8,40,1536]{2,1,0:T(8,128)(2,1)}, u32[]{:S(2)}, u32[]{:S(2)}) async-start(bf16[8,40,1536]{2,1,0:T(8,128)(2,1)} %broadcast_in_dim.47), calls=%async_computation.2 | async-start | bytes 1966080 | tf_op jit(solution)/shard_map/all_to_all | solution.py:47
  110.6 61.3 %reduce-scatter.2.cloned.1.call-start = ((), (), s32[]{:S(2)}) async-start(), calls=%async_computation.9 | async-start | bytes 2211840 | tf_op jit(solution)/shard_map/reduce_scatter | solution.py:129
  132.9 1.2 copy-start.1
  152.3 12.5 %collective-permute-start.10 = (bf16[40,1536]{1,0:T(8,128)(2,1)S(1)}, bf16[40,1536]{1,0:T(8,128)(2,1)S(1)}, u32[]{:S(2)}, u32[]{:S(2)}) collective-permute-start(bf16[40,1536]{1,0:T(8,128)(2,1)S(1)} %multiply_convert_fusion.1), channel_id=1, source_target_pairs={{0,258},{1,259},{4,262},{5,263},{8,266},{9,267},{12,270},{13,271},... | collective-permute-start | bytes 368648 | tf_op jit(solution)/shard_map/ppermute | solution.py:39
  155.9 16.0 %collective-permute-start.9 = (bf16[40,1536]{1,0:T(8,128)(2,1)S(1)}, bf16[40,1536]{1,0:T(8,128)(2,1)S(1)}, u32[]{:S(2)}, u32[]{:S(2)}) collective-permute-start(bf16[40,1536]{1,0:T(8,128)(2,1)S(1)} %multiply_convert_fusion.1), channel_id=1, source_target_pairs={{0,256},{1,257},{4,260},{5,261},{8,264},{9,265},{12,268},{13,269},... | collective-permute-start | bytes 368648 | tf_op jit(solution)/shard_map/ppermute | solution.py:39
  172.0 5.4 %copy-start.4 = (bf16[1,144,1536]{2,1,0:T(8,128)(2,1)S(1)}, bf16[1,144,1536]{2,1,0:T(8,128)(2,1)}, u32[]{:S(2)}) copy-start(bf16[1,144,1536]{2,1,0:T(8,128)(2,1)} %reduce-scatter.2.cloned.1.call-done) | copy-start | bytes 1327108
  172.0 19.7 %copy-start.3 = (bf16[8,40,96]{2,1,0:T(8,128)(2,1)S(1)}, bf16[8,40,96]{2,1,0:T(8,128)(2,1)}, u32[]{:S(2)}) copy-start(bf16[8,40,96]{2,1,0:T(8,128)(2,1)} %copy-done.2) | copy-start | bytes 184324
  173.0 18.7 %all-to-all-start.4 = ((bf16[8,40,1536]{2,1,0:T(8,128)(2,1)}), bf16[8,40,1536]{2,1,0:T(8,128)(2,1)S(1)}, u32[]{:S(2)}, u32[]{:S(2)}) async-start(bf16[8,40,1536]{2,1,0:T(8,128)(2,1)} %broadcast_in_dim.48), calls=%async_computation.5 | async-start | bytes 1966080 | tf_op jit(solution)/shard_map/all_to_all | solution.py:47
  177.4 10.1 %collective-permute-start.11 = (bf16[72,1536]{1,0:T(8,128)(2,1)S(1)}, bf16[72,1536]{1,0:T(8,128)(2,1)S(1)}, u32[]{:S(2)}, u32[]{:S(2)}) collective-permute-start(bf16[72,1536]{1,0:T(8,128)(2,1)S(1)} %slice_bitcast_fusion.1), channel_id=1, source_target_pairs={{0,450},{1,451},{4,454},{5,455},{8,458},{9,459},{12,462},{13,463},... | collective-permute-start | bytes 663560 | tf_op jit(solution)/shard_map/ppermute | solution.py:39
  192.9 15.5 %all-to-all-start.5 = ((bf16[16,24,384]{2,1,0:T(8,128)(2,1)}), bf16[16,24,384]{2,1,0:T(8,128)(2,1)S(1)}, u32[]{:S(2)}, u32[]{:S(2)}) async-start(bf16[16,24,384]{2,1,0:T(8,128)(2,1)} %bitcast.33), calls=%async_computation.6 | async-start | bytes 589824 | tf_op jit(solution)/shard_map/all_to_all | solution.py:47
  197.3 12.5 %collective-permute-start.13 = (bf16[18,1536]{1,0:T(8,128)(2,1)S(1)}, bf16[18,1536]{1,0:T(8,128)(2,1)S(1)}, u32[]{:S(2)}, u32[]{:S(2)}) collective-permute-start(bf16[18,1536]{1,0:T(8,128)(2,1)S(1)} %select_convert_fusion.1), channel_id=1, source_target_pairs={{0,128},{1,129},{4,132},{5,133},{8,136},{9,137},{12,140},{13,141},... | collective-permute-start | bytes 165896 | tf_op jit(solution)/shard_map/ppermute | solution.py:39
  201.6 8.3 %collective-permute-start.14 = (bf16[18,1536]{1,0:T(8,128)(2,1)S(1)}, bf16[18,1536]{1,0:T(8,128)(2,1)S(1)}, u32[]{:S(2)}, u32[]{:S(2)}) collective-permute-start(bf16[18,1536]{1,0:T(8,128)(2,1)S(1)} %get-tuple-element.51), channel_id=1, source_target_pairs={{0,192},{1,193},{4,196},{5,197},{8,200},{9,201},{12,204},{13,205},... | collective-permute-start | bytes 165896 | tf_op jit(solution)/shard_map/ppermute | solution.py:39
  204.7 13.4 %collective-permute-start.12 = (bf16[18,1536]{1,0:T(8,128)(2,1)S(1)}, bf16[18,1536]{1,0:T(8,128)(2,1)S(1)}, u32[]{:S(2)}, u32[]{:S(2)}) collective-permute-start(bf16[18,1536]{1,0:T(8,128)(2,1)S(1)} %get-tuple-element.52), channel_id=1, source_target_pairs={{0,64},{1,65},{4,68},{5,69},{8,72},{9,73},{12,76},{13,77},{16,80},... | collective-permute-start | bytes 165896 | tf_op jit(solution)/shard_map/ppermute | solution.py:39
  218.1 16.3 %collective-permute-start.15 = (bf16[24,384]{1,0:T(8,128)(2,1)S(1)}, bf16[24,384]{1,0:T(8,128)(2,1)S(1)}, u32[]{:S(2)}, u32[]{:S(2)}) collective-permute-start(bf16[24,384]{1,0:T(8,128)(2,1)S(1)} %reduce-precision_convert_fusion), channel_id=1, source_target_pairs={{0,256},{16,272},{32,288},{48,304},{64,320},{80,336},{96,352},{112... | collective-permute-start | bytes 55304 | tf_op jit(solution)/shard_map/ppermute | solution.py:149
  223.3 25.8 %all-to-all-start.6 = ((bf16[16,18,96]{2,1,0:T(8,128)(2,1)}), bf16[16,18,96]{2,1,0:T(8,128)(2,1)S(1)}, u32[]{:S(2)}, u32[]{:S(2)}) async-start(bf16[16,18,96]{2,1,0:T(8,128)(2,1)} %copy.59), calls=%async_computation.7 | async-start | bytes 196608 | tf_op jit(solution)/shard_map/all_to_all | solution.py:47
  249.8 19.5 %all-to-all-start.7 = ((bf16[16,24,384]{2,1,0:T(8,128)(2,1)}), bf16[16,24,384]{2,1,0:T(8,128)(2,1)S(1)}, u32[]{:S(2)}, u32[]{:S(2)}) async-start(bf16[16,24,384]{2,1,0:T(8,128)(2,1)} %broadcast_in_dim.49), calls=%async_computation.8 | async-start | bytes 589824 | tf_op jit(solution)/shard_map/all_to_all | solution.py:47
Sparse Core Ops, SparseCore 0:
  74.6 28.2 all-gather.2
  133.0 30.8 reduce-scatter.1

commit v10 on v9

--- a/solution.py
+++ b/solution.py
@@ -56,7 +56,6 @@
     rows, width = image_feats.shape
     embed_width = image_head.shape[1]
     cycle = lax.axis_size("dp")
-    group = lax.axis_size("fsdp")
     plane = X * CORE
     own = rows // plane
     held = -(-own // 8) * 8
@@ -65,35 +64,40 @@
     f = lax.axis_index("fsdp")
 
     zl, zh = d // Y, f // CORE % ZH
-    k = f // 4 * CORE + f % CORE
     z = zh * ZL + zl
     second = (z >= 6) & (z < 14)
-    parts = jnp.broadcast_to(text_embed.reshape(X, 1, CORE, own, width), (X, ZH, CORE, own, width))
-    text_part = swap(parts.reshape(group, own, width), "fsdp")
-    text_vals = text_part.transpose(1, 0, 2).reshape(own, embed_width).astype(F32)
+    above = (z + 4) % 16 // ZL == 1
+
+    raw = jnp.stack([text_ids // 128, text_ids % 128], axis=1).astype(BF16)
+    raw = jnp.concatenate([text_embed, raw], axis=1)
+    up, down = send(raw, UP), send(raw, DOWN)
+    raw = jnp.where(above, jnp.concatenate([up[:, :width], down], axis=1), jnp.concatenate([down[:, :width], up], axis=1))
+    raw = jnp.pad(raw.reshape(plane, own, -1), ((0, 0), (0, held - own), (0, 0))).reshape(plane * held, -1)
+    feats = jnp.pad(image_feats.reshape(plane, own, width), ((0, 0), (0, held - own), (0, 0)))
+    feats = feats.reshape(plane * held, width)
+    wide = jnp.pad(image_head, ((0, 0), (0, raw.shape[1])))
+    term = jnp.dot(feats, wide, preferred_element_type=F32).astype(BF16)
+    term = lax.dynamic_update_slice(term, raw, (0, embed_width))
+    came = swap(term.reshape(plane, held, -1), "fsdp", PLANE)
+    half = jnp.sum(came[:, :, :embed_width].astype(F32), axis=0).astype(BF16)
+
+    text_part = came[:, :own, embed_width : embed_width + ZH * width].reshape(X, CORE, own, ZH, width)
+    text_vals = text_part.transpose(2, 0, 3, 1, 4).reshape(own, embed_width).astype(F32)
     text_scale = lax.rsqrt(jnp.sum(text_vals * text_vals, axis=1, keepdims=True) + 1e-06)
     text_unit = text_vals * text_scale
-    my_ids = lax.dynamic_slice_in_dim(text_ids, k * own, own, 0).reshape(ZH, share)
-    marks = jnp.concatenate([my_ids // 128, my_ids % 128], axis=1).astype(BF16)
+    marks = came[0, :own, embed_width + ZH * width :].reshape(ZH, share, 2)
+    marks = marks.transpose(0, 2, 1).reshape(ZH, 2 * share)
     piece = -(-share // 8) * 8
     marks = jnp.pad(marks[:, None], ((0, 0), (0, piece - share - 1), (0, embed_width - 2 * share)))
     halves = jnp.concatenate([text_unit.astype(BF16).reshape(ZH, share, embed_width), marks], axis=1)
     text_unit = jnp.where(second, text_unit[share:], text_unit[:share])
     text_scale = jnp.where(second, text_scale[share:], text_scale[:share])
 
-    feats = jnp.pad(image_feats.reshape(plane, own, width), ((0, 0), (0, held - own), (0, 0)))
-    feats = feats.reshape(plane * held, width)
-    term = jnp.dot(feats, image_head, preferred_element_type=F32).astype(BF16)
-    term, halves = lax.optimization_barrier((term, halves))
-
     parts = [jnp.where(second, halves[1], halves[0])]
     for by in (1, 2, 3):
         there = z ^ by
         part = jnp.where((there >= 6) & (there < 14), halves[1], halves[0])
         parts.append(lax.ppermute(part, "dp", [(i, i ^ (by * Y)) for i in range(cycle)]))
-    half = swap(term.reshape(plane, held, embed_width), "fsdp", PLANE)
-    half = jnp.sum(half.astype(F32), axis=0).astype(BF16)
-    half, *parts = lax.optimization_barrier((half, *parts))
     blocks = jnp.stack([pick(z % 4 ^ i, parts) for i in range(4)])
     count = 4 * share
     quad = jnp.concatenate([blocks[:, :share].reshape(count, embed_width), blocks[:, share]], axis=0)
@@ -102,13 +106,15 @@
     near = lax.all_gather(quad, "dp", axis_index_groups=RING)
     embed = send(half, UP).astype(F32) + send(half, DOWN).astype(F32)
     crossed = send(quad[: count + 8], MIRROR)
-    embed, crossed = lax.optimization_barrier((embed, crossed))
 
     image_scale = lax.rsqrt(jnp.sum(embed * embed, axis=1, keepdims=True) + 1e-06)
     image_unit = embed * image_scale
     image_low = spread(image_unit.astype(BF16), "fsdp", PLANE, plane).reshape(plane * held, embed_width)
     y = d % Y
-    far = [crossed] + [lax.ppermute(crossed, "dp", [(i, i ^ by) for i in range(cycle)]) for by in (1, 2, 3)]
+    far = [lax.ppermute(crossed, "dp", [(i, i ^ by) for i in range(cycle)]) for by in (1, 3)]
+    image_low, last = lax.optimization_barrier((image_low, crossed))
+    last = lax.ppermute(last, "dp", [(i, i ^ 2) for i in range(cycle)])
+    far = [crossed, far[0], last, far[1]]
     far = jnp.stack([pick(y ^ i, far) for i in range(Y)])
     lines = (near, far)
     text_low = jnp.stack([part[:, :count] for part in lines], axis=1).reshape(cycle * share, embed_width)
@@ -147,20 +153,23 @@
     head_sum, *parts = lax.optimization_barrier((head_sum, *parts))
     head_sum = lax.reduce_precision(head_sum, 8, 7)
     head_sum = head_sum + lax.ppermute(head_sum.astype(BF16), "dp", ACROSS).astype(F32)
+    head_all = spread(head_sum.astype(BF16), "dp", SLAB, 4 * Y)
+
     text_acc = pick(i, text_acc)
     for part in parts:
         text_acc = text_acc + part.astype(F32)
     text_dot = jnp.sum(text_unit * text_acc, axis=1, keepdims=True)
     text_rows = (text_scale * (text_acc - text_unit * text_dot)).astype(BF16)
-    text_rows = text_rows.reshape(share, group, width).transpose(1, 0, 2)
-    text_grad = swap(text_rows, "fsdp")
-    text_grad, head_sum = lax.optimization_barrier((text_grad, head_sum))
-    text_grad = text_grad.reshape(X, ZH, CORE, share, width)
-    text_grad = jnp.where(zl < 6, text_grad, text_grad[:, ::-1])
-    text_grad = text_grad.transpose(0, 2, 1, 3, 4).reshape(rows, width)
-
-    head_all = spread(head_sum.astype(BF16), "dp", SLAB, 4 * Y).reshape(Y, 4, width // Y, embed_width // 4)
-    head_all = head_all.transpose(0, 2, 1, 3).reshape(width, embed_width)
+    text_rows = text_rows.reshape(share, X, ZH, CORE, width).transpose(2, 1, 3, 0, 4)
+    text_rows = text_rows.reshape(ZH, plane, share, width)
+    up = send(jnp.where(above, text_rows[1], text_rows[0]), UP)
+    down = send(jnp.where(above, text_rows[0], text_rows[1]), DOWN)
+    below = (z + 12) % 16
+    below = (below >= 6) & (below < 14)
+    text_grad = jnp.where(below, jnp.stack([down, up], axis=1), jnp.stack([up, down], axis=1))
+    text_grad, head_all = lax.optimization_barrier((text_grad.reshape(plane, own, width), head_all))
+    text_grad = swap(text_grad, "fsdp", PLANE).reshape(rows, width)
+    head_all = head_all.reshape(Y, 4, width // Y, embed_width // 4).transpose(0, 2, 1, 3).reshape(width, embed_width)
     head_grad = head_all.astype(F32)
     feature_grad = jnp.einsum("re,we->rw", grads, image_head, preferred_element_type=F32).astype(BF16)
     feature_grad = feature_grad.reshape(plane, held, width)[:, :own].reshape(rows, width)

time: 279 us -> 289 us (1.036)
  starting transfers between devices: 116 us -> 121 us
  waiting for transfers between devices: 98.3 us -> 102 us
    ppermute x9 -> x13, starting transfers between devices: 32.1 us -> 59.6 us  [send(): return lax.ppermute(value, ('dp', 'fsdp'), pairs)]
    all_to_all x7 -> x6, waiting for transfers between devices: 51.4 us -> 25.9 us  [swap(): lax.all_to_all(value, axis, 0, 0, axis_index_groups=groups, tiled=True)]
    all_to_all x7 -> x6, starting transfers between devices: 58 us -> 39.5 us  [swap(): lax.all_to_all(value, axis, 0, 0, axis_index_groups=groups, tiled=True)]
    ppermute x9 -> x13, waiting for transfers between devices: 44.1 us -> 54.9 us  [send(): return lax.ppermute(value, ('dp', 'fsdp'), pairs)]
    ppermute x0 -> x1, waiting for transfers between devices: none -> 7.03 us  [on_device(): last = lax.ppermute(last, 'dp', [(i, i ^ 2) for i in range(cycle)])]
    ppermute x1, waiting for transfers between devices: 0.01 us -> 6.58 us  [on_device(): lax.ppermute(head_sum.astype(BF16), 'dp', ACROSS).astype(F32)]
    ppermute x3 -> x2, waiting for transfers between devices: 0.92 us -> 7.08 us  [on_device(): lax.ppermute(crossed, 'dp', [(i, i ^ by) for i in range(cycle)])]
    ppermute x0 -> x1, starting transfers between devices: none -> 3.09 us  [on_device(): last = lax.ppermute(last, 'dp', [(i, i ^ 2) for i in range(cycle)])]
  transfers between devices with their start and end apart: 25 -> 28, of which waited for: 15 -> 18; matrix products, arithmetic and copies ran while one was open for 5% -> 3% of each run, Pallas kernels for 0% -> 0%
where the time goes in v10:
time: 289 us; the launch traced here: 287 us
  starting transfers between devices  121 us (42%)
  waiting for transfers between devices  102 us (35%)
  blocking collectives  19.3 us (7%)
  between operations  16 us (6%)
  local copies, waits for them, and re-layouts  15.7 us (5%)
  matrix products  8.58 us (3%)
  other arithmetic  5.23 us (2%)
    ppermute x13, starting transfers between devices, send(): return lax.ppermute(value, ('dp', 'fsdp'), pairs)  59.6 us
    ppermute x13, waiting for transfers between devices, send(): return lax.ppermute(value, ('dp', 'fsdp'), pairs)  54.9 us
    all_to_all x6, starting transfers between devices, swap(): lax.all_to_all(value, axis, 0, 0, axis_index_groups=groups, tiled=True)  39.5 us
    all_to_all x6, waiting for transfers between devices, swap(): lax.all_to_all(value, axis, 0, 0, axis_index_groups=groups, tiled=True)  25.9 us
    all_to_all x1, blocking collectives, swap(): lax.all_to_all(value, axis, 0, 0, axis_index_groups=groups, tiled=True)  19.3 us
    ppermute x3, starting transfers between devices, on_device(): lax.ppermute(part, 'dp', [(i, i ^ by * Y) for i in range(cycle)])  10 us
    ppermute x2, waiting for transfers between devices, on_device(): lax.ppermute(crossed, 'dp', [(i, i ^ by) for i in range(cycle)])  7.08 us
    ppermute x1, waiting for transfers between devices, on_device(): last = lax.ppermute(last, 'dp', [(i, i ^ 2) for i in range(cycle)])  7.03 us
  transfers between devices with their start and end apart: 28, of which 18 were waited for; matrix products, arithmetic and copies ran while one was open for 3% of the time, Pallas kernels for 0%

profile of v10, /device:TPU:1, one launch (start us, length us, event | category | flops | bytes accessed | tf_op | source)
XLA Modules:
  0.0 287.3 jit_solution(5202634224109502230)
XLA Ops:
  9.1 13.3 %collective-permute-start.1 = (bf16[288,98]{1,0:T(8,128)(2,1)S(1)}, bf16[288,98]{1,0:T(8,128)(2,1)S(1)}, u32[]{:S(2)}, u32[]{:S(2)}) collective-permute-start(bf16[288,98]{1,0:T(8,128)(2,1)S(1)} %pad_maximum_fusion.5), channel_id=1, source_target_pairs={{0,258},{1,259},{4,262},{5,263},{8,266},{9,267},{12,270},{13,271},... | collective-permute-start | bytes 169352 | tf_op jit(solution)/shard_map/ppermute | solution.py:39
  22.4 1.9 collective-permute-start
  25.2 2.4 convolution_convert_fusion.1
  27.7 4.0 %collective-permute-done = bf16[288,98]{1,0:T(8,128)(2,1)S(1)} collective-permute-done((bf16[288,98]{1,0:T(8,128)(2,1)S(1)}, bf16[288,98]{1,0:T(8,128)(2,1)S(1)}, u32[]{:S(2)}, u32[]{:S(2)}) %collective-permute-start) | collective-permute-done | bytes 56480 | tf_op jit(solution)/shard_map/ppermute | solution.py:39
  32.7 7.9 %all-to-all-start = ((bf16[8,40,1730]{2,1,0:T(8,128)(2,1)}), bf16[8,40,1730]{2,1,0:T(8,128)(2,1)S(1)}, u32[]{:S(2)}, u32[]{:S(2)}) async-start(bf16[8,40,1730]{2,1,0:T(8,128)(2,1)} %bitcast.2), calls=%async_computation | async-start | bytes 2293760 | tf_op jit(solution)/shard_map/all_to_all | solution.py:47
  40.5 16.2 %all-to-all-done = bf16[8,40,1730]{2,1,0:T(8,128)(2,1)S(1)} async-done(((bf16[8,40,1730]{2,1,0:T(8,128)(2,1)}), bf16[8,40,1730]{2,1,0:T(8,128)(2,1)S(1)}, u32[]{:S(2)}, u32[]{:S(2)}) %all-to-all-start) | async-done | bytes 1107232 | tf_op jit(solution)/shard_map/all_to_all | solution.py:47
  58.2 5.9 %collective-permute-start.6 = (bf16[24,1536]{1,0:T(8,128)(2,1)S(1)}, bf16[24,1536]{1,0:T(8,128)(2,1)S(1)}, u32[]{:S(2)}, u32[]{:S(2)}) collective-permute-start(bf16[24,1536]{1,0:T(8,128)(2,1)S(1)} %get-tuple-element.44), channel_id=1, source_target_pairs={{0,192},{16,208},{32,224},{48,240},{64,128},{80,144},{96,160},{112... | collective-permute-start | bytes 221192 | tf_op jit(solution)/shard_map/ppermute | solution.py:100
  64.2 1.9 collective-permute-start.5
  66.1 2.2 collective-permute-start.4
  68.4 1.9 collective-permute-start.2
  70.4 7.3 %collective-permute-start.3 = (bf16[40,1536]{1,0:T(8,128)(2,1)S(1)}, bf16[40,1536]{1,0:T(8,128)(2,1)S(1)}, u32[]{:S(2)}, u32[]{:S(2)}) collective-permute-start(bf16[40,1536]{1,0:T(8,128)(2,1)S(1)} %slice_reduce_fusion), channel_id=1, source_target_pairs={{0,258},{1,259},{4,262},{5,263},{8,266},{9,267},{12,270},{13,271},... | collective-permute-start | bytes 368648 | tf_op jit(solution)/shard_map/ppermute | solution.py:39
  78.3 5.2 %collective-permute-done.3 = bf16[40,1536]{1,0:T(8,128)(2,1)S(1)} collective-permute-done((bf16[40,1536]{1,0:T(8,128)(2,1)S(1)}, bf16[40,1536]{1,0:T(8,128)(2,1)S(1)}, u32[]{:S(2)}, u32[]{:S(2)}) %collective-permute-start.3) | collective-permute-done | bytes 122912 | tf_op jit(solution)/shard_map/ppermute | solution.py:39
  84.7 9.4 %all-to-all-start.1 = ((bf16[8,40,1536]{2,1,0:T(8,128)(2,1)}), bf16[8,40,1536]{2,1,0:T(8,128)(2,1)S(1)}, u32[]{:S(2)}, u32[]{:S(2)}) async-start(bf16[8,40,1536]{2,1,0:T(8,128)(2,1)} %broadcast_in_dim.19), calls=%async_computation.1 | async-start | bytes 1966080 | tf_op jit(solution)/shard_map/all_to_all | solution.py:47
  96.0 4.9 %collective-permute-start.7 = (bf16[80,1536]{1,0:T(8,128)(2,1)S(1)}, bf16[80,1536]{1,0:T(8,128)(2,1)S(1)}, u32[]{:S(2)}, u32[]{:S(2)}) collective-permute-start(bf16[80,1536]{1,0:T(8,128)(2,1)S(1)} %slice.153), channel_id=1, source_target_pairs={{0,450},{1,451},{4,454},{5,455},{8,458},{9,459},{12,462},{13,463},... | collective-permute-start | bytes 737288 | tf_op jit(solution)/shard_map/ppermute | solution.py:39
  100.9 11.4 %collective-permute-done.7 = bf16[80,1536]{1,0:T(8,128)(2,1)S(1)} collective-permute-done((bf16[80,1536]{1,0:T(8,128)(2,1)S(1)}, bf16[80,1536]{1,0:T(8,128)(2,1)S(1)}, u32[]{:S(2)}, u32[]{:S(2)}) %collective-permute-start.7) | collective-permute-done | bytes 245792 | tf_op jit(solution)/shard_map/ppermute | solution.py:39
  112.3 4.6 %collective-permute-start.10 = (bf16[80,1536]{1,0:T(8,128)(2,1)S(1)}, bf16[80,1536]{1,0:T(8,128)(2,1)S(1)}, u32[]{:S(2)}, u32[]{:S(2)}) collective-permute-start(bf16[80,1536]{1,0:T(8,128)(2,1)S(1)} %collective-permute-done.7), channel_id=1, source_target_pairs={{0,48},{16,32},{32,16},{48,0},{64,112},{80,96},{96,80},{112,64},{1... | collective-permute-start | bytes 737288 | tf_op jit(solution)/shard_map/ppermute | solution.py:114
  117.0 1.9 collective-permute-start.8
  118.9 3.1 %collective-permute-start.9 = (bf16[80,1536]{1,0:T(8,128)(2,1)S(1)}, bf16[80,1536]{1,0:T(8,128)(2,1)S(1)}, u32[]{:S(2)}, u32[]{:S(2)}) collective-permute-start(bf16[80,1536]{1,0:T(8,128)(2,1)S(1)} %collective-permute-done.7), channel_id=1, source_target_pairs={{0,32},{16,48},{32,0},{48,16},{64,96},{80,112},{96,64},{112,80},{1... | collective-permute-start | bytes 737288 | tf_op jit(solution)/shard_map/ppermute | solution.py:116
  123.5 4.2 %collective-permute-done.10 = bf16[80,1536]{1,0:T(8,128)(2,1)S(1)} collective-permute-done((bf16[80,1536]{1,0:T(8,128)(2,1)S(1)}, bf16[80,1536]{1,0:T(8,128)(2,1)S(1)}, u32[]{:S(2)}, u32[]{:S(2)}) %collective-permute-start.10) | collective-permute-done | bytes 245792 | tf_op jit(solution)/shard_map/ppermute | solution.py:114
  127.8 2.8 collective-permute-done.8
  130.6 7.0 %collective-permute-done.9 = bf16[80,1536]{1,0:T(8,128)(2,1)S(1)} collective-permute-done((bf16[80,1536]{1,0:T(8,128)(2,1)S(1)}, bf16[80,1536]{1,0:T(8,128)(2,1)S(1)}, u32[]{:S(2)}, u32[]{:S(2)}) %collective-permute-start.9) | collective-permute-done | bytes 245792 | tf_op jit(solution)/shard_map/ppermute | solution.py:116
  138.6 1.2 slice_bitcast_fusion
  142.3 1.9 convolution_convert_fusion.2
  144.2 2.4 convolution_convert_fusion
  146.6 1.2 copy-done.3
  147.8 19.3 %all_to_all.35 = bf16[8,40,1536]{2,1,0:T(8,128)(2,1)S(1)} all-to-all(bf16[8,40,1536]{2,1,0:T(8,128)(2,1)S(1)} %bitcast.118), channel_id=1, replica_groups={{0,1,4,5,8,9,12,13},{2,3,6,7,10,11,14,15},{16,17,20,21,24,25,28,29},{18..., dimensions={0} | all-to-all | bytes 1966080 | tf_op jit(solution)/shard_map/all_to_all | solution.py:47
  167.5 8.1 %collective-permute-start.12 = (bf16[40,1536]{1,0:T(8,128)(2,1)S(1)}, bf16[40,1536]{1,0:T(8,128)(2,1)S(1)}, u32[]{:S(2)}, u32[]{:S(2)}) collective-permute-start(bf16[40,1536]{1,0:T(8,128)(2,1)S(1)} %multiply_convert_fusion.1), channel_id=1, source_target_pairs={{0,258},{1,259},{4,262},{5,263},{8,266},{9,267},{12,270},{13,271},... | collective-permute-start | bytes 368648 | tf_op jit(solution)/shard_map/ppermute | solution.py:39
  175.6 1.9 collective-permute-start.11
  178.0 3.2 %collective-permute-done.12 = bf16[40,1536]{1,0:T(8,128)(2,1)S(1)} collective-permute-done((bf16[40,1536]{1,0:T(8,128)(2,1)S(1)}, bf16[40,1536]{1,0:T(8,128)(2,1)S(1)}, u32[]{:S(2)}, u32[]{:S(2)}) %collective-permute-start.12) | collective-permute-done | bytes 122912 | tf_op jit(solution)/shard_map/ppermute | solution.py:39
  181.2 11.3 %collective-permute-done.11 = bf16[40,1536]{1,0:T(8,128)(2,1)S(1)} collective-permute-done((bf16[40,1536]{1,0:T(8,128)(2,1)S(1)}, bf16[40,1536]{1,0:T(8,128)(2,1)S(1)}, u32[]{:S(2)}, u32[]{:S(2)}) %collective-permute-start.11) | collective-permute-done | bytes 122912 | tf_op jit(solution)/shard_map/ppermute | solution.py:39
  193.6 4.0 %all-to-all-start.3 = ((bf16[8,40,1536]{2,1,0:T(8,128)(2,1)}), bf16[8,40,1536]{2,1,0:T(8,128)(2,1)S(1)}, u32[]{:S(2)}, u32[]{:S(2)}) async-start(bf16[8,40,1536]{2,1,0:T(8,128)(2,1)} %broadcast_in_dim.38), calls=%async_computation.4 | async-start | bytes 1966080 | tf_op jit(solution)/shard_map/all_to_all | solution.py:47
  197.5 1.9 collective-permute-start.13
  199.6 8.0 %collective-permute-done.13 = bf16[72,1536]{1,0:T(8,128)(2,1)S(1)} collective-permute-done((bf16[72,1536]{1,0:T(8,128)(2,1)S(1)}, bf16[72,1536]{1,0:T(8,128)(2,1)S(1)}, u32[]{:S(2)}, u32[]{:S(2)}) %collective-permute-start.13) | collective-permute-done | bytes 221216 | tf_op jit(solution)/shard_map/ppermute | solution.py:39
  207.5 4.4 %all-to-all-done.3 = bf16[8,40,1536]{2,1,0:T(8,128)(2,1)S(1)} async-done(((bf16[8,40,1536]{2,1,0:T(8,128)(2,1)}), bf16[8,40,1536]{2,1,0:T(8,128)(2,1)S(1)}, u32[]{:S(2)}, u32[]{:S(2)}) %all-to-all-start.3) | async-done | bytes 983072 | tf_op jit(solution)/shard_map/all_to_all | solution.py:47
  213.1 3.5 %all-to-all-start.4 = ((bf16[16,24,384]{2,1,0:T(8,128)(2,1)}), bf16[16,24,384]{2,1,0:T(8,128)(2,1)S(1)}, u32[]{:S(2)}, u32[]{:S(2)}) async-start(bf16[16,24,384]{2,1,0:T(8,128)(2,1)} %bitcast.33), calls=%async_computation.5 | async-start | bytes 589824 | tf_op jit(solution)/shard_map/all_to_all | solution.py:47
  216.8 4.1 %collective-permute-start.15 = (bf16[18,1536]{1,0:T(8,128)(2,1)S(1)}, bf16[18,1536]{1,0:T(8,128)(2,1)S(1)}, u32[]{:S(2)}, u32[]{:S(2)}) collective-permute-start(bf16[18,1536]{1,0:T(8,128)(2,1)S(1)} %select_convert_fusion.1), channel_id=1, source_target_pairs={{0,128},{1,129},{4,132},{5,133},{8,136},{9,137},{12,140},{13,141},... | collective-permute-start | bytes 165896 | tf_op jit(solution)/shard_map/ppermute | solution.py:39
  220.9 3.2 %collective-permute-start.16 = (bf16[18,1536]{1,0:T(8,128)(2,1)S(1)}, bf16[18,1536]{1,0:T(8,128)(2,1)S(1)}, u32[]{:S(2)}, u32[]{:S(2)}) collective-permute-start(bf16[18,1536]{1,0:T(8,128)(2,1)S(1)} %get-tuple-element.39), channel_id=1, source_target_pairs={{0,192},{1,193},{4,196},{5,197},{8,200},{9,201},{12,204},{13,205},... | collective-permute-start | bytes 165896 | tf_op jit(solution)/shard_map/ppermute | solution.py:39
  224.2 1.9 collective-permute-start.14
  226.1 1.5 all-to-all-done.4
  227.7 8.6 %collective-permute-done.15 = bf16[18,1536]{1,0:T(8,128)(2,1)S(1)} collective-permute-done((bf16[18,1536]{1,0:T(8,128)(2,1)S(1)}, bf16[18,1536]{1,0:T(8,128)(2,1)S(1)}, u32[]{:S(2)}, u32[]{:S(2)}) %collective-permute-start.15) | collective-permute-done | bytes 55328 | tf_op jit(solution)/shard_map/ppermute | solution.py:39
  236.3 1.6 collective-permute-done.14
  237.9 1.9 collective-permute-start.19
  239.9 6.6 %collective-permute-done.19 = bf16[24,384]{1,0:T(8,128)(2,1)S(1)} collective-permute-done((bf16[24,384]{1,0:T(8,128)(2,1)S(1)}, bf16[24,384]{1,0:T(8,128)(2,1)S(1)}, u32[]{:S(2)}, u32[]{:S(2)}) %collective-permute-start.19) | collective-permute-done | bytes 18464 | tf_op jit(solution)/shard_map/ppermute | solution.py:155
  247.3 5.2 %all-to-all-start.5 = ((bf16[16,24,384]{2,1,0:T(8,128)(2,1)}), bf16[16,24,384]{2,1,0:T(8,128)(2,1)S(1)}, u32[]{:S(2)}, u32[]{:S(2)}) async-start(bf16[16,24,384]{2,1,0:T(8,128)(2,1)} %broadcast_in_dim.39), calls=%async_computation.6 | async-start | bytes 589824 | tf_op jit(solution)/shard_map/all_to_all | solution.py:47
  253.0 2.9 collective-permute-start.18
  255.9 6.3 %collective-permute-start.17 = (bf16[8,18,96]{2,0,1:T(8,128)(2,1)S(1)}, bf16[8,18,96]{2,0,1:T(8,128)(2,1)S(1)}, u32[]{:S(2)}, u32[]{:S(2)}) collective-permute-start(bf16[8,18,96]{2,0,1:T(8,128)(2,1)S(1)} %bitcast.133), channel_id=1, source_target_pairs={{0,258},{1,259},{4,262},{5,263},{8,266},{9,267},{12,270},{13,271},... | collective-permute-start | bytes 82952 | tf_op jit(solution)/shard_map/ppermute | solution.py:39
  265.3 9.6 %all-to-all-start.6 = ((bf16[8,36,96]{2,1,0:T(8,128)(2,1)}), bf16[8,36,96]{2,1,0:T(8,128)(2,1)S(1)}, u32[]{:S(2)}, u32[]{:S(2)}) async-start(bf16[8,36,96]{2,1,0:T(8,128)(2,1)} %copy.91), calls=%async_computation.7 | async-start | bytes 163840 | tf_op jit(solution)/shard_map/all_to_all | solution.py:47
  275.9 3.9 %all-to-all-done.6 = bf16[8,36,96]{2,1,0:T(8,128)(2,1)S(1)} async-done(((bf16[8,36,96]{2,1,0:T(8,128)(2,1)}), bf16[8,36,96]{2,1,0:T(8,128)(2,1)S(1)}, u32[]{:S(2)}, u32[]{:S(2)}) %all-to-all-start.6) | async-done | bytes 55328 | tf_op jit(solution)/shard_map/all_to_all | solution.py:47
  (113 shorter events, 22.2 us)
Async XLA Ops:
  9.1 18.6 %collective-permute-start.1 = (bf16[288,98]{1,0:T(8,128)(2,1)S(1)}, bf16[288,98]{1,0:T(8,128)(2,1)S(1)}, u32[]{:S(2)}, u32[]{:S(2)}) collective-permute-start(bf16[288,98]{1,0:T(8,128)(2,1)S(1)} %pad_maximum_fusion.5), channel_id=1, source_target_pairs={{0,258},{1,259},{4,262},{5,263},{8,266},{9,267},{12,270},{13,271},... | collective-permute-start | bytes 169352 | tf_op jit(solution)/shard_map/ppermute | solution.py:39
  22.4 9.3 %collective-permute-start = (bf16[288,98]{1,0:T(8,128)(2,1)S(1)}, bf16[288,98]{1,0:T(8,128)(2,1)S(1)}, u32[]{:S(2)}, u32[]{:S(2)}) collective-permute-start(bf16[288,98]{1,0:T(8,128)(2,1)S(1)} %pad_maximum_fusion.5), channel_id=1, source_target_pairs={{0,256},{1,257},{4,260},{5,261},{8,264},{9,265},{12,268},{13,269},... | collective-permute-start | bytes 169352 | tf_op jit(solution)/shard_map/ppermute | solution.py:39
  32.7 24.0 %all-to-all-start = ((bf16[8,40,1730]{2,1,0:T(8,128)(2,1)}), bf16[8,40,1730]{2,1,0:T(8,128)(2,1)S(1)}, u32[]{:S(2)}, u32[]{:S(2)}) async-start(bf16[8,40,1730]{2,1,0:T(8,128)(2,1)} %bitcast.2), calls=%async_computation | async-start | bytes 2293760 | tf_op jit(solution)/shard_map/all_to_all | solution.py:47
  58.2 19.4 %collective-permute-start.6 = (bf16[24,1536]{1,0:T(8,128)(2,1)S(1)}, bf16[24,1536]{1,0:T(8,128)(2,1)S(1)}, u32[]{:S(2)}, u32[]{:S(2)}) collective-permute-start(bf16[24,1536]{1,0:T(8,128)(2,1)S(1)} %get-tuple-element.44), channel_id=1, source_target_pairs={{0,192},{16,208},{32,224},{48,240},{64,128},{80,144},{96,160},{112... | collective-permute-start | bytes 221192 | tf_op jit(solution)/shard_map/ppermute | solution.py:100
  64.2 13.5 %collective-permute-start.5 = (bf16[24,1536]{1,0:T(8,128)(2,1)S(1)}, bf16[24,1536]{1,0:T(8,128)(2,1)S(1)}, u32[]{:S(2)}, u32[]{:S(2)}) collective-permute-start(bf16[24,1536]{1,0:T(8,128)(2,1)S(1)} %get-tuple-element.45), channel_id=1, source_target_pairs={{0,128},{16,144},{32,160},{48,176},{64,192},{80,208},{96,224},{112... | collective-permute-start | bytes 221192 | tf_op jit(solution)/shard_map/ppermute | solution.py:100
  66.1 11.6 %collective-permute-start.4 = (bf16[24,1536]{1,0:T(8,128)(2,1)S(1)}, bf16[24,1536]{1,0:T(8,128)(2,1)S(1)}, u32[]{:S(2)}, u32[]{:S(2)}) collective-permute-start(bf16[24,1536]{1,0:T(8,128)(2,1)S(1)} %get-tuple-element.46), channel_id=1, source_target_pairs={{0,64},{16,80},{32,96},{48,112},{64,0},{80,16},{96,32},{112,48},{1... | collective-permute-start | bytes 221192 | tf_op jit(solution)/shard_map/ppermute | solution.py:100
  68.4 9.8 %collective-permute-start.2 = (bf16[40,1536]{1,0:T(8,128)(2,1)S(1)}, bf16[40,1536]{1,0:T(8,128)(2,1)S(1)}, u32[]{:S(2)}, u32[]{:S(2)}) collective-permute-start(bf16[40,1536]{1,0:T(8,128)(2,1)S(1)} %slice_reduce_fusion), channel_id=1, source_target_pairs={{0,256},{1,257},{4,260},{5,261},{8,264},{9,265},{12,268},{13,269},... | collective-permute-start | bytes 368648 | tf_op jit(solution)/shard_map/ppermute | solution.py:39
  70.4 13.1 %collective-permute-start.3 = (bf16[40,1536]{1,0:T(8,128)(2,1)S(1)}, bf16[40,1536]{1,0:T(8,128)(2,1)S(1)}, u32[]{:S(2)}, u32[]{:S(2)}) collective-permute-start(bf16[40,1536]{1,0:T(8,128)(2,1)S(1)} %slice_reduce_fusion), channel_id=1, source_target_pairs={{0,258},{1,259},{4,262},{5,263},{8,266},{9,267},{12,270},{13,271},... | collective-permute-start | bytes 368648 | tf_op jit(solution)/shard_map/ppermute | solution.py:39
  84.7 34.2 %all-to-all-start.1 = ((bf16[8,40,1536]{2,1,0:T(8,128)(2,1)}), bf16[8,40,1536]{2,1,0:T(8,128)(2,1)S(1)}, u32[]{:S(2)}, u32[]{:S(2)}) async-start(bf16[8,40,1536]{2,1,0:T(8,128)(2,1)} %broadcast_in_dim.19), calls=%async_computation.1 | async-start | bytes 1966080 | tf_op jit(solution)/shard_map/all_to_all | solution.py:47
  94.1 43.7 %all-gather.3.cloned.1.call-start = ((), (), s32[]{:S(2)}) async-start(), calls=%async_computation.9 | async-start | bytes 1351680 | tf_op jit(solution)/shard_map/all_gather | solution.py:106
  95.0 97.5 %reduce-scatter.2.cloned.1.call-start = ((), (), s32[]{:S(2)}) async-start(), calls=%async_computation.8 | async-start | bytes 2211840 | tf_op jit(solution)/shard_map/reduce_scatter | solution.py:135
  96.0 16.3 %collective-permute-start.7 = (bf16[80,1536]{1,0:T(8,128)(2,1)S(1)}, bf16[80,1536]{1,0:T(8,128)(2,1)S(1)}, u32[]{:S(2)}, u32[]{:S(2)}) collective-permute-start(bf16[80,1536]{1,0:T(8,128)(2,1)S(1)} %slice.153), channel_id=1, source_target_pairs={{0,450},{1,451},{4,454},{5,455},{8,458},{9,459},{12,462},{13,463},... | collective-permute-start | bytes 737288 | tf_op jit(solution)/shard_map/ppermute | solution.py:39
  112.3 15.4 %collective-permute-start.10 = (bf16[80,1536]{1,0:T(8,128)(2,1)S(1)}, bf16[80,1536]{1,0:T(8,128)(2,1)S(1)}, u32[]{:S(2)}, u32[]{:S(2)}) collective-permute-start(bf16[80,1536]{1,0:T(8,128)(2,1)S(1)} %collective-permute-done.7), channel_id=1, source_target_pairs={{0,48},{16,32},{32,16},{48,0},{64,112},{80,96},{96,80},{112,64},{1... | collective-permute-start | bytes 737288 | tf_op jit(solution)/shard_map/ppermute | solution.py:114
  117.0 13.6 %collective-permute-start.8 = (bf16[80,1536]{1,0:T(8,128)(2,1)S(1)}, bf16[80,1536]{1,0:T(8,128)(2,1)S(1)}, u32[]{:S(2)}, u32[]{:S(2)}) collective-permute-start(bf16[80,1536]{1,0:T(8,128)(2,1)S(1)} %collective-permute-done.7), channel_id=1, source_target_pairs={{0,16},{16,0},{32,48},{48,32},{64,80},{80,64},{96,112},{112,96},{1... | collective-permute-start | bytes 737288 | tf_op jit(solution)/shard_map/ppermute | solution.py:114
  118.9 18.9 %copy-start.1 = (bf16[8,40,1536]{2,1,0:T(8,128)(2,1)}, bf16[8,40,1536]{2,1,0:T(8,128)(2,1)S(1)}, u32[]{:S(2)}) copy-start(bf16[8,40,1536]{2,1,0:T(8,128)(2,1)S(1)} %all-to-all-done.1) | copy-start | bytes 2949124
  118.9 18.7 %collective-permute-start.9 = (bf16[80,1536]{1,0:T(8,128)(2,1)S(1)}, bf16[80,1536]{1,0:T(8,128)(2,1)S(1)}, u32[]{:S(2)}, u32[]{:S(2)}) collective-permute-start(bf16[80,1536]{1,0:T(8,128)(2,1)S(1)} %collective-permute-done.7), channel_id=1, source_target_pairs={{0,32},{16,48},{32,0},{48,16},{64,96},{80,112},{96,64},{112,80},{1... | collective-permute-start | bytes 737288 | tf_op jit(solution)/shard_map/ppermute | solution.py:116
  140.0 1.2 copy-start.2
  146.6 1.2 copy-start.3
  167.5 13.7 %collective-permute-start.12 = (bf16[40,1536]{1,0:T(8,128)(2,1)S(1)}, bf16[40,1536]{1,0:T(8,128)(2,1)S(1)}, u32[]{:S(2)}, u32[]{:S(2)}) collective-permute-start(bf16[40,1536]{1,0:T(8,128)(2,1)S(1)} %multiply_convert_fusion.1), channel_id=1, source_target_pairs={{0,258},{1,259},{4,262},{5,263},{8,266},{9,267},{12,270},{13,271},... | collective-permute-start | bytes 368648 | tf_op jit(solution)/shard_map/ppermute | solution.py:39
  175.6 16.9 %collective-permute-start.11 = (bf16[40,1536]{1,0:T(8,128)(2,1)S(1)}, bf16[40,1536]{1,0:T(8,128)(2,1)S(1)}, u32[]{:S(2)}, u32[]{:S(2)}) collective-permute-start(bf16[40,1536]{1,0:T(8,128)(2,1)S(1)} %multiply_convert_fusion.1), channel_id=1, source_target_pairs={{0,256},{1,257},{4,260},{5,261},{8,264},{9,265},{12,268},{13,269},... | collective-permute-start | bytes 368648 | tf_op jit(solution)/shard_map/ppermute | solution.py:39
  192.5 5.0 %copy-start.4 = (bf16[1,144,1536]{2,1,0:T(8,128)(2,1)S(1)}, bf16[1,144,1536]{2,1,0:T(8,128)(2,1)}, u32[]{:S(2)}) copy-start(bf16[1,144,1536]{2,1,0:T(8,128)(2,1)} %reduce-scatter.2.cloned.1.call-done) | copy-start | bytes 1327108
  193.6 18.4 %all-to-all-start.3 = ((bf16[8,40,1536]{2,1,0:T(8,128)(2,1)}), bf16[8,40,1536]{2,1,0:T(8,128)(2,1)S(1)}, u32[]{:S(2)}, u32[]{:S(2)}) async-start(bf16[8,40,1536]{2,1,0:T(8,128)(2,1)} %broadcast_in_dim.38), calls=%async_computation.4 | async-start | bytes 1966080 | tf_op jit(solution)/shard_map/all_to_all | solution.py:47
  197.5 10.0 %collective-permute-start.13 = (bf16[72,1536]{1,0:T(8,128)(2,1)S(1)}, bf16[72,1536]{1,0:T(8,128)(2,1)S(1)}, u32[]{:S(2)}, u32[]{:S(2)}) collective-permute-start(bf16[72,1536]{1,0:T(8,128)(2,1)S(1)} %slice_bitcast_fusion.1), channel_id=1, source_target_pairs={{0,450},{1,451},{4,454},{5,455},{8,458},{9,459},{12,462},{13,463},... | collective-permute-start | bytes 663560 | tf_op jit(solution)/shard_map/ppermute | solution.py:39
  213.1 14.5 %all-to-all-start.4 = ((bf16[16,24,384]{2,1,0:T(8,128)(2,1)}), bf16[16,24,384]{2,1,0:T(8,128)(2,1)S(1)}, u32[]{:S(2)}, u32[]{:S(2)}) async-start(bf16[16,24,384]{2,1,0:T(8,128)(2,1)} %bitcast.33), calls=%async_computation.5 | async-start | bytes 589824 | tf_op jit(solution)/shard_map/all_to_all | solution.py:47
  216.8 19.5 %collective-permute-start.15 = (bf16[18,1536]{1,0:T(8,128)(2,1)S(1)}, bf16[18,1536]{1,0:T(8,128)(2,1)S(1)}, u32[]{:S(2)}, u32[]{:S(2)}) collective-permute-start(bf16[18,1536]{1,0:T(8,128)(2,1)S(1)} %select_convert_fusion.1), channel_id=1, source_target_pairs={{0,128},{1,129},{4,132},{5,133},{8,136},{9,137},{12,140},{13,141},... | collective-permute-start | bytes 165896 | tf_op jit(solution)/shard_map/ppermute | solution.py:39
  220.9 41.3 %copy-start = (bf16[96,1536]{1,0:T(8,128)(2,1)S(1)}, bf16[96,1536]{1,0:T(8,128)(2,1)}, u32[]{:S(2)}) copy-start(bf16[96,1536]{1,0:T(8,128)(2,1)} %param.7) | copy-start | bytes 884740
  220.9 15.4 %collective-permute-start.16 = (bf16[18,1536]{1,0:T(8,128)(2,1)S(1)}, bf16[18,1536]{1,0:T(8,128)(2,1)S(1)}, u32[]{:S(2)}, u32[]{:S(2)}) collective-permute-start(bf16[18,1536]{1,0:T(8,128)(2,1)S(1)} %get-tuple-element.39), channel_id=1, source_target_pairs={{0,192},{1,193},{4,196},{5,197},{8,200},{9,201},{12,204},{13,205},... | collective-permute-start | bytes 165896 | tf_op jit(solution)/shard_map/ppermute | solution.py:39
  224.2 13.8 %collective-permute-start.14 = (bf16[18,1536]{1,0:T(8,128)(2,1)S(1)}, bf16[18,1536]{1,0:T(8,128)(2,1)S(1)}, u32[]{:S(2)}, u32[]{:S(2)}) collective-permute-start(bf16[18,1536]{1,0:T(8,128)(2,1)S(1)} %get-tuple-element.40), channel_id=1, source_target_pairs={{0,64},{1,65},{4,68},{5,69},{8,72},{9,73},{12,76},{13,77},{16,80},... | collective-permute-start | bytes 165896 | tf_op jit(solution)/shard_map/ppermute | solution.py:39
  237.9 8.6 %collective-permute-start.19 = (bf16[24,384]{1,0:T(8,128)(2,1)S(1)}, bf16[24,384]{1,0:T(8,128)(2,1)S(1)}, u32[]{:S(2)}, u32[]{:S(2)}) collective-permute-start(bf16[24,384]{1,0:T(8,128)(2,1)S(1)} %reduce-precision_convert_fusion), channel_id=1, source_target_pairs={{0,256},{16,272},{32,288},{48,304},{64,320},{80,336},{96,352},{112... | collective-permute-start | bytes 55304 | tf_op jit(solution)/shard_map/ppermute | solution.py:155
  247.3 17.4 %all-to-all-start.5 = ((bf16[16,24,384]{2,1,0:T(8,128)(2,1)}), bf16[16,24,384]{2,1,0:T(8,128)(2,1)S(1)}, u32[]{:S(2)}, u32[]{:S(2)}) async-start(bf16[16,24,384]{2,1,0:T(8,128)(2,1)} %broadcast_in_dim.39), calls=%async_computation.6 | async-start | bytes 589824 | tf_op jit(solution)/shard_map/all_to_all | solution.py:47
  253.0 10.5 %collective-permute-start.18 = (bf16[8,18,96]{2,0,1:T(8,128)(2,1)S(1)}, bf16[8,18,96]{2,0,1:T(8,128)(2,1)S(1)}, u32[]{:S(2)}, u32[]{:S(2)}) collective-permute-start(bf16[8,18,96]{2,0,1:T(8,128)(2,1)S(1)} %bitcast.135), channel_id=1, source_target_pairs={{0,256},{1,257},{4,260},{5,261},{8,264},{9,265},{12,268},{13,269},... | collective-permute-start | bytes 82952 | tf_op jit(solution)/shard_map/ppermute | solution.py:39
  255.9 8.8 %collective-permute-start.17 = (bf16[8,18,96]{2,0,1:T(8,128)(2,1)S(1)}, bf16[8,18,96]{2,0,1:T(8,128)(2,1)S(1)}, u32[]{:S(2)}, u32[]{:S(2)}) collective-permute-start(bf16[8,18,96]{2,0,1:T(8,128)(2,1)S(1)} %bitcast.133), channel_id=1, source_target_pairs={{0,258},{1,259},{4,262},{5,263},{8,266},{9,267},{12,270},{13,271},... | collective-permute-start | bytes 82952 | tf_op jit(solution)/shard_map/ppermute | solution.py:39
  265.3 14.5 %all-to-all-start.6 = ((bf16[8,36,96]{2,1,0:T(8,128)(2,1)}), bf16[8,36,96]{2,1,0:T(8,128)(2,1)S(1)}, u32[]{:S(2)}, u32[]{:S(2)}) async-start(bf16[8,36,96]{2,1,0:T(8,128)(2,1)} %copy.91), calls=%async_computation.7 | async-start | bytes 163840 | tf_op jit(solution)/shard_map/all_to_all | solution.py:47
Sparse Core Ops, SparseCore 0:
  97.6 35.0 all-gather.2
  146.7 34.4 reduce-scatter.1

commit v11 on v9

--- a/solution.py
+++ b/solution.py
@@ -8,6 +8,7 @@
 ZL, Y = 8, 4
 PLANE = [[x * 4 + zh * 2 + c for x in range(X) for c in range(CORE)] for zh in range(ZH)]
 RING = [[z * Y + y for y in range(Y)] for z in range(ZL)]
+PAIR = [(i, i ^ 2) for i in range(16)]
 SLAB = [[(q * 4 + i) * Y + y for y in range(Y) for i in range(4)] for q in range(ZL // 4)]
 ACROSS = [(i, i ^ (4 * Y)) for i in range(ZL * Y)]
 
@@ -23,8 +24,8 @@
 
 COLUMNS = [(y, x, c) for y in range(Y) for x in range(X) for c in range(CORE)]
 MIRROR = [(place(z, *at), place(mirror(z), *at)) for z in range(16) for at in COLUMNS]
-UP = [(place(z, *at), place(z + 4, *at)) for z in range(16) for at in COLUMNS]
-DOWN = [(place(z, *at), place(z - 4, *at)) for z in range(16) for at in COLUMNS]
+FOUR_UP = [(place(z, y, x, c), place(z + 4 - 8 * c, y, x, c)) for z in range(16) for y, x, c in COLUMNS]
+FOUR_DOWN = [(place(z, y, x, c), place(z - 4 + 8 * c, y, x, c)) for z in range(16) for y, x, c in COLUMNS]
 
 
 def across(by):
@@ -99,10 +100,10 @@
     quad = jnp.concatenate([blocks[:, :share].reshape(count, embed_width), blocks[:, share]], axis=0)
     quad = jnp.pad(quad, ((0, 12), (0, 0)))
 
+
     near = lax.all_gather(quad, "dp", axis_index_groups=RING)
-    embed = send(half, UP).astype(F32) + send(half, DOWN).astype(F32)
+    embed = send(half, FOUR_UP).astype(F32) + send(half, FOUR_DOWN).astype(F32)
     crossed = send(quad[: count + 8], MIRROR)
-    embed, crossed = lax.optimization_barrier((embed, crossed))
 
     image_scale = lax.rsqrt(jnp.sum(embed * embed, axis=1, keepdims=True) + 1e-06)
     image_unit = embed * image_scale
@@ -110,30 +111,31 @@
     y = d % Y
     far = [crossed] + [lax.ppermute(crossed, "dp", [(i, i ^ by) for i in range(cycle)]) for by in (1, 2, 3)]
     far = jnp.stack([pick(y ^ i, far) for i in range(Y)])
-    lines = (near, far)
-    text_low = jnp.stack([part[:, :count] for part in lines], axis=1).reshape(cycle * share, embed_width)
-    notes = jnp.stack([part[:, count : count + 4, : 2 * share] for part in lines], axis=1).astype(jnp.int32)
-    ids = (notes[..., :share] * 128 + notes[..., share:]).reshape(cycle * share)
 
-    partial_value = jnp.einsum("ie,je->ij", image_low, text_low, preferred_element_type=F32)
-    logits = logit_scale * partial_value + logit_bias
     row = lax.broadcasted_iota(jnp.int32, (plane, held), 1)
     row_index = (d ^ (4 * Y)) * rows + lax.broadcasted_iota(jnp.int32, (plane, held), 0) * own + row
     row_index = jnp.where(row < own, row_index, -1).reshape(plane * held, 1)
-    sign = jnp.where(row_index == ids[None, :], 1.0, -1.0).astype(F32)
-    coef = (-sign * jax.nn.sigmoid(-sign * logits) * logit_scale).astype(BF16)
-    unit_part = jnp.einsum("ij,je->ie", coef, text_low, preferred_element_type=F32).astype(BF16)
-    unit_part, coef = lax.optimization_barrier((unit_part, coef))
-    text_acc = jnp.einsum("ij,ie->je", coef, image_low, preferred_element_type=F32).astype(BF16)
+    unit_part, text_acc = 0.0, []
+    for part in (near, far):
+        texts = part[:, :count].reshape(Y * count, embed_width)
+        notes = part[:, count : count + 4, : 2 * share].astype(jnp.int32)
+        ids = (notes[..., :share] * 128 + notes[..., share:]).reshape(Y * count)
+        partial_value = jnp.einsum("ie,je->ij", image_low, texts, preferred_element_type=F32)
+        logits = logit_scale * partial_value + logit_bias
+        sign = jnp.where(row_index == ids[None, :], 1.0, -1.0).astype(F32)
+        coef = (-sign * jax.nn.sigmoid(-sign * logits) * logit_scale).astype(BF16)
+        coef, image_low = lax.optimization_barrier((coef, image_low))
+        unit_part = unit_part + jnp.einsum("ij,je->ie", coef, texts, preferred_element_type=F32)
+        acc = jnp.einsum("ij,ie->je", coef, image_low, preferred_element_type=F32).astype(BF16)
+        text_acc.append(lax.psum_scatter(acc.reshape(Y, count, embed_width), "dp", axis_index_groups=RING))
+    unit_part = unit_part.astype(BF16)
 
-    text_acc = lax.psum_scatter(text_acc.reshape(Y, ZL * share, embed_width), "dp", axis_index_groups=RING)
     back = swap(unit_part.reshape(plane, held, embed_width), "fsdp", PLANE)
     unit_grad = jnp.sum(back.astype(F32), axis=0)
     image_dot = jnp.sum(image_unit * unit_grad, axis=1, keepdims=True)
     embed_grad = (image_scale * (unit_grad - image_unit * image_dot)).astype(BF16)
-    embed_grad = (send(embed_grad, UP).astype(F32) + send(embed_grad, DOWN).astype(F32)).astype(BF16)
-    text_acc = text_acc.reshape(2, count, embed_width)
-    embed_grad, text_acc = lax.optimization_barrier((embed_grad, text_acc))
+    embed_grad = (send(embed_grad, FOUR_UP).astype(F32) + send(embed_grad, FOUR_DOWN).astype(F32)).astype(BF16)
+    embed_grad, *text_acc = lax.optimization_barrier((embed_grad, *text_acc))
     crossed = send(text_acc[1], MIRROR)
     grads = spread(embed_grad, "fsdp", PLANE, plane).reshape(plane * held, embed_width)
     grads, crossed = lax.optimization_barrier((grads, crossed))
@@ -147,20 +149,21 @@
     head_sum, *parts = lax.optimization_barrier((head_sum, *parts))
     head_sum = lax.reduce_precision(head_sum, 8, 7)
     head_sum = head_sum + lax.ppermute(head_sum.astype(BF16), "dp", ACROSS).astype(F32)
+    head_all = spread(head_sum.astype(BF16), "dp", SLAB, 4 * Y)
+
     text_acc = pick(i, text_acc)
     for part in parts:
         text_acc = text_acc + part.astype(F32)
     text_dot = jnp.sum(text_unit * text_acc, axis=1, keepdims=True)
     text_rows = (text_scale * (text_acc - text_unit * text_dot)).astype(BF16)
-    text_rows = text_rows.reshape(share, group, width).transpose(1, 0, 2)
-    text_grad = swap(text_rows, "fsdp")
-    text_grad, head_sum = lax.optimization_barrier((text_grad, head_sum))
-    text_grad = text_grad.reshape(X, ZH, CORE, share, width)
-    text_grad = jnp.where(zl < 6, text_grad, text_grad[:, ::-1])
-    text_grad = text_grad.transpose(0, 2, 1, 3, 4).reshape(rows, width)
-
-    head_all = spread(head_sum.astype(BF16), "dp", SLAB, 4 * Y).reshape(Y, 4, width // Y, embed_width // 4)
-    head_all = head_all.transpose(0, 2, 1, 3).reshape(width, embed_width)
+    text_rows = text_rows.reshape(share, X, ZH, CORE, width).transpose(2, 1, 3, 0, 4)
+    text_rows = text_rows.reshape(ZH, plane, share, width)
+    kept = jnp.where(zh == 0, text_rows[0], text_rows[1])
+    came = lax.ppermute(jnp.where(zh == 0, text_rows[1], text_rows[0]), "fsdp", PAIR)
+    text_grad = jnp.where(second, jnp.stack([came, kept], axis=1), jnp.stack([kept, came], axis=1))
+    text_grad, head_all = lax.optimization_barrier((text_grad.reshape(plane, own, width), head_all))
+    text_grad = swap(text_grad, "fsdp", PLANE).reshape(rows, width)
+    head_all = head_all.reshape(Y, 4, width // Y, embed_width // 4).transpose(0, 2, 1, 3).reshape(width, embed_width)
     head_grad = head_all.astype(F32)
     feature_grad = jnp.einsum("re,we->rw", grads, image_head, preferred_element_type=F32).astype(BF16)
     feature_grad = feature_grad.reshape(plane, held, width)[:, :own].reshape(rows, width)

time: 279 us -> 286 us (1.025)
  starting transfers between devices: 116 us -> 136 us
  blocking collectives: 17.8 us -> 0 us
  waiting for transfers between devices: 98.3 us -> 104 us
    reduce_scatter x1 -> x2, waiting for transfers between devices: 0.02 us -> 19.2 us  [on_device(): lax.psum_scatter(acc.reshape(Y, count, embed_width), 'dp', axis_index_gro...]
    all_to_all x1 -> x0, blocking collectives: 17.8 us -> none  [swap(): lax.all_to_all(value, axis, 0, 0, axis_index_groups=groups, tiled=True)]
    all_to_all x7 -> x8, waiting for transfers between devices: 51.4 us -> 38.2 us  [swap(): lax.all_to_all(value, axis, 0, 0, axis_index_groups=groups, tiled=True)]
    ppermute x0 -> x1, starting transfers between devices: none -> 11.3 us  [on_device(): lax.ppermute(jnp.where(zh == 0, text_rows[1], text_rows[0]), 'fsdp', PAIR)]
    ppermute x9, waiting for transfers between devices: 44.1 us -> 38.9 us  [send(): return lax.ppermute(value, ('dp', 'fsdp'), pairs)]
    ppermute x9, starting transfers between devices: 32.1 us -> 35.7 us  [send(): return lax.ppermute(value, ('dp', 'fsdp'), pairs)]
    ppermute x1, starting transfers between devices: 4.01 us -> 7.6 us  [on_device(): lax.ppermute(head_sum.astype(BF16), 'dp', ACROSS).astype(F32)]
    all_to_all x7 -> x8, starting transfers between devices: 58 us -> 59.5 us  [swap(): lax.all_to_all(value, axis, 0, 0, axis_index_groups=groups, tiled=True)]
  transfers between devices with their start and end apart: 25 -> 28, of which waited for: 15 -> 19; matrix products, arithmetic and copies ran while one was open for 5% -> 7% of each run, Pallas kernels for 0% -> 0%
where the time goes in v11:
time: 286 us; the launch traced here: 285 us
  starting transfers between devices  136 us (48%)
  waiting for transfers between devices  104 us (36%)
  between operations  15.6 us (5%)
  local copies, waits for them, and re-layouts  14 us (5%)
  matrix products  10.7 us (4%)
  other arithmetic  5.01 us (2%)
    all_to_all x8, starting transfers between devices, swap(): lax.all_to_all(value, axis, 0, 0, axis_index_groups=groups, tiled=True)  59.5 us
    ppermute x9, waiting for transfers between devices, send(): return lax.ppermute(value, ('dp', 'fsdp'), pairs)  38.9 us
    all_to_all x8, waiting for transfers between devices, swap(): lax.all_to_all(value, axis, 0, 0, axis_index_groups=groups, tiled=True)  38.2 us
    ppermute x9, starting transfers between devices, send(): return lax.ppermute(value, ('dp', 'fsdp'), pairs)  35.7 us
    reduce_scatter x2, waiting for transfers between devices, on_device(): lax.psum_scatter(acc.reshape(Y, count, embed_width), 'dp', axis_index_gro...  19.2 us
    ppermute x3, starting transfers between devices, on_device(): lax.ppermute(part, 'dp', [(i, i ^ by * Y) for i in range(cycle)])  12.8 us
    ppermute x1, starting transfers between devices, on_device(): lax.ppermute(jnp.where(zh == 0, text_rows[1], text_rows[0]), 'fsdp', PAIR)  11.3 us
    ppermute x3, starting transfers between devices, on_device(): lax.ppermute(crossed, 'dp', [(i, i ^ by) for i in range(cycle)])  9.04 us
  transfers between devices with their start and end apart: 28, of which 19 were waited for; matrix products, arithmetic and copies ran while one was open for 7% of the time, Pallas kernels for 0%

profile of v11, /device:TPU:1, one launch (start us, length us, event | category | flops | bytes accessed | tf_op | source)
XLA Modules:
  0.0 285.0 jit_solution(13263966450326768402)
XLA Ops:
  8.8 19.1 %all-to-all-start = ((bf16[16,36,96]{2,1,0:T(8,128)(2,1)}), bf16[16,36,96]{2,1,0:T(8,128)(2,1)S(1)}, u32[]{:S(2)}, u32[]{:S(2)}) async-start(bf16[16,36,96]{2,1,0:T(8,128)(2,1)} %bitcast.1), calls=%async_computation | async-start | bytes 327680 | tf_op jit(solution)/shard_map/all_to_all | solution.py:48
  29.8 1.4 convolution_convert_fusion
  31.2 11.9 %all-to-all-done = bf16[16,36,96]{2,1,0:T(8,128)(2,1)S(1)} async-done(((bf16[16,36,96]{2,1,0:T(8,128)(2,1)}), bf16[16,36,96]{2,1,0:T(8,128)(2,1)S(1)}, u32[]{:S(2)}, u32[]{:S(2)}) %all-to-all-start) | async-done | bytes 110624 | tf_op jit(solution)/shard_map/all_to_all | solution.py:48
  43.8 4.2 %all-to-all-start.1 = ((bf16[8,40,1536]{2,1,0:T(8,128)(2,1)}), bf16[8,40,1536]{2,1,0:T(8,128)(2,1)S(1)}, u32[]{:S(2)}, u32[]{:S(2)}) async-start(bf16[8,40,1536]{2,1,0:T(8,128)(2,1)} %bitcast.5), calls=%async_computation.1 | async-start | bytes 1966080 | tf_op jit(solution)/shard_map/all_to_all | solution.py:48
  48.0 7.1 %collective-permute-start.2 = (bf16[24,1536]{1,0:T(8,128)(2,1)S(1)}, bf16[24,1536]{1,0:T(8,128)(2,1)S(1)}, u32[]{:S(2)}, u32[]{:S(2)}) collective-permute-start(bf16[24,1536]{1,0:T(8,128)(2,1)S(1)} %get-tuple-element.59), channel_id=1, source_target_pairs={{0,192},{16,208},{32,224},{48,240},{64,128},{80,144},{96,160},{112... | collective-permute-start | bytes 221192 | tf_op jit(solution)/shard_map/ppermute | solution.py:94
  55.1 3.8 %collective-permute-start.1 = (bf16[24,1536]{1,0:T(8,128)(2,1)S(1)}, bf16[24,1536]{1,0:T(8,128)(2,1)S(1)}, u32[]{:S(2)}, u32[]{:S(2)}) collective-permute-start(bf16[24,1536]{1,0:T(8,128)(2,1)S(1)} %get-tuple-element.60), channel_id=1, source_target_pairs={{0,128},{16,144},{32,160},{48,176},{64,192},{80,208},{96,224},{112... | collective-permute-start | bytes 221192 | tf_op jit(solution)/shard_map/ppermute | solution.py:94
  59.0 1.9 collective-permute-start
  63.2 1.1 collective-permute-done
  64.4 3.1 %collective-permute-start.4 = (bf16[40,1536]{1,0:T(8,128)(2,1)S(1)}, bf16[40,1536]{1,0:T(8,128)(2,1)S(1)}, u32[]{:S(2)}, u32[]{:S(2)}) collective-permute-start(bf16[40,1536]{1,0:T(8,128)(2,1)S(1)} %reduce_sum.67), channel_id=1, source_target_pairs={{0,258},{1,257},{4,262},{5,261},{8,266},{9,265},{12,270},{13,269},... | collective-permute-start | bytes 368648 | tf_op jit(solution)/shard_map/ppermute | solution.py:40
  67.5 6.1 %collective-permute-start.3 = (bf16[40,1536]{1,0:T(8,128)(2,1)S(1)}, bf16[40,1536]{1,0:T(8,128)(2,1)S(1)}, u32[]{:S(2)}, u32[]{:S(2)}) collective-permute-start(bf16[40,1536]{1,0:T(8,128)(2,1)S(1)} %reduce_sum.67), channel_id=1, source_target_pairs={{0,256},{1,259},{4,260},{5,263},{8,264},{9,267},{12,268},{13,271},... | collective-permute-start | bytes 368648 | tf_op jit(solution)/shard_map/ppermute | solution.py:40
  75.4 2.4 collective-permute-start.5
  77.9 1.5 collective-permute-done.3
  79.5 12.7 %collective-permute-done.5 = bf16[80,1536]{1,0:T(8,128)(2,1)S(1)} collective-permute-done((bf16[80,1536]{1,0:T(8,128)(2,1)S(1)}, bf16[80,1536]{1,0:T(8,128)(2,1)S(1)}, u32[]{:S(2)}, u32[]{:S(2)}) %collective-permute-start.5) | collective-permute-done | bytes 245792 | tf_op jit(solution)/shard_map/ppermute | solution.py:40
  92.2 4.6 %collective-permute-start.8 = (bf16[80,1536]{1,0:T(8,128)(2,1)S(1)}, bf16[80,1536]{1,0:T(8,128)(2,1)S(1)}, u32[]{:S(2)}, u32[]{:S(2)}) collective-permute-start(bf16[80,1536]{1,0:T(8,128)(2,1)S(1)} %collective-permute-done.5), channel_id=1, source_target_pairs={{0,48},{16,32},{32,16},{48,0},{64,112},{80,96},{96,80},{112,64},{1... | collective-permute-start | bytes 737288 | tf_op jit(solution)/shard_map/ppermute | solution.py:112
  96.8 2.3 collective-permute-start.7
  99.1 2.1 collective-permute-start.6
  102.4 5.7 %all-to-all-start.2 = ((bf16[8,40,1536]{2,1,0:T(8,128)(2,1)}), bf16[8,40,1536]{2,1,0:T(8,128)(2,1)S(1)}, u32[]{:S(2)}, u32[]{:S(2)}) async-start(bf16[8,40,1536]{2,1,0:T(8,128)(2,1)} %broadcast_in_dim.49), calls=%async_computation.2 | async-start | bytes 1966080 | tf_op jit(solution)/shard_map/all_to_all | solution.py:48
  108.1 3.0 %collective-permute-done.8 = bf16[80,1536]{1,0:T(8,128)(2,1)S(1)} collective-permute-done((bf16[80,1536]{1,0:T(8,128)(2,1)S(1)}, bf16[80,1536]{1,0:T(8,128)(2,1)S(1)}, u32[]{:S(2)}, u32[]{:S(2)}) %collective-permute-start.8) | collective-permute-done | bytes 245792 | tf_op jit(solution)/shard_map/ppermute | solution.py:112
  112.6 1.2 slice.128
  114.7 7.7 %all-to-all-done.2 = bf16[8,40,1536]{2,1,0:T(8,128)(2,1)S(1)} async-done(((bf16[8,40,1536]{2,1,0:T(8,128)(2,1)}), bf16[8,40,1536]{2,1,0:T(8,128)(2,1)S(1)}, u32[]{:S(2)}, u32[]{:S(2)}) %all-to-all-start.2) | async-done | bytes 983072 | tf_op jit(solution)/shard_map/all_to_all | solution.py:48
  122.5 1.4 fusion.18
  125.3 1.5 convolution_convert_fusion.1
  126.8 1.7 fusion.35
  128.5 1.7 fusion
  130.2 4.5 %all-to-all-start.3 = ((bf16[8,40,1536]{2,1,0:T(8,128)(2,1)}), bf16[8,40,1536]{2,1,0:T(8,128)(2,1)S(1)}, u32[]{:S(2)}, u32[]{:S(2)}) async-start(bf16[8,40,1536]{2,1,0:T(8,128)(2,1)} %bitcast.22), calls=%async_computation.3 | async-start | bytes 1966080 | tf_op jit(solution)/shard_map/all_to_all | solution.py:48
  134.7 1.5 convolution_convert_fusion.2
  136.3 12.8 %all-to-all-done.3 = bf16[8,40,1536]{2,1,0:T(8,128)(2,1)S(1)} async-done(((bf16[8,40,1536]{2,1,0:T(8,128)(2,1)}), bf16[8,40,1536]{2,1,0:T(8,128)(2,1)S(1)}, u32[]{:S(2)}, u32[]{:S(2)}) %all-to-all-start.3) | async-done | bytes 983072 | tf_op jit(solution)/shard_map/all_to_all | solution.py:48
  149.6 5.9 %collective-permute-start.10 = (bf16[40,1536]{1,0:T(8,128)(2,1)S(1)}, bf16[40,1536]{1,0:T(8,128)(2,1)S(1)}, u32[]{:S(2)}, u32[]{:S(2)}) collective-permute-start(bf16[40,1536]{1,0:T(8,128)(2,1)S(1)} %multiply_convert_fusion.1), channel_id=1, source_target_pairs={{0,258},{1,257},{4,262},{5,261},{8,266},{9,265},{12,270},{13,269},... | collective-permute-start | bytes 368648 | tf_op jit(solution)/shard_map/ppermute | solution.py:40
  155.4 3.3 %collective-permute-start.9 = (bf16[40,1536]{1,0:T(8,128)(2,1)S(1)}, bf16[40,1536]{1,0:T(8,128)(2,1)S(1)}, u32[]{:S(2)}, u32[]{:S(2)}) collective-permute-start(bf16[40,1536]{1,0:T(8,128)(2,1)S(1)} %multiply_convert_fusion.1), channel_id=1, source_target_pairs={{0,256},{1,259},{4,260},{5,263},{8,264},{9,267},{12,268},{13,271},... | collective-permute-start | bytes 368648 | tf_op jit(solution)/shard_map/ppermute | solution.py:40
  158.8 1.6 collective-permute-done.10
  160.3 6.0 %collective-permute-done.9 = bf16[40,1536]{1,0:T(8,128)(2,1)S(1)} collective-permute-done((bf16[40,1536]{1,0:T(8,128)(2,1)S(1)}, bf16[40,1536]{1,0:T(8,128)(2,1)S(1)}, u32[]{:S(2)}, u32[]{:S(2)}) %collective-permute-start.9) | collective-permute-done | bytes 122912 | tf_op jit(solution)/shard_map/ppermute | solution.py:40
  166.4 19.2 %reduce-scatter.3.cloned.1.call-done = bf16[1,72,1536]{2,1,0:T(8,128)(2,1)} async-done(((bf16[4,72,1536]{2,1,0:T(8,128)(2,1)}), bf16[1,72,1536]{2,1,0:T(8,128)(2,1)}) %reduce-scatter.3.cloned.1.call-update) | async-done | bytes 221200 | tf_op jit(solution)/shard_map/reduce_scatter | solution.py:130
  186.6 6.2 %all-to-all-start.4 = ((bf16[8,40,1536]{2,1,0:T(8,128)(2,1)}), bf16[8,40,1536]{2,1,0:T(8,128)(2,1)S(1)}, u32[]{:S(2)}, u32[]{:S(2)}) async-start(bf16[8,40,1536]{2,1,0:T(8,128)(2,1)} %broadcast_in_dim.50), calls=%async_computation.6 | async-start | bytes 1966080 | tf_op jit(solution)/shard_map/all_to_all | solution.py:48
  193.0 5.8 %collective-permute-start.11 = (bf16[72,1536]{1,0:T(8,128)(2,1)S(1)}, bf16[72,1536]{1,0:T(8,128)(2,1)S(1)}, u32[]{:S(2)}, u32[]{:S(2)}) collective-permute-start(bf16[72,1536]{1,0:T(8,128)(2,1)S(1)} %bitcast.110), channel_id=1, source_target_pairs={{0,450},{1,451},{4,454},{5,455},{8,458},{9,459},{12,462},{13,463},... | collective-permute-start | bytes 663560 | tf_op jit(solution)/shard_map/ppermute | solution.py:40
  198.8 10.4 %collective-permute-done.11 = bf16[72,1536]{1,0:T(8,128)(2,1)S(1)} collective-permute-done((bf16[72,1536]{1,0:T(8,128)(2,1)S(1)}, bf16[72,1536]{1,0:T(8,128)(2,1)S(1)}, u32[]{:S(2)}, u32[]{:S(2)}) %collective-permute-start.11) | collective-permute-done | bytes 221216 | tf_op jit(solution)/shard_map/ppermute | solution.py:40
  210.5 4.3 %all-to-all-start.5 = ((bf16[16,24,384]{2,1,0:T(8,128)(2,1)}), bf16[16,24,384]{2,1,0:T(8,128)(2,1)S(1)}, u32[]{:S(2)}, u32[]{:S(2)}) async-start(bf16[16,24,384]{2,1,0:T(8,128)(2,1)} %bitcast.30), calls=%async_computation.7 | async-start | bytes 589824 | tf_op jit(solution)/shard_map/all_to_all | solution.py:48
  214.9 4.2 %collective-permute-start.13 = (bf16[18,1536]{1,0:T(8,128)(2,1)S(1)}, bf16[18,1536]{1,0:T(8,128)(2,1)S(1)}, u32[]{:S(2)}, u32[]{:S(2)}) collective-permute-start(bf16[18,1536]{1,0:T(8,128)(2,1)S(1)} %select_convert_fusion.1), channel_id=1, source_target_pairs={{0,128},{1,129},{4,132},{5,133},{8,136},{9,137},{12,140},{13,141},... | collective-permute-start | bytes 165896 | tf_op jit(solution)/shard_map/ppermute | solution.py:40
  219.1 3.1 %collective-permute-start.14 = (bf16[18,1536]{1,0:T(8,128)(2,1)S(1)}, bf16[18,1536]{1,0:T(8,128)(2,1)S(1)}, u32[]{:S(2)}, u32[]{:S(2)}) collective-permute-start(bf16[18,1536]{1,0:T(8,128)(2,1)S(1)} %get-tuple-element.53), channel_id=1, source_target_pairs={{0,192},{1,193},{4,196},{5,197},{8,200},{9,201},{12,204},{13,205},... | collective-permute-start | bytes 165896 | tf_op jit(solution)/shard_map/ppermute | solution.py:40
  222.2 1.9 collective-permute-start.12
  224.1 1.8 all-to-all-done.5
  226.0 2.9 %collective-permute-done.13 = bf16[18,1536]{1,0:T(8,128)(2,1)S(1)} collective-permute-done((bf16[18,1536]{1,0:T(8,128)(2,1)S(1)}, bf16[18,1536]{1,0:T(8,128)(2,1)S(1)}, u32[]{:S(2)}, u32[]{:S(2)}) %collective-permute-start.13) | collective-permute-done | bytes 55328 | tf_op jit(solution)/shard_map/ppermute | solution.py:40
  228.9 3.9 %collective-permute-done.12 = bf16[18,1536]{1,0:T(8,128)(2,1)S(1)} collective-permute-done((bf16[18,1536]{1,0:T(8,128)(2,1)S(1)}, bf16[18,1536]{1,0:T(8,128)(2,1)S(1)}, u32[]{:S(2)}, u32[]{:S(2)}) %collective-permute-start.12) | collective-permute-done | bytes 55328 | tf_op jit(solution)/shard_map/ppermute | solution.py:40
  232.7 7.6 %collective-permute-start.16 = (bf16[24,384]{1,0:T(8,128)(2,1)S(1)}, bf16[24,384]{1,0:T(8,128)(2,1)S(1)}, u32[]{:S(2)}, u32[]{:S(2)}) collective-permute-start(bf16[24,384]{1,0:T(8,128)(2,1)S(1)} %reduce-precision_convert_fusion), channel_id=1, source_target_pairs={{0,256},{16,272},{32,288},{48,304},{64,320},{80,336},{96,352},{112... | collective-permute-start | bytes 55304 | tf_op jit(solution)/shard_map/ppermute | solution.py:151
  242.2 7.2 %all-to-all-start.6 = ((bf16[16,24,384]{2,1,0:T(8,128)(2,1)}), bf16[16,24,384]{2,1,0:T(8,128)(2,1)S(1)}, u32[]{:S(2)}, u32[]{:S(2)}) async-start(bf16[16,24,384]{2,1,0:T(8,128)(2,1)} %broadcast_in_dim.51), calls=%async_computation.8 | async-start | bytes 589824 | tf_op jit(solution)/shard_map/all_to_all | solution.py:48
  249.9 11.3 %collective-permute-start.15 = (bf16[8,18,96]{2,0,1:T(8,128)(2,1)S(1)}, bf16[8,18,96]{2,0,1:T(8,128)(2,1)S(1)}, u32[]{:S(2)}, u32[]{:S(2)}) collective-permute-start(bf16[8,18,96]{2,0,1:T(8,128)(2,1)S(1)} %bitcast.108), channel_id=1, source_target_pairs={{0,2},{1,3},{2,0},{3,1},{4,6},{5,7},{6,4},{7,5},{8,10},{9,11},{10,... | collective-permute-start | bytes 82952 | tf_op jit(solution)/shard_map/ppermute | solution.py:162
  262.5 1.3 collective-permute-done.15
  264.5 8.4 %all-to-all-start.7 = ((bf16[8,36,96]{2,1,0:T(8,128)(2,1)}), bf16[8,36,96]{2,1,0:T(8,128)(2,1)S(1)}, u32[]{:S(2)}, u32[]{:S(2)}) async-start(bf16[8,36,96]{2,1,0:T(8,128)(2,1)} %copy.53), calls=%async_computation.9 | async-start | bytes 163840 | tf_op jit(solution)/shard_map/all_to_all | solution.py:48
  274.0 3.9 %all-to-all-done.7 = bf16[8,36,96]{2,1,0:T(8,128)(2,1)S(1)} async-done(((bf16[8,36,96]{2,1,0:T(8,128)(2,1)}), bf16[8,36,96]{2,1,0:T(8,128)(2,1)S(1)}, u32[]{:S(2)}, u32[]{:S(2)}) %all-to-all-start.7) | async-done | bytes 55328 | tf_op jit(solution)/shard_map/all_to_all | solution.py:48
  (113 shorter events, 21.4 us)
Async XLA Ops:
  7.2 22.7 %copy-start = (bf16[96,1536]{1,0:T(8,128)(2,1)S(1)}, bf16[96,1536]{1,0:T(8,128)(2,1)}, u32[]{:S(2)}) copy-start(bf16[96,1536]{1,0:T(8,128)(2,1)} %param.7) | copy-start | bytes 884740
  8.8 34.3 %all-to-all-start = ((bf16[16,36,96]{2,1,0:T(8,128)(2,1)}), bf16[16,36,96]{2,1,0:T(8,128)(2,1)S(1)}, u32[]{:S(2)}, u32[]{:S(2)}) async-start(bf16[16,36,96]{2,1,0:T(8,128)(2,1)} %bitcast.1), calls=%async_computation | async-start | bytes 327680 | tf_op jit(solution)/shard_map/all_to_all | solution.py:48
  43.8 18.6 %all-to-all-start.1 = ((bf16[8,40,1536]{2,1,0:T(8,128)(2,1)}), bf16[8,40,1536]{2,1,0:T(8,128)(2,1)S(1)}, u32[]{:S(2)}, u32[]{:S(2)}) async-start(bf16[8,40,1536]{2,1,0:T(8,128)(2,1)} %bitcast.5), calls=%async_computation.1 | async-start | bytes 1966080 | tf_op jit(solution)/shard_map/all_to_all | solution.py:48
  48.0 64.6 %all-gather.3.cloned.1.call-start = ((), (), s32[]{:S(2)}) async-start(), calls=%async_computation.12 | async-start | bytes 1351680 | tf_op jit(solution)/shard_map/all_gather | solution.py:104
  48.0 14.5 %collective-permute-start.2 = (bf16[24,1536]{1,0:T(8,128)(2,1)S(1)}, bf16[24,1536]{1,0:T(8,128)(2,1)S(1)}, u32[]{:S(2)}, u32[]{:S(2)}) collective-permute-start(bf16[24,1536]{1,0:T(8,128)(2,1)S(1)} %get-tuple-element.59), channel_id=1, source_target_pairs={{0,192},{16,208},{32,224},{48,240},{64,128},{80,144},{96,160},{112... | collective-permute-start | bytes 221192 | tf_op jit(solution)/shard_map/ppermute | solution.py:94
  55.1 8.1 %collective-permute-start.1 = (bf16[24,1536]{1,0:T(8,128)(2,1)S(1)}, bf16[24,1536]{1,0:T(8,128)(2,1)S(1)}, u32[]{:S(2)}, u32[]{:S(2)}) collective-permute-start(bf16[24,1536]{1,0:T(8,128)(2,1)S(1)} %get-tuple-element.60), channel_id=1, source_target_pairs={{0,128},{16,144},{32,160},{48,176},{64,192},{80,208},{96,224},{112... | collective-permute-start | bytes 221192 | tf_op jit(solution)/shard_map/ppermute | solution.py:94
  59.0 5.3 %collective-permute-start = (bf16[24,1536]{1,0:T(8,128)(2,1)S(1)}, bf16[24,1536]{1,0:T(8,128)(2,1)S(1)}, u32[]{:S(2)}, u32[]{:S(2)}) collective-permute-start(bf16[24,1536]{1,0:T(8,128)(2,1)S(1)} %get-tuple-element.62), channel_id=1, source_target_pairs={{0,64},{16,80},{32,96},{48,112},{64,0},{80,16},{96,32},{112,48},{1... | collective-permute-start | bytes 221192 | tf_op jit(solution)/shard_map/ppermute | solution.py:94
  64.4 13.4 %collective-permute-start.4 = (bf16[40,1536]{1,0:T(8,128)(2,1)S(1)}, bf16[40,1536]{1,0:T(8,128)(2,1)S(1)}, u32[]{:S(2)}, u32[]{:S(2)}) collective-permute-start(bf16[40,1536]{1,0:T(8,128)(2,1)S(1)} %reduce_sum.67), channel_id=1, source_target_pairs={{0,258},{1,257},{4,262},{5,261},{8,266},{9,265},{12,270},{13,269},... | collective-permute-start | bytes 368648 | tf_op jit(solution)/shard_map/ppermute | solution.py:40
  67.5 11.9 %collective-permute-start.3 = (bf16[40,1536]{1,0:T(8,128)(2,1)S(1)}, bf16[40,1536]{1,0:T(8,128)(2,1)S(1)}, u32[]{:S(2)}, u32[]{:S(2)}) collective-permute-start(bf16[40,1536]{1,0:T(8,128)(2,1)S(1)} %reduce_sum.67), channel_id=1, source_target_pairs={{0,256},{1,259},{4,260},{5,263},{8,264},{9,267},{12,268},{13,271},... | collective-permute-start | bytes 368648 | tf_op jit(solution)/shard_map/ppermute | solution.py:40
  75.4 16.8 %collective-permute-start.5 = (bf16[80,1536]{1,0:T(8,128)(2,1)S(1)}, bf16[80,1536]{1,0:T(8,128)(2,1)S(1)}, u32[]{:S(2)}, u32[]{:S(2)}) collective-permute-start(bf16[80,1536]{1,0:T(8,128)(2,1)S(1)} %slice.129), channel_id=1, source_target_pairs={{0,450},{1,451},{4,454},{5,455},{8,458},{9,459},{12,462},{13,463},... | collective-permute-start | bytes 737288 | tf_op jit(solution)/shard_map/ppermute | solution.py:40
  77.8 24.5 %copy-start.1 = (bf16[40,1536]{1,0:T(8,128)(2,1)}, bf16[40,1536]{1,0:T(8,128)(2,1)S(1)}, u32[]{:S(2)}) copy-start(bf16[40,1536]{1,0:T(8,128)(2,1)S(1)} %collective-permute-done.4) | copy-start | bytes 368644
  79.4 23.0 %copy-start.3 = (bf16[40,1536]{1,0:T(8,128)(2,1)}, bf16[40,1536]{1,0:T(8,128)(2,1)S(1)}, u32[]{:S(2)}) copy-start(bf16[40,1536]{1,0:T(8,128)(2,1)S(1)} %collective-permute-done.3) | copy-start | bytes 368644
  92.2 18.8 %collective-permute-start.8 = (bf16[80,1536]{1,0:T(8,128)(2,1)S(1)}, bf16[80,1536]{1,0:T(8,128)(2,1)S(1)}, u32[]{:S(2)}, u32[]{:S(2)}) collective-permute-start(bf16[80,1536]{1,0:T(8,128)(2,1)S(1)} %collective-permute-done.5), channel_id=1, source_target_pairs={{0,48},{16,32},{32,16},{48,0},{64,112},{80,96},{96,80},{112,64},{1... | collective-permute-start | bytes 737288 | tf_op jit(solution)/shard_map/ppermute | solution.py:112
  96.8 14.2 %collective-permute-start.7 = (bf16[80,1536]{1,0:T(8,128)(2,1)S(1)}, bf16[80,1536]{1,0:T(8,128)(2,1)S(1)}, u32[]{:S(2)}, u32[]{:S(2)}) collective-permute-start(bf16[80,1536]{1,0:T(8,128)(2,1)S(1)} %collective-permute-done.5), channel_id=1, source_target_pairs={{0,32},{16,48},{32,0},{48,16},{64,96},{80,112},{96,64},{112,80},{1... | collective-permute-start | bytes 737288 | tf_op jit(solution)/shard_map/ppermute | solution.py:112
  99.1 12.2 %collective-permute-start.6 = (bf16[80,1536]{1,0:T(8,128)(2,1)S(1)}, bf16[80,1536]{1,0:T(8,128)(2,1)}, u32[]{:S(2)}, u32[]{:S(2)}) collective-permute-start(bf16[80,1536]{1,0:T(8,128)(2,1)S(1)} %collective-permute-done.5), channel_id=1, source_target_pairs={{0,16},{16,0},{32,48},{48,32},{64,80},{80,64},{96,112},{112,96},{1... | collective-permute-start | bytes 737288 | tf_op jit(solution)/shard_map/ppermute | solution.py:112
  102.4 20.1 %all-to-all-start.2 = ((bf16[8,40,1536]{2,1,0:T(8,128)(2,1)}), bf16[8,40,1536]{2,1,0:T(8,128)(2,1)S(1)}, u32[]{:S(2)}, u32[]{:S(2)}) async-start(bf16[8,40,1536]{2,1,0:T(8,128)(2,1)} %broadcast_in_dim.49), calls=%async_computation.2 | async-start | bytes 1966080 | tf_op jit(solution)/shard_map/all_to_all | solution.py:48
  108.0 58.4 %reduce-scatter.5.cloned.1.call-start = ((), (), s32[]{:S(2)}) async-start(), calls=%async_computation.11 | async-start | bytes 1105920 | tf_op jit(solution)/shard_map/reduce_scatter | solution.py:130
  124.6 0.7 copy-start.6
  126.8 1.7 copy-start.7
  130.2 4.5 %copy-start.5 = (bf16[320,288]{0,1:T(8,128)(2,1)S(1)}, bf16[320,288]{0,1:T(8,128)(2,1)}, u32[]{:S(2)}) copy-start(bf16[320,288]{0,1:T(8,128)(2,1)} %fusion.18) | copy-start | bytes 552964
  130.2 18.9 %all-to-all-start.3 = ((bf16[8,40,1536]{2,1,0:T(8,128)(2,1)}), bf16[8,40,1536]{2,1,0:T(8,128)(2,1)S(1)}, u32[]{:S(2)}, u32[]{:S(2)}) async-start(bf16[8,40,1536]{2,1,0:T(8,128)(2,1)} %bitcast.22), calls=%async_computation.3 | async-start | bytes 1966080 | tf_op jit(solution)/shard_map/all_to_all | solution.py:48
  134.7 14.6 %copy-start.2 = (bf16[40,1536]{1,0:T(8,128)(2,1)S(1)}, bf16[40,1536]{1,0:T(8,128)(2,1)}, u32[]{:S(2)}) copy-start(bf16[40,1536]{1,0:T(8,128)(2,1)} %copy-done.1) | copy-start | bytes 368644
  134.7 14.6 %copy-start.4 = (bf16[40,1536]{1,0:T(8,128)(2,1)S(1)}, bf16[40,1536]{1,0:T(8,128)(2,1)}, u32[]{:S(2)}) copy-start(bf16[40,1536]{1,0:T(8,128)(2,1)} %copy-done.3) | copy-start | bytes 368644
  134.7 50.9 %reduce-scatter.3.cloned.1.call-start = ((), (), s32[]{:S(2)}) async-start(), calls=%async_computation.10 | async-start | bytes 1105920 | tf_op jit(solution)/shard_map/reduce_scatter | solution.py:130
  149.6 10.8 %collective-permute-start.10 = (bf16[40,1536]{1,0:T(8,128)(2,1)S(1)}, bf16[40,1536]{1,0:T(8,128)(2,1)S(1)}, u32[]{:S(2)}, u32[]{:S(2)}) collective-permute-start(bf16[40,1536]{1,0:T(8,128)(2,1)S(1)} %multiply_convert_fusion.1), channel_id=1, source_target_pairs={{0,258},{1,257},{4,262},{5,261},{8,266},{9,265},{12,270},{13,269},... | collective-permute-start | bytes 368648 | tf_op jit(solution)/shard_map/ppermute | solution.py:40
  155.4 10.9 %collective-permute-start.9 = (bf16[40,1536]{1,0:T(8,128)(2,1)S(1)}, bf16[40,1536]{1,0:T(8,128)(2,1)S(1)}, u32[]{:S(2)}, u32[]{:S(2)}) collective-permute-start(bf16[40,1536]{1,0:T(8,128)(2,1)S(1)} %multiply_convert_fusion.1), channel_id=1, source_target_pairs={{0,256},{1,259},{4,260},{5,263},{8,264},{9,267},{12,268},{13,271},... | collective-permute-start | bytes 368648 | tf_op jit(solution)/shard_map/ppermute | solution.py:40
  185.6 7.4 %copy-start.9 = (bf16[1,72,1536]{2,1,0:T(8,128)(2,1)S(1)}, bf16[1,72,1536]{2,1,0:T(8,128)(2,1)}, u32[]{:S(2)}) copy-start(bf16[1,72,1536]{2,1,0:T(8,128)(2,1)} %reduce-scatter.5.cloned.1.call-done) | copy-start | bytes 663556
  186.6 22.7 %all-to-all-start.4 = ((bf16[8,40,1536]{2,1,0:T(8,128)(2,1)}), bf16[8,40,1536]{2,1,0:T(8,128)(2,1)S(1)}, u32[]{:S(2)}, u32[]{:S(2)}) async-start(bf16[8,40,1536]{2,1,0:T(8,128)(2,1)} %broadcast_in_dim.50), calls=%async_computation.6 | async-start | bytes 1966080 | tf_op jit(solution)/shard_map/all_to_all | solution.py:48
  193.0 21.8 %copy-start.8 = (bf16[1,72,1536]{2,1,0:T(8,128)(2,1)S(1)}, bf16[1,72,1536]{2,1,0:T(8,128)(2,1)}, u32[]{:S(2)}) copy-start(bf16[1,72,1536]{2,1,0:T(8,128)(2,1)} %reduce-scatter.3.cloned.1.call-done) | copy-start | bytes 663556
  193.0 16.3 %collective-permute-start.11 = (bf16[72,1536]{1,0:T(8,128)(2,1)S(1)}, bf16[72,1536]{1,0:T(8,128)(2,1)S(1)}, u32[]{:S(2)}, u32[]{:S(2)}) collective-permute-start(bf16[72,1536]{1,0:T(8,128)(2,1)S(1)} %bitcast.110), channel_id=1, source_target_pairs={{0,450},{1,451},{4,454},{5,455},{8,458},{9,459},{12,462},{13,463},... | collective-permute-start | bytes 663560 | tf_op jit(solution)/shard_map/ppermute | solution.py:40
  210.5 15.5 %all-to-all-start.5 = ((bf16[16,24,384]{2,1,0:T(8,128)(2,1)}), bf16[16,24,384]{2,1,0:T(8,128)(2,1)S(1)}, u32[]{:S(2)}, u32[]{:S(2)}) async-start(bf16[16,24,384]{2,1,0:T(8,128)(2,1)} %bitcast.30), calls=%async_computation.7 | async-start | bytes 589824 | tf_op jit(solution)/shard_map/all_to_all | solution.py:48
  214.9 14.0 %collective-permute-start.13 = (bf16[18,1536]{1,0:T(8,128)(2,1)S(1)}, bf16[18,1536]{1,0:T(8,128)(2,1)S(1)}, u32[]{:S(2)}, u32[]{:S(2)}) collective-permute-start(bf16[18,1536]{1,0:T(8,128)(2,1)S(1)} %select_convert_fusion.1), channel_id=1, source_target_pairs={{0,128},{1,129},{4,132},{5,133},{8,136},{9,137},{12,140},{13,141},... | collective-permute-start | bytes 165896 | tf_op jit(solution)/shard_map/ppermute | solution.py:40
  219.1 9.7 %collective-permute-start.14 = (bf16[18,1536]{1,0:T(8,128)(2,1)S(1)}, bf16[18,1536]{1,0:T(8,128)(2,1)S(1)}, u32[]{:S(2)}, u32[]{:S(2)}) collective-permute-start(bf16[18,1536]{1,0:T(8,128)(2,1)S(1)} %get-tuple-element.53), channel_id=1, source_target_pairs={{0,192},{1,193},{4,196},{5,197},{8,200},{9,201},{12,204},{13,205},... | collective-permute-start | bytes 165896 | tf_op jit(solution)/shard_map/ppermute | solution.py:40
  222.2 10.5 %collective-permute-start.12 = (bf16[18,1536]{1,0:T(8,128)(2,1)S(1)}, bf16[18,1536]{1,0:T(8,128)(2,1)S(1)}, u32[]{:S(2)}, u32[]{:S(2)}) collective-permute-start(bf16[18,1536]{1,0:T(8,128)(2,1)S(1)} %get-tuple-element.54), channel_id=1, source_target_pairs={{0,64},{1,65},{4,68},{5,69},{8,72},{9,73},{12,76},{13,77},{16,80},... | collective-permute-start | bytes 165896 | tf_op jit(solution)/shard_map/ppermute | solution.py:40
  232.7 8.7 %collective-permute-start.16 = (bf16[24,384]{1,0:T(8,128)(2,1)S(1)}, bf16[24,384]{1,0:T(8,128)(2,1)S(1)}, u32[]{:S(2)}, u32[]{:S(2)}) collective-permute-start(bf16[24,384]{1,0:T(8,128)(2,1)S(1)} %reduce-precision_convert_fusion), channel_id=1, source_target_pairs={{0,256},{16,272},{32,288},{48,304},{64,320},{80,336},{96,352},{112... | collective-permute-start | bytes 55304 | tf_op jit(solution)/shard_map/ppermute | solution.py:151
  242.2 21.6 %all-to-all-start.6 = ((bf16[16,24,384]{2,1,0:T(8,128)(2,1)}), bf16[16,24,384]{2,1,0:T(8,128)(2,1)S(1)}, u32[]{:S(2)}, u32[]{:S(2)}) async-start(bf16[16,24,384]{2,1,0:T(8,128)(2,1)} %broadcast_in_dim.51), calls=%async_computation.8 | async-start | bytes 589824 | tf_op jit(solution)/shard_map/all_to_all | solution.py:48
  249.9 13.8 %collective-permute-start.15 = (bf16[8,18,96]{2,0,1:T(8,128)(2,1)S(1)}, bf16[8,18,96]{2,0,1:T(8,128)(2,1)S(1)}, u32[]{:S(2)}, u32[]{:S(2)}) collective-permute-start(bf16[8,18,96]{2,0,1:T(8,128)(2,1)S(1)} %bitcast.108), channel_id=1, source_target_pairs={{0,2},{1,3},{2,0},{3,1},{4,6},{5,7},{6,4},{7,5},{8,10},{9,11},{10,... | collective-permute-start | bytes 82952 | tf_op jit(solution)/shard_map/ppermute | solution.py:162
  264.5 13.4 %all-to-all-start.7 = ((bf16[8,36,96]{2,1,0:T(8,128)(2,1)}), bf16[8,36,96]{2,1,0:T(8,128)(2,1)S(1)}, u32[]{:S(2)}, u32[]{:S(2)}) async-start(bf16[8,36,96]{2,1,0:T(8,128)(2,1)} %copy.53), calls=%async_computation.9 | async-start | bytes 163840 | tf_op jit(solution)/shard_map/all_to_all | solution.py:48
Sparse Core Ops, SparseCore 0:
  74.6 31.8 all-gather.2
  126.9 25.2 reduce-scatter.4
  155.2 30.3 reduce-scatter.2

commit v12 on v11

--- a/solution.py
+++ b/solution.py
@@ -135,7 +135,7 @@
     image_dot = jnp.sum(image_unit * unit_grad, axis=1, keepdims=True)
     embed_grad = (image_scale * (unit_grad - image_unit * image_dot)).astype(BF16)
     embed_grad = (send(embed_grad, FOUR_UP).astype(F32) + send(embed_grad, FOUR_DOWN).astype(F32)).astype(BF16)
-    embed_grad, *text_acc = lax.optimization_barrier((embed_grad, *text_acc))
+    embed_grad, text_acc[1] = lax.optimization_barrier((embed_grad, text_acc[1]))
     crossed = send(text_acc[1], MIRROR)
     grads = spread(embed_grad, "fsdp", PLANE, plane).reshape(plane * held, embed_width)
     grads, crossed = lax.optimization_barrier((grads, crossed))

time: 286 us -> 268 us (0.937)
  starting transfers between devices: 136 us -> 125 us
  waiting for transfers between devices: 104 us -> 95.3 us
    reduce_scatter x2, waiting for transfers between devices: 19.2 us -> 0.04 us  [on_device(): lax.psum_scatter(acc.reshape(Y, count, embed_width), 'dp', axis_index_gro...]
    ppermute x1, starting transfers between devices: 7.6 us -> 2.46 us  [on_device(): lax.ppermute(head_sum.astype(BF16), 'dp', ACROSS).astype(F32)]
    ppermute x1, waiting for transfers between devices: 1.06 us -> 5.94 us  [on_device(): lax.ppermute(head_sum.astype(BF16), 'dp', ACROSS).astype(F32)]
    ppermute x1, starting transfers between devices: 11.3 us -> 7.05 us  [on_device(): lax.ppermute(jnp.where(zh == 0, text_rows[1], text_rows[0]), 'fsdp', PAIR)]
    ppermute x1, waiting for transfers between devices: 1.28 us -> 5.13 us  [on_device(): lax.ppermute(jnp.where(zh == 0, text_rows[1], text_rows[0]), 'fsdp', PAIR)]
  transfers between devices with their start and end apart: 28 -> 28, of which waited for: 19 -> 19; matrix products, arithmetic and copies ran while one was open for 7% -> 8% of each run, Pallas kernels for 0% -> 0%
where the time goes in v12:
time: 268 us; the launch traced here: 266 us
  starting transfers between devices  125 us (47%)
  waiting for transfers between devices  95.3 us (36%)
  between operations  15.6 us (6%)
  local copies, waits for them, and re-layouts  14 us (5%)
  matrix products  10.7 us (4%)
  other arithmetic  5.94 us (2%)
    all_to_all x8, starting transfers between devices, swap(): lax.all_to_all(value, axis, 0, 0, axis_index_groups=groups, tiled=True)  58.3 us
    ppermute x9, waiting for transfers between devices, send(): return lax.ppermute(value, ('dp', 'fsdp'), pairs)  39.9 us
    all_to_all x8, waiting for transfers between devices, swap(): lax.all_to_all(value, axis, 0, 0, axis_index_groups=groups, tiled=True)  39.3 us
    ppermute x9, starting transfers between devices, send(): return lax.ppermute(value, ('dp', 'fsdp'), pairs)  34.9 us
    ppermute x3, starting transfers between devices, on_device(): lax.ppermute(part, 'dp', [(i, i ^ by * Y) for i in range(cycle)])  12.8 us
    ppermute x3, starting transfers between devices, on_device(): lax.ppermute(crossed, 'dp', [(i, i ^ by) for i in range(cycle)])  9.04 us
    ppermute x1, starting transfers between devices, on_device(): lax.ppermute(jnp.where(zh == 0, text_rows[1], text_rows[0]), 'fsdp', PAIR)  7.05 us
    ppermute x1, waiting for transfers between devices, on_device(): lax.ppermute(head_sum.astype(BF16), 'dp', ACROSS).astype(F32)  5.94 us
  transfers between devices with their start and end apart: 28, of which 19 were waited for; matrix products, arithmetic and copies ran while one was open for 8% of the time, Pallas kernels for 0%

profile of v12, /device:TPU:1, one launch (start us, length us, event | category | flops | bytes accessed | tf_op | source)
XLA Modules:
  0.0 266.3 jit_solution(14142766833343878423)
XLA Ops:
  8.8 19.1 %all-to-all-start = ((bf16[16,36,96]{2,1,0:T(8,128)(2,1)}), bf16[16,36,96]{2,1,0:T(8,128)(2,1)S(1)}, u32[]{:S(2)}, u32[]{:S(2)}) async-start(bf16[16,36,96]{2,1,0:T(8,128)(2,1)} %bitcast.1), calls=%async_computation | async-start | bytes 327680 | tf_op jit(solution)/shard_map/all_to_all | solution.py:48
  29.8 1.4 convolution_convert_fusion
  31.2 11.9 %all-to-all-done = bf16[16,36,96]{2,1,0:T(8,128)(2,1)S(1)} async-done(((bf16[16,36,96]{2,1,0:T(8,128)(2,1)}), bf16[16,36,96]{2,1,0:T(8,128)(2,1)S(1)}, u32[]{:S(2)}, u32[]{:S(2)}) %all-to-all-start) | async-done | bytes 110624 | tf_op jit(solution)/shard_map/all_to_all | solution.py:48
  43.8 4.2 %all-to-all-start.1 = ((bf16[8,40,1536]{2,1,0:T(8,128)(2,1)}), bf16[8,40,1536]{2,1,0:T(8,128)(2,1)S(1)}, u32[]{:S(2)}, u32[]{:S(2)}) async-start(bf16[8,40,1536]{2,1,0:T(8,128)(2,1)} %bitcast.5), calls=%async_computation.1 | async-start | bytes 1966080 | tf_op jit(solution)/shard_map/all_to_all | solution.py:48
  48.0 7.1 %collective-permute-start.2 = (bf16[24,1536]{1,0:T(8,128)(2,1)S(1)}, bf16[24,1536]{1,0:T(8,128)(2,1)S(1)}, u32[]{:S(2)}, u32[]{:S(2)}) collective-permute-start(bf16[24,1536]{1,0:T(8,128)(2,1)S(1)} %get-tuple-element.57), channel_id=1, source_target_pairs={{0,192},{16,208},{32,224},{48,240},{64,128},{80,144},{96,160},{112... | collective-permute-start | bytes 221192 | tf_op jit(solution)/shard_map/ppermute | solution.py:94
  55.1 3.8 %collective-permute-start.1 = (bf16[24,1536]{1,0:T(8,128)(2,1)S(1)}, bf16[24,1536]{1,0:T(8,128)(2,1)S(1)}, u32[]{:S(2)}, u32[]{:S(2)}) collective-permute-start(bf16[24,1536]{1,0:T(8,128)(2,1)S(1)} %get-tuple-element.58), channel_id=1, source_target_pairs={{0,128},{16,144},{32,160},{48,176},{64,192},{80,208},{96,224},{112... | collective-permute-start | bytes 221192 | tf_op jit(solution)/shard_map/ppermute | solution.py:94
  59.0 1.9 collective-permute-start
  63.2 1.1 collective-permute-done
  64.4 3.1 %collective-permute-start.4 = (bf16[40,1536]{1,0:T(8,128)(2,1)S(1)}, bf16[40,1536]{1,0:T(8,128)(2,1)S(1)}, u32[]{:S(2)}, u32[]{:S(2)}) collective-permute-start(bf16[40,1536]{1,0:T(8,128)(2,1)S(1)} %reduce_sum.67), channel_id=1, source_target_pairs={{0,258},{1,257},{4,262},{5,261},{8,266},{9,265},{12,270},{13,269},... | collective-permute-start | bytes 368648 | tf_op jit(solution)/shard_map/ppermute | solution.py:40
  67.5 6.1 %collective-permute-start.3 = (bf16[40,1536]{1,0:T(8,128)(2,1)S(1)}, bf16[40,1536]{1,0:T(8,128)(2,1)S(1)}, u32[]{:S(2)}, u32[]{:S(2)}) collective-permute-start(bf16[40,1536]{1,0:T(8,128)(2,1)S(1)} %reduce_sum.67), channel_id=1, source_target_pairs={{0,256},{1,259},{4,260},{5,263},{8,264},{9,267},{12,268},{13,271},... | collective-permute-start | bytes 368648 | tf_op jit(solution)/shard_map/ppermute | solution.py:40
  75.4 2.4 collective-permute-start.5
  77.9 1.5 collective-permute-done.3
  79.5 12.7 %collective-permute-done.5 = bf16[80,1536]{1,0:T(8,128)(2,1)S(1)} collective-permute-done((bf16[80,1536]{1,0:T(8,128)(2,1)S(1)}, bf16[80,1536]{1,0:T(8,128)(2,1)S(1)}, u32[]{:S(2)}, u32[]{:S(2)}) %collective-permute-start.5) | collective-permute-done | bytes 245792 | tf_op jit(solution)/shard_map/ppermute | solution.py:40
  92.2 4.6 %collective-permute-start.8 = (bf16[80,1536]{1,0:T(8,128)(2,1)S(1)}, bf16[80,1536]{1,0:T(8,128)(2,1)S(1)}, u32[]{:S(2)}, u32[]{:S(2)}) collective-permute-start(bf16[80,1536]{1,0:T(8,128)(2,1)S(1)} %collective-permute-done.5), channel_id=1, source_target_pairs={{0,48},{16,32},{32,16},{48,0},{64,112},{80,96},{96,80},{112,64},{1... | collective-permute-start | bytes 737288 | tf_op jit(solution)/shard_map/ppermute | solution.py:112
  96.8 2.3 collective-permute-start.7
  99.1 2.1 collective-permute-start.6
  102.3 5.7 %all-to-all-start.2 = ((bf16[8,40,1536]{2,1,0:T(8,128)(2,1)}), bf16[8,40,1536]{2,1,0:T(8,128)(2,1)S(1)}, u32[]{:S(2)}, u32[]{:S(2)}) async-start(bf16[8,40,1536]{2,1,0:T(8,128)(2,1)} %broadcast_in_dim.49), calls=%async_computation.2 | async-start | bytes 1966080 | tf_op jit(solution)/shard_map/all_to_all | solution.py:48
  108.0 3.0 %collective-permute-done.8 = bf16[80,1536]{1,0:T(8,128)(2,1)S(1)} collective-permute-done((bf16[80,1536]{1,0:T(8,128)(2,1)S(1)}, bf16[80,1536]{1,0:T(8,128)(2,1)S(1)}, u32[]{:S(2)}, u32[]{:S(2)}) %collective-permute-start.8) | collective-permute-done | bytes 245792 | tf_op jit(solution)/shard_map/ppermute | solution.py:112
  112.6 1.2 slice.128
  114.7 7.7 %all-to-all-done.2 = bf16[8,40,1536]{2,1,0:T(8,128)(2,1)S(1)} async-done(((bf16[8,40,1536]{2,1,0:T(8,128)(2,1)}), bf16[8,40,1536]{2,1,0:T(8,128)(2,1)S(1)}, u32[]{:S(2)}, u32[]{:S(2)}) %all-to-all-start.2) | async-done | bytes 983072 | tf_op jit(solution)/shard_map/all_to_all | solution.py:48
  122.5 1.4 fusion.18
  125.3 1.5 convolution_convert_fusion.2
  126.8 1.7 fusion.35
  128.5 1.7 fusion
  130.2 4.5 %all-to-all-start.3 = ((bf16[8,40,1536]{2,1,0:T(8,128)(2,1)}), bf16[8,40,1536]{2,1,0:T(8,128)(2,1)S(1)}, u32[]{:S(2)}, u32[]{:S(2)}) async-start(bf16[8,40,1536]{2,1,0:T(8,128)(2,1)} %bitcast.22), calls=%async_computation.3 | async-start | bytes 1966080 | tf_op jit(solution)/shard_map/all_to_all | solution.py:48
  134.7 1.5 convolution_convert_fusion.1
  136.3 12.8 %all-to-all-done.3 = bf16[8,40,1536]{2,1,0:T(8,128)(2,1)S(1)} async-done(((bf16[8,40,1536]{2,1,0:T(8,128)(2,1)}), bf16[8,40,1536]{2,1,0:T(8,128)(2,1)S(1)}, u32[]{:S(2)}, u32[]{:S(2)}) %all-to-all-start.3) | async-done | bytes 983072 | tf_op jit(solution)/shard_map/all_to_all | solution.py:48
  149.5 5.9 %collective-permute-start.10 = (bf16[40,1536]{1,0:T(8,128)(2,1)S(1)}, bf16[40,1536]{1,0:T(8,128)(2,1)S(1)}, u32[]{:S(2)}, u32[]{:S(2)}) collective-permute-start(bf16[40,1536]{1,0:T(8,128)(2,1)S(1)} %multiply_convert_fusion.1), channel_id=1, source_target_pairs={{0,258},{1,257},{4,262},{5,261},{8,266},{9,265},{12,270},{13,269},... | collective-permute-start | bytes 368648 | tf_op jit(solution)/shard_map/ppermute | solution.py:40
  155.4 3.3 %collective-permute-start.9 = (bf16[40,1536]{1,0:T(8,128)(2,1)S(1)}, bf16[40,1536]{1,0:T(8,128)(2,1)S(1)}, u32[]{:S(2)}, u32[]{:S(2)}) collective-permute-start(bf16[40,1536]{1,0:T(8,128)(2,1)S(1)} %multiply_convert_fusion.1), channel_id=1, source_target_pairs={{0,256},{1,259},{4,260},{5,263},{8,264},{9,267},{12,268},{13,271},... | collective-permute-start | bytes 368648 | tf_op jit(solution)/shard_map/ppermute | solution.py:40
  158.7 1.6 collective-permute-done.10
  160.3 6.0 %collective-permute-done.9 = bf16[40,1536]{1,0:T(8,128)(2,1)S(1)} collective-permute-done((bf16[40,1536]{1,0:T(8,128)(2,1)S(1)}, bf16[40,1536]{1,0:T(8,128)(2,1)S(1)}, u32[]{:S(2)}, u32[]{:S(2)}) %collective-permute-start.9) | collective-permute-done | bytes 122912 | tf_op jit(solution)/shard_map/ppermute | solution.py:40
  167.5 5.7 %all-to-all-start.4 = ((bf16[8,40,1536]{2,1,0:T(8,128)(2,1)}), bf16[8,40,1536]{2,1,0:T(8,128)(2,1)S(1)}, u32[]{:S(2)}, u32[]{:S(2)}) async-start(bf16[8,40,1536]{2,1,0:T(8,128)(2,1)} %broadcast_in_dim.50), calls=%async_computation.5 | async-start | bytes 1966080 | tf_op jit(solution)/shard_map/all_to_all | solution.py:48
  173.3 5.0 %collective-permute-start.11 = (bf16[72,1536]{1,0:T(8,128)(2,1)S(1)}, bf16[72,1536]{1,0:T(8,128)(2,1)S(1)}, u32[]{:S(2)}, u32[]{:S(2)}) collective-permute-start(bf16[72,1536]{1,0:T(8,128)(2,1)S(1)} %bitcast.111), channel_id=1, source_target_pairs={{0,450},{1,451},{4,454},{5,455},{8,458},{9,459},{12,462},{13,463},... | collective-permute-start | bytes 663560 | tf_op jit(solution)/shard_map/ppermute | solution.py:40
  178.3 7.1 %collective-permute-done.11 = bf16[72,1536]{1,0:T(8,128)(2,1)S(1)} collective-permute-done((bf16[72,1536]{1,0:T(8,128)(2,1)S(1)}, bf16[72,1536]{1,0:T(8,128)(2,1)S(1)}, u32[]{:S(2)}, u32[]{:S(2)}) %collective-permute-start.11) | collective-permute-done | bytes 221216 | tf_op jit(solution)/shard_map/ppermute | solution.py:40
  185.5 2.1 all-to-all-done.4
  188.7 6.7 %all-to-all-start.5 = ((bf16[16,24,384]{2,1,0:T(8,128)(2,1)}), bf16[16,24,384]{2,1,0:T(8,128)(2,1)S(1)}, u32[]{:S(2)}, u32[]{:S(2)}) async-start(bf16[16,24,384]{2,1,0:T(8,128)(2,1)} %bitcast.30), calls=%async_computation.7 | async-start | bytes 589824 | tf_op jit(solution)/shard_map/all_to_all | solution.py:48
  196.5 4.2 %collective-permute-start.13 = (bf16[18,1536]{1,0:T(8,128)(2,1)S(1)}, bf16[18,1536]{1,0:T(8,128)(2,1)S(1)}, u32[]{:S(2)}, u32[]{:S(2)}) collective-permute-start(bf16[18,1536]{1,0:T(8,128)(2,1)S(1)} %select_convert_fusion.1), channel_id=1, source_target_pairs={{0,128},{1,129},{4,132},{5,133},{8,136},{9,137},{12,140},{13,141},... | collective-permute-start | bytes 165896 | tf_op jit(solution)/shard_map/ppermute | solution.py:40
  200.8 3.1 %collective-permute-start.14 = (bf16[18,1536]{1,0:T(8,128)(2,1)S(1)}, bf16[18,1536]{1,0:T(8,128)(2,1)S(1)}, u32[]{:S(2)}, u32[]{:S(2)}) collective-permute-start(bf16[18,1536]{1,0:T(8,128)(2,1)S(1)} %get-tuple-element.51), channel_id=1, source_target_pairs={{0,192},{1,193},{4,196},{5,197},{8,200},{9,201},{12,204},{13,205},... | collective-permute-start | bytes 165896 | tf_op jit(solution)/shard_map/ppermute | solution.py:40
  203.9 1.9 collective-permute-start.12
  206.7 3.4 %collective-permute-done.13 = bf16[18,1536]{1,0:T(8,128)(2,1)S(1)} collective-permute-done((bf16[18,1536]{1,0:T(8,128)(2,1)S(1)}, bf16[18,1536]{1,0:T(8,128)(2,1)S(1)}, u32[]{:S(2)}, u32[]{:S(2)}) %collective-permute-start.13) | collective-permute-done | bytes 55328 | tf_op jit(solution)/shard_map/ppermute | solution.py:40
  210.1 7.7 %collective-permute-done.12 = bf16[18,1536]{1,0:T(8,128)(2,1)S(1)} collective-permute-done((bf16[18,1536]{1,0:T(8,128)(2,1)S(1)}, bf16[18,1536]{1,0:T(8,128)(2,1)S(1)}, u32[]{:S(2)}, u32[]{:S(2)}) %collective-permute-start.12) | collective-permute-done | bytes 55328 | tf_op jit(solution)/shard_map/ppermute | solution.py:40
  217.7 2.5 collective-permute-start.16
  220.3 5.9 %collective-permute-done.16 = bf16[24,384]{1,0:T(8,128)(2,1)S(1)} collective-permute-done((bf16[24,384]{1,0:T(8,128)(2,1)S(1)}, bf16[24,384]{1,0:T(8,128)(2,1)S(1)}, u32[]{:S(2)}, u32[]{:S(2)}) %collective-permute-start.16) | collective-permute-done | bytes 18464 | tf_op jit(solution)/shard_map/ppermute | solution.py:151
  227.0 4.0 %all-to-all-start.6 = ((bf16[16,24,384]{2,1,0:T(8,128)(2,1)}), bf16[16,24,384]{2,1,0:T(8,128)(2,1)S(1)}, u32[]{:S(2)}, u32[]{:S(2)}) async-start(bf16[16,24,384]{2,1,0:T(8,128)(2,1)} %broadcast_in_dim.51), calls=%async_computation.8 | async-start | bytes 589824 | tf_op jit(solution)/shard_map/all_to_all | solution.py:48
  231.5 7.1 %collective-permute-start.15 = (bf16[8,18,96]{2,0,1:T(8,128)(2,1)S(1)}, bf16[8,18,96]{2,0,1:T(8,128)(2,1)S(1)}, u32[]{:S(2)}, u32[]{:S(2)}) collective-permute-start(bf16[8,18,96]{2,0,1:T(8,128)(2,1)S(1)} %bitcast.109), channel_id=1, source_target_pairs={{0,2},{1,3},{2,0},{3,1},{4,6},{5,7},{6,4},{7,5},{8,10},{9,11},{10,... | collective-permute-start | bytes 82952 | tf_op jit(solution)/shard_map/ppermute | solution.py:162
  239.8 5.1 %collective-permute-done.15 = bf16[8,18,96]{2,0,1:T(8,128)(2,1)S(1)} collective-permute-done((bf16[8,18,96]{2,0,1:T(8,128)(2,1)S(1)}, bf16[8,18,96]{2,0,1:T(8,128)(2,1)S(1)}, u32[]{:S(2)}, u32[]{:S(2)}) %collective-permute-start.15) | collective-permute-done | bytes 27680 | tf_op jit(solution)/shard_map/ppermute | solution.py:162
  245.6 8.5 %all-to-all-start.7 = ((bf16[8,36,96]{2,1,0:T(8,128)(2,1)}), bf16[8,36,96]{2,1,0:T(8,128)(2,1)S(1)}, u32[]{:S(2)}, u32[]{:S(2)}) async-start(bf16[8,36,96]{2,1,0:T(8,128)(2,1)} %copy.53), calls=%async_computation.9 | async-start | bytes 163840 | tf_op jit(solution)/shard_map/all_to_all | solution.py:48
  255.2 3.9 %all-to-all-done.7 = bf16[8,36,96]{2,1,0:T(8,128)(2,1)S(1)} async-done(((bf16[8,36,96]{2,1,0:T(8,128)(2,1)}), bf16[8,36,96]{2,1,0:T(8,128)(2,1)S(1)}, u32[]{:S(2)}, u32[]{:S(2)}) %all-to-all-start.7) | async-done | bytes 55328 | tf_op jit(solution)/shard_map/all_to_all | solution.py:48
  (111 shorter events, 22.1 us)
Async XLA Ops:
  7.2 22.7 %copy-start = (bf16[96,1536]{1,0:T(8,128)(2,1)S(1)}, bf16[96,1536]{1,0:T(8,128)(2,1)}, u32[]{:S(2)}) copy-start(bf16[96,1536]{1,0:T(8,128)(2,1)} %param.7) | copy-start | bytes 884740
  8.8 34.3 %all-to-all-start = ((bf16[16,36,96]{2,1,0:T(8,128)(2,1)}), bf16[16,36,96]{2,1,0:T(8,128)(2,1)S(1)}, u32[]{:S(2)}, u32[]{:S(2)}) async-start(bf16[16,36,96]{2,1,0:T(8,128)(2,1)} %bitcast.1), calls=%async_computation | async-start | bytes 327680 | tf_op jit(solution)/shard_map/all_to_all | solution.py:48
  43.8 18.6 %all-to-all-start.1 = ((bf16[8,40,1536]{2,1,0:T(8,128)(2,1)}), bf16[8,40,1536]{2,1,0:T(8,128)(2,1)S(1)}, u32[]{:S(2)}, u32[]{:S(2)}) async-start(bf16[8,40,1536]{2,1,0:T(8,128)(2,1)} %bitcast.5), calls=%async_computation.1 | async-start | bytes 1966080 | tf_op jit(solution)/shard_map/all_to_all | solution.py:48
  48.0 64.6 %all-gather.3.cloned.1.call-start = ((), (), s32[]{:S(2)}) async-start(), calls=%async_computation.12 | async-start | bytes 1351680 | tf_op jit(solution)/shard_map/all_gather | solution.py:104
  48.0 14.5 %collective-permute-start.2 = (bf16[24,1536]{1,0:T(8,128)(2,1)S(1)}, bf16[24,1536]{1,0:T(8,128)(2,1)S(1)}, u32[]{:S(2)}, u32[]{:S(2)}) collective-permute-start(bf16[24,1536]{1,0:T(8,128)(2,1)S(1)} %get-tuple-element.57), channel_id=1, source_target_pairs={{0,192},{16,208},{32,224},{48,240},{64,128},{80,144},{96,160},{112... | collective-permute-start | bytes 221192 | tf_op jit(solution)/shard_map/ppermute | solution.py:94
  55.1 8.1 %collective-permute-start.1 = (bf16[24,1536]{1,0:T(8,128)(2,1)S(1)}, bf16[24,1536]{1,0:T(8,128)(2,1)S(1)}, u32[]{:S(2)}, u32[]{:S(2)}) collective-permute-start(bf16[24,1536]{1,0:T(8,128)(2,1)S(1)} %get-tuple-element.58), channel_id=1, source_target_pairs={{0,128},{16,144},{32,160},{48,176},{64,192},{80,208},{96,224},{112... | collective-permute-start | bytes 221192 | tf_op jit(solution)/shard_map/ppermute | solution.py:94
  59.0 5.3 %collective-permute-start = (bf16[24,1536]{1,0:T(8,128)(2,1)S(1)}, bf16[24,1536]{1,0:T(8,128)(2,1)S(1)}, u32[]{:S(2)}, u32[]{:S(2)}) collective-permute-start(bf16[24,1536]{1,0:T(8,128)(2,1)S(1)} %get-tuple-element.60), channel_id=1, source_target_pairs={{0,64},{16,80},{32,96},{48,112},{64,0},{80,16},{96,32},{112,48},{1... | collective-permute-start | bytes 221192 | tf_op jit(solution)/shard_map/ppermute | solution.py:94
  64.4 13.4 %collective-permute-start.4 = (bf16[40,1536]{1,0:T(8,128)(2,1)S(1)}, bf16[40,1536]{1,0:T(8,128)(2,1)S(1)}, u32[]{:S(2)}, u32[]{:S(2)}) collective-permute-start(bf16[40,1536]{1,0:T(8,128)(2,1)S(1)} %reduce_sum.67), channel_id=1, source_target_pairs={{0,258},{1,257},{4,262},{5,261},{8,266},{9,265},{12,270},{13,269},... | collective-permute-start | bytes 368648 | tf_op jit(solution)/shard_map/ppermute | solution.py:40
  67.5 11.9 %collective-permute-start.3 = (bf16[40,1536]{1,0:T(8,128)(2,1)S(1)}, bf16[40,1536]{1,0:T(8,128)(2,1)S(1)}, u32[]{:S(2)}, u32[]{:S(2)}) collective-permute-start(bf16[40,1536]{1,0:T(8,128)(2,1)S(1)} %reduce_sum.67), channel_id=1, source_target_pairs={{0,256},{1,259},{4,260},{5,263},{8,264},{9,267},{12,268},{13,271},... | collective-permute-start | bytes 368648 | tf_op jit(solution)/shard_map/ppermute | solution.py:40
  75.4 16.8 %collective-permute-start.5 = (bf16[80,1536]{1,0:T(8,128)(2,1)S(1)}, bf16[80,1536]{1,0:T(8,128)(2,1)S(1)}, u32[]{:S(2)}, u32[]{:S(2)}) collective-permute-start(bf16[80,1536]{1,0:T(8,128)(2,1)S(1)} %slice.129), channel_id=1, source_target_pairs={{0,450},{1,451},{4,454},{5,455},{8,458},{9,459},{12,462},{13,463},... | collective-permute-start | bytes 737288 | tf_op jit(solution)/shard_map/ppermute | solution.py:40
  77.8 24.5 %copy-start.1 = (bf16[40,1536]{1,0:T(8,128)(2,1)}, bf16[40,1536]{1,0:T(8,128)(2,1)S(1)}, u32[]{:S(2)}) copy-start(bf16[40,1536]{1,0:T(8,128)(2,1)S(1)} %collective-permute-done.4) | copy-start | bytes 368644
  79.4 23.0 %copy-start.3 = (bf16[40,1536]{1,0:T(8,128)(2,1)}, bf16[40,1536]{1,0:T(8,128)(2,1)S(1)}, u32[]{:S(2)}) copy-start(bf16[40,1536]{1,0:T(8,128)(2,1)S(1)} %collective-permute-done.3) | copy-start | bytes 368644
  92.2 18.8 %collective-permute-start.8 = (bf16[80,1536]{1,0:T(8,128)(2,1)S(1)}, bf16[80,1536]{1,0:T(8,128)(2,1)S(1)}, u32[]{:S(2)}, u32[]{:S(2)}) collective-permute-start(bf16[80,1536]{1,0:T(8,128)(2,1)S(1)} %collective-permute-done.5), channel_id=1, source_target_pairs={{0,48},{16,32},{32,16},{48,0},{64,112},{80,96},{96,80},{112,64},{1... | collective-permute-start | bytes 737288 | tf_op jit(solution)/shard_map/ppermute | solution.py:112
  96.8 14.2 %collective-permute-start.7 = (bf16[80,1536]{1,0:T(8,128)(2,1)S(1)}, bf16[80,1536]{1,0:T(8,128)(2,1)S(1)}, u32[]{:S(2)}, u32[]{:S(2)}) collective-permute-start(bf16[80,1536]{1,0:T(8,128)(2,1)S(1)} %collective-permute-done.5), channel_id=1, source_target_pairs={{0,32},{16,48},{32,0},{48,16},{64,96},{80,112},{96,64},{112,80},{1... | collective-permute-start | bytes 737288 | tf_op jit(solution)/shard_map/ppermute | solution.py:112
  99.1 12.2 %collective-permute-start.6 = (bf16[80,1536]{1,0:T(8,128)(2,1)S(1)}, bf16[80,1536]{1,0:T(8,128)(2,1)}, u32[]{:S(2)}, u32[]{:S(2)}) collective-permute-start(bf16[80,1536]{1,0:T(8,128)(2,1)S(1)} %collective-permute-done.5), channel_id=1, source_target_pairs={{0,16},{16,0},{32,48},{48,32},{64,80},{80,64},{96,112},{112,96},{1... | collective-permute-start | bytes 737288 | tf_op jit(solution)/shard_map/ppermute | solution.py:112
  102.3 20.1 %all-to-all-start.2 = ((bf16[8,40,1536]{2,1,0:T(8,128)(2,1)}), bf16[8,40,1536]{2,1,0:T(8,128)(2,1)S(1)}, u32[]{:S(2)}, u32[]{:S(2)}) async-start(bf16[8,40,1536]{2,1,0:T(8,128)(2,1)} %broadcast_in_dim.49), calls=%async_computation.2 | async-start | bytes 1966080 | tf_op jit(solution)/shard_map/all_to_all | solution.py:48
  108.0 58.4 %reduce-scatter.3.cloned.1.call-start = ((), (), s32[]{:S(2)}) async-start(), calls=%async_computation.10 | async-start | bytes 1105920 | tf_op jit(solution)/shard_map/reduce_scatter | solution.py:130
  124.6 0.7 copy-start.6
  126.8 1.7 copy-start.7
  130.2 4.5 %copy-start.5 = (bf16[320,288]{0,1:T(8,128)(2,1)S(1)}, bf16[320,288]{0,1:T(8,128)(2,1)}, u32[]{:S(2)}) copy-start(bf16[320,288]{0,1:T(8,128)(2,1)} %fusion.18) | copy-start | bytes 552964
  130.2 18.9 %all-to-all-start.3 = ((bf16[8,40,1536]{2,1,0:T(8,128)(2,1)}), bf16[8,40,1536]{2,1,0:T(8,128)(2,1)S(1)}, u32[]{:S(2)}, u32[]{:S(2)}) async-start(bf16[8,40,1536]{2,1,0:T(8,128)(2,1)} %bitcast.22), calls=%async_computation.3 | async-start | bytes 1966080 | tf_op jit(solution)/shard_map/all_to_all | solution.py:48
  134.6 14.6 %copy-start.2 = (bf16[40,1536]{1,0:T(8,128)(2,1)S(1)}, bf16[40,1536]{1,0:T(8,128)(2,1)}, u32[]{:S(2)}) copy-start(bf16[40,1536]{1,0:T(8,128)(2,1)} %copy-done.1) | copy-start | bytes 368644
  134.7 14.6 %copy-start.4 = (bf16[40,1536]{1,0:T(8,128)(2,1)S(1)}, bf16[40,1536]{1,0:T(8,128)(2,1)}, u32[]{:S(2)}) copy-start(bf16[40,1536]{1,0:T(8,128)(2,1)} %copy-done.3) | copy-start | bytes 368644
  134.7 60.8 %reduce-scatter.5.cloned.1.call-start = ((), (), s32[]{:S(2)}) async-start(), calls=%async_computation.11 | async-start | bytes 1105920 | tf_op jit(solution)/shard_map/reduce_scatter | solution.py:130
  149.5 10.8 %collective-permute-start.10 = (bf16[40,1536]{1,0:T(8,128)(2,1)S(1)}, bf16[40,1536]{1,0:T(8,128)(2,1)S(1)}, u32[]{:S(2)}, u32[]{:S(2)}) collective-permute-start(bf16[40,1536]{1,0:T(8,128)(2,1)S(1)} %multiply_convert_fusion.1), channel_id=1, source_target_pairs={{0,258},{1,257},{4,262},{5,261},{8,266},{9,265},{12,270},{13,269},... | collective-permute-start | bytes 368648 | tf_op jit(solution)/shard_map/ppermute | solution.py:40
  155.4 10.9 %collective-permute-start.9 = (bf16[40,1536]{1,0:T(8,128)(2,1)S(1)}, bf16[40,1536]{1,0:T(8,128)(2,1)S(1)}, u32[]{:S(2)}, u32[]{:S(2)}) collective-permute-start(bf16[40,1536]{1,0:T(8,128)(2,1)S(1)} %multiply_convert_fusion.1), channel_id=1, source_target_pairs={{0,256},{1,259},{4,260},{5,263},{8,264},{9,267},{12,268},{13,271},... | collective-permute-start | bytes 368648 | tf_op jit(solution)/shard_map/ppermute | solution.py:40
  166.4 6.9 %copy-start.8 = (bf16[1,72,1536]{2,1,0:T(8,128)(2,1)S(1)}, bf16[1,72,1536]{2,1,0:T(8,128)(2,1)}, u32[]{:S(2)}) copy-start(bf16[1,72,1536]{2,1,0:T(8,128)(2,1)} %reduce-scatter.3.cloned.1.call-done) | copy-start | bytes 663556
  167.5 20.1 %all-to-all-start.4 = ((bf16[8,40,1536]{2,1,0:T(8,128)(2,1)}), bf16[8,40,1536]{2,1,0:T(8,128)(2,1)S(1)}, u32[]{:S(2)}, u32[]{:S(2)}) async-start(bf16[8,40,1536]{2,1,0:T(8,128)(2,1)} %broadcast_in_dim.50), calls=%async_computation.5 | async-start | bytes 1966080 | tf_op jit(solution)/shard_map/all_to_all | solution.py:48
  173.3 12.2 %collective-permute-start.11 = (bf16[72,1536]{1,0:T(8,128)(2,1)S(1)}, bf16[72,1536]{1,0:T(8,128)(2,1)S(1)}, u32[]{:S(2)}, u32[]{:S(2)}) collective-permute-start(bf16[72,1536]{1,0:T(8,128)(2,1)S(1)} %bitcast.111), channel_id=1, source_target_pairs={{0,450},{1,451},{4,454},{5,455},{8,458},{9,459},{12,462},{13,463},... | collective-permute-start | bytes 663560 | tf_op jit(solution)/shard_map/ppermute | solution.py:40
  188.7 17.9 %all-to-all-start.5 = ((bf16[16,24,384]{2,1,0:T(8,128)(2,1)}), bf16[16,24,384]{2,1,0:T(8,128)(2,1)S(1)}, u32[]{:S(2)}, u32[]{:S(2)}) async-start(bf16[16,24,384]{2,1,0:T(8,128)(2,1)} %bitcast.30), calls=%async_computation.7 | async-start | bytes 589824 | tf_op jit(solution)/shard_map/all_to_all | solution.py:48
  196.5 13.5 %collective-permute-start.13 = (bf16[18,1536]{1,0:T(8,128)(2,1)S(1)}, bf16[18,1536]{1,0:T(8,128)(2,1)S(1)}, u32[]{:S(2)}, u32[]{:S(2)}) collective-permute-start(bf16[18,1536]{1,0:T(8,128)(2,1)S(1)} %select_convert_fusion.1), channel_id=1, source_target_pairs={{0,128},{1,129},{4,132},{5,133},{8,136},{9,137},{12,140},{13,141},... | collective-permute-start | bytes 165896 | tf_op jit(solution)/shard_map/ppermute | solution.py:40
  200.8 9.3 %collective-permute-start.14 = (bf16[18,1536]{1,0:T(8,128)(2,1)S(1)}, bf16[18,1536]{1,0:T(8,128)(2,1)S(1)}, u32[]{:S(2)}, u32[]{:S(2)}) collective-permute-start(bf16[18,1536]{1,0:T(8,128)(2,1)S(1)} %get-tuple-element.51), channel_id=1, source_target_pairs={{0,192},{1,193},{4,196},{5,197},{8,200},{9,201},{12,204},{13,205},... | collective-permute-start | bytes 165896 | tf_op jit(solution)/shard_map/ppermute | solution.py:40
  203.9 13.9 %collective-permute-start.12 = (bf16[18,1536]{1,0:T(8,128)(2,1)S(1)}, bf16[18,1536]{1,0:T(8,128)(2,1)S(1)}, u32[]{:S(2)}, u32[]{:S(2)}) collective-permute-start(bf16[18,1536]{1,0:T(8,128)(2,1)S(1)} %get-tuple-element.52), channel_id=1, source_target_pairs={{0,64},{1,65},{4,68},{5,69},{8,72},{9,73},{12,76},{13,77},{16,80},... | collective-permute-start | bytes 165896 | tf_op jit(solution)/shard_map/ppermute | solution.py:40
  217.7 8.5 %collective-permute-start.16 = (bf16[24,384]{1,0:T(8,128)(2,1)S(1)}, bf16[24,384]{1,0:T(8,128)(2,1)S(1)}, u32[]{:S(2)}, u32[]{:S(2)}) collective-permute-start(bf16[24,384]{1,0:T(8,128)(2,1)S(1)} %reduce-precision_convert_fusion), channel_id=1, source_target_pairs={{0,256},{16,272},{32,288},{48,304},{64,320},{80,336},{96,352},{112... | collective-permute-start | bytes 55304 | tf_op jit(solution)/shard_map/ppermute | solution.py:151
  227.0 18.0 %all-to-all-start.6 = ((bf16[16,24,384]{2,1,0:T(8,128)(2,1)}), bf16[16,24,384]{2,1,0:T(8,128)(2,1)S(1)}, u32[]{:S(2)}, u32[]{:S(2)}) async-start(bf16[16,24,384]{2,1,0:T(8,128)(2,1)} %broadcast_in_dim.51), calls=%async_computation.8 | async-start | bytes 589824 | tf_op jit(solution)/shard_map/all_to_all | solution.py:48
  231.5 13.4 %collective-permute-start.15 = (bf16[8,18,96]{2,0,1:T(8,128)(2,1)S(1)}, bf16[8,18,96]{2,0,1:T(8,128)(2,1)S(1)}, u32[]{:S(2)}, u32[]{:S(2)}) collective-permute-start(bf16[8,18,96]{2,0,1:T(8,128)(2,1)S(1)} %bitcast.109), channel_id=1, source_target_pairs={{0,2},{1,3},{2,0},{3,1},{4,6},{5,7},{6,4},{7,5},{8,10},{9,11},{10,... | collective-permute-start | bytes 82952 | tf_op jit(solution)/shard_map/ppermute | solution.py:162
  245.6 13.5 %all-to-all-start.7 = ((bf16[8,36,96]{2,1,0:T(8,128)(2,1)}), bf16[8,36,96]{2,1,0:T(8,128)(2,1)S(1)}, u32[]{:S(2)}, u32[]{:S(2)}) async-start(bf16[8,36,96]{2,1,0:T(8,128)(2,1)} %copy.53), calls=%async_computation.9 | async-start | bytes 163840 | tf_op jit(solution)/shard_map/all_to_all | solution.py:48
Sparse Core Ops, SparseCore 0:
  74.6 31.8 all-gather.2
  126.9 25.3 reduce-scatter.2
  155.2 30.3 reduce-scatter.4
